TPU v7x, 32 devices: a whole 2x2x4 slice. The times are simulated.
32 devices in a mesh: gx: 8 (over y, x, core), gy: 4 (over z).
Axes of the slice: x: 2, y: 2, z: 4, core: 2. Of those that a mesh axis runs over, the one named last changes fastest.
Arguments:
- points: bfloat16 [32768, 64], P(('gx', 'gy')), may hold values from -6 to 6
- pivots: int32 [2, 128], replicated, may hold values from 0 to 1023, as said below
- owners: int32 [2], replicated, may hold values from 0 to 31
- coeffs: float32 [256, 64], replicated, may hold values from -6 to 6
- noise: float32 [32768, 64], P(('gx', 'gy')), may hold values from -4 to 4
Outputs:
- kernel_probes: float32 [32768, 64], P(('gx', 'gy'))
- factor: float32 [32768, 256], P(('gx', 'gy'))
Inputs may be any that keep to these rules, and one draw needn't show every extreme that they name: `pivots`: the two rows together hold 256 distinct indices, among them 0 and 1023.
All inputs are finite; a program needn't handle non-finite values.
Results may differ from a plain program's by a relative error of at most 0.0003.
Values may be sent and summed in bfloat16 or wider, within the bound.
No kernel may reach another device: no remote copies, remote signals or barrier semaphores. Data moves between devices by JAX's collectives and lax.ppermute only.
A program may use at most 64 MiB of HBM per device.

v0:
```python
import jax
import jax.numpy as jnp
from jax import lax
from jax.sharding import PartitionSpec as P

PIVOTS = 128
KERNEL_SCALE = 32


jitter = 0.1
noise_weight = 0.5


def spread(value, axis, source):
    kept = jnp.where(lax.axis_index(axis) == source, value, 0).astype(value.dtype)
    return lax.psum(kept, axis)


def passed_along(value, axis, steps):
    count = lax.axis_size(axis)
    pairs = [(source, (source + steps) % count) for source in range(count)]
    return lax.ppermute(value, axis, pairs)


def kern(left, right):
    left_square_norm = jnp.sum(jnp.square(left.astype(jnp.float32)), axis=1)
    right_square_norm = jnp.sum(jnp.square(right.astype(jnp.float32)), axis=1)
    cross_term = jnp.dot(left, right.T, preferred_element_type=jnp.float32)
    return jnp.exp(
        -(left_square_norm[:, None] + right_square_norm[None, :] - 2.0 * cross_term)
        / (1.0 * KERNEL_SCALE)
    )


def shards(points, pivots, owners, coeffs, noise):
    hp = lax.Precision.HIGHEST
    solve = jax.scipy.linalg.solve_triangular
    width = points.shape[1]
    count = points.shape[0]
    ident = jnp.eye(PIVOTS, dtype=jnp.float32)
    first = spread(points[pivots[0]], ("gx", "gy"), owners[0])
    second = spread(points[pivots[1]], ("gx", "gy"), owners[1])
    chol_one = jnp.linalg.cholesky(kern(first, first) + jitter * ident)
    first_cols = solve(chol_one, kern(points, first).T, lower=True).T
    rows = solve(chol_one, kern(second, first).T, lower=True).T
    chol_two = jnp.linalg.cholesky(
        kern(second, second) - jnp.dot(rows, rows.T, precision=hp) + jitter * ident
    )
    residual_cols = kern(points, second) - jnp.dot(first_cols, rows.T, precision=hp)
    second_cols = solve(chol_two, residual_cols.T, lower=True).T
    factor = jnp.concatenate([first_cols, second_cols], axis=1)
    probes = jnp.dot(factor, coeffs, precision=hp, preferred_element_type=jnp.float32) + noise
    packed = jnp.concatenate([points, probes.astype(jnp.bfloat16)], axis=1)

    def contribute(total, piece):
        tile = kern(points, piece[:, :width]).astype(jnp.bfloat16)
        return total + jnp.dot(tile, piece[:, width:], preferred_element_type=jnp.float32)

    total = contribute(jnp.zeros((count, probes.shape[1]), jnp.float32), packed)
    piece = passed_along(packed, ("gx", "gy"), -3)
    total = contribute(total, piece)
    for stop_index in range(5):
        if stop_index == 2:
            piece = passed_along(piece, ("gx", "gy"), 2)
        else:
            piece = passed_along(piece, ("gx", "gy"), 1)
        total = contribute(total, piece)
    kernel_probes = total / jnp.sqrt(1.0 * count) + noise_weight * probes
    return (kernel_probes, factor)


def solution(mesh):
    in_specs = (P(("gx", "gy"), None), P(), P(), P(), P(("gx", "gy"), None))
    out_specs = (P(("gx", "gy"), None), P(("gx", "gy"), None))
    return jax.shard_map(shards, mesh=mesh, in_specs=in_specs, out_specs=out_specs, check_vma=False)
```

profile of v0, /device:TPU:0, one launch (start us, length us, event | category | flops | bytes accessed | tf_op | source)
XLA Modules:
  0.0 165.7 jit_solution(12636152769345428454)
XLA Ops:
  0.7 1.1 copy.9
  1.8 0.9 multiply_reduce_fusion.6
  2.7 0.8 fusion.88
  3.5 1.3 fusion.104
  4.8 0.7 gather_fusion.1
  5.5 0.7 gather_fusion
  7.6 42.5 %all-reduce = (bf16[128,64]{1,0:T(8,128)(2,1)S(1)}, bf16[128,64]{1,0:T(8,128)(2,1)S(1)}) all-reduce(bf16[128,64]{1,0:T(8,128)(2,1)S(1)} %broadcast_select_fusion, bf16[128,64]{1,0:T(8,128)(2,1)S(1)} %broadcast_select_fusion.1), channel_id=1, replica_groups=mesh['gx'=8,'gy'=4] {'gx','gy'}, use_global_device_ids=true, to_apply=%region_5.0 | all-reduce | flops 16384 | bytes 65536 | tf_op jit(solution)/shard_map/psum | solution.py:16
  51.5 11.7 %cholesky.44 = f32[128,128]{1,0:T(8,128)S(1)} custom-call(f32[128,128]{1,0:T(8,128)S(1)} %fusion.87), custom_call_target="Cholesky" | custom-call | tf_op jit(solution)/shard_map/jit(cholesky)/cholesky | solution.py:43
  63.4 0.6 compare_reduce_fusion.1
  64.1 0.7 fusion.79
  64.8 9.8 %custom-call.11 = f32[1,128,128]{1,2,0:T(8,128)S(1)} custom-call(f32[1,128,128]{2,1,0:T(8,128)S(1)} %copy.14), custom_call_target="InvertDiagBlocksLowerTriangular" | custom-call | tf_op jit(solution)/shard_map/jit(_solve_triangular)/triangular_solve | solution.py:44
  76.0 11.7 %cholesky.55 = f32[128,128]{1,0:T(8,128)S(1)} custom-call(f32[128,128]{1,0:T(8,128)S(1)} %fusion.82), custom_call_target="Cholesky" | custom-call | tf_op jit(solution)/shard_map/jit(cholesky)/cholesky | solution.py:46
  87.8 0.6 compare_reduce_fusion
  88.4 0.7 fusion.80
  89.1 10.0 %custom-call.12 = f32[1,128,128]{1,2,0:T(8,128)S(1)} custom-call(f32[1,128,128]{2,1,0:T(8,128)S(1)} %fusion.80), custom_call_target="InvertDiagBlocksLowerTriangular" | custom-call | tf_op jit(solution)/shard_map/jit(_solve_triangular)/triangular_solve | solution.py:50
  99.7 0.6 convolution_bitcast_fusion
  100.3 0.8 fusion.105
  101.2 1.9 %collective-permute-start = (bf16[1024,128]{0,1:T(8,128)(2,1)S(1)}, bf16[1024,128]{0,1:T(8,128)(2,1)S(1)}, u32[]{:S(2)}, u32[]{:S(2)}) collective-permute-start(bf16[1024,128]{0,1:T(8,128)(2,1)S(1)} %pad_maximum_fusion.1), channel_id=1, source_target_pairs={{0,29},{1,30},{2,31},{3,0},{4,1},{5,2},{6,3},{7,4},{8,5},{9,6},{10... | collective-permute-start | bytes 786440 | tf_op jit(solution)/shard_map/ppermute | solution.py:22
  103.2 1.3 copy.20
  104.5 1.4 fusion.24
  105.9 4.3 %collective-permute-done = bf16[1024,128]{0,1:T(8,128)(2,1)S(1)} collective-permute-done((bf16[1024,128]{0,1:T(8,128)(2,1)S(1)}, bf16[1024,128]{0,1:T(8,128)(2,1)S(1)}, u32[]{:S(2)}, u32[]{:S(2)}) %collective-permute-start) | collective-permute-done | bytes 262176 | tf_op jit(solution)/shard_map/ppermute | solution.py:22
  110.5 1.6 fusion.46
  112.2 8.6 %collective-permute-done.1 = bf16[1024,128]{0,1:T(8,128)(2,1)S(1)} collective-permute-done((bf16[1024,128]{0,1:T(8,128)(2,1)S(1)}, bf16[1024,128]{0,1:T(8,128)(2,1)S(1)}, u32[]{:S(2)}, u32[]{:S(2)}) %collective-permute-start.1) | collective-permute-done | bytes 262176 | tf_op jit(solution)/shard_map/ppermute | solution.py:22
  120.9 1.6 fusion.45
  122.6 7.7 %collective-permute-done.2 = bf16[1024,128]{0,1:T(8,128)(2,1)S(1)} collective-permute-done((bf16[1024,128]{0,1:T(8,128)(2,1)S(1)}, bf16[1024,128]{0,1:T(8,128)(2,1)S(1)}, u32[]{:S(2)}, u32[]{:S(2)}) %collective-permute-start.2) | collective-permute-done | bytes 262176 | tf_op jit(solution)/shard_map/ppermute | solution.py:22
  130.4 1.6 fusion.44
  132.1 10.8 %collective-permute-done.3 = bf16[1024,128]{0,1:T(8,128)(2,1)S(1)} collective-permute-done((bf16[1024,128]{0,1:T(8,128)(2,1)S(1)}, bf16[1024,128]{0,1:T(8,128)(2,1)S(1)}, u32[]{:S(2)}, u32[]{:S(2)}) %collective-permute-start.3) | collective-permute-done | bytes 262176 | tf_op jit(solution)/shard_map/ppermute | solution.py:22
  143.0 1.6 fusion.43
  144.6 8.9 %collective-permute-done.4 = bf16[1024,128]{0,1:T(8,128)(2,1)S(1)} collective-permute-done((bf16[1024,128]{0,1:T(8,128)(2,1)S(1)}, bf16[1024,128]{0,1:T(8,128)(2,1)S(1)}, u32[]{:S(2)}, u32[]{:S(2)}) %collective-permute-start.4) | collective-permute-done | bytes 262176 | tf_op jit(solution)/shard_map/ppermute | solution.py:22
  153.9 1.6 fusion.42
  155.6 7.7 %collective-permute-done.5 = bf16[1024,128]{0,1:T(8,128)(2,1)S(1)} collective-permute-done((bf16[1024,128]{0,1:T(8,128)(2,1)S(1)}, bf16[1024,128]{0,1:T(8,128)(2,1)S(1)}, u32[]{:S(2)}, u32[]{:S(2)}) %collective-permute-start.5) | collective-permute-done | bytes 262176 | tf_op jit(solution)/shard_map/ppermute | solution.py:22
  163.3 2.3 %fusion.41 = f32[1024,64]{0,1:T(8,128)} fusion(f32[1024,64]{0,1:T(8,128)S(1)} %fusion.42, bf16[1024,64]{0,1:T(8,128)(2,1)S(1)} %copy-done.1, f32[1024]{0:T(1024)S(1)} %multiply_reduce_fusion, f32[1024]{0:T(1024)S(1)} %multiply_reduce_fusion.6, f32[1024,64]{0,1:T(8,128)S(1)} %get-tuple-element.13, bf16[1024,128]{0,1:T(8,128)(2,1)S(1)} %collective-permute-done.5), kind=kOutput, calls=%fused_computation.55 | convolution fusion | flops 274989056 | bytes 1187840 | tf_op jit(solution)/shard_map/dot_general | solution.py:57
  (41 shorter events, 4.7 us)
Async XLA Ops:
  0.6 99.7 %copy-start = (f32[256,64]{0,1:T(8,128)S(1)}, f32[256,64]{0,1:T(8,128)}, u32[]{:S(2)}) copy-start(f32[256,64]{0,1:T(8,128)} %param.11) | copy-start | bytes 196612
  0.6 50.1 %copy-start.1 = (bf16[1024,64]{0,1:T(8,128)(2,1)S(1)}, bf16[1024,64]{0,1:T(8,128)(2,1)}, u32[]{:S(2)}) copy-start(bf16[1024,64]{0,1:T(8,128)(2,1)} %param.8) | copy-start | bytes 393220
  99.0 1.3 copy-start.2
  101.2 9.1 %collective-permute-start = (bf16[1024,128]{0,1:T(8,128)(2,1)S(1)}, bf16[1024,128]{0,1:T(8,128)(2,1)S(1)}, u32[]{:S(2)}, u32[]{:S(2)}) collective-permute-start(bf16[1024,128]{0,1:T(8,128)(2,1)S(1)} %pad_maximum_fusion.1), channel_id=1, source_target_pairs={{0,29},{1,30},{2,31},{3,0},{4,1},{5,2},{6,3},{7,4},{8,5},{9,6},{10... | collective-permute-start | bytes 786440 | tf_op jit(solution)/shard_map/ppermute | solution.py:22
  110.3 10.5 %collective-permute-start.1 = (bf16[1024,128]{0,1:T(8,128)(2,1)S(1)}, bf16[1024,128]{0,1:T(8,128)(2,1)S(1)}, u32[]{:S(2)}, u32[]{:S(2)}) collective-permute-start(bf16[1024,128]{0,1:T(8,128)(2,1)S(1)} %collective-permute-done), channel_id=1, source_target_pairs={{0,1},{1,2},{2,3},{3,4},{4,5},{5,6},{6,7},{7,8},{8,9},{9,10},{10,1... | collective-permute-start | bytes 786440 | tf_op jit(solution)/shard_map/ppermute | solution.py:22
  120.9 9.5 %collective-permute-start.2 = (bf16[1024,128]{0,1:T(8,128)(2,1)S(1)}, bf16[1024,128]{0,1:T(8,128)(2,1)S(1)}, u32[]{:S(2)}, u32[]{:S(2)}) collective-permute-start(bf16[1024,128]{0,1:T(8,128)(2,1)S(1)} %collective-permute-done.1), channel_id=1, source_target_pairs={{0,1},{1,2},{2,3},{3,4},{4,5},{5,6},{6,7},{7,8},{8,9},{9,10},{10,1... | collective-permute-start | bytes 786440 | tf_op jit(solution)/shard_map/ppermute | solution.py:22
  130.4 12.5 %collective-permute-start.3 = (bf16[1024,128]{0,1:T(8,128)(2,1)S(1)}, bf16[1024,128]{0,1:T(8,128)(2,1)S(1)}, u32[]{:S(2)}, u32[]{:S(2)}) collective-permute-start(bf16[1024,128]{0,1:T(8,128)(2,1)S(1)} %collective-permute-done.2), channel_id=1, source_target_pairs={{0,2},{1,3},{2,4},{3,5},{4,6},{5,7},{6,8},{7,9},{8,10},{9,11},{10,... | collective-permute-start | bytes 786440 | tf_op jit(solution)/shard_map/ppermute | solution.py:22
  142.9 10.7 %collective-permute-start.4 = (bf16[1024,128]{0,1:T(8,128)(2,1)S(1)}, bf16[1024,128]{0,1:T(8,128)(2,1)S(1)}, u32[]{:S(2)}, u32[]{:S(2)}) collective-permute-start(bf16[1024,128]{0,1:T(8,128)(2,1)S(1)} %collective-permute-done.3), channel_id=1, source_target_pairs={{0,1},{1,2},{2,3},{3,4},{4,5},{5,6},{6,7},{7,8},{8,9},{9,10},{10,1... | collective-permute-start | bytes 786440 | tf_op jit(solution)/shard_map/ppermute | solution.py:22
  153.6 9.7 %collective-permute-start.5 = (bf16[1024,128]{0,1:T(8,128)(2,1)S(1)}, bf16[1024,128]{0,1:T(8,128)(2,1)S(1)}, u32[]{:S(2)}, u32[]{:S(2)}) collective-permute-start(bf16[1024,128]{0,1:T(8,128)(2,1)S(1)} %collective-permute-done.4), channel_id=1, source_target_pairs={{0,1},{1,2},{2,3},{3,4},{4,5},{5,6},{6,7},{7,8},{8,9},{9,10},{10,1... | collective-permute-start | bytes 786440 | tf_op jit(solution)/shard_map/ppermute | solution.py:22
where the time goes:
time: 166 us
  other arithmetic  48.3 us (29%)
  waiting for transfers between devices  48.2 us (29%)
  blocking collectives  42.5 us (26%)
  matrix products  16.2 us (10%)
  local copies, waits for them, and re-layouts  5.55 us (3%)
  starting transfers between devices  2.63 us (2%)
  between operations  2.26 us (1%)
    ppermute x6, waiting for transfers between devices, passed_along(): return lax.ppermute(value, axis, pairs)  48.2 us
    psum x1, blocking collectives, spread(): return lax.psum(kept, axis)  42.5 us
    another operation x3, other arithmetic, shards(): chol_one = jnp.linalg.cholesky(kern(first, first) + jitter * ident)  12.5 us
    another operation x3, other arithmetic, shards(): jnp.linalg.cholesky(kern(second, second) - jnp.dot(rows, rows.T, precisio...  12.4 us
    dot_general x7, matrix products, contribute(): jnp.dot(tile, piece[:, width:], preferred_element_type=jnp.float32)  12 us
    another operation x2, other arithmetic, shards(): second_cols = solve(chol_two, residual_cols.T, lower=True).T  10.6 us
    another operation x2, other arithmetic, shards(): first_cols = solve(chol_one, kern(points, first).T, lower=True).T  10.5 us
  transfers between devices with their start and end apart: 6, of which 6 were waited for; matrix products, arithmetic and copies ran while one was open for 7% of the time, Pallas kernels for 0%

commit v1 on v0

v1 whole, which is shorter than its diff:
```python
import jax
import jax.numpy as jnp
from jax import lax
from jax.sharding import PartitionSpec as P

PIVOTS = 128
KERNEL_SCALE = 32
BAND = 3


jitter = 0.1
noise_weight = 0.5


def shifted(value, axis, steps):
    count = lax.axis_size(axis)
    return lax.ppermute(value, axis, [((i + steps) % count, i) for i in range(count)])


def summed(value, axis):
    count = lax.axis_size(axis)
    if count > 8:
        return lax.psum(value, axis)
    total = value
    for steps in range(1, count):
        total = total + shifted(value, axis, steps)
    return total


def kern(left, right):
    left_square_norm = jnp.sum(jnp.square(left.astype(jnp.float32)), axis=1)
    right_square_norm = jnp.sum(jnp.square(right.astype(jnp.float32)), axis=1)
    cross_term = jnp.dot(left, right.T, preferred_element_type=jnp.float32)
    return jnp.exp(
        -(left_square_norm[:, None] + right_square_norm[None, :] - 2.0 * cross_term)
        / (1.0 * KERNEL_SCALE)
    )


def neighbours(value, tall):
    outer, inner = lax.axis_size("gx"), lax.axis_size("gy")
    if not tall:
        return [shifted(value, ("gx", "gy"), k) for k in range(-BAND, BAND + 1) if k != 0]
    own, other = [], []
    for k in range(1, inner):
        own.append(shifted(value, "gy", k))
    for k in range(1, inner):
        pairs = []
        for x in range(outer):
            for z in range(inner):
                source = (x - 1 if z + k < inner else x + 1) % outer
                pairs.append((source * inner + z, x * inner + z))
        other.append(lax.ppermute(own[k - 1], ("gx", "gy"), pairs))
    return own + other


def shards(points, pivots, owners, coeffs, noise):
    hp = lax.Precision.HIGHEST
    solve = jax.scipy.linalg.solve_triangular
    count, width = points.shape
    tall = lax.axis_size("gy") == BAND + 1
    me = lax.axis_index(("gx", "gy"))

    index = lax.broadcasted_iota(jnp.int32, (2, PIVOTS, count), 2)
    wanted = jnp.where((owners == me)[:, None], pivots, -1)
    chosen = (index == wanted[:, :, None]).astype(jnp.bfloat16).reshape(2 * PIVOTS, count)
    picked = jnp.dot(chosen, points, preferred_element_type=jnp.float32).astype(jnp.bfloat16)
    pivot_points = summed(summed(picked, "gy"), "gx")
    near_points = neighbours(points, tall)

    size = 2 * PIVOTS
    ident = jnp.eye(size, dtype=jnp.float32)
    chol = jnp.linalg.cholesky(kern(pivot_points, pivot_points) + jitter * ident)
    inverse = solve(chol, ident, lower=True)
    cols = kern(points, pivot_points)
    weights = jnp.dot(inverse.T, coeffs, precision=hp)
    probes = jnp.dot(cols, weights, precision=hp, preferred_element_type=jnp.float32) + noise
    sent = probes.astype(jnp.bfloat16)
    near_probes = neighbours(sent, tall)
    factor = jnp.dot(cols, inverse.T, precision=hp, preferred_element_type=jnp.float32)

    total = jnp.zeros((count, probes.shape[1]), jnp.float32)
    for other, probe in zip([points] + near_points, [sent] + near_probes):
        tile = kern(points, other).astype(jnp.bfloat16)
        total = total + jnp.dot(tile, probe, preferred_element_type=jnp.float32)
    kernel_probes = total / jnp.sqrt(1.0 * count) + noise_weight * probes
    return (kernel_probes, factor)


def solution(mesh):
    in_specs = (P(("gx", "gy"), None), P(), P(), P(), P(("gx", "gy"), None))
    out_specs = (P(("gx", "gy"), None), P(("gx", "gy"), None))
    return jax.shard_map(shards, mesh=mesh, in_specs=in_specs, out_specs=out_specs, check_vma=False)
```

time: 166 us -> 118 us (0.71)
  blocking collectives: 42.5 us -> 0 us
  waiting for transfers between devices: 48.2 us -> 12.9 us
  starting transfers between devices: 2.63 us -> 22.3 us
  other arithmetic: 48.3 us -> 56.6 us
  matrix products: 16.2 us -> 19.3 us
    psum x1 -> x0, blocking collectives: 42.5 us -> none  [spread(): return lax.psum(kept, axis)]
    ppermute x6 -> x22, waiting for transfers between devices: 48.2 us -> 12.9 us  [the longest x16 12.2 us: shifted(): lax.ppermute(value, axis, [((i + steps) % count, i) for i in range(count)])]
    ppermute x6 -> x22, starting transfers between devices: 2.63 us -> 22.3 us  [the longest x16 18.4 us: shifted(): lax.ppermute(value, axis, [((i + steps) % count, i) for i in range(count)])]
    another operation x10 -> x9, other arithmetic: 45.9 us -> 53.7 us  [the longest x6 34 us: shards(): jnp.linalg.cholesky(kern(pivot_points, pivot_points) + jitter * ident)]
    another operation x2 -> x9, local copies, waits for them, and re-layouts: 0.18 us -> 4.15 us  [the longest x1 0.09 us: shards(): chol_one = jnp.linalg.cholesky(kern(first, first) + jitter * ident)]
    dot_general x10 -> x11, matrix products: 13.7 us -> 17.3 us  [the longest x7 11.9 us: shards(): total = total + jnp.dot(tile, probe, preferred_element_type=jnp.float32)]
    unnamed x8 -> x6, local copies, waits for them, and re-layouts: 2.47 us -> 0.02 us
  transfers between devices with their start and end apart: 6 -> 22, of which waited for: 6 -> 9; matrix products, arithmetic and copies ran while one was open for 7% -> 64% of each run, Pallas kernels for 0% -> 0%
where the time goes in v1:
time: 118 us
  other arithmetic  56.6 us (48%)
  starting transfers between devices  22.3 us (19%)
  matrix products  19.3 us (16%)
  waiting for transfers between devices  12.9 us (11%)
  local copies, waits for them, and re-layouts  4.43 us (4%)
  between operations  2.29 us (2%)
    another operation x6, other arithmetic, shards(): jnp.linalg.cholesky(kern(pivot_points, pivot_points) + jitter * ident)  34 us
    another operation x3, other arithmetic, shards(): inverse = solve(chol, ident, lower=True)  19.7 us
    ppermute x16, starting transfers between devices, shifted(): lax.ppermute(value, axis, [((i + steps) % count, i) for i in range(count)])  18.4 us
    ppermute x16, waiting for transfers between devices, shifted(): lax.ppermute(value, axis, [((i + steps) % count, i) for i in range(count)])  12.2 us
    dot_general x7, matrix products, shards(): total = total + jnp.dot(tile, probe, preferred_element_type=jnp.float32)  11.9 us
    another operation x6, local copies, waits for them, and re-layouts  4.06 us
    ppermute x6, starting transfers between devices, neighbours(): other.append(lax.ppermute(own[k - 1], ('gx', 'gy'), pairs))  3.92 us
    dot_general x1, matrix products, shards(): jnp.dot(cols, inverse.T, precision=hp, preferred_element_type=jnp.float32)  2.79 us
  transfers between devices with their start and end apart: 22, of which 9 were waited for; matrix products, arithmetic and copies ran while one was open for 64% of the time, Pallas kernels for 0%

profile of v1, /device:TPU:0, one launch (start us, length us, event | category | flops | bytes accessed | tf_op | source)
XLA Modules:
  0.0 117.9 jit_solution(7890774038140885137)
XLA Ops:
  2.1 1.3 %convolution_convert_fusion = bf16[256,64]{0,1:T(8,128)(2,1)S(1)} fusion(bf16[1024,64]{0,1:T(8,128)(2,1)} %param.5, s32[256]{0:T(256)S(1)} %select_bitcast_fusion.1), kind=kOutput, calls=%fused_computation.34 | convolution fusion | flops 33832960 | bytes 164864 | tf_op jit(solution)/shard_map/dot_general | solution.py:67
  3.4 5.1 %collective-permute-start = (bf16[256,64]{0,1:T(8,128)(2,1)S(1)}, bf16[256,64]{0,1:T(8,128)(2,1)S(1)}, u32[]{:S(2)}, u32[]{:S(2)}) collective-permute-start(bf16[256,64]{0,1:T(8,128)(2,1)S(1)} %convolution_convert_fusion), channel_id=1, source_target_pairs={{1,0},{2,1},{3,2},{0,3},{5,4},{6,5},{7,6},{4,7},{9,8},{10,9},{11,1... | collective-permute-start | bytes 98312 | tf_op jit(solution)/shard_map/ppermute | solution.py:17
  8.5 1.0 collective-permute-start.2
  9.5 0.9 multiply_reduce_fusion.6
  10.4 2.8 %collective-permute-done.1 = bf16[256,64]{0,1:T(8,128)(2,1)S(1)} collective-permute-done((bf16[256,64]{0,1:T(8,128)(2,1)S(1)}, bf16[256,64]{0,1:T(8,128)(2,1)S(1)}, u32[]{:S(2)}, u32[]{:S(2)}) %collective-permute-start.1) | collective-permute-done | bytes 32800 | tf_op jit(solution)/shard_map/ppermute | solution.py:17
  14.7 2.1 %collective-permute-start.4 = (bf16[256,64]{0,1:T(8,128)(2,1)S(1)}, bf16[256,64]{0,1:T(8,128)(2,1)S(1)}, u32[]{:S(2)}, u32[]{:S(2)}) collective-permute-start(bf16[256,64]{0,1:T(8,128)(2,1)S(1)} %add_add_fusion.1), channel_id=1, source_target_pairs={{8,0},{12,4},{16,8},{20,12},{24,16},{28,20},{0,24},{4,28},{9,1},{1... | collective-permute-start | bytes 98312 | tf_op jit(solution)/shard_map/ppermute | solution.py:17
  17.1 1.5 %collective-permute-start.6 = (bf16[256,64]{0,1:T(8,128)(2,1)S(1)}, bf16[256,64]{0,1:T(8,128)(2,1)S(1)}, u32[]{:S(2)}, u32[]{:S(2)}) collective-permute-start(bf16[256,64]{0,1:T(8,128)(2,1)S(1)} %add_add_fusion.1), channel_id=1, source_target_pairs={{16,0},{20,4},{24,8},{28,12},{0,16},{4,20},{8,24},{12,28},{17,1},{... | collective-permute-start | bytes 98312 | tf_op jit(solution)/shard_map/ppermute | solution.py:17
  18.8 1.5 %collective-permute-start.8 = (bf16[256,64]{0,1:T(8,128)(2,1)S(1)}, bf16[256,64]{0,1:T(8,128)(2,1)S(1)}, u32[]{:S(2)}, u32[]{:S(2)}) collective-permute-start(bf16[256,64]{0,1:T(8,128)(2,1)S(1)} %add_add_fusion.1), channel_id=1, source_target_pairs={{24,0},{28,4},{0,8},{4,12},{8,16},{12,20},{16,24},{20,28},{25,1},{... | collective-permute-start | bytes 98312 | tf_op jit(solution)/shard_map/ppermute | solution.py:17
  21.1 1.3 %collective-permute-start.14 = (bf16[1024,64]{0,1:T(8,128)(2,1)}, bf16[1024,64]{0,1:T(8,128)(2,1)S(1)}, u32[]{:S(2)}, u32[]{:S(2)}) collective-permute-start(bf16[1024,64]{0,1:T(8,128)(2,1)} %param.5), channel_id=1, source_target_pairs={{3,0},{0,1},{1,2},{2,3},{7,4},{4,5},{5,6},{6,7},{11,8},{8,9},{9,10... | collective-permute-start | bytes 393224 | tf_op jit(solution)/shard_map/ppermute | solution.py:17
  22.4 1.1 collective-permute-start.12
  25.3 11.7 %cholesky.49 = f32[128,128]{1,0:T(8,128)S(1)} custom-call(f32[128,128]{1,0:T(8,128)S(1)} %cholesky.115), custom_call_target="Cholesky" | custom-call | tf_op jit(solution)/shard_map/jit(cholesky)/cholesky | solution.py:73
  37.0 9.8 %custom-call.15 = f32[1,128,128]{1,2,0:T(8,128)S(1)} custom-call(f32[1,128,128]{2,1,0:T(8,128)S(1)} %get-tuple-element.25), custom_call_target="InvertDiagBlocksLowerTriangular" | custom-call | tf_op jit(solution)/shard_map/jit(cholesky)/cholesky | solution.py:73
  47.3 11.7 %cholesky.103 = f32[128,128]{1,0:T(8,128)S(1)} custom-call(f32[128,128]{1,0:T(8,128)S(1)} %convolution_subtract_fusion.1), custom_call_target="Cholesky" | custom-call | tf_op jit(solution)/shard_map/jit(cholesky)/cholesky | solution.py:73
  61.3 4.2 %while.1 = (s32[]{:T(128)}, f32[256,256]{1,0:T(8,128)S(1)}, s32[2,2]{1,0:T(2,128)S(1)}, f32[2,128,128]{2,1,0:T(8,128)S(1)}, s32[]{:T(128)}) while((s32[]{:T(128)}, f32[256,256]{1,0:T(8,128)S(1)}, s32[2,2]{1,0:T(2,128)S(1)}, f32[2,128,128]{2,1,0:T(8,128)S(1)}, s32[]{:T(128)}) %tuple.31), condition=%wide.while_cond, body=%wide.while_body.sunk | while | flops 2 | bytes 131181 | solution.py:74
  62.0 1.4 %bitcast_dynamic-update-slice_fusion.2 = f32[2,128,128]{2,1,0:T(8,128)S(1)} fusion(f32[2,128,128]{2,1,0:T(8,128)S(1)} %get-tuple-element.72, s32[]{:T(128)} %get-tuple-element.69, f32[256,256]{1,0:T(8,128)S(1)} %get-tuple-element.75, s32[]{:T(128)} %bitcast.81, s32[]{:T(128)} %bitcast.82), kind=kLoop, calls=%fused_computation.clone.1 | loop fusion | bytes 131084 | tf_op jit(solution)/shard_map/jit(_solve_triangular)/triangular_solve
  64.1 1.4 %bitcast_dynamic-update-slice_fusion.2 = f32[2,128,128]{2,1,0:T(8,128)S(1)} fusion(f32[2,128,128]{2,1,0:T(8,128)S(1)} %get-tuple-element.72, s32[]{:T(128)} %get-tuple-element.69, f32[256,256]{1,0:T(8,128)S(1)} %get-tuple-element.75, s32[]{:T(128)} %bitcast.81, s32[]{:T(128)} %bitcast.82), kind=kLoop, calls=%fused_computation.clone.1 | loop fusion | bytes 131084 | tf_op jit(solution)/shard_map/jit(_solve_triangular)/triangular_solve
  65.5 19.7 %custom-call.16 = f32[2,128,128]{1,2,0:T(8,128)S(1)} custom-call(f32[2,128,128]{2,1,0:T(8,128)S(1)} %get-tuple-element.9), custom_call_target="InvertDiagBlocksLowerTriangular" | custom-call | tf_op jit(solution)/shard_map/jit(_solve_triangular)/triangular_solve | solution.py:74
  87.9 1.6 %fusion = f32[1024,64]{0,1:T(8,128)S(1)} fusion(bf16[1024,64]{0,1:T(8,128)(2,1)S(1)} %get-tuple-element.31, bf16[1024,64]{0,1:T(8,128)(2,1)S(1)} %copy-done.2, f32[1024]{0:T(1024)S(1)} %multiply_reduce_fusion.6), kind=kOutput, calls=%fused_computation.9 | convolution fusion | flops 274726912 | bytes 528384 | tf_op jit(solution)/shard_map/dot_general | solution.py:85
  89.5 2.8 %fusion.27 = f32[1024,256]{1,0:T(8,128)} fusion(f32[1024,256]{0,1:T(8,128)S(1)} %fusion.11, f32[128,256]{1,0:T(8,128)S(1)} %fusion.32, f32[128,256]{1,0:T(8,128)S(1)} %fusion.29), kind=kOutput, calls=%fused_computation.57 | convolution fusion | flops 805371904 | bytes 2359296 | tf_op jit(solution)/shard_map/dot_general | solution.py:80
  92.9 1.4 %collective-permute-start.15 = (bf16[1024,64]{0,1:T(8,128)(2,1)S(1)}, bf16[1024,64]{0,1:T(8,128)(2,1)S(1)}, u32[]{:S(2)}, u32[]{:S(2)}) collective-permute-start(bf16[1024,64]{0,1:T(8,128)(2,1)S(1)} %get-tuple-element.31), channel_id=1, source_target_pairs={{3,0},{0,1},{1,2},{2,3},{7,4},{4,5},{5,6},{6,7},{11,8},{8,9},{9,10... | collective-permute-start | bytes 393224 | tf_op jit(solution)/shard_map/ppermute | solution.py:17
  94.3 1.1 collective-permute-start.13
  95.6 1.4 %collective-permute-start.20 = (bf16[1024,64]{0,1:T(8,128)(2,1)S(1)}, bf16[1024,64]{0,1:T(8,128)(2,1)S(1)}, u32[]{:S(2)}, u32[]{:S(2)}) collective-permute-start(bf16[1024,64]{0,1:T(8,128)(2,1)S(1)} %collective-permute-done.14), channel_id=1, source_target_pairs={{28,0},{5,1},{6,2},{7,3},{0,4},{9,5},{10,6},{11,7},{4,8},{13,9},{1... | collective-permute-start | bytes 393224 | tf_op jit(solution)/shard_map/ppermute | solution.py:53
  97.0 5.0 %collective-permute-done.15 = bf16[1024,64]{0,1:T(8,128)(2,1)S(1)} collective-permute-done((bf16[1024,64]{0,1:T(8,128)(2,1)S(1)}, bf16[1024,64]{0,1:T(8,128)(2,1)S(1)}, u32[]{:S(2)}, u32[]{:S(2)}) %collective-permute-start.15) | collective-permute-done | bytes 131104 | tf_op jit(solution)/shard_map/ppermute | solution.py:17
  102.1 1.6 %fusion.3 = f32[1024,64]{0,1:T(8,128)S(1)} fusion(bf16[1024,64]{0,1:T(8,128)(2,1)S(1)} %collective-permute-done.15, bf16[1024,64]{0,1:T(8,128)(2,1)S(1)} %copy-done.2, bf16[1024,64]{0,1:T(8,128)(2,1)S(1)} %collective-permute-done.14, f32[1024]{0:T(1024)S(1)} %multiply_reduce_fusion.3, f32[1024]{0:T(1024)S(1)} %multiply_reduce_fusion.6), kind=kOutput, calls=%fused_computation.12 | convolution fusion | flops 274726912 | bytes 663552 | tf_op jit(solution)/shard_map/dot_general | solution.py:85
  103.7 1.1 collective-permute-start.21
  104.8 2.3 %collective-permute-done.13 = bf16[1024,64]{0,1:T(8,128)(2,1)S(1)} collective-permute-done((bf16[1024,64]{0,1:T(8,128)(2,1)S(1)}, bf16[1024,64]{0,1:T(8,128)(2,1)S(1)}, u32[]{:S(2)}, u32[]{:S(2)}) %collective-permute-start.13) | collective-permute-done | bytes 131104 | tf_op jit(solution)/shard_map/ppermute | solution.py:17
  107.0 1.6 %fusion.17 = f32[1024,64]{0,1:T(8,128)S(1)} fusion(f32[1024,64]{0,1:T(8,128)S(1)} %fusion, bf16[1024,64]{0,1:T(8,128)(2,1)S(1)} %collective-permute-done.11, bf16[1024,64]{0,1:T(8,128)(2,1)S(1)} %copy-done.2, bf16[1024,64]{0,1:T(8,128)(2,1)S(1)} %collective-permute-done.10, f32[1024]{0:T(1024)S(1)} %multiply_reduce_fusion.5, f32[1024]{0:T(1024)S(1)} %multiply_reduce_fusion.6), kind=kOutput, calls=%fused_computation.29 | convolution fusion | flops 274792448 | bytes 925696 | tf_op jit(solution)/shard_map/dot_general | solution.py:85
  108.6 1.6 %fusion.16 = f32[1024,64]{0,1:T(8,128)S(1)} fusion(f32[1024,64]{0,1:T(8,128)S(1)} %fusion.3, f32[1024,64]{0,1:T(8,128)S(1)} %fusion.17, bf16[1024,64]{0,1:T(8,128)(2,1)S(1)} %collective-permute-done.13, bf16[1024,64]{0,1:T(8,128)(2,1)S(1)} %copy-done.2, bf16[1024,64]{0,1:T(8,128)(2,1)S(1)} %collective-permute-done.12, f32[1024]{0:T(1024)S(1)} %multiply_reduce_fusion.4, ...), kind=kOutput, calls=%fused_computation.28 | convolution fusion | flops 274857984 | bytes 1187840 | tf_op jit(solution)/shard_map/dot_general | solution.py:85
  110.3 1.4 %collective-permute-start.17 = (bf16[1024,64]{0,1:T(8,128)(2,1)S(1)}, bf16[1024,64]{0,1:T(8,128)(2,1)S(1)}, u32[]{:S(2)}, u32[]{:S(2)}) collective-permute-start(bf16[1024,64]{0,1:T(8,128)(2,1)S(1)} %collective-permute-done.11), channel_id=1, source_target_pairs={{28,0},{29,1},{30,2},{7,3},{0,4},{1,5},{2,6},{11,7},{4,8},{5,9},{6... | collective-permute-start | bytes 393224 | tf_op jit(solution)/shard_map/ppermute | solution.py:53
  112.3 1.6 %fusion.5 = f32[1024,64]{0,1:T(8,128)S(1)} fusion(bf16[1024,64]{0,1:T(8,128)(2,1)S(1)} %collective-permute-done.19, bf16[1024,64]{0,1:T(8,128)(2,1)S(1)} %copy-done.2, bf16[1024,64]{0,1:T(8,128)(2,1)S(1)} %collective-permute-done.18, f32[1024]{0:T(1024)S(1)} %multiply_reduce_fusion.1, f32[1024]{0:T(1024)S(1)} %multiply_reduce_fusion.6), kind=kOutput, calls=%fused_computation.14 | convolution fusion | flops 274726912 | bytes 663552 | tf_op jit(solution)/shard_map/dot_general | solution.py:85
  113.9 1.6 %fusion.6 = f32[1024,64]{0,1:T(8,128)S(1)} fusion(bf16[1024,64]{0,1:T(8,128)(2,1)S(1)} %collective-permute-done.21, bf16[1024,64]{0,1:T(8,128)(2,1)S(1)} %copy-done.2, bf16[1024,64]{0,1:T(8,128)(2,1)S(1)} %collective-permute-done.20, f32[1024]{0:T(1024)S(1)} %multiply_reduce_fusion, f32[1024]{0:T(1024)S(1)} %multiply_reduce_fusion.6), kind=kOutput, calls=%fused_computation.15 | convolution fusion | flops 274726912 | bytes 663552 | tf_op jit(solution)/shard_map/dot_general | solution.py:85
  115.6 2.3 %fusion.19 = f32[1024,64]{0,1:T(8,128)} fusion(f32[1024,64]{0,1:T(8,128)S(1)} %fusion.6, f32[1024,64]{0,1:T(8,128)S(1)} %fusion.5, f32[1024,64]{0,1:T(8,128)S(1)} %fusion.16, bf16[1024,64]{0,1:T(8,128)(2,1)S(1)} %collective-permute-done.17, bf16[1024,64]{0,1:T(8,128)(2,1)S(1)} %copy-done.2, bf16[1024,64]{0,1:T(8,128)(2,1)S(1)} %collective-permute-done.16, ...), kind=kOutput, calls=%fused_computation.31 | convolution fusion | flops 275120128 | bytes 1712128 | tf_op jit(solution)/shard_map/dot_general | solution.py:85
  (71 shorter events, 12.7 us)
Async XLA Ops:
  0.6 85.8 %copy-start = (f32[256,64]{0,1:T(8,128)S(1)}, f32[256,64]{0,1:T(8,128)}, u32[]{:S(2)}) copy-start(f32[256,64]{0,1:T(8,128)} %param.8) | copy-start | bytes 196612
  3.4 7.1 %collective-permute-start = (bf16[256,64]{0,1:T(8,128)(2,1)S(1)}, bf16[256,64]{0,1:T(8,128)(2,1)S(1)}, u32[]{:S(2)}, u32[]{:S(2)}) collective-permute-start(bf16[256,64]{0,1:T(8,128)(2,1)S(1)} %convolution_convert_fusion), channel_id=1, source_target_pairs={{1,0},{2,1},{3,2},{0,3},{5,4},{6,5},{7,6},{4,7},{9,8},{10,9},{11,1... | collective-permute-start | bytes 98312 | tf_op jit(solution)/shard_map/ppermute | solution.py:17
  8.5 4.8 %collective-permute-start.1 = (bf16[256,64]{0,1:T(8,128)(2,1)S(1)}, bf16[256,64]{0,1:T(8,128)(2,1)S(1)}, u32[]{:S(2)}, u32[]{:S(2)}) collective-permute-start(bf16[256,64]{0,1:T(8,128)(2,1)S(1)} %convolution_convert_fusion), channel_id=1, source_target_pairs={{2,0},{3,1},{0,2},{1,3},{6,4},{7,5},{4,6},{5,7},{10,8},{11,9},{8,1... | collective-permute-start | bytes 98312 | tf_op jit(solution)/shard_map/ppermute | solution.py:17
  8.5 5.7 %collective-permute-start.2 = (bf16[256,64]{0,1:T(8,128)(2,1)S(1)}, bf16[256,64]{0,1:T(8,128)(2,1)S(1)}, u32[]{:S(2)}, u32[]{:S(2)}) collective-permute-start(bf16[256,64]{0,1:T(8,128)(2,1)S(1)} %convolution_convert_fusion), channel_id=1, source_target_pairs={{3,0},{0,1},{1,2},{2,3},{7,4},{4,5},{5,6},{6,7},{11,8},{8,9},{9,10... | collective-permute-start | bytes 98312 | tf_op jit(solution)/shard_map/ppermute | solution.py:17
  14.2 4.6 %collective-permute-start.3 = (bf16[256,64]{0,1:T(8,128)(2,1)S(1)}, bf16[256,64]{0,1:T(8,128)(2,1)S(1)}, u32[]{:S(2)}, u32[]{:S(2)}) collective-permute-start(bf16[256,64]{0,1:T(8,128)(2,1)S(1)} %add_add_fusion.1), channel_id=1, source_target_pairs={{4,0},{8,4},{12,8},{16,12},{20,16},{24,20},{28,24},{0,28},{5,1},{9... | collective-permute-start | bytes 98312 | tf_op jit(solution)/shard_map/ppermute | solution.py:17
  14.7 5.6 %collective-permute-start.4 = (bf16[256,64]{0,1:T(8,128)(2,1)S(1)}, bf16[256,64]{0,1:T(8,128)(2,1)S(1)}, u32[]{:S(2)}, u32[]{:S(2)}) collective-permute-start(bf16[256,64]{0,1:T(8,128)(2,1)S(1)} %add_add_fusion.1), channel_id=1, source_target_pairs={{8,0},{12,4},{16,8},{20,12},{24,16},{28,20},{0,24},{4,28},{9,1},{1... | collective-permute-start | bytes 98312 | tf_op jit(solution)/shard_map/ppermute | solution.py:17
  16.8 3.5 %collective-permute-start.5 = (bf16[256,64]{0,1:T(8,128)(2,1)S(1)}, bf16[256,64]{0,1:T(8,128)(2,1)S(1)}, u32[]{:S(2)}, u32[]{:S(2)}) collective-permute-start(bf16[256,64]{0,1:T(8,128)(2,1)S(1)} %add_add_fusion.1), channel_id=1, source_target_pairs={{12,0},{16,4},{20,8},{24,12},{28,16},{0,20},{4,24},{8,28},{13,1},{... | collective-permute-start | bytes 98312 | tf_op jit(solution)/shard_map/ppermute | solution.py:17
  17.1 4.0 %collective-permute-start.6 = (bf16[256,64]{0,1:T(8,128)(2,1)S(1)}, bf16[256,64]{0,1:T(8,128)(2,1)S(1)}, u32[]{:S(2)}, u32[]{:S(2)}) collective-permute-start(bf16[256,64]{0,1:T(8,128)(2,1)S(1)} %add_add_fusion.1), channel_id=1, source_target_pairs={{16,0},{20,4},{24,8},{28,12},{0,16},{4,20},{8,24},{12,28},{17,1},{... | collective-permute-start | bytes 98312 | tf_op jit(solution)/shard_map/ppermute | solution.py:17
  18.6 3.8 %collective-permute-start.7 = (bf16[256,64]{0,1:T(8,128)(2,1)S(1)}, bf16[256,64]{0,1:T(8,128)(2,1)S(1)}, u32[]{:S(2)}, u32[]{:S(2)}) collective-permute-start(bf16[256,64]{0,1:T(8,128)(2,1)S(1)} %add_add_fusion.1), channel_id=1, source_target_pairs={{20,0},{24,4},{28,8},{0,12},{4,16},{8,20},{12,24},{16,28},{21,1},{... | collective-permute-start | bytes 98312 | tf_op jit(solution)/shard_map/ppermute | solution.py:17
  18.8 4.8 %collective-permute-start.8 = (bf16[256,64]{0,1:T(8,128)(2,1)S(1)}, bf16[256,64]{0,1:T(8,128)(2,1)S(1)}, u32[]{:S(2)}, u32[]{:S(2)}) collective-permute-start(bf16[256,64]{0,1:T(8,128)(2,1)S(1)} %add_add_fusion.1), channel_id=1, source_target_pairs={{24,0},{28,4},{0,8},{4,12},{8,16},{12,20},{16,24},{20,28},{25,1},{... | collective-permute-start | bytes 98312 | tf_op jit(solution)/shard_map/ppermute | solution.py:17
  20.3 4.2 %collective-permute-start.9 = (bf16[256,64]{0,1:T(8,128)(2,1)S(1)}, bf16[256,64]{0,1:T(8,128)(2,1)S(1)}, u32[]{:S(2)}, u32[]{:S(2)}) collective-permute-start(bf16[256,64]{0,1:T(8,128)(2,1)S(1)} %add_add_fusion.1), channel_id=1, source_target_pairs={{28,0},{0,4},{4,8},{8,12},{12,16},{16,20},{20,24},{24,28},{29,1},{... | collective-permute-start | bytes 98312 | tf_op jit(solution)/shard_map/ppermute | solution.py:17
  20.3 75.3 %collective-permute-start.10 = (bf16[1024,64]{0,1:T(8,128)(2,1)}, bf16[1024,64]{0,1:T(8,128)(2,1)S(1)}, u32[]{:S(2)}, u32[]{:S(2)}) collective-permute-start(bf16[1024,64]{0,1:T(8,128)(2,1)} %param.5), channel_id=1, source_target_pairs={{1,0},{2,1},{3,2},{0,3},{5,4},{6,5},{7,6},{4,7},{9,8},{10,9},{11,1... | collective-permute-start | bytes 393224 | tf_op jit(solution)/shard_map/ppermute | solution.py:17
  21.1 74.3 %collective-permute-start.14 = (bf16[1024,64]{0,1:T(8,128)(2,1)}, bf16[1024,64]{0,1:T(8,128)(2,1)S(1)}, u32[]{:S(2)}, u32[]{:S(2)}) collective-permute-start(bf16[1024,64]{0,1:T(8,128)(2,1)} %param.5), channel_id=1, source_target_pairs={{3,0},{0,1},{1,2},{2,3},{7,4},{4,5},{5,6},{6,7},{11,8},{8,9},{9,10... | collective-permute-start | bytes 393224 | tf_op jit(solution)/shard_map/ppermute | solution.py:17
  22.4 71.9 %collective-permute-start.12 = (bf16[1024,64]{0,1:T(8,128)(2,1)}, bf16[1024,64]{0,1:T(8,128)(2,1)S(1)}, u32[]{:S(2)}, u32[]{:S(2)}) collective-permute-start(bf16[1024,64]{0,1:T(8,128)(2,1)} %param.5), channel_id=1, source_target_pairs={{2,0},{3,1},{0,2},{1,3},{6,4},{7,5},{4,6},{5,7},{10,8},{11,9},{8,1... | collective-permute-start | bytes 393224 | tf_op jit(solution)/shard_map/ppermute | solution.py:17
  61.1 24.9 %copy-start.2 = (bf16[1024,64]{0,1:T(8,128)(2,1)S(1)}, bf16[1024,64]{0,1:T(8,128)(2,1)}, u32[]{:S(2)}) copy-start(bf16[1024,64]{0,1:T(8,128)(2,1)} %param.5) | copy-start | bytes 393220
  86.1 1.0 copy-start.1
  92.3 11.4 %collective-permute-start.11 = (bf16[1024,64]{0,1:T(8,128)(2,1)S(1)}, bf16[1024,64]{0,1:T(8,128)(2,1)S(1)}, u32[]{:S(2)}, u32[]{:S(2)}) collective-permute-start(bf16[1024,64]{0,1:T(8,128)(2,1)S(1)} %get-tuple-element.31), channel_id=1, source_target_pairs={{1,0},{2,1},{3,2},{0,3},{5,4},{6,5},{7,6},{4,7},{9,8},{10,9},{11,1... | collective-permute-start | bytes 393224 | tf_op jit(solution)/shard_map/ppermute | solution.py:17
  92.9 9.2 %collective-permute-start.15 = (bf16[1024,64]{0,1:T(8,128)(2,1)S(1)}, bf16[1024,64]{0,1:T(8,128)(2,1)S(1)}, u32[]{:S(2)}, u32[]{:S(2)}) collective-permute-start(bf16[1024,64]{0,1:T(8,128)(2,1)S(1)} %get-tuple-element.31), channel_id=1, source_target_pairs={{3,0},{0,1},{1,2},{2,3},{7,4},{4,5},{5,6},{6,7},{11,8},{8,9},{9,10... | collective-permute-start | bytes 393224 | tf_op jit(solution)/shard_map/ppermute | solution.py:17
  94.3 12.7 %collective-permute-start.13 = (bf16[1024,64]{0,1:T(8,128)(2,1)S(1)}, bf16[1024,64]{0,1:T(8,128)(2,1)S(1)}, u32[]{:S(2)}, u32[]{:S(2)}) collective-permute-start(bf16[1024,64]{0,1:T(8,128)(2,1)S(1)} %get-tuple-element.31), channel_id=1, source_target_pairs={{2,0},{3,1},{0,2},{1,3},{6,4},{7,5},{4,6},{5,7},{10,8},{11,9},{8,1... | collective-permute-start | bytes 393224 | tf_op jit(solution)/shard_map/ppermute | solution.py:17
  95.5 14.8 %collective-permute-start.18 = (bf16[1024,64]{0,1:T(8,128)(2,1)S(1)}, bf16[1024,64]{0,1:T(8,128)(2,1)S(1)}, u32[]{:S(2)}, u32[]{:S(2)}) collective-permute-start(bf16[1024,64]{0,1:T(8,128)(2,1)S(1)} %collective-permute-done.12), channel_id=1, source_target_pairs={{28,0},{29,1},{6,2},{7,3},{0,4},{1,5},{10,6},{11,7},{4,8},{5,9},{1... | collective-permute-start | bytes 393224 | tf_op jit(solution)/shard_map/ppermute | solution.py:53
  95.6 16.1 %collective-permute-start.20 = (bf16[1024,64]{0,1:T(8,128)(2,1)S(1)}, bf16[1024,64]{0,1:T(8,128)(2,1)S(1)}, u32[]{:S(2)}, u32[]{:S(2)}) collective-permute-start(bf16[1024,64]{0,1:T(8,128)(2,1)S(1)} %collective-permute-done.14), channel_id=1, source_target_pairs={{28,0},{5,1},{6,2},{7,3},{0,4},{9,5},{10,6},{11,7},{4,8},{13,9},{1... | collective-permute-start | bytes 393224 | tf_op jit(solution)/shard_map/ppermute | solution.py:53
  102.1 9.7 %collective-permute-start.16 = (bf16[1024,64]{0,1:T(8,128)(2,1)S(1)}, bf16[1024,64]{0,1:T(8,128)(2,1)S(1)}, u32[]{:S(2)}, u32[]{:S(2)}) collective-permute-start(bf16[1024,64]{0,1:T(8,128)(2,1)S(1)} %collective-permute-done.10), channel_id=1, source_target_pairs={{28,0},{29,1},{30,2},{7,3},{0,4},{1,5},{2,6},{11,7},{4,8},{5,9},{6... | collective-permute-start | bytes 393224 | tf_op jit(solution)/shard_map/ppermute | solution.py:53
  103.7 10.2 %collective-permute-start.21 = (bf16[1024,64]{0,1:T(8,128)(2,1)S(1)}, bf16[1024,64]{0,1:T(8,128)(2,1)S(1)}, u32[]{:S(2)}, u32[]{:S(2)}) collective-permute-start(bf16[1024,64]{0,1:T(8,128)(2,1)S(1)} %collective-permute-done.15), channel_id=1, source_target_pairs={{28,0},{5,1},{6,2},{7,3},{0,4},{9,5},{10,6},{11,7},{4,8},{13,9},{1... | collective-permute-start | bytes 393224 | tf_op jit(solution)/shard_map/ppermute | solution.py:53
  107.0 5.3 %collective-permute-start.19 = (bf16[1024,64]{0,1:T(8,128)(2,1)S(1)}, bf16[1024,64]{0,1:T(8,128)(2,1)S(1)}, u32[]{:S(2)}, u32[]{:S(2)}) collective-permute-start(bf16[1024,64]{0,1:T(8,128)(2,1)S(1)} %collective-permute-done.13), channel_id=1, source_target_pairs={{28,0},{29,1},{6,2},{7,3},{0,4},{1,5},{10,6},{11,7},{4,8},{5,9},{1... | collective-permute-start | bytes 393224 | tf_op jit(solution)/shard_map/ppermute | solution.py:53
  110.3 5.3 %collective-permute-start.17 = (bf16[1024,64]{0,1:T(8,128)(2,1)S(1)}, bf16[1024,64]{0,1:T(8,128)(2,1)S(1)}, u32[]{:S(2)}, u32[]{:S(2)}) collective-permute-start(bf16[1024,64]{0,1:T(8,128)(2,1)S(1)} %collective-permute-done.11), channel_id=1, source_target_pairs={{28,0},{29,1},{30,2},{7,3},{0,4},{1,5},{2,6},{11,7},{4,8},{5,9},{6... | collective-permute-start | bytes 393224 | tf_op jit(solution)/shard_map/ppermute | solution.py:53

commit v2 on v1

--- a/solution.py
+++ b/solution.py
@@ -1,11 +1,15 @@
 import jax
 import jax.numpy as jnp
 from jax import lax
+from jax.experimental import pallas as pl
+from jax.experimental.pallas import tpu as pltpu
 from jax.sharding import PartitionSpec as P
 
 PIVOTS = 128
 KERNEL_SCALE = 32
 BAND = 3
+STRIP = 8
+LANES = 128
 
 
 jitter = 0.1
@@ -35,6 +39,123 @@
         -(left_square_norm[:, None] + right_square_norm[None, :] - 2.0 * cross_term)
         / (1.0 * KERNEL_SCALE)
     )
+
+
+def column(strip, lane):
+    index = jnp.full(strip.shape, lane, jnp.int32)
+    return jnp.take_along_axis(strip, index, axis=1, mode="promise_in_bounds")
+
+
+def row(strip, i):
+    return jnp.broadcast_to(strip[i:i + 1, :], strip.shape)
+
+
+def halves(value):
+    return jnp.concatenate([value, value], axis=1)
+
+
+def thirds(value):
+    high = value.astype(jnp.bfloat16).astype(jnp.float32)
+    rest = value - high
+    middle = rest.astype(jnp.bfloat16).astype(jnp.float32)
+    return high, middle, rest - middle
+
+
+def invert_factor_kernel(pivot_ref, coeff_ref, inverse_ref, weight_ref, state_ref):
+    size = pivot_ref.shape[0]
+    pivots = pivot_ref[...]
+    cross = lax.dot_general(pivots, pivots, (((1,), (1,)), ((), ())), preferred_element_type=jnp.float32)
+    equal = lax.broadcasted_iota(jnp.int32, cross.shape, 0) == lax.broadcasted_iota(jnp.int32, cross.shape, 1)
+    diagonal = jnp.where(equal, cross, 0.0)
+    norms = jnp.sum(diagonal, axis=1, keepdims=True) + jnp.sum(diagonal, axis=0, keepdims=True)
+    state_ref[...] = jnp.exp(-(norms - 2.0 * cross) * (1.0 / KERNEL_SCALE)) + jnp.where(equal, jitter, 0.0)
+    lane = lax.broadcasted_iota(jnp.int32, (STRIP, size), 1)
+    level = lax.broadcasted_iota(jnp.int32, (STRIP, size), 0)
+    low = level[:, :LANES]
+
+    def body(p, carry):
+        strip, before = carry
+        start = p * STRIP
+        base = lax.rem(start, LANES)
+
+        def part(wide):
+            return jnp.where(start < LANES, wide[:, :LANES], wide[:, LANES:])
+
+        high, middle, little = thirds(before)
+        left = jnp.concatenate([high, high, middle, high, little, middle], axis=0).astype(jnp.bfloat16)
+        right = jnp.concatenate([high, middle, high, little, high, middle], axis=0).astype(jnp.bfloat16)
+        change = lax.dot_general(left, right, (((0,), (0,)), ((), ())), preferred_element_type=jnp.float32)
+        all_lanes = lax.broadcasted_iota(jnp.int32, change.shape, 1)
+        cleared = (all_lanes >= start - STRIP) & (all_lanes < start)
+        state_ref[...] = jnp.where(cleared, 0.0, state_ref[...]) - change
+
+        near = part(strip)
+        columns = [column(near, base + k) for k in range(STRIP)]
+        a = [[row(columns[k], i) for k in range(i + 1)] for i in range(STRIP)]
+        scale = [None] * STRIP
+        for k in range(STRIP):
+            scale[k] = lax.rsqrt(a[k][k])
+            for i in range(k + 1, STRIP):
+                a[i][k] = a[i][k] * scale[k]
+            for i in range(k + 1, STRIP):
+                for j in range(k + 1, i + 1):
+                    a[i][j] = a[i][j] - a[i][k] * a[j][k]
+        t = [[None] * STRIP for _ in range(STRIP)]
+        for j in range(STRIP):
+            t[j][j] = scale[j]
+            for i in range(j + 1, STRIP):
+                total = a[i][j] * t[j][j]
+                for q in range(j + 1, i):
+                    total = total + a[i][q] * t[q][j]
+                t[i][j] = -scale[i] * total
+
+        own = (lane >= start) & (lane < start + STRIP)
+        entered = jnp.where(own, jnp.where(lane - start == level, 1.0, 0.0), strip)
+        done = jnp.zeros_like(strip)
+        for k in range(STRIP):
+            t_column = jnp.zeros((STRIP, LANES), jnp.float32)
+            for i in range(k, STRIP):
+                t_column = jnp.where(low == i, t[i][k], t_column)
+            done = done + halves(t_column) * row(entered, k)
+        inverse_ref[pl.ds(pl.multiple_of(start, STRIP), STRIP), :] = jnp.where(lane < start + STRIP, done, 0.0)
+
+        following = jnp.minimum(start + STRIP, size - STRIP)
+        coming = state_ref[pl.ds(pl.multiple_of(following, STRIP), STRIP), :]
+        near = part(coming)
+        columns = [column(near, base + k) for k in range(STRIP)]
+        update = jnp.zeros_like(strip)
+        for k in range(STRIP):
+            l_column = columns[0] * t[k][0]
+            for j in range(1, k + 1):
+                l_column = l_column + columns[j] * t[k][j]
+            update = update + halves(l_column) * row(done, k)
+        return jnp.where(own, 0.0, coming) - update, done
+
+    first = state_ref[0:STRIP, :]
+    lax.fori_loop(0, size // STRIP, body, (first, jnp.zeros_like(first)))
+    weight_ref[...] = lax.dot_general(
+        inverse_ref[...],
+        coeff_ref[...],
+        (((0,), (0,)), ((), ())),
+        precision=lax.Precision.HIGHEST,
+        preferred_element_type=jnp.float32,
+    )
+
+
+def invert_factor(pivots, coeffs):
+    size = pivots.shape[0]
+    return pl.pallas_call(
+        invert_factor_kernel,
+        out_shape=(
+            jax.ShapeDtypeStruct((size, size), jnp.float32),
+            jax.ShapeDtypeStruct(coeffs.shape, jnp.float32),
+        ),
+        in_specs=[pl.BlockSpec(memory_space=pltpu.VMEM)] * 2,
+        out_specs=(pl.BlockSpec(memory_space=pltpu.VMEM),) * 2,
+        scratch_shapes=[pltpu.VMEM((size, size), jnp.float32)],
+        cost_estimate=pl.CostEstimate(flops=size * size * size * 6, bytes_accessed=size * size * 4, transcendentals=size * size),
+        name="invert_factor",
+    )(pivots, coeffs)
 
 
 def neighbours(value, tall):
@@ -56,7 +177,6 @@
 
 def shards(points, pivots, owners, coeffs, noise):
     hp = lax.Precision.HIGHEST
-    solve = jax.scipy.linalg.solve_triangular
     count, width = points.shape
     tall = lax.axis_size("gy") == BAND + 1
     me = lax.axis_index(("gx", "gy"))
@@ -68,12 +188,8 @@
     pivot_points = summed(summed(picked, "gy"), "gx")
     near_points = neighbours(points, tall)
 
-    size = 2 * PIVOTS
-    ident = jnp.eye(size, dtype=jnp.float32)
-    chol = jnp.linalg.cholesky(kern(pivot_points, pivot_points) + jitter * ident)
-    inverse = solve(chol, ident, lower=True)
+    inverse, weights = invert_factor(pivot_points, coeffs)
     cols = kern(points, pivot_points)
-    weights = jnp.dot(inverse.T, coeffs, precision=hp)
     probes = jnp.dot(cols, weights, precision=hp, preferred_element_type=jnp.float32) + noise
     sent = probes.astype(jnp.bfloat16)
     near_probes = neighbours(sent, tall)

time: 118 us -> 71.1 us (0.60)
  other arithmetic: 56.6 us -> 3.36 us
  Pallas kernels: 0 us -> 12.3 us
  local copies, waits for them, and re-layouts: 4.43 us -> 0.78 us
  starting transfers between devices: 22.3 us -> 24.8 us
  waiting for transfers between devices: 12.9 us -> 10.8 us
  between operations: 2.29 us -> 0.81 us
  matrix products: 19.3 us -> 17.9 us
    another operation x9 -> x0, other arithmetic: 53.7 us -> none  [the longest x6 34 us: shards(): jnp.linalg.cholesky(kern(pivot_points, pivot_points) + jitter * ident)]
    pallas_call x0 -> x1, Pallas kernels: none -> 12.3 us  [invert_factor(): pl.pallas_call(invert_factor_kernel, out_shape=(jax.ShapeDtypeStruct((siz...]
    another operation x9 -> x0, local copies, waits for them, and re-layouts: 4.15 us -> none
    ppermute x16, starting transfers between devices: 18.4 us -> 21 us  [shifted(): lax.ppermute(value, axis, [((i + steps) % count, i) for i in range(count)])]
    ppermute x16, waiting for transfers between devices: 12.2 us -> 10.2 us  [shifted(): lax.ppermute(value, axis, [((i + steps) % count, i) for i in range(count)])]
    another operation x5 -> x0, matrix products: 1.31 us -> none  [the longest x3 0.84 us: shards(): inverse = solve(chol, ident, lower=True)]
  transfers between devices with their start and end apart: 22 -> 22, of which waited for: 9 -> 6; matrix products, arithmetic and copies ran while one was open for 64% -> 24% of each run, Pallas kernels for 0% -> 17%
where the time goes in v2:
time: 71.1 us; the launch traced here: 70.9 us
  starting transfers between devices  24.8 us (35%)
  matrix products  17.9 us (25%)
  Pallas kernels  12.3 us (17%)
  waiting for transfers between devices  10.8 us (15%)
  other arithmetic  3.36 us (5%)
  between operations  0.81 us (1%)
  local copies, waits for them, and re-layouts  0.78 us (1%)
    ppermute x16, starting transfers between devices, shifted(): lax.ppermute(value, axis, [((i + steps) % count, i) for i in range(count)])  21 us
    pallas_call x1, Pallas kernels, invert_factor(): pl.pallas_call(invert_factor_kernel, out_shape=(jax.ShapeDtypeStruct((siz...  12.3 us
    dot_general x7, matrix products, shards(): total = total + jnp.dot(tile, probe, preferred_element_type=jnp.float32)  11.8 us
    ppermute x16, waiting for transfers between devices, shifted(): lax.ppermute(value, axis, [((i + steps) % count, i) for i in range(count)])  10.2 us
    ppermute x6, starting transfers between devices, neighbours(): other.append(lax.ppermute(own[k - 1], ('gx', 'gy'), pairs))  3.82 us
    dot_general x1, matrix products, shards(): jnp.dot(cols, inverse.T, precision=hp, preferred_element_type=jnp.float32)  2.78 us
  transfers between devices with their start and end apart: 22, of which 6 were waited for; matrix products, arithmetic and copies ran while one was open for 24% of the time, Pallas kernels for 17%

profile of v2, /device:TPU:0, one launch (start us, length us, event | category | flops | bytes accessed | tf_op | source)
XLA Modules:
  0.0 70.9 jit_solution(16717800325318318558)
XLA Ops:
  1.4 0.7 %select_bitcast_fusion = s32[256]{0:T(256)S(1)} fusion(s32[2,128]{1,0:T(2,128)} %param.6, pred[2]{0:T(512)(128)(4,1)S(1)} %broadcast_compare_fusion), kind=kLoop, calls=%fused_computation.42 | loop fusion | flops 256 | bytes 2050 | tf_op jit(solution)/shard_map/eq | solution.py:186
  2.1 1.3 %convolution_convert_fusion = bf16[256,64]{1,0:T(8,128)(2,1)S(1)} fusion(bf16[1024,64]{0,1:T(8,128)(2,1)} %param.5, s32[256]{0:T(256)S(1)} %select_bitcast_fusion), kind=kOutput, calls=%fused_computation.29 | convolution fusion | flops 33832960 | bytes 164864 | tf_op jit(solution)/shard_map/dot_general | solution.py:187
  3.4 5.1 %collective-permute-start = (bf16[256,64]{1,0:T(8,128)(2,1)S(1)}, bf16[256,64]{1,0:T(8,128)(2,1)S(1)}, u32[]{:S(2)}, u32[]{:S(2)}) collective-permute-start(bf16[256,64]{1,0:T(8,128)(2,1)S(1)} %convolution_convert_fusion), channel_id=1, source_target_pairs={{1,0},{2,1},{3,2},{0,3},{5,4},{6,5},{7,6},{4,7},{9,8},{10,9},{11,1... | collective-permute-start | bytes 98312 | tf_op jit(solution)/shard_map/ppermute | solution.py:21
  8.5 1.0 %collective-permute-start.2 = (bf16[256,64]{1,0:T(8,128)(2,1)S(1)}, bf16[256,64]{1,0:T(8,128)(2,1)S(1)}, u32[]{:S(2)}, u32[]{:S(2)}) collective-permute-start(bf16[256,64]{1,0:T(8,128)(2,1)S(1)} %convolution_convert_fusion), channel_id=1, source_target_pairs={{3,0},{0,1},{1,2},{2,3},{7,4},{4,5},{5,6},{6,7},{11,8},{8,9},{9,10... | collective-permute-start | bytes 98312 | tf_op jit(solution)/shard_map/ppermute | solution.py:21
  9.5 1.5 %collective-permute-done = bf16[256,64]{1,0:T(8,128)(2,1)S(1)} collective-permute-done((bf16[256,64]{1,0:T(8,128)(2,1)S(1)}, bf16[256,64]{1,0:T(8,128)(2,1)S(1)}, u32[]{:S(2)}, u32[]{:S(2)}) %collective-permute-start) | collective-permute-done | bytes 32800 | tf_op jit(solution)/shard_map/ppermute | solution.py:21
  11.0 4.0 %collective-permute-done.1 = bf16[256,64]{1,0:T(8,128)(2,1)S(1)} collective-permute-done((bf16[256,64]{1,0:T(8,128)(2,1)S(1)}, bf16[256,64]{1,0:T(8,128)(2,1)S(1)}, u32[]{:S(2)}, u32[]{:S(2)}) %collective-permute-start.1) | collective-permute-done | bytes 32800 | tf_op jit(solution)/shard_map/ppermute | solution.py:21
  15.0 1.9 %collective-permute-start.3 = (bf16[256,64]{1,0:T(8,128)(2,1)S(1)}, bf16[256,64]{1,0:T(8,128)(2,1)S(1)}, u32[]{:S(2)}, u32[]{:S(2)}) collective-permute-start(bf16[256,64]{1,0:T(8,128)(2,1)S(1)} %add_add_fusion.1), channel_id=1, source_target_pairs={{4,0},{8,4},{12,8},{16,12},{20,16},{24,20},{28,24},{0,28},{5,1},{9... | collective-permute-start | bytes 98312 | tf_op jit(solution)/shard_map/ppermute | solution.py:21
  17.8 1.5 %collective-permute-start.6 = (bf16[256,64]{1,0:T(8,128)(2,1)S(1)}, bf16[256,64]{1,0:T(8,128)(2,1)S(1)}, u32[]{:S(2)}, u32[]{:S(2)}) collective-permute-start(bf16[256,64]{1,0:T(8,128)(2,1)S(1)} %add_add_fusion.1), channel_id=1, source_target_pairs={{16,0},{20,4},{24,8},{28,12},{0,16},{4,20},{8,24},{12,28},{17,1},{... | collective-permute-start | bytes 98312 | tf_op jit(solution)/shard_map/ppermute | solution.py:21
  19.5 2.3 %collective-permute-start.8 = (bf16[256,64]{1,0:T(8,128)(2,1)S(1)}, bf16[256,64]{1,0:T(8,128)(2,1)S(1)}, u32[]{:S(2)}, u32[]{:S(2)}) collective-permute-start(bf16[256,64]{1,0:T(8,128)(2,1)S(1)} %add_add_fusion.1), channel_id=1, source_target_pairs={{24,0},{28,4},{0,8},{4,12},{8,16},{12,20},{16,24},{20,28},{25,1},{... | collective-permute-start | bytes 98312 | tf_op jit(solution)/shard_map/ppermute | solution.py:21
  21.8 0.9 %multiply_reduce_fusion.6 = f32[1024]{0:T(1024)S(1)} fusion(bf16[1024,64]{0,1:T(8,128)(2,1)} %param.5), kind=kLoop, calls=%fused_computation.38 | loop fusion | flops 195584 | bytes 135168 | tf_op jit(solution)/shard_map/reduce_sum | solution.py:35
  22.8 0.8 %copy.8.coeff_ref = f32[256,64]{1,0:T(8,128)} copy(f32[256,64]{0,1:T(8,128)S(1)} %copy-done.4) | data formatting | bytes 131072 | tf_op args[3]
  23.5 1.1 %collective-permute-start.10 = (bf16[1024,64]{0,1:T(8,128)(2,1)S(1)}, bf16[1024,64]{0,1:T(8,128)(2,1)S(1)}, u32[]{:S(2)}, u32[]{:S(2)}) collective-permute-start(bf16[1024,64]{0,1:T(8,128)(2,1)S(1)} %copy-done.3), channel_id=1, source_target_pairs={{1,0},{2,1},{3,2},{0,3},{5,4},{6,5},{7,6},{4,7},{9,8},{10,9},{11,1... | collective-permute-start | bytes 393224 | tf_op jit(solution)/shard_map/ppermute | solution.py:21
  24.6 2.0 %collective-permute-start.14 = (bf16[1024,64]{0,1:T(8,128)(2,1)S(1)}, bf16[1024,64]{0,1:T(8,128)(2,1)S(1)}, u32[]{:S(2)}, u32[]{:S(2)}) collective-permute-start(bf16[1024,64]{0,1:T(8,128)(2,1)S(1)} %copy-done.3), channel_id=1, source_target_pairs={{3,0},{0,1},{1,2},{2,3},{7,4},{4,5},{5,6},{6,7},{11,8},{8,9},{9,10... | collective-permute-start | bytes 393224 | tf_op jit(solution)/shard_map/ppermute | solution.py:21
  26.6 2.1 %collective-permute-start.12 = (bf16[1024,64]{0,1:T(8,128)(2,1)S(1)}, bf16[1024,64]{0,1:T(8,128)(2,1)S(1)}, u32[]{:S(2)}, u32[]{:S(2)}) collective-permute-start(bf16[1024,64]{0,1:T(8,128)(2,1)S(1)} %copy-done.3), channel_id=1, source_target_pairs={{2,0},{3,1},{0,2},{1,3},{6,4},{7,5},{4,6},{5,7},{10,8},{11,9},{8,1... | collective-permute-start | bytes 393224 | tf_op jit(solution)/shard_map/ppermute | solution.py:21
  29.4 12.3 %invert_factor.1 = (f32[256,256]{1,0:T(8,128)}, f32[256,64]{1,0:T(8,128)}) custom-call(bf16[256,64]{1,0:T(8,128)(2,1)} %get-tuple-element.7.pivot_ref, f32[256,64]{1,0:T(8,128)} %copy.8.coeff_ref), custom_call_target="tpu_custom_call" | custom-call | flops 100663296 | bytes 262144 | tf_op jit(solution)/shard_map/invert_factor/pallas_call | solution.py:147
  41.7 1.2 %fusion.11 = f32[1024,256]{0,1:T(8,128)S(1)} fusion(bf16[256,64]{1,0:T(8,128)(2,1)} %get-tuple-element.7.pivot_ref, bf16[1024,64]{0,1:T(8,128)(2,1)S(1)} %copy-done.3, f32[256]{0:T(256)S(1)} %get-tuple-element.6, f32[1024]{0:T(1024)S(1)} %multiply_reduce_fusion.6), kind=kOutput, calls=%fused_computation.19 | convolution fusion | flops 34865152 | bytes 1217536 | tf_op jit(solution)/shard_map/dot_general | solution.py:37
  43.0 0.8 %fusion.35 = (bf16[1024,64]{0,1:T(8,128)(2,1)S(1)}, f32[1024,64]{0,1:T(8,128)S(1)}) fusion(f32[1024,64]{0,1:T(8,128)S(1)} %copy-done, f32[1024,256]{0,1:T(8,128)S(1)} %fusion.11, f32[256,64]{1,0:T(8,128)S(1)} %copy-done.2), kind=kOutput, calls=%fused_computation.58 | convolution fusion | flops 201457664 | bytes 1769472 | tf_op jit(solution)/shard_map/dot_general | solution.py:193
  43.8 1.6 %fusion = f32[1024,64]{0,1:T(8,128)S(1)} fusion(bf16[1024,64]{0,1:T(8,128)(2,1)S(1)} %get-tuple-element.8, bf16[1024,64]{0,1:T(8,128)(2,1)S(1)} %copy-done.3, f32[1024]{0:T(1024)S(1)} %multiply_reduce_fusion.6), kind=kOutput, calls=%fused_computation.7 | convolution fusion | flops 274726912 | bytes 528384 | tf_op jit(solution)/shard_map/dot_general | solution.py:201
  45.8 1.7 %collective-permute-start.15 = (bf16[1024,64]{0,1:T(8,128)(2,1)S(1)}, bf16[1024,64]{0,1:T(8,128)(2,1)S(1)}, u32[]{:S(2)}, u32[]{:S(2)}) collective-permute-start(bf16[1024,64]{0,1:T(8,128)(2,1)S(1)} %get-tuple-element.8), channel_id=1, source_target_pairs={{3,0},{0,1},{1,2},{2,3},{7,4},{4,5},{5,6},{6,7},{11,8},{8,9},{9,10... | collective-permute-start | bytes 393224 | tf_op jit(solution)/shard_map/ppermute | solution.py:21
  47.4 2.8 %fusion.36 = f32[1024,256]{1,0:T(8,128)} fusion(f32[1024,256]{0,1:T(8,128)S(1)} %fusion.11, f32[256,256]{1,0:T(8,128)S(1)} %copy-done.1), kind=kOutput, calls=%fused_computation.59 | convolution fusion | flops 805306368 | bytes 2359296 | tf_op jit(solution)/shard_map/dot_general | solution.py:196
  50.2 0.9 %collective-permute-start.13 = (bf16[1024,64]{0,1:T(8,128)(2,1)S(1)}, bf16[1024,64]{0,1:T(8,128)(2,1)S(1)}, u32[]{:S(2)}, u32[]{:S(2)}) collective-permute-start(bf16[1024,64]{0,1:T(8,128)(2,1)S(1)} %get-tuple-element.8), channel_id=1, source_target_pairs={{2,0},{3,1},{0,2},{1,3},{6,4},{7,5},{4,6},{5,7},{10,8},{11,9},{8,1... | collective-permute-start | bytes 393224 | tf_op jit(solution)/shard_map/ppermute | solution.py:21
  51.3 0.8 %collective-permute-start.20 = (bf16[1024,64]{0,1:T(8,128)(2,1)S(1)}, bf16[1024,64]{0,1:T(8,128)(2,1)S(1)}, u32[]{:S(2)}, u32[]{:S(2)}) collective-permute-start(bf16[1024,64]{0,1:T(8,128)(2,1)S(1)} %collective-permute-done.14), channel_id=1, source_target_pairs={{28,0},{5,1},{6,2},{7,3},{0,4},{9,5},{10,6},{11,7},{4,8},{13,9},{1... | collective-permute-start | bytes 393224 | tf_op jit(solution)/shard_map/ppermute | solution.py:174
  52.1 1.5 %collective-permute-done.15 = bf16[1024,64]{0,1:T(8,128)(2,1)S(1)} collective-permute-done((bf16[1024,64]{0,1:T(8,128)(2,1)S(1)}, bf16[1024,64]{0,1:T(8,128)(2,1)S(1)}, u32[]{:S(2)}, u32[]{:S(2)}) %collective-permute-start.15) | collective-permute-done | bytes 131104 | tf_op jit(solution)/shard_map/ppermute | solution.py:21
  53.6 1.6 %fusion.3 = f32[1024,64]{0,1:T(8,128)S(1)} fusion(bf16[1024,64]{0,1:T(8,128)(2,1)S(1)} %collective-permute-done.15, bf16[1024,64]{0,1:T(8,128)(2,1)S(1)} %copy-done.3, bf16[1024,64]{0,1:T(8,128)(2,1)S(1)} %collective-permute-done.14, f32[1024]{0:T(1024)S(1)} %multiply_reduce_fusion.3, f32[1024]{0:T(1024)S(1)} %multiply_reduce_fusion.6), kind=kOutput, calls=%fused_computation.10 | convolution fusion | flops 274726912 | bytes 663552 | tf_op jit(solution)/shard_map/dot_general | solution.py:201
  55.2 1.4 %collective-permute-start.21 = (bf16[1024,64]{0,1:T(8,128)(2,1)S(1)}, bf16[1024,64]{0,1:T(8,128)(2,1)S(1)}, u32[]{:S(2)}, u32[]{:S(2)}) collective-permute-start(bf16[1024,64]{0,1:T(8,128)(2,1)S(1)} %collective-permute-done.15), channel_id=1, source_target_pairs={{28,0},{5,1},{6,2},{7,3},{0,4},{9,5},{10,6},{11,7},{4,8},{13,9},{1... | collective-permute-start | bytes 393224 | tf_op jit(solution)/shard_map/ppermute | solution.py:174
  56.6 3.2 %collective-permute-done.13 = bf16[1024,64]{0,1:T(8,128)(2,1)S(1)} collective-permute-done((bf16[1024,64]{0,1:T(8,128)(2,1)S(1)}, bf16[1024,64]{0,1:T(8,128)(2,1)S(1)}, u32[]{:S(2)}, u32[]{:S(2)}) %collective-permute-start.13) | collective-permute-done | bytes 131104 | tf_op jit(solution)/shard_map/ppermute | solution.py:21
  59.8 1.6 %fusion.17 = f32[1024,64]{0,1:T(8,128)S(1)} fusion(f32[1024,64]{0,1:T(8,128)S(1)} %fusion, bf16[1024,64]{0,1:T(8,128)(2,1)S(1)} %collective-permute-done.11, bf16[1024,64]{0,1:T(8,128)(2,1)S(1)} %copy-done.3, bf16[1024,64]{0,1:T(8,128)(2,1)S(1)} %collective-permute-done.10, f32[1024]{0:T(1024)S(1)} %multiply_reduce_fusion.5, f32[1024]{0:T(1024)S(1)} %multiply_reduce_fusion.6), kind=kOutput, calls=%fused_computation.26 | convolution fusion | flops 274792448 | bytes 925696 | tf_op jit(solution)/shard_map/dot_general | solution.py:201
  61.4 1.6 %fusion.16 = f32[1024,64]{0,1:T(8,128)S(1)} fusion(f32[1024,64]{0,1:T(8,128)S(1)} %fusion.3, f32[1024,64]{0,1:T(8,128)S(1)} %fusion.17, bf16[1024,64]{0,1:T(8,128)(2,1)S(1)} %collective-permute-done.13, bf16[1024,64]{0,1:T(8,128)(2,1)S(1)} %copy-done.3, bf16[1024,64]{0,1:T(8,128)(2,1)S(1)} %collective-permute-done.12, f32[1024]{0:T(1024)S(1)} %multiply_reduce_fusion.4, ...), kind=kOutput, calls=%fused_computation.25 | convolution fusion | flops 274857984 | bytes 1187840 | tf_op jit(solution)/shard_map/dot_general | solution.py:201
  63.0 1.6 %collective-permute-start.17 = (bf16[1024,64]{0,1:T(8,128)(2,1)S(1)}, bf16[1024,64]{0,1:T(8,128)(2,1)S(1)}, u32[]{:S(2)}, u32[]{:S(2)}) collective-permute-start(bf16[1024,64]{0,1:T(8,128)(2,1)S(1)} %collective-permute-done.11), channel_id=1, source_target_pairs={{28,0},{29,1},{30,2},{7,3},{0,4},{1,5},{2,6},{11,7},{4,8},{5,9},{6... | collective-permute-start | bytes 393224 | tf_op jit(solution)/shard_map/ppermute | solution.py:174
  65.1 1.6 %fusion.5 = f32[1024,64]{0,1:T(8,128)S(1)} fusion(bf16[1024,64]{0,1:T(8,128)(2,1)S(1)} %collective-permute-done.19, bf16[1024,64]{0,1:T(8,128)(2,1)S(1)} %copy-done.3, bf16[1024,64]{0,1:T(8,128)(2,1)S(1)} %collective-permute-done.18, f32[1024]{0:T(1024)S(1)} %multiply_reduce_fusion.1, f32[1024]{0:T(1024)S(1)} %multiply_reduce_fusion.6), kind=kOutput, calls=%fused_computation.12 | convolution fusion | flops 274726912 | bytes 663552 | tf_op jit(solution)/shard_map/dot_general | solution.py:201
  66.7 1.6 %fusion.6 = f32[1024,64]{0,1:T(8,128)S(1)} fusion(bf16[1024,64]{0,1:T(8,128)(2,1)S(1)} %collective-permute-done.21, bf16[1024,64]{0,1:T(8,128)(2,1)S(1)} %copy-done.3, bf16[1024,64]{0,1:T(8,128)(2,1)S(1)} %collective-permute-done.20, f32[1024]{0:T(1024)S(1)} %multiply_reduce_fusion, f32[1024]{0:T(1024)S(1)} %multiply_reduce_fusion.6), kind=kOutput, calls=%fused_computation.13 | convolution fusion | flops 274726912 | bytes 663552 | tf_op jit(solution)/shard_map/dot_general | solution.py:201
  68.5 2.3 %fusion.19 = f32[1024,64]{0,1:T(8,128)} fusion(f32[1024,64]{0,1:T(8,128)S(1)} %fusion.6, f32[1024,64]{0,1:T(8,128)S(1)} %fusion.5, f32[1024,64]{0,1:T(8,128)S(1)} %fusion.16, bf16[1024,64]{0,1:T(8,128)(2,1)S(1)} %collective-permute-done.17, bf16[1024,64]{0,1:T(8,128)(2,1)S(1)} %copy-done.3, bf16[1024,64]{0,1:T(8,128)(2,1)S(1)} %collective-permute-done.16, ...), kind=kOutput, calls=%fused_computation.28 | convolution fusion | flops 275120128 | bytes 1712128 | tf_op jit(solution)/shard_map/dot_general | solution.py:201
  (46 shorter events, 3.8 us)
Async XLA Ops:
  0.6 22.9 %copy-start.3 = (bf16[1024,64]{0,1:T(8,128)(2,1)S(1)}, bf16[1024,64]{0,1:T(8,128)(2,1)}, u32[]{:S(2)}) copy-start(bf16[1024,64]{0,1:T(8,128)(2,1)} %param.5) | copy-start | bytes 393220
  0.6 22.1 %copy-start.4 = (f32[256,64]{0,1:T(8,128)S(1)}, f32[256,64]{0,1:T(8,128)}, u32[]{:S(2)}) copy-start(f32[256,64]{0,1:T(8,128)} %param.8) | copy-start | bytes 196612
  3.4 7.6 %collective-permute-start = (bf16[256,64]{1,0:T(8,128)(2,1)S(1)}, bf16[256,64]{1,0:T(8,128)(2,1)S(1)}, u32[]{:S(2)}, u32[]{:S(2)}) collective-permute-start(bf16[256,64]{1,0:T(8,128)(2,1)S(1)} %convolution_convert_fusion), channel_id=1, source_target_pairs={{1,0},{2,1},{3,2},{0,3},{5,4},{6,5},{7,6},{4,7},{9,8},{10,9},{11,1... | collective-permute-start | bytes 98312 | tf_op jit(solution)/shard_map/ppermute | solution.py:21
  8.5 6.5 %collective-permute-start.1 = (bf16[256,64]{1,0:T(8,128)(2,1)S(1)}, bf16[256,64]{1,0:T(8,128)(2,1)S(1)}, u32[]{:S(2)}, u32[]{:S(2)}) collective-permute-start(bf16[256,64]{1,0:T(8,128)(2,1)S(1)} %convolution_convert_fusion), channel_id=1, source_target_pairs={{2,0},{3,1},{0,2},{1,3},{6,4},{7,5},{4,6},{5,7},{10,8},{11,9},{8,1... | collective-permute-start | bytes 98312 | tf_op jit(solution)/shard_map/ppermute | solution.py:21
  8.5 6.5 %collective-permute-start.2 = (bf16[256,64]{1,0:T(8,128)(2,1)S(1)}, bf16[256,64]{1,0:T(8,128)(2,1)S(1)}, u32[]{:S(2)}, u32[]{:S(2)}) collective-permute-start(bf16[256,64]{1,0:T(8,128)(2,1)S(1)} %convolution_convert_fusion), channel_id=1, source_target_pairs={{3,0},{0,1},{1,2},{2,3},{7,4},{4,5},{5,6},{6,7},{11,8},{8,9},{9,10... | collective-permute-start | bytes 98312 | tf_op jit(solution)/shard_map/ppermute | solution.py:21
  15.0 4.5 %collective-permute-start.3 = (bf16[256,64]{1,0:T(8,128)(2,1)S(1)}, bf16[256,64]{1,0:T(8,128)(2,1)S(1)}, u32[]{:S(2)}, u32[]{:S(2)}) collective-permute-start(bf16[256,64]{1,0:T(8,128)(2,1)S(1)} %add_add_fusion.1), channel_id=1, source_target_pairs={{4,0},{8,4},{12,8},{16,12},{20,16},{24,20},{28,24},{0,28},{5,1},{9... | collective-permute-start | bytes 98312 | tf_op jit(solution)/shard_map/ppermute | solution.py:21
  16.9 4.9 %collective-permute-start.4 = (bf16[256,64]{1,0:T(8,128)(2,1)S(1)}, bf16[256,64]{1,0:T(8,128)(2,1)S(1)}, u32[]{:S(2)}, u32[]{:S(2)}) collective-permute-start(bf16[256,64]{1,0:T(8,128)(2,1)S(1)} %add_add_fusion.1), channel_id=1, source_target_pairs={{8,0},{12,4},{16,8},{20,12},{24,16},{28,20},{0,24},{4,28},{9,1},{1... | collective-permute-start | bytes 98312 | tf_op jit(solution)/shard_map/ppermute | solution.py:21
  17.5 6.0 %collective-permute-start.5 = (bf16[256,64]{1,0:T(8,128)(2,1)S(1)}, bf16[256,64]{1,0:T(8,128)(2,1)S(1)}, u32[]{:S(2)}, u32[]{:S(2)}) collective-permute-start(bf16[256,64]{1,0:T(8,128)(2,1)S(1)} %add_add_fusion.1), channel_id=1, source_target_pairs={{12,0},{16,4},{20,8},{24,12},{28,16},{0,20},{4,24},{8,28},{13,1},{... | collective-permute-start | bytes 98312 | tf_op jit(solution)/shard_map/ppermute | solution.py:21
  17.8 6.8 %collective-permute-start.6 = (bf16[256,64]{1,0:T(8,128)(2,1)S(1)}, bf16[256,64]{1,0:T(8,128)(2,1)S(1)}, u32[]{:S(2)}, u32[]{:S(2)}) collective-permute-start(bf16[256,64]{1,0:T(8,128)(2,1)S(1)} %add_add_fusion.1), channel_id=1, source_target_pairs={{16,0},{20,4},{24,8},{28,12},{0,16},{4,20},{8,24},{12,28},{17,1},{... | collective-permute-start | bytes 98312 | tf_op jit(solution)/shard_map/ppermute | solution.py:21
  19.3 7.3 %collective-permute-start.7 = (bf16[256,64]{1,0:T(8,128)(2,1)S(1)}, bf16[256,64]{1,0:T(8,128)(2,1)S(1)}, u32[]{:S(2)}, u32[]{:S(2)}) collective-permute-start(bf16[256,64]{1,0:T(8,128)(2,1)S(1)} %add_add_fusion.1), channel_id=1, source_target_pairs={{20,0},{24,4},{28,8},{0,12},{4,16},{8,20},{12,24},{16,28},{21,1},{... | collective-permute-start | bytes 98312 | tf_op jit(solution)/shard_map/ppermute | solution.py:21
  19.5 9.2 %collective-permute-start.8 = (bf16[256,64]{1,0:T(8,128)(2,1)S(1)}, bf16[256,64]{1,0:T(8,128)(2,1)S(1)}, u32[]{:S(2)}, u32[]{:S(2)}) collective-permute-start(bf16[256,64]{1,0:T(8,128)(2,1)S(1)} %add_add_fusion.1), channel_id=1, source_target_pairs={{24,0},{28,4},{0,8},{4,12},{8,16},{12,20},{16,24},{20,28},{25,1},{... | collective-permute-start | bytes 98312 | tf_op jit(solution)/shard_map/ppermute | solution.py:21
  21.8 6.9 %collective-permute-start.9 = (bf16[256,64]{1,0:T(8,128)(2,1)S(1)}, bf16[256,64]{1,0:T(8,128)(2,1)S(1)}, u32[]{:S(2)}, u32[]{:S(2)}) collective-permute-start(bf16[256,64]{1,0:T(8,128)(2,1)S(1)} %add_add_fusion.1), channel_id=1, source_target_pairs={{28,0},{0,4},{4,8},{8,12},{12,16},{16,20},{20,24},{24,28},{29,1},{... | collective-permute-start | bytes 98312 | tf_op jit(solution)/shard_map/ppermute | solution.py:21
  23.5 27.7 %collective-permute-start.10 = (bf16[1024,64]{0,1:T(8,128)(2,1)S(1)}, bf16[1024,64]{0,1:T(8,128)(2,1)S(1)}, u32[]{:S(2)}, u32[]{:S(2)}) collective-permute-start(bf16[1024,64]{0,1:T(8,128)(2,1)S(1)} %copy-done.3), channel_id=1, source_target_pairs={{1,0},{2,1},{3,2},{0,3},{5,4},{6,5},{7,6},{4,7},{9,8},{10,9},{11,1... | collective-permute-start | bytes 393224 | tf_op jit(solution)/shard_map/ppermute | solution.py:21
  24.6 26.5 %collective-permute-start.14 = (bf16[1024,64]{0,1:T(8,128)(2,1)S(1)}, bf16[1024,64]{0,1:T(8,128)(2,1)S(1)}, u32[]{:S(2)}, u32[]{:S(2)}) collective-permute-start(bf16[1024,64]{0,1:T(8,128)(2,1)S(1)} %copy-done.3), channel_id=1, source_target_pairs={{3,0},{0,1},{1,2},{2,3},{7,4},{4,5},{5,6},{6,7},{11,8},{8,9},{9,10... | collective-permute-start | bytes 393224 | tf_op jit(solution)/shard_map/ppermute | solution.py:21
  26.6 23.6 %collective-permute-start.12 = (bf16[1024,64]{0,1:T(8,128)(2,1)S(1)}, bf16[1024,64]{0,1:T(8,128)(2,1)S(1)}, u32[]{:S(2)}, u32[]{:S(2)}) collective-permute-start(bf16[1024,64]{0,1:T(8,128)(2,1)S(1)} %copy-done.3), channel_id=1, source_target_pairs={{2,0},{3,1},{0,2},{1,3},{6,4},{7,5},{4,6},{5,7},{10,8},{11,9},{8,1... | collective-permute-start | bytes 393224 | tf_op jit(solution)/shard_map/ppermute | solution.py:21
  29.4 13.6 %copy-start = (f32[1024,64]{0,1:T(8,128)S(1)}, f32[1024,64]{0,1:T(8,128)}, u32[]{:S(2)}) copy-start(f32[1024,64]{0,1:T(8,128)} %param.9) | copy-start | bytes 786436
  41.7 1.2 %copy-start.2 = (f32[256,64]{1,0:T(8,128)S(1)}, f32[256,64]{1,0:T(8,128)}, u32[]{:S(2)}) copy-start(f32[256,64]{1,0:T(8,128)} %get-tuple-element.4) | copy-start | bytes 196612
  43.8 3.7 %copy-start.1 = (f32[256,256]{1,0:T(8,128)S(1)}, f32[256,256]{1,0:T(8,128)}, u32[]{:S(2)}) copy-start(f32[256,256]{1,0:T(8,128)} %get-tuple-element.5) | copy-start | bytes 786436
  45.4 9.8 %collective-permute-start.11 = (bf16[1024,64]{0,1:T(8,128)(2,1)S(1)}, bf16[1024,64]{0,1:T(8,128)(2,1)S(1)}, u32[]{:S(2)}, u32[]{:S(2)}) collective-permute-start(bf16[1024,64]{0,1:T(8,128)(2,1)S(1)} %get-tuple-element.8), channel_id=1, source_target_pairs={{1,0},{2,1},{3,2},{0,3},{5,4},{6,5},{7,6},{4,7},{9,8},{10,9},{11,1... | collective-permute-start | bytes 393224 | tf_op jit(solution)/shard_map/ppermute | solution.py:21
  45.8 7.8 %collective-permute-start.15 = (bf16[1024,64]{0,1:T(8,128)(2,1)S(1)}, bf16[1024,64]{0,1:T(8,128)(2,1)S(1)}, u32[]{:S(2)}, u32[]{:S(2)}) collective-permute-start(bf16[1024,64]{0,1:T(8,128)(2,1)S(1)} %get-tuple-element.8), channel_id=1, source_target_pairs={{3,0},{0,1},{1,2},{2,3},{7,4},{4,5},{5,6},{6,7},{11,8},{8,9},{9,10... | collective-permute-start | bytes 393224 | tf_op jit(solution)/shard_map/ppermute | solution.py:21
  50.2 9.6 %collective-permute-start.13 = (bf16[1024,64]{0,1:T(8,128)(2,1)S(1)}, bf16[1024,64]{0,1:T(8,128)(2,1)S(1)}, u32[]{:S(2)}, u32[]{:S(2)}) collective-permute-start(bf16[1024,64]{0,1:T(8,128)(2,1)S(1)} %get-tuple-element.8), channel_id=1, source_target_pairs={{2,0},{3,1},{0,2},{1,3},{6,4},{7,5},{4,6},{5,7},{10,8},{11,9},{8,1... | collective-permute-start | bytes 393224 | tf_op jit(solution)/shard_map/ppermute | solution.py:21
  51.1 11.9 %collective-permute-start.18 = (bf16[1024,64]{0,1:T(8,128)(2,1)S(1)}, bf16[1024,64]{0,1:T(8,128)(2,1)S(1)}, u32[]{:S(2)}, u32[]{:S(2)}) collective-permute-start(bf16[1024,64]{0,1:T(8,128)(2,1)S(1)} %collective-permute-done.12), channel_id=1, source_target_pairs={{28,0},{29,1},{6,2},{7,3},{0,4},{1,5},{10,6},{11,7},{4,8},{5,9},{1... | collective-permute-start | bytes 393224 | tf_op jit(solution)/shard_map/ppermute | solution.py:174
  51.3 13.4 %collective-permute-start.20 = (bf16[1024,64]{0,1:T(8,128)(2,1)S(1)}, bf16[1024,64]{0,1:T(8,128)(2,1)S(1)}, u32[]{:S(2)}, u32[]{:S(2)}) collective-permute-start(bf16[1024,64]{0,1:T(8,128)(2,1)S(1)} %collective-permute-done.14), channel_id=1, source_target_pairs={{28,0},{5,1},{6,2},{7,3},{0,4},{9,5},{10,6},{11,7},{4,8},{13,9},{1... | collective-permute-start | bytes 393224 | tf_op jit(solution)/shard_map/ppermute | solution.py:174
  53.6 11.1 %collective-permute-start.16 = (bf16[1024,64]{0,1:T(8,128)(2,1)S(1)}, bf16[1024,64]{0,1:T(8,128)(2,1)S(1)}, u32[]{:S(2)}, u32[]{:S(2)}) collective-permute-start(bf16[1024,64]{0,1:T(8,128)(2,1)S(1)} %collective-permute-done.10), channel_id=1, source_target_pairs={{28,0},{29,1},{30,2},{7,3},{0,4},{1,5},{2,6},{11,7},{4,8},{5,9},{6... | collective-permute-start | bytes 393224 | tf_op jit(solution)/shard_map/ppermute | solution.py:174
  55.2 11.5 %collective-permute-start.21 = (bf16[1024,64]{0,1:T(8,128)(2,1)S(1)}, bf16[1024,64]{0,1:T(8,128)(2,1)S(1)}, u32[]{:S(2)}, u32[]{:S(2)}) collective-permute-start(bf16[1024,64]{0,1:T(8,128)(2,1)S(1)} %collective-permute-done.15), channel_id=1, source_target_pairs={{28,0},{5,1},{6,2},{7,3},{0,4},{9,5},{10,6},{11,7},{4,8},{13,9},{1... | collective-permute-start | bytes 393224 | tf_op jit(solution)/shard_map/ppermute | solution.py:174
  59.8 5.3 %collective-permute-start.19 = (bf16[1024,64]{0,1:T(8,128)(2,1)S(1)}, bf16[1024,64]{0,1:T(8,128)(2,1)S(1)}, u32[]{:S(2)}, u32[]{:S(2)}) collective-permute-start(bf16[1024,64]{0,1:T(8,128)(2,1)S(1)} %collective-permute-done.13), channel_id=1, source_target_pairs={{28,0},{29,1},{6,2},{7,3},{0,4},{1,5},{10,6},{11,7},{4,8},{5,9},{1... | collective-permute-start | bytes 393224 | tf_op jit(solution)/shard_map/ppermute | solution.py:174
  63.0 5.5 %collective-permute-start.17 = (bf16[1024,64]{0,1:T(8,128)(2,1)S(1)}, bf16[1024,64]{0,1:T(8,128)(2,1)S(1)}, u32[]{:S(2)}, u32[]{:S(2)}) collective-permute-start(bf16[1024,64]{0,1:T(8,128)(2,1)S(1)} %collective-permute-done.11), channel_id=1, source_target_pairs={{28,0},{29,1},{30,2},{7,3},{0,4},{1,5},{2,6},{11,7},{4,8},{5,9},{6... | collective-permute-start | bytes 393224 | tf_op jit(solution)/shard_map/ppermute | solution.py:174

commit v3 on v2

--- a/solution.py
+++ b/solution.py
@@ -19,16 +19,6 @@
 def shifted(value, axis, steps):
     count = lax.axis_size(axis)
     return lax.ppermute(value, axis, [((i + steps) % count, i) for i in range(count)])
-
-
-def summed(value, axis):
-    count = lax.axis_size(axis)
-    if count > 8:
-        return lax.psum(value, axis)
-    total = value
-    for steps in range(1, count):
-        total = total + shifted(value, axis, steps)
-    return total
 
 
 def kern(left, right):
@@ -158,45 +148,71 @@
     )(pivots, coeffs)
 
 
-def neighbours(value, tall):
+def from_owners(picked, owners):
     outer, inner = lax.axis_size("gx"), lax.axis_size("gy")
-    if not tall:
-        return [shifted(value, ("gx", "gy"), k) for k in range(-BAND, BAND + 1) if k != 0]
-    own, other = [], []
-    for k in range(1, inner):
-        own.append(shifted(value, "gy", k))
-    for k in range(1, inner):
+    rounds = picked.reshape(2, PIVOTS, -1)
+
+    def owned(offered, places):
+        return jnp.stack([lax.dynamic_index_in_dim(offered, places[r], 0, keepdims=False)[r] for r in range(2)])
+
+    if outer * inner <= 64:
+        kept = owned(lax.all_gather(rounds, ("gx", "gy")), owners)
+    else:
+        kept = owned(lax.all_gather(rounds, "gy"), lax.rem(owners, inner))
+        kept = owned(lax.all_gather(kept, "gx"), lax.div(owners, inner))
+    return kept.reshape(picked.shape)
+
+
+def column_blocks(value):
+    return lax.all_gather(value, "gy", axis=0, tiled=True)
+
+
+def crossing(value, count):
+    outer, inner = lax.axis_size("gx"), lax.axis_size("gy")
+    z = lax.axis_index("gy")
+    pair = jnp.where(z < 2, value[2 * count:], value[:2 * count])
+    order = (1, 0, 3, 2)
+    single = lax.dynamic_slice_in_dim(value, jnp.where(z < 2, 1 - z, 5 - z) * count, count, 0)
+
+    def send(piece, before):
         pairs = []
         for x in range(outer):
-            for z in range(inner):
-                source = (x - 1 if z + k < inner else x + 1) % outer
-                pairs.append((source * inner + z, x * inner + z))
-        other.append(lax.ppermute(own[k - 1], ("gx", "gy"), pairs))
-    return own + other
+            for place in range(inner):
+                source = (x - 1 if place in before else x + 1) % outer
+                pairs.append((source * inner + place, x * inner + place))
+        return lax.ppermute(piece, ("gx", "gy"), pairs)
+
+    return [send(pair, (0, 1)), send(single, (0, 2))]
+
+
+def band(value, tall):
+    count = value.shape[0]
+    if not tall:
+        return [value] + [shifted(value, ("gx", "gy"), k) for k in range(-BAND, BAND + 1) if k != 0]
+    whole = column_blocks(value)
+    return [whole] + crossing(whole, count)
 
 
 def shards(points, pivots, owners, coeffs, noise):
     hp = lax.Precision.HIGHEST
     count, width = points.shape
     tall = lax.axis_size("gy") == BAND + 1
-    me = lax.axis_index(("gx", "gy"))
 
     index = lax.broadcasted_iota(jnp.int32, (2, PIVOTS, count), 2)
-    wanted = jnp.where((owners == me)[:, None], pivots, -1)
-    chosen = (index == wanted[:, :, None]).astype(jnp.bfloat16).reshape(2 * PIVOTS, count)
+    chosen = (index == pivots[:, :, None]).astype(jnp.bfloat16).reshape(2 * PIVOTS, count)
     picked = jnp.dot(chosen, points, preferred_element_type=jnp.float32).astype(jnp.bfloat16)
-    pivot_points = summed(summed(picked, "gy"), "gx")
-    near_points = neighbours(points, tall)
+    pivot_points = from_owners(picked, owners)
+    near_points = band(points, tall)
 
     inverse, weights = invert_factor(pivot_points, coeffs)
     cols = kern(points, pivot_points)
     probes = jnp.dot(cols, weights, precision=hp, preferred_element_type=jnp.float32) + noise
     sent = probes.astype(jnp.bfloat16)
-    near_probes = neighbours(sent, tall)
+    near_probes = band(sent, tall)
     factor = jnp.dot(cols, inverse.T, precision=hp, preferred_element_type=jnp.float32)
 
     total = jnp.zeros((count, probes.shape[1]), jnp.float32)
-    for other, probe in zip([points] + near_points, [sent] + near_probes):
+    for other, probe in zip(near_points, near_probes):
         tile = kern(points, other).astype(jnp.bfloat16)
         total = total + jnp.dot(tile, probe, preferred_element_type=jnp.float32)
     kernel_probes = total / jnp.sqrt(1.0 * count) + noise_weight * probes

time: 71.1 us -> 126 us (1.77)
  blocking collectives: 0 us -> 33.5 us
  waiting for transfers between devices: 10.8 us -> 35.3 us
  starting transfers between devices: 24.8 us -> 3.1 us
  between operations: 0.81 us -> 18 us
  local copies, waits for them, and re-layouts: 0.78 us -> 3.54 us
  other arithmetic: 3.36 us -> 1.55 us
    all_gather x0 -> x2, blocking collectives: none -> 33.5 us  [column_blocks(): return lax.all_gather(value, 'gy', axis=0, tiled=True)]
    all_gather x0 -> x1, waiting for transfers between devices: none -> 31.7 us  [from_owners(): kept = owned(lax.all_gather(rounds, ('gx', 'gy')), owners)]
    ppermute x22 -> x4, starting transfers between devices: 24.8 us -> 3.07 us  [send(): return lax.ppermute(piece, ('gx', 'gy'), pairs)]
    ppermute x22 -> x4, waiting for transfers between devices: 10.8 us -> 3.64 us  [send(): return lax.ppermute(piece, ('gx', 'gy'), pairs)]
    eq x2 -> x0, other arithmetic: 1.46 us -> none  [the longest x1 0.75 us: shards(): index == wanted[:, :, None]]
    another operation x0 -> x3, local copies, waits for them, and re-layouts: none -> 1.36 us  [the longest x1 0.73 us: owned(): jnp.stack([lax.dynamic_index_in_dim(offered, places[r], 0, keepdims=False...]
    slice x0 -> x2, local copies, waits for them, and re-layouts: none -> 1.34 us  [the longest x1 0.74 us: owned(): lax.dynamic_index_in_dim(offered, places[r], 0, keepdims=False)[r]]
    dot_general x7 -> x3, matrix products: 11.8 us -> 12.5 us  [shards(): total = total + jnp.dot(tile, probe, preferred_element_type=jnp.float32)]
  transfers between devices with their start and end apart: 22 -> 5, of which waited for: 6 -> 3; matrix products, arithmetic and copies ran while one was open for 24% -> 7% of each run, Pallas kernels for 17% -> 0%
where the time goes in v3:
time: 126 us
  waiting for transfers between devices  35.3 us (28%)
  blocking collectives  33.5 us (27%)
  matrix products  18.6 us (15%)
  between operations  18 us (14%)
  Pallas kernels  12.3 us (10%)
  local copies, waits for them, and re-layouts  3.54 us (3%)
  starting transfers between devices  3.1 us (2%)
  other arithmetic  1.55 us (1%)
    all_gather x2, blocking collectives, column_blocks(): return lax.all_gather(value, 'gy', axis=0, tiled=True)  33.5 us
    all_gather x1, waiting for transfers between devices, from_owners(): kept = owned(lax.all_gather(rounds, ('gx', 'gy')), owners)  31.7 us
    dot_general x3, matrix products, shards(): total = total + jnp.dot(tile, probe, preferred_element_type=jnp.float32)  12.5 us
    pallas_call x1, Pallas kernels, invert_factor(): pl.pallas_call(invert_factor_kernel, out_shape=(jax.ShapeDtypeStruct((siz...  12.3 us
    ppermute x4, waiting for transfers between devices, send(): return lax.ppermute(piece, ('gx', 'gy'), pairs)  3.64 us
    ppermute x4, starting transfers between devices, send(): return lax.ppermute(piece, ('gx', 'gy'), pairs)  3.07 us
    dot_general x1, matrix products, shards(): jnp.dot(cols, inverse.T, precision=hp, preferred_element_type=jnp.float32)  2.78 us
  transfers between devices with their start and end apart: 5, of which 3 were waited for; matrix products, arithmetic and copies ran while one was open for 7% of the time, Pallas kernels for 0%

profile of v3, /device:TPU:0, one launch (start us, length us, event | category | flops | bytes accessed | tf_op | source)
XLA Modules:
  0.0 125.8 jit_solution(2427015009694419056)
XLA Ops:
  7.2 0.0 all-gather.2.cloned.1.call-start
  7.2 1.3 %convolution_convert_fusion = bf16[256,64]{0,1:T(8,128)(2,1)S(1)} fusion(bf16[1024,64]{0,1:T(8,128)(2,1)} %param.5, s32[256]{0:T(256)} %bitcast.72), kind=kOutput, calls=%fused_computation.25 | convolution fusion | flops 33832960 | bytes 164864 | tf_op jit(solution)/shard_map/dot_general | solution.py:203
  8.5 0.6 copy.9
  9.1 0.0 all-gather.2.cloned.1.call-update
  9.2 0.0 copy-start.9
  9.2 0.0 copy-start.4
  9.2 17.7 %all_gather.9 = bf16[4096,64]{0,1:T(8,128)(2,1)S(1)} all-gather(bf16[1024,64]{0,1:T(8,128)(2,1)} %param.5), channel_id=1, replica_groups=mesh['gx'=8,'gy'=4] {'gy'}, dimensions={0}, use_global_device_ids=true | all-gather | bytes 655360 | tf_op jit(solution)/shard_map/all_gather | solution.py:167
  26.9 0.1 collective-permute-start
  27.0 1.6 %collective-permute-start.2 = (bf16[1024,64]{0,1:T(8,128)(2,1)S(1)}, bf16[1024,64]{0,1:T(8,128)(2,1)S(1)}, u32[]{:S(2)}, u32[]{:S(2)}) collective-permute-start(bf16[1024,64]{0,1:T(8,128)(2,1)S(1)} %constant_dynamic-slice_fusion.1), channel_id=1, source_target_pairs={{28,0},{5,1},{30,2},{7,3},{0,4},{9,5},{2,6},{11,7},{4,8},{13,9},{6... | collective-permute-start | bytes 393224 | tf_op jit(solution)/shard_map/ppermute | solution.py:183
  28.7 0.1 multiply_reduce_fusion
  28.8 0.6 fusion.27
  31.9 0.8 copy.11.coeff_ref
  34.0 1.1 collective-permute-done.2
  35.1 0.6 multiply_reduce_fusion.2
  35.7 0.0 collective-permute-done
  35.7 0.7 multiply_reduce_fusion.1
  36.4 31.7 %all-gather.2.cloned.1.call-done = bf16[32,2,128,64]{2,3,1,0:T(8,128)(2,1)} async-done(((bf16[1,2,128,64]{2,3,1,0:T(8,128)(2,1)}), bf16[32,2,128,64]{2,3,1,0:T(8,128)(2,1)}) %all-gather.2.cloned.1.call-update) | async-done | bytes 1048592 | tf_op jit(solution)/shard_map/all_gather | solution.py:159
  68.1 0.7 dynamic-slice_bitcast_fusion.1
  68.8 0.7 copy.10
  69.6 12.3 %invert_factor.1 = (f32[256,256]{1,0:T(8,128)}, f32[256,64]{1,0:T(8,128)}) custom-call(bf16[256,64]{1,0:T(8,128)(2,1)} %bitcast.69, f32[256,64]{1,0:T(8,128)} %copy.11.coeff_ref), custom_call_target="tpu_custom_call" | custom-call | flops 100663296 | bytes 262144 | tf_op jit(solution)/shard_map/invert_factor/pallas_call | solution.py:137
  81.9 1.2 fusion.15
  83.1 0.8 fusion.28
  83.9 15.8 %all_gather.11 = bf16[4096,64]{0,1:T(8,128)(2,1)S(1)} all-gather(bf16[1024,64]{0,1:T(8,128)(2,1)S(1)} %get-tuple-element.10), channel_id=1, replica_groups=mesh['gx'=8,'gy'=4] {'gy'}, dimensions={0}, use_global_device_ids=true | all-gather | bytes 655360 | tf_op jit(solution)/shard_map/all_gather | solution.py:167
  99.8 0.0 copy-start.2
  99.8 7.2 %fusion.8 = f32[1024,64]{0,1:T(8,128)} fusion(bf16[4096,64]{0,1:T(8,128)(2,1)S(1)} %all_gather.11, bf16[1024,64]{0,1:T(8,128)(2,1)S(1)} %copy-done, bf16[4096,64]{0,1:T(8,128)(2,1)S(1)} %all_gather.9, f32[4096]{0:T(1024)S(1)} %multiply_reduce_fusion, f32[1024]{0:T(1024)} %copy-done.6), kind=kOutput, calls=%fused_computation.11 | convolution fusion | flops 1098907648 | bytes 1462272 | tf_op jit(solution)/shard_map/dot_general | solution.py:217
  107.0 0.0 collective-permute-start.1
  107.0 1.4 %collective-permute-start.3 = (bf16[1024,64]{0,1:T(8,128)(2,1)S(1)}, bf16[1024,64]{0,1:T(8,128)(2,1)S(1)}, u32[]{:S(2)}, u32[]{:S(2)}) collective-permute-start(bf16[1024,64]{0,1:T(8,128)(2,1)S(1)} %constant_dynamic-slice_fusion), channel_id=1, source_target_pairs={{28,0},{5,1},{30,2},{7,3},{0,4},{9,5},{2,6},{11,7},{4,8},{13,9},{6... | collective-permute-start | bytes 393224 | tf_op jit(solution)/shard_map/ppermute | solution.py:183
  108.4 2.8 %fusion.29 = f32[1024,256]{1,0:T(8,128)} fusion(f32[1024,256]{0,1:T(8,128)S(1)} %fusion.15, f32[256,256]{1,0:T(8,128)S(1)} %copy-done.2), kind=kOutput, calls=%fused_computation.48 | convolution fusion | flops 805306368 | bytes 2359296 | tf_op jit(solution)/shard_map/dot_general | solution.py:212
  111.2 2.5 %collective-permute-done.1 = bf16[2048,64]{0,1:T(8,128)(2,1)S(1)} collective-permute-done((bf16[2048,64]{0,1:T(8,128)(2,1)S(1)}, bf16[2048,64]{0,1:T(8,128)(2,1)S(1)}, u32[]{:S(2)}, u32[]{:S(2)}) %collective-permute-start.1) | collective-permute-done | bytes 262176 | tf_op jit(solution)/shard_map/ppermute | solution.py:183
  113.7 3.0 %fusion.19 = f32[1024,64]{0,1:T(8,128)S(1)} fusion(f32[1024,64]{0,1:T(8,128)S(1)} %copy-done.10, bf16[2048,64]{0,1:T(8,128)(2,1)S(1)} %collective-permute-done.1, bf16[2048,64]{0,1:T(8,128)(2,1)S(1)} %collective-permute-done, bf16[1024,64]{0,1:T(8,128)(2,1)S(1)} %copy-done, f32[2048]{0:T(1024)S(1)} %copy-done.5, f32[1024]{0:T(1024)S(1)} %copy-done.7), kind=kOutput, calls=%fused_computation.24 | convolution fusion | flops 549519360 | bytes 1191936 | tf_op jit(solution)/shard_map/dot_general | solution.py:217
  116.6 0.0 collective-permute-done.3
  116.6 2.3 %fusion.18 = f32[1024,64]{0,1:T(8,128)} fusion(f32[1024,64]{0,1:T(8,128)S(1)} %fusion.19, bf16[1024,64]{0,1:T(8,128)(2,1)S(1)} %collective-permute-done.3, bf16[1024,64]{0,1:T(8,128)(2,1)S(1)} %collective-permute-done.2, bf16[1024,64]{0,1:T(8,128)(2,1)S(1)} %copy-done, f32[1024]{0:T(1024)S(1)} %copy-done.8, f32[1024]{0:T(1024)S(1)} %copy-done.7, ...), kind=kOutput, calls=%fused_computation.23 | convolution fusion | flops 274989056 | bytes 1187840 | tf_op jit(solution)/shard_map/dot_general | solution.py:217
  (27 shorter events, 0.2 us)
Async XLA Ops:
  7.2 60.9 %all-gather.2.cloned.1.call-start = ((), (), s32[]{:S(2)}) async-start(), calls=%async_computation | async-start | bytes 1081344 | tf_op jit(solution)/shard_map/all_gather | solution.py:159
  9.2 19.6 %copy-start.9 = (s32[2]{0:T(128)S(1)}, s32[2]{0:T(128)}, u32[]{:S(2)}) copy-start(s32[2]{0:T(128)} %param.7) | copy-start | bytes 28
  9.2 22.7 %copy-start.4 = (f32[256,64]{0,1:T(8,128)S(1)}, f32[256,64]{0,1:T(8,128)}, u32[]{:S(2)}) copy-start(f32[256,64]{0,1:T(8,128)} %param.8) | copy-start | bytes 196612
  26.9 7.0 %copy-start = (bf16[1024,64]{0,1:T(8,128)(2,1)S(1)}, bf16[1024,64]{0,1:T(8,128)(2,1)}, u32[]{:S(2)}) copy-start(bf16[1024,64]{0,1:T(8,128)(2,1)} %param.5) | copy-start | bytes 393220
  26.9 8.8 %collective-permute-start = (bf16[2048,64]{0,1:T(8,128)(2,1)S(1)}, bf16[2048,64]{0,1:T(8,128)(2,1)S(1)}, u32[]{:S(2)}, u32[]{:S(2)}) collective-permute-start(bf16[2048,64]{0,1:T(8,128)(2,1)S(1)} %slice_select_fusion.1), channel_id=1, source_target_pairs={{28,0},{29,1},{6,2},{7,3},{0,4},{1,5},{10,6},{11,7},{4,8},{5,9},{1... | collective-permute-start | bytes 786440 | tf_op jit(solution)/shard_map/ppermute | solution.py:183
  27.0 8.0 %collective-permute-start.2 = (bf16[1024,64]{0,1:T(8,128)(2,1)S(1)}, bf16[1024,64]{0,1:T(8,128)(2,1)S(1)}, u32[]{:S(2)}, u32[]{:S(2)}) collective-permute-start(bf16[1024,64]{0,1:T(8,128)(2,1)S(1)} %constant_dynamic-slice_fusion.1), channel_id=1, source_target_pairs={{28,0},{5,1},{30,2},{7,3},{0,4},{9,5},{2,6},{11,7},{4,8},{13,9},{6... | collective-permute-start | bytes 393224 | tf_op jit(solution)/shard_map/ppermute | solution.py:183
  34.0 49.1 %copy-start.6 = (f32[1024]{0:T(1024)}, f32[1024]{0:T(1024)S(1)}, u32[]{:S(2)}) copy-start(f32[1024]{0:T(1024)S(1)} %multiply_reduce_fusion.3) | copy-start | bytes 12292
  68.8 14.3 %copy-start.1 = (f32[1024,64]{0,1:T(8,128)S(1)}, f32[1024,64]{0,1:T(8,128)}, u32[]{:S(2)}) copy-start(f32[1024,64]{0,1:T(8,128)} %param.9) | copy-start | bytes 786436
  81.9 1.2 copy-start.3
  99.8 8.6 %copy-start.2 = (f32[256,256]{1,0:T(8,128)S(1)}, f32[256,256]{1,0:T(8,128)}, u32[]{:S(2)}) copy-start(f32[256,256]{1,0:T(8,128)} %get-tuple-element.5) | copy-start | bytes 786436
  107.0 6.7 %collective-permute-start.1 = (bf16[2048,64]{0,1:T(8,128)(2,1)S(1)}, bf16[2048,64]{0,1:T(8,128)(2,1)S(1)}, u32[]{:S(2)}, u32[]{:S(2)}) collective-permute-start(bf16[2048,64]{0,1:T(8,128)(2,1)S(1)} %slice_select_fusion), channel_id=1, source_target_pairs={{28,0},{29,1},{6,2},{7,3},{0,4},{1,5},{10,6},{11,7},{4,8},{5,9},{1... | collective-permute-start | bytes 786440 | tf_op jit(solution)/shard_map/ppermute | solution.py:183
  107.0 9.7 %collective-permute-start.3 = (bf16[1024,64]{0,1:T(8,128)(2,1)S(1)}, bf16[1024,64]{0,1:T(8,128)(2,1)S(1)}, u32[]{:S(2)}, u32[]{:S(2)}) collective-permute-start(bf16[1024,64]{0,1:T(8,128)(2,1)S(1)} %constant_dynamic-slice_fusion), channel_id=1, source_target_pairs={{28,0},{5,1},{30,2},{7,3},{0,4},{9,5},{2,6},{11,7},{4,8},{13,9},{6... | collective-permute-start | bytes 393224 | tf_op jit(solution)/shard_map/ppermute | solution.py:183
  108.4 5.3 %copy-start.5 = (f32[2048]{0:T(1024)S(1)}, f32[2048]{0:T(1024)}, u32[]{:S(2)}) copy-start(f32[2048]{0:T(1024)} %multiply_reduce_fusion.1) | copy-start | bytes 24580
  108.4 5.3 %copy-start.7 = (f32[1024]{0:T(1024)S(1)}, f32[1024]{0:T(1024)}, u32[]{:S(2)}) copy-start(f32[1024]{0:T(1024)} %copy-done.6) | copy-start | bytes 12292
  108.4 5.3 %copy-start.10 = (f32[1024,64]{0,1:T(8,128)S(1)}, f32[1024,64]{0,1:T(8,128)}, u32[]{:S(2)}) copy-start(f32[1024,64]{0,1:T(8,128)} %fusion.8) | copy-start | bytes 786436
  111.2 5.5 %copy-start.8 = (f32[1024]{0:T(1024)S(1)}, f32[1024]{0:T(1024)}, u32[]{:S(2)}) copy-start(f32[1024]{0:T(1024)} %multiply_reduce_fusion.2) | copy-start | bytes 12292
Sparse Core Ops, SparseCore 0:
  11.6 56.4 all-gather.1

commit v4 on v2

--- a/solution.py
+++ b/solution.py
@@ -21,14 +21,16 @@
     return lax.ppermute(value, axis, [((i + steps) % count, i) for i in range(count)])
 
 
+def swapped(value, axis, bit):
+    return lax.ppermute(value, axis, [(i ^ bit, i) for i in range(lax.axis_size(axis))])
+
+
 def summed(value, axis):
-    count = lax.axis_size(axis)
-    if count > 8:
-        return lax.psum(value, axis)
-    total = value
-    for steps in range(1, count):
-        total = total + shifted(value, axis, steps)
-    return total
+    bit = 1
+    while bit < lax.axis_size(axis):
+        value = value + swapped(value, axis, bit)
+        bit *= 2
+    return value
 
 
 def kern(left, right):
@@ -162,17 +164,19 @@
     outer, inner = lax.axis_size("gx"), lax.axis_size("gy")
     if not tall:
         return [shifted(value, ("gx", "gy"), k) for k in range(-BAND, BAND + 1) if k != 0]
-    own, other = [], []
-    for k in range(1, inner):
-        own.append(shifted(value, "gy", k))
-    for k in range(1, inner):
+
+    def cross(piece, bits):
         pairs = []
         for x in range(outer):
             for z in range(inner):
-                source = (x - 1 if z + k < inner else x + 1) % outer
+                source = (x - 1 if z ^ bits > z else x + 1) % outer
                 pairs.append((source * inner + z, x * inner + z))
-        other.append(lax.ppermute(own[k - 1], ("gx", "gy"), pairs))
-    return own + other
+        return lax.ppermute(piece, ("gx", "gy"), pairs)
+
+    two = swapped(value, "gy", 2)
+    one = swapped(value, "gy", 1)
+    three = swapped(two, "gy", 1)
+    return [one, two, cross(one, 1), cross(two, 2), three, cross(three, 3)]
 
 
 def shards(points, pivots, owners, coeffs, noise):
@@ -185,8 +189,9 @@
     wanted = jnp.where((owners == me)[:, None], pivots, -1)
     chosen = (index == wanted[:, :, None]).astype(jnp.bfloat16).reshape(2 * PIVOTS, count)
     picked = jnp.dot(chosen, points, preferred_element_type=jnp.float32).astype(jnp.bfloat16)
-    pivot_points = summed(summed(picked, "gy"), "gx")
-    near_points = neighbours(points, tall)
+    picked, settled = lax.optimization_barrier((summed(picked, "gy"), points))
+    pivot_points = summed(picked, "gx")
+    near_points = neighbours(settled, tall)
 
     inverse, weights = invert_factor(pivot_points, coeffs)
     cols = kern(points, pivot_points)

time: 71.1 us -> 67.5 us (0.949)
  starting transfers between devices: 24.8 us -> 23.2 us
  waiting for transfers between devices: 10.8 us -> 9.57 us
  other arithmetic: 3.36 us -> 2.45 us
    ppermute x22 -> x17, starting transfers between devices: 24.8 us -> 23.2 us  [the longest x11 18.5 us: swapped(): lax.ppermute(value, axis, [(i ^ bit, i) for i in range(lax.axis_size(axis...]
    ppermute x22 -> x17, waiting for transfers between devices: 10.8 us -> 9.57 us  [the longest x11 9.55 us: swapped(): lax.ppermute(value, axis, [(i ^ bit, i) for i in range(lax.axis_size(axis...]
    reduce_sum x1, other arithmetic: 0.94 us -> 0.04 us  [kern(): left_square_norm = jnp.sum(jnp.square(left.astype(jnp.float32)), axis=1)]
  transfers between devices with their start and end apart: 22 -> 17, of which waited for: 6 -> 5; matrix products, arithmetic and copies ran while one was open for 24% -> 24% of each run, Pallas kernels for 17% -> 18%
where the time goes in v4:
time: 67.5 us; the launch traced here: 67.3 us
  starting transfers between devices  23.2 us (34%)
  matrix products  18.1 us (27%)
  Pallas kernels  12.3 us (18%)
  waiting for transfers between devices  9.57 us (14%)
  other arithmetic  2.45 us (4%)
  between operations  0.84 us (1%)
  local copies, waits for them, and re-layouts  0.78 us (1%)
    ppermute x11, starting transfers between devices, swapped(): lax.ppermute(value, axis, [(i ^ bit, i) for i in range(lax.axis_size(axis...  18.5 us
    pallas_call x1, Pallas kernels, invert_factor(): pl.pallas_call(invert_factor_kernel, out_shape=(jax.ShapeDtypeStruct((siz...  12.3 us
    dot_general x7, matrix products, shards(): total = total + jnp.dot(tile, probe, preferred_element_type=jnp.float32)  12 us
    ppermute x11, waiting for transfers between devices, swapped(): lax.ppermute(value, axis, [(i ^ bit, i) for i in range(lax.axis_size(axis...  9.55 us
    ppermute x6, starting transfers between devices, cross(): return lax.ppermute(piece, ('gx', 'gy'), pairs)  4.76 us
    dot_general x1, matrix products, shards(): jnp.dot(cols, inverse.T, precision=hp, preferred_element_type=jnp.float32)  2.78 us
  transfers between devices with their start and end apart: 17, of which 5 were waited for; matrix products, arithmetic and copies ran while one was open for 24% of the time, Pallas kernels for 18%

profile of v4, /device:TPU:0, one launch (start us, length us, event | category | flops | bytes accessed | tf_op | source)
XLA Modules:
  0.0 67.3 jit_solution(10707315218387000736)
XLA Ops:
  0.7 0.7 %broadcast_compare_fusion = pred[2]{0:T(512)(128)(4,1)S(1)} fusion(s32[2]{0:T(128)} %param.7, s32[]{:T(128)S(6)} %add.68), kind=kLoop, calls=%fused_computation.65 | loop fusion | flops 2 | bytes 14 | tf_op jit(solution)/shard_map/eq | solution.py:189
  1.4 0.7 %select_bitcast_fusion = s32[256]{0:T(256)S(1)} fusion(s32[2,128]{1,0:T(2,128)} %param.6, pred[2]{0:T(512)(128)(4,1)S(1)} %broadcast_compare_fusion), kind=kLoop, calls=%fused_computation.64 | loop fusion | flops 256 | bytes 2050 | tf_op jit(solution)/shard_map/eq | solution.py:190
  2.1 1.3 %convolution_convert_fusion = bf16[256,64]{1,0:T(8,128)(2,1)S(1)} fusion(bf16[1024,64]{0,1:T(8,128)(2,1)} %param.5, s32[256]{0:T(256)S(1)} %select_bitcast_fusion), kind=kOutput, calls=%fused_computation.53 | convolution fusion | flops 33832960 | bytes 164864 | tf_op jit(solution)/shard_map/dot_general | solution.py:191
  3.4 3.1 %collective-permute-start = (bf16[256,64]{1,0:T(8,128)(2,1)S(1)}, bf16[256,64]{1,0:T(8,128)(2,1)S(1)}, u32[]{:S(2)}, u32[]{:S(2)}) collective-permute-start(bf16[256,64]{1,0:T(8,128)(2,1)S(1)} %convolution_convert_fusion), channel_id=1, source_target_pairs={{1,0},{0,1},{3,2},{2,3},{5,4},{4,5},{7,6},{6,7},{9,8},{8,9},{11,10... | collective-permute-start | bytes 98312 | tf_op jit(solution)/shard_map/ppermute | solution.py:25
  6.5 2.2 %collective-permute-done = bf16[256,64]{1,0:T(8,128)(2,1)S(1)} collective-permute-done((bf16[256,64]{1,0:T(8,128)(2,1)S(1)}, bf16[256,64]{1,0:T(8,128)(2,1)S(1)}, u32[]{:S(2)}, u32[]{:S(2)}) %collective-permute-start) | collective-permute-done | bytes 32800 | tf_op jit(solution)/shard_map/ppermute | solution.py:25
  8.7 3.1 %collective-permute-start.1 = (bf16[256,64]{1,0:T(8,128)(2,1)S(1)}, bf16[256,64]{1,0:T(8,128)(2,1)S(1)}, u32[]{:S(2)}, u32[]{:S(2)}) collective-permute-start(bf16[256,64]{1,0:T(8,128)(2,1)S(1)} %add.69), channel_id=1, source_target_pairs={{2,0},{3,1},{0,2},{1,3},{6,4},{7,5},{4,6},{5,7},{10,8},{11,9},{8,1... | collective-permute-start | bytes 98312 | tf_op jit(solution)/shard_map/ppermute | solution.py:25
  11.8 2.2 %collective-permute-done.1 = bf16[256,64]{1,0:T(8,128)(2,1)S(1)} collective-permute-done((bf16[256,64]{1,0:T(8,128)(2,1)S(1)}, bf16[256,64]{1,0:T(8,128)(2,1)S(1)}, u32[]{:S(2)}, u32[]{:S(2)}) %collective-permute-start.1) | collective-permute-done | bytes 32800 | tf_op jit(solution)/shard_map/ppermute | solution.py:25
  14.2 1.2 %collective-permute-done.2 = bf16[256,64]{1,0:T(8,128)(2,1)S(1)} collective-permute-done((bf16[256,64]{1,0:T(8,128)(2,1)S(1)}, bf16[256,64]{1,0:T(8,128)(2,1)S(1)}, u32[]{:S(2)}, u32[]{:S(2)}) %collective-permute-start.2) | collective-permute-done | bytes 32800 | tf_op jit(solution)/shard_map/ppermute | solution.py:25
  15.4 1.9 %collective-permute-start.3 = (bf16[256,64]{1,0:T(8,128)(2,1)S(1)}, bf16[256,64]{1,0:T(8,128)(2,1)S(1)}, u32[]{:S(2)}, u32[]{:S(2)}) collective-permute-start(bf16[256,64]{1,0:T(8,128)(2,1)S(1)} %add.141), channel_id=1, source_target_pairs={{8,0},{12,4},{0,8},{4,12},{24,16},{28,20},{16,24},{20,28},{9,1},{1... | collective-permute-start | bytes 98312 | tf_op jit(solution)/shard_map/ppermute | solution.py:25
  17.3 2.4 %collective-permute-done.3 = bf16[256,64]{1,0:T(8,128)(2,1)S(1)} collective-permute-done((bf16[256,64]{1,0:T(8,128)(2,1)S(1)}, bf16[256,64]{1,0:T(8,128)(2,1)S(1)}, u32[]{:S(2)}, u32[]{:S(2)}) %collective-permute-start.3) | collective-permute-done | bytes 32800 | tf_op jit(solution)/shard_map/ppermute | solution.py:25
  19.8 1.9 %collective-permute-start.4 = (bf16[256,64]{1,0:T(8,128)(2,1)S(1)}, bf16[256,64]{1,0:T(8,128)(2,1)S(1)}, u32[]{:S(2)}, u32[]{:S(2)}) collective-permute-start(bf16[256,64]{1,0:T(8,128)(2,1)S(1)} %add.142), channel_id=1, source_target_pairs={{16,0},{20,4},{24,8},{28,12},{0,16},{4,20},{8,24},{12,28},{17,1},{... | collective-permute-start | bytes 98312 | tf_op jit(solution)/shard_map/ppermute | solution.py:25
  21.8 0.8 %copy.10.coeff_ref = f32[256,64]{1,0:T(8,128)} copy(f32[256,64]{0,1:T(8,128)S(1)} %copy-done.4) | data formatting | bytes 131072 | tf_op args[3]
  22.5 1.6 %collective-permute-start.5 = (bf16[1024,64]{0,1:T(8,128)(2,1)S(1)}, bf16[1024,64]{0,1:T(8,128)(2,1)S(1)}, u32[]{:S(2)}, u32[]{:S(2)}) collective-permute-start(bf16[1024,64]{0,1:T(8,128)(2,1)S(1)} %copy-done.3), channel_id=1, source_target_pairs={{1,0},{0,1},{3,2},{2,3},{5,4},{4,5},{7,6},{6,7},{9,8},{8,9},{11,10... | collective-permute-start | bytes 393224 | tf_op jit(solution)/shard_map/ppermute | solution.py:25
  24.1 3.2 %collective-permute-start.7 = (bf16[1024,64]{0,1:T(8,128)(2,1)S(1)}, bf16[1024,64]{0,1:T(8,128)(2,1)S(1)}, u32[]{:S(2)}, u32[]{:S(2)}) collective-permute-start(bf16[1024,64]{0,1:T(8,128)(2,1)S(1)} %copy-done.3), channel_id=1, source_target_pairs={{2,0},{3,1},{0,2},{1,3},{6,4},{7,5},{4,6},{5,7},{10,8},{11,9},{8,1... | collective-permute-start | bytes 393224 | tf_op jit(solution)/shard_map/ppermute | solution.py:25
  27.3 0.6 multiply_reduce_fusion.7
  27.9 12.3 %invert_factor.1 = (f32[256,256]{1,0:T(8,128)}, f32[256,64]{1,0:T(8,128)}) custom-call(bf16[256,64]{1,0:T(8,128)(2,1)} %get-tuple-element.11.pivot_ref, f32[256,64]{1,0:T(8,128)} %copy.10.coeff_ref), custom_call_target="tpu_custom_call" | custom-call | flops 100663296 | bytes 262144 | tf_op jit(solution)/shard_map/invert_factor/pallas_call | solution.py:149
  40.2 1.2 %fusion.35 = f32[1024,256]{0,1:T(8,128)S(1)} fusion(bf16[256,64]{1,0:T(8,128)(2,1)} %get-tuple-element.11.pivot_ref, bf16[1024,64]{0,1:T(8,128)(2,1)S(1)} %copy-done.3, f32[256]{0:T(256)S(1)} %get-tuple-element.10, f32[1024]{0:T(1024)S(1)} %multiply_reduce_fusion.6), kind=kOutput, calls=%fused_computation.43 | convolution fusion | flops 34865152 | bytes 1217536 | tf_op jit(solution)/shard_map/dot_general | solution.py:39
  41.5 0.8 %fusion.59 = (bf16[1024,64]{0,1:T(8,128)(2,1)S(1)}, f32[1024,64]{0,1:T(8,128)S(1)}) fusion(f32[1024,64]{0,1:T(8,128)S(1)} %copy-done, f32[1024,256]{0,1:T(8,128)S(1)} %fusion.35, f32[256,64]{1,0:T(8,128)S(1)} %copy-done.2), kind=kOutput, calls=%fused_computation.80 | convolution fusion | flops 201457664 | bytes 1769472 | tf_op jit(solution)/shard_map/dot_general | solution.py:198
  42.3 1.4 %fusion.24 = f32[1024,64]{0,1:T(8,128)S(1)} fusion(bf16[1024,64]{0,1:T(8,128)(2,1)S(1)} %get-tuple-element.12, bf16[1024,64]{0,1:T(8,128)(2,1)S(1)} %copy-done.3, f32[1024]{0:T(1024)S(1)} %multiply_reduce_fusion.6), kind=kOutput, calls=%fused_computation.31 | convolution fusion | flops 274726912 | bytes 528384 | tf_op jit(solution)/shard_map/dot_general | solution.py:206
  43.8 1.9 %collective-permute-start.8 = (bf16[1024,64]{0,1:T(8,128)(2,1)S(1)}, bf16[1024,64]{0,1:T(8,128)(2,1)S(1)}, u32[]{:S(2)}, u32[]{:S(2)}) collective-permute-start(bf16[1024,64]{0,1:T(8,128)(2,1)S(1)} %get-tuple-element.12), channel_id=1, source_target_pairs={{2,0},{3,1},{0,2},{1,3},{6,4},{7,5},{4,6},{5,7},{10,8},{11,9},{8,1... | collective-permute-start | bytes 393224 | tf_op jit(solution)/shard_map/ppermute | solution.py:25
  45.7 2.8 %fusion.60 = f32[1024,256]{1,0:T(8,128)} fusion(f32[1024,256]{0,1:T(8,128)S(1)} %fusion.35, f32[256,256]{1,0:T(8,128)S(1)} %copy-done.1), kind=kOutput, calls=%fused_computation.81 | convolution fusion | flops 805306368 | bytes 2359296 | tf_op jit(solution)/shard_map/dot_general | solution.py:201
  48.7 1.6 %collective-permute-start.9 = (bf16[1024,64]{0,1:T(8,128)(2,1)S(1)}, bf16[1024,64]{0,1:T(8,128)(2,1)S(1)}, u32[]{:S(2)}, u32[]{:S(2)}) collective-permute-start(bf16[1024,64]{0,1:T(8,128)(2,1)S(1)} %collective-permute-done.5), channel_id=1, source_target_pairs={{28,0},{5,1},{30,2},{7,3},{0,4},{9,5},{2,6},{11,7},{4,8},{13,9},{6... | collective-permute-start | bytes 393224 | tf_op jit(solution)/shard_map/ppermute | solution.py:174
  50.3 1.4 %collective-permute-done.8 = bf16[1024,64]{0,1:T(8,128)(2,1)S(1)} collective-permute-done((bf16[1024,64]{0,1:T(8,128)(2,1)S(1)}, bf16[1024,64]{0,1:T(8,128)(2,1)S(1)}, u32[]{:S(2)}, u32[]{:S(2)}) %collective-permute-start.8) | collective-permute-done | bytes 131104 | tf_op jit(solution)/shard_map/ppermute | solution.py:25
  51.6 1.6 %collective-permute-start.14 = (bf16[1024,64]{0,1:T(8,128)(2,1)S(1)}, bf16[1024,64]{0,1:T(8,128)(2,1)S(1)}, u32[]{:S(2)}, u32[]{:S(2)}) collective-permute-start(bf16[1024,64]{0,1:T(8,128)(2,1)S(1)} %collective-permute-done.8), channel_id=1, source_target_pairs={{1,0},{0,1},{3,2},{2,3},{5,4},{4,5},{7,6},{6,7},{9,8},{8,9},{11,10... | collective-permute-start | bytes 393224 | tf_op jit(solution)/shard_map/ppermute | solution.py:25
  53.2 1.7 %fusion.43 = f32[1024,64]{0,1:T(8,128)S(1)} fusion(f32[1024,64]{0,1:T(8,128)S(1)} %fusion.24, bf16[1024,64]{0,1:T(8,128)(2,1)S(1)} %collective-permute-done.6, bf16[1024,64]{0,1:T(8,128)(2,1)S(1)} %collective-permute-done.5, bf16[1024,64]{0,1:T(8,128)(2,1)S(1)} %copy-done.3, f32[1024]{0:T(1024)S(1)} %multiply_reduce_fusion.5, ...), kind=kOutput, calls=%fused_computation.52 | convolution fusion | flops 274792448 | bytes 925696 | tf_op jit(solution)/shard_map/dot_general | solution.py:206
  54.8 1.7 %fusion.42 = f32[1024,64]{0,1:T(8,128)S(1)} fusion(f32[1024,64]{0,1:T(8,128)S(1)} %fusion.43, bf16[1024,64]{0,1:T(8,128)(2,1)S(1)} %collective-permute-done.8, bf16[1024,64]{0,1:T(8,128)(2,1)S(1)} %collective-permute-done.7, bf16[1024,64]{0,1:T(8,128)(2,1)S(1)} %copy-done.3, f32[1024]{0:T(1024)S(1)} %multiply_reduce_fusion.4, ...), kind=kOutput, calls=%fused_computation.51 | convolution fusion | flops 274792448 | bytes 925696 | tf_op jit(solution)/shard_map/dot_general | solution.py:206
  56.5 0.4 collective-permute-start.10
  57.5 2.4 %collective-permute-start.16 = (bf16[1024,64]{0,1:T(8,128)(2,1)S(1)}, bf16[1024,64]{0,1:T(8,128)(2,1)S(1)}, u32[]{:S(2)}, u32[]{:S(2)}) collective-permute-start(bf16[1024,64]{0,1:T(8,128)(2,1)S(1)} %collective-permute-done.14), channel_id=1, source_target_pairs={{28,0},{29,1},{6,2},{7,3},{0,4},{1,5},{10,6},{11,7},{4,8},{5,9},{1... | collective-permute-start | bytes 393224 | tf_op jit(solution)/shard_map/ppermute | solution.py:174
  59.9 1.6 %fusion.29 = f32[1024,64]{0,1:T(8,128)S(1)} fusion(bf16[1024,64]{0,1:T(8,128)(2,1)S(1)} %collective-permute-done.14, bf16[1024,64]{0,1:T(8,128)(2,1)S(1)} %collective-permute-done.13, bf16[1024,64]{0,1:T(8,128)(2,1)S(1)} %copy-done.3, f32[1024]{0:T(1024)S(1)} %multiply_reduce_fusion.1, f32[1024]{0:T(1024)S(1)} %multiply_reduce_fusion.6), kind=kOutput, calls=%fused_computation.36 | convolution fusion | flops 274726912 | bytes 663552 | tf_op jit(solution)/shard_map/dot_general | solution.py:206
  61.5 1.6 %fusion.28 = f32[1024,64]{0,1:T(8,128)S(1)} fusion(bf16[1024,64]{0,1:T(8,128)(2,1)S(1)} %collective-permute-done.12, bf16[1024,64]{0,1:T(8,128)(2,1)S(1)} %collective-permute-done.11, bf16[1024,64]{0,1:T(8,128)(2,1)S(1)} %copy-done.3, f32[1024]{0:T(1024)S(1)} %multiply_reduce_fusion.2, f32[1024]{0:T(1024)S(1)} %multiply_reduce_fusion.6), kind=kOutput, calls=%fused_computation.35 | convolution fusion | flops 274726912 | bytes 663552 | tf_op jit(solution)/shard_map/dot_general | solution.py:206
  63.2 1.7 %fusion.41 = f32[1024,64]{0,1:T(8,128)S(1)} fusion(f32[1024,64]{0,1:T(8,128)S(1)} %fusion.29, f32[1024,64]{0,1:T(8,128)S(1)} %fusion.28, f32[1024,64]{0,1:T(8,128)S(1)} %fusion.42, bf16[1024,64]{0,1:T(8,128)(2,1)S(1)} %collective-permute-done.10, bf16[1024,64]{0,1:T(8,128)(2,1)S(1)} %collective-permute-done.9, bf16[1024,64]{0,1:T(8,128)(2,1)S(1)} %copy-done.3, ...), kind=kOutput, calls=%fused_computation.50 | convolution fusion | flops 274923520 | bytes 1449984 | tf_op jit(solution)/shard_map/dot_general | solution.py:206
  64.9 2.4 %fusion.38 = f32[1024,64]{0,1:T(8,128)} fusion(f32[1024,64]{0,1:T(8,128)S(1)} %fusion.41, bf16[1024,64]{0,1:T(8,128)(2,1)S(1)} %collective-permute-done.16, bf16[1024,64]{0,1:T(8,128)(2,1)S(1)} %collective-permute-done.15, bf16[1024,64]{0,1:T(8,128)(2,1)S(1)} %copy-done.3, f32[1024]{0:T(1024)S(1)} %multiply_reduce_fusion, ...), kind=kOutput, calls=%fused_computation.47 | convolution fusion | flops 274989056 | bytes 1187840 | tf_op jit(solution)/shard_map/dot_general | solution.py:206
  (39 shorter events, 1.1 us)
Async XLA Ops:
  0.6 21.1 %copy-start.3 = (bf16[1024,64]{0,1:T(8,128)(2,1)S(1)}, bf16[1024,64]{0,1:T(8,128)(2,1)}, u32[]{:S(2)}) copy-start(bf16[1024,64]{0,1:T(8,128)(2,1)} %param.5) | copy-start | bytes 393220
  0.6 21.1 %copy-start.4 = (f32[256,64]{0,1:T(8,128)S(1)}, f32[256,64]{0,1:T(8,128)}, u32[]{:S(2)}) copy-start(f32[256,64]{0,1:T(8,128)} %param.8) | copy-start | bytes 196612
  3.4 5.3 %collective-permute-start = (bf16[256,64]{1,0:T(8,128)(2,1)S(1)}, bf16[256,64]{1,0:T(8,128)(2,1)S(1)}, u32[]{:S(2)}, u32[]{:S(2)}) collective-permute-start(bf16[256,64]{1,0:T(8,128)(2,1)S(1)} %convolution_convert_fusion), channel_id=1, source_target_pairs={{1,0},{0,1},{3,2},{2,3},{5,4},{4,5},{7,6},{6,7},{9,8},{8,9},{11,10... | collective-permute-start | bytes 98312 | tf_op jit(solution)/shard_map/ppermute | solution.py:25
  8.7 5.3 %collective-permute-start.1 = (bf16[256,64]{1,0:T(8,128)(2,1)S(1)}, bf16[256,64]{1,0:T(8,128)(2,1)S(1)}, u32[]{:S(2)}, u32[]{:S(2)}) collective-permute-start(bf16[256,64]{1,0:T(8,128)(2,1)S(1)} %add.69), channel_id=1, source_target_pairs={{2,0},{3,1},{0,2},{1,3},{6,4},{7,5},{4,6},{5,7},{10,8},{11,9},{8,1... | collective-permute-start | bytes 98312 | tf_op jit(solution)/shard_map/ppermute | solution.py:25
  14.1 1.3 %collective-permute-start.2 = (bf16[256,64]{1,0:T(8,128)(2,1)S(1)}, bf16[256,64]{1,0:T(8,128)(2,1)S(1)}, u32[]{:S(2)}, u32[]{:S(2)}) collective-permute-start(bf16[256,64]{1,0:T(8,128)(2,1)S(1)} %add.140), channel_id=1, source_target_pairs={{4,0},{0,4},{12,8},{8,12},{20,16},{16,20},{28,24},{24,28},{5,1},{1... | collective-permute-start | bytes 98312 | tf_op jit(solution)/shard_map/ppermute | solution.py:25
  15.4 4.3 %collective-permute-start.3 = (bf16[256,64]{1,0:T(8,128)(2,1)S(1)}, bf16[256,64]{1,0:T(8,128)(2,1)S(1)}, u32[]{:S(2)}, u32[]{:S(2)}) collective-permute-start(bf16[256,64]{1,0:T(8,128)(2,1)S(1)} %add.141), channel_id=1, source_target_pairs={{8,0},{12,4},{0,8},{4,12},{24,16},{28,20},{16,24},{20,28},{9,1},{1... | collective-permute-start | bytes 98312 | tf_op jit(solution)/shard_map/ppermute | solution.py:25
  19.8 7.5 %collective-permute-start.4 = (bf16[256,64]{1,0:T(8,128)(2,1)S(1)}, bf16[256,64]{1,0:T(8,128)(2,1)S(1)}, u32[]{:S(2)}, u32[]{:S(2)}) collective-permute-start(bf16[256,64]{1,0:T(8,128)(2,1)S(1)} %add.142), channel_id=1, source_target_pairs={{16,0},{20,4},{24,8},{28,12},{0,16},{4,20},{8,24},{12,28},{17,1},{... | collective-permute-start | bytes 98312 | tf_op jit(solution)/shard_map/ppermute | solution.py:25
  22.5 18.9 %copy-start = (f32[1024,64]{0,1:T(8,128)S(1)}, f32[1024,64]{0,1:T(8,128)}, u32[]{:S(2)}) copy-start(f32[1024,64]{0,1:T(8,128)} %param.9) | copy-start | bytes 786436
  22.5 26.1 %collective-permute-start.5 = (bf16[1024,64]{0,1:T(8,128)(2,1)S(1)}, bf16[1024,64]{0,1:T(8,128)(2,1)S(1)}, u32[]{:S(2)}, u32[]{:S(2)}) collective-permute-start(bf16[1024,64]{0,1:T(8,128)(2,1)S(1)} %copy-done.3), channel_id=1, source_target_pairs={{1,0},{0,1},{3,2},{2,3},{5,4},{4,5},{7,6},{6,7},{9,8},{8,9},{11,10... | collective-permute-start | bytes 393224 | tf_op jit(solution)/shard_map/ppermute | solution.py:25
  24.1 24.4 %collective-permute-start.7 = (bf16[1024,64]{0,1:T(8,128)(2,1)S(1)}, bf16[1024,64]{0,1:T(8,128)(2,1)S(1)}, u32[]{:S(2)}, u32[]{:S(2)}) collective-permute-start(bf16[1024,64]{0,1:T(8,128)(2,1)S(1)} %copy-done.3), channel_id=1, source_target_pairs={{2,0},{3,1},{0,2},{1,3},{6,4},{7,5},{4,6},{5,7},{10,8},{11,9},{8,1... | collective-permute-start | bytes 393224 | tf_op jit(solution)/shard_map/ppermute | solution.py:25
  40.2 1.2 %copy-start.2 = (f32[256,64]{1,0:T(8,128)S(1)}, f32[256,64]{1,0:T(8,128)}, u32[]{:S(2)}) copy-start(f32[256,64]{1,0:T(8,128)} %get-tuple-element.7) | copy-start | bytes 196612
  42.3 3.4 %copy-start.1 = (f32[256,256]{1,0:T(8,128)S(1)}, f32[256,256]{1,0:T(8,128)}, u32[]{:S(2)}) copy-start(f32[256,256]{1,0:T(8,128)} %get-tuple-element.9) | copy-start | bytes 786436
  43.7 7.9 %collective-permute-start.6 = (bf16[1024,64]{0,1:T(8,128)(2,1)S(1)}, bf16[1024,64]{0,1:T(8,128)(2,1)S(1)}, u32[]{:S(2)}, u32[]{:S(2)}) collective-permute-start(bf16[1024,64]{0,1:T(8,128)(2,1)S(1)} %get-tuple-element.12), channel_id=1, source_target_pairs={{1,0},{0,1},{3,2},{2,3},{5,4},{4,5},{7,6},{6,7},{9,8},{8,9},{11,10... | collective-permute-start | bytes 393224 | tf_op jit(solution)/shard_map/ppermute | solution.py:25
  43.8 7.8 %collective-permute-start.8 = (bf16[1024,64]{0,1:T(8,128)(2,1)S(1)}, bf16[1024,64]{0,1:T(8,128)(2,1)S(1)}, u32[]{:S(2)}, u32[]{:S(2)}) collective-permute-start(bf16[1024,64]{0,1:T(8,128)(2,1)S(1)} %get-tuple-element.12), channel_id=1, source_target_pairs={{2,0},{3,1},{0,2},{1,3},{6,4},{7,5},{4,6},{5,7},{10,8},{11,9},{8,1... | collective-permute-start | bytes 393224 | tf_op jit(solution)/shard_map/ppermute | solution.py:25
  48.5 8.5 %collective-permute-start.11 = (bf16[1024,64]{0,1:T(8,128)(2,1)S(1)}, bf16[1024,64]{0,1:T(8,128)(2,1)S(1)}, u32[]{:S(2)}, u32[]{:S(2)}) collective-permute-start(bf16[1024,64]{0,1:T(8,128)(2,1)S(1)} %collective-permute-done.7), channel_id=1, source_target_pairs={{28,0},{29,1},{6,2},{7,3},{0,4},{1,5},{10,6},{11,7},{4,8},{5,9},{1... | collective-permute-start | bytes 393224 | tf_op jit(solution)/shard_map/ppermute | solution.py:174
  48.5 8.0 %collective-permute-start.13 = (bf16[1024,64]{0,1:T(8,128)(2,1)S(1)}, bf16[1024,64]{0,1:T(8,128)(2,1)S(1)}, u32[]{:S(2)}, u32[]{:S(2)}) collective-permute-start(bf16[1024,64]{0,1:T(8,128)(2,1)S(1)} %collective-permute-done.7), channel_id=1, source_target_pairs={{1,0},{0,1},{3,2},{2,3},{5,4},{4,5},{7,6},{6,7},{9,8},{8,9},{11,10... | collective-permute-start | bytes 393224 | tf_op jit(solution)/shard_map/ppermute | solution.py:25
  48.7 8.7 %collective-permute-start.9 = (bf16[1024,64]{0,1:T(8,128)(2,1)S(1)}, bf16[1024,64]{0,1:T(8,128)(2,1)S(1)}, u32[]{:S(2)}, u32[]{:S(2)}) collective-permute-start(bf16[1024,64]{0,1:T(8,128)(2,1)S(1)} %collective-permute-done.5), channel_id=1, source_target_pairs={{28,0},{5,1},{30,2},{7,3},{0,4},{9,5},{2,6},{11,7},{4,8},{13,9},{6... | collective-permute-start | bytes 393224 | tf_op jit(solution)/shard_map/ppermute | solution.py:174
  51.6 9.9 %collective-permute-start.12 = (bf16[1024,64]{0,1:T(8,128)(2,1)S(1)}, bf16[1024,64]{0,1:T(8,128)(2,1)S(1)}, u32[]{:S(2)}, u32[]{:S(2)}) collective-permute-start(bf16[1024,64]{0,1:T(8,128)(2,1)S(1)} %collective-permute-done.8), channel_id=1, source_target_pairs={{28,0},{29,1},{6,2},{7,3},{0,4},{1,5},{10,6},{11,7},{4,8},{5,9},{1... | collective-permute-start | bytes 393224 | tf_op jit(solution)/shard_map/ppermute | solution.py:174
  51.6 5.8 %collective-permute-start.14 = (bf16[1024,64]{0,1:T(8,128)(2,1)S(1)}, bf16[1024,64]{0,1:T(8,128)(2,1)S(1)}, u32[]{:S(2)}, u32[]{:S(2)}) collective-permute-start(bf16[1024,64]{0,1:T(8,128)(2,1)S(1)} %collective-permute-done.8), channel_id=1, source_target_pairs={{1,0},{0,1},{3,2},{2,3},{5,4},{4,5},{7,6},{6,7},{9,8},{8,9},{11,10... | collective-permute-start | bytes 393224 | tf_op jit(solution)/shard_map/ppermute | solution.py:25
  56.5 6.7 %collective-permute-start.10 = (bf16[1024,64]{0,1:T(8,128)(2,1)S(1)}, bf16[1024,64]{0,1:T(8,128)(2,1)S(1)}, u32[]{:S(2)}, u32[]{:S(2)}) collective-permute-start(bf16[1024,64]{0,1:T(8,128)(2,1)S(1)} %collective-permute-done.6), channel_id=1, source_target_pairs={{28,0},{5,1},{30,2},{7,3},{0,4},{9,5},{2,6},{11,7},{4,8},{13,9},{6... | collective-permute-start | bytes 393224 | tf_op jit(solution)/shard_map/ppermute | solution.py:174
  57.0 7.9 %collective-permute-start.15 = (bf16[1024,64]{0,1:T(8,128)(2,1)S(1)}, bf16[1024,64]{0,1:T(8,128)(2,1)S(1)}, u32[]{:S(2)}, u32[]{:S(2)}) collective-permute-start(bf16[1024,64]{0,1:T(8,128)(2,1)S(1)} %collective-permute-done.13), channel_id=1, source_target_pairs={{28,0},{29,1},{6,2},{7,3},{0,4},{1,5},{10,6},{11,7},{4,8},{5,9},{1... | collective-permute-start | bytes 393224 | tf_op jit(solution)/shard_map/ppermute | solution.py:174
  57.5 7.4 %collective-permute-start.16 = (bf16[1024,64]{0,1:T(8,128)(2,1)S(1)}, bf16[1024,64]{0,1:T(8,128)(2,1)S(1)}, u32[]{:S(2)}, u32[]{:S(2)}) collective-permute-start(bf16[1024,64]{0,1:T(8,128)(2,1)S(1)} %collective-permute-done.14), channel_id=1, source_target_pairs={{28,0},{29,1},{6,2},{7,3},{0,4},{1,5},{10,6},{11,7},{4,8},{5,9},{1... | collective-permute-start | bytes 393224 | tf_op jit(solution)/shard_map/ppermute | solution.py:174

commit v5 on v4

--- a/solution.py
+++ b/solution.py
@@ -26,11 +26,8 @@
 
 
 def summed(value, axis):
-    bit = 1
-    while bit < lax.axis_size(axis):
-        value = value + swapped(value, axis, bit)
-        bit *= 2
-    return value
+    copies = jnp.broadcast_to(value, (lax.axis_size(axis),) + value.shape)
+    return jnp.sum(lax.all_to_all(copies, axis, 0, 0), axis=0, dtype=value.dtype)
 
 
 def kern(left, right):

time: 67.5 us -> 69.6 us (1.031)
  blocking collectives: 0 us -> 12.2 us
  starting transfers between devices: 23.2 us -> 13.1 us
  waiting for transfers between devices: 9.57 us -> 8.05 us
  local copies, waits for them, and re-layouts: 0.78 us -> 2.23 us
    ppermute x11 -> x6, starting transfers between devices: 18.5 us -> 5.67 us  [swapped(): lax.ppermute(value, axis, [(i ^ bit, i) for i in range(lax.axis_size(axis...]
    all_to_all x0 -> x1, blocking collectives: none -> 12.2 us  [summed(): lax.all_to_all(copies, axis, 0, 0)]
    ppermute x11 -> x6, waiting for transfers between devices: 9.55 us -> 3.37 us  [swapped(): lax.ppermute(value, axis, [(i ^ bit, i) for i in range(lax.axis_size(axis...]
    all_to_all x0 -> x1, waiting for transfers between devices: none -> 4.4 us  [summed(): lax.all_to_all(copies, axis, 0, 0)]
    all_to_all x0 -> x1, starting transfers between devices: none -> 3.72 us  [summed(): lax.all_to_all(copies, axis, 0, 0)]
    ppermute x6, starting transfers between devices: 4.76 us -> 3.71 us  [cross(): return lax.ppermute(piece, ('gx', 'gy'), pairs)]
    dot_general x1, matrix products: 0.81 us -> 1.71 us  [shards(): jnp.dot(cols, weights, precision=hp, preferred_element_type=jnp.float32)]
    dot_general x1, matrix products: 1.21 us -> 0.38 us  [kern(): cross_term = jnp.dot(left, right.T, preferred_element_type=jnp.float32)]
  transfers between devices with their start and end apart: 17 -> 13, of which waited for: 5 -> 4; matrix products, arithmetic and copies ran while one was open for 24% -> 25% of each run, Pallas kernels for 18% -> 18%
where the time goes in v5:
time: 69.6 us; the launch traced here: 68.8 us
  matrix products  18.4 us (26%)
  starting transfers between devices  13.1 us (19%)
  Pallas kernels  12.3 us (18%)
  blocking collectives  12.2 us (18%)
  waiting for transfers between devices  8.05 us (12%)
  local copies, waits for them, and re-layouts  2.23 us (3%)
  other arithmetic  1.81 us (3%)
  between operations  0.81 us (1%)
    pallas_call x1, Pallas kernels, invert_factor(): pl.pallas_call(invert_factor_kernel, out_shape=(jax.ShapeDtypeStruct((siz...  12.3 us
    dot_general x7, matrix products, shards(): total = total + jnp.dot(tile, probe, preferred_element_type=jnp.float32)  12.2 us
    all_to_all x1, blocking collectives, summed(): lax.all_to_all(copies, axis, 0, 0)  12.2 us
    ppermute x6, starting transfers between devices, swapped(): lax.ppermute(value, axis, [(i ^ bit, i) for i in range(lax.axis_size(axis...  5.67 us
    all_to_all x1, waiting for transfers between devices, summed(): lax.all_to_all(copies, axis, 0, 0)  4.4 us
    all_to_all x1, starting transfers between devices, summed(): lax.all_to_all(copies, axis, 0, 0)  3.72 us
    ppermute x6, starting transfers between devices, cross(): return lax.ppermute(piece, ('gx', 'gy'), pairs)  3.71 us
    ppermute x6, waiting for transfers between devices, swapped(): lax.ppermute(value, axis, [(i ^ bit, i) for i in range(lax.axis_size(axis...  3.37 us
  transfers between devices with their start and end apart: 13, of which 4 were waited for; matrix products, arithmetic and copies ran while one was open for 25% of the time, Pallas kernels for 18%

profile of v5, /device:TPU:0, one launch (start us, length us, event | category | flops | bytes accessed | tf_op | source)
XLA Modules:
  0.0 68.8 jit_solution(17625489885704270261)
XLA Ops:
  0.7 0.7 %broadcast_compare_fusion = pred[2]{0:T(512)(128)(4,1)S(1)} fusion(s32[2]{0:T(128)} %param.7, s32[]{:T(128)S(6)} %add.58), kind=kLoop, calls=%fused_computation.65 | loop fusion | flops 2 | bytes 14 | tf_op jit(solution)/shard_map/eq | solution.py:186
  1.4 0.7 %select_bitcast_fusion = s32[256]{0:T(256)S(1)} fusion(s32[2,128]{1,0:T(2,128)} %param.6, pred[2]{0:T(512)(128)(4,1)S(1)} %broadcast_compare_fusion), kind=kLoop, calls=%fused_computation.64 | loop fusion | flops 256 | bytes 2050 | tf_op jit(solution)/shard_map/eq | solution.py:187
  2.1 1.3 %convolution_convert_fusion = bf16[256,64]{0,1:T(8,128)(2,1)S(1)} fusion(bf16[1024,64]{0,1:T(8,128)(2,1)} %param.5, s32[256]{0:T(256)S(1)} %select_bitcast_fusion), kind=kOutput, calls=%fused_computation.53 | convolution fusion | flops 33832960 | bytes 164864 | tf_op jit(solution)/shard_map/dot_general | solution.py:188
  3.4 12.2 %all_to_all.10 = bf16[4,256,64]{1,2,0:T(8,128)(2,1)S(1)} all-to-all(bf16[4,256,64]{1,2,0:T(8,128)(2,1)S(1)} %broadcast_in_dim.18), channel_id=1, replica_groups=mesh['gx'=8,'gy'=4] {'gy'}, dimensions={0} | all-to-all | bytes 262144 | tf_op jit(solution)/shard_map/all_to_all | solution.py:30
  15.6 0.8 %collective-permute-start.2 = (bf16[1024,64]{0,1:T(8,128)(2,1)S(1)}, bf16[1024,64]{0,1:T(8,128)(2,1)S(1)}, u32[]{:S(2)}, u32[]{:S(2)}) collective-permute-start(bf16[1024,64]{0,1:T(8,128)(2,1)S(1)} %copy-done.2), channel_id=1, source_target_pairs={{2,0},{3,1},{0,2},{1,3},{6,4},{7,5},{4,6},{5,7},{10,8},{11,9},{8,1... | collective-permute-start | bytes 393224 | tf_op jit(solution)/shard_map/ppermute | solution.py:25
  16.5 1.3 %collective-permute-start = (bf16[1024,64]{0,1:T(8,128)(2,1)S(1)}, bf16[1024,64]{0,1:T(8,128)(2,1)S(1)}, u32[]{:S(2)}, u32[]{:S(2)}) collective-permute-start(bf16[1024,64]{0,1:T(8,128)(2,1)S(1)} %copy-done.2), channel_id=1, source_target_pairs={{1,0},{0,1},{3,2},{2,3},{5,4},{4,5},{7,6},{6,7},{9,8},{8,9},{11,10... | collective-permute-start | bytes 393224 | tf_op jit(solution)/shard_map/ppermute | solution.py:25
  17.7 0.8 %copy.16.coeff_ref = f32[256,64]{1,0:T(8,128)} copy(f32[256,64]{0,1:T(8,128)S(1)} %copy-done.3) | data formatting | bytes 131072 | tf_op args[3]
  18.5 0.7 %broadcast_in_dim.19 = bf16[8,256,64]{1,2,0:T(8,128)(2,1)} broadcast(bf16[256,64]{0,1:T(8,128)(2,1)S(1)} %reduce_sum.90), dimensions={1,2} | broadcast | bytes 294912 | tf_op jit(solution)/shard_map/broadcast_in_dim | solution.py:29
  19.2 3.7 %all-to-all-start.1 = ((bf16[8,256,64]{1,2,0:T(8,128)(2,1)}), bf16[8,256,64]{1,2,0:T(8,128)(2,1)S(1)}, u32[]{:S(2)}, u32[]{:S(2)}) async-start(bf16[8,256,64]{1,2,0:T(8,128)(2,1)} %broadcast_in_dim.19), calls=%async_computation.1 | async-start | bytes 524288 | tf_op jit(solution)/shard_map/all_to_all | solution.py:30
  23.1 0.7 %collective-permute-start.8 = (bf16[1024,64]{0,1:T(8,128)(2,1)S(1)}, bf16[1024,64]{0,1:T(8,128)(2,1)S(1)}, u32[]{:S(2)}, u32[]{:S(2)}) collective-permute-start(bf16[1024,64]{0,1:T(8,128)(2,1)S(1)} %collective-permute-done.2), channel_id=1, source_target_pairs={{1,0},{0,1},{3,2},{2,3},{5,4},{4,5},{7,6},{6,7},{9,8},{8,9},{11,10... | collective-permute-start | bytes 393224 | tf_op jit(solution)/shard_map/ppermute | solution.py:25
  23.8 0.2 collective-permute-start.6
  24.0 1.9 %collective-permute-start.4 = (bf16[1024,64]{0,1:T(8,128)(2,1)S(1)}, bf16[1024,64]{0,1:T(8,128)(2,1)S(1)}, u32[]{:S(2)}, u32[]{:S(2)}) collective-permute-start(bf16[1024,64]{0,1:T(8,128)(2,1)S(1)} %collective-permute-done), channel_id=1, source_target_pairs={{28,0},{5,1},{30,2},{7,3},{0,4},{9,5},{2,6},{11,7},{4,8},{13,9},{6... | collective-permute-start | bytes 393224 | tf_op jit(solution)/shard_map/ppermute | solution.py:171
  26.0 4.4 %all-to-all-done.1 = bf16[8,256,64]{1,2,0:T(8,128)(2,1)S(1)} async-done(((bf16[8,256,64]{1,2,0:T(8,128)(2,1)}), bf16[8,256,64]{1,2,0:T(8,128)(2,1)S(1)}, u32[]{:S(2)}, u32[]{:S(2)}) %all-to-all-start.1) | async-done | bytes 262176 | tf_op jit(solution)/shard_map/all_to_all | solution.py:30
  30.4 0.7 %copy.15.pivot_ref = bf16[256,64]{1,0:T(8,128)(2,1)} copy(bf16[256,64]{0,1:T(8,128)(2,1)S(1)} %reduce_sum.91) | data formatting | bytes 65536 | tf_op jit(solution)/shard_map/reduce_sum | solution.py:30
  31.2 0.4 fusion.35
  31.6 12.3 %invert_factor.1 = (f32[256,256]{1,0:T(8,128)}, f32[256,64]{1,0:T(8,128)}) custom-call(bf16[256,64]{1,0:T(8,128)(2,1)} %copy.15.pivot_ref, f32[256,64]{1,0:T(8,128)} %copy.16.coeff_ref), custom_call_target="tpu_custom_call" | custom-call | flops 100663296 | bytes 262144 | tf_op jit(solution)/shard_map/invert_factor/pallas_call | solution.py:146
  43.9 1.7 %fusion.59 = (bf16[1024,64]{0,1:T(8,128)(2,1)S(1)}, f32[1024,64]{0,1:T(8,128)S(1)}) fusion(f32[1024,64]{0,1:T(8,128)S(1)} %copy-done, f32[1024,256]{0,1:T(8,128)S(1)} %fusion.35, f32[256,64]{1,0:T(8,128)} %get-tuple-element.7), kind=kOutput, calls=%fused_computation.80 | convolution fusion | flops 201457664 | bytes 1769472 | tf_op jit(solution)/shard_map/dot_general | solution.py:195
  45.6 1.6 %fusion.24 = f32[1024,64]{0,1:T(8,128)S(1)} fusion(bf16[1024,64]{0,1:T(8,128)(2,1)S(1)} %get-tuple-element.10, bf16[1024,64]{0,1:T(8,128)(2,1)S(1)} %copy-done.2, f32[1024]{0:T(1024)S(1)} %multiply_reduce_fusion.6), kind=kOutput, calls=%fused_computation.31 | convolution fusion | flops 274726912 | bytes 528384 | tf_op jit(solution)/shard_map/dot_general | solution.py:203
  47.1 0.8 %collective-permute-start.1 = (bf16[1024,64]{0,1:T(8,128)(2,1)S(1)}, bf16[1024,64]{0,1:T(8,128)(2,1)S(1)}, u32[]{:S(2)}, u32[]{:S(2)}) collective-permute-start(bf16[1024,64]{0,1:T(8,128)(2,1)S(1)} %get-tuple-element.10), channel_id=1, source_target_pairs={{1,0},{0,1},{3,2},{2,3},{5,4},{4,5},{7,6},{6,7},{9,8},{8,9},{11,10... | collective-permute-start | bytes 393224 | tf_op jit(solution)/shard_map/ppermute | solution.py:25
  48.0 1.7 %collective-permute-start.3 = (bf16[1024,64]{0,1:T(8,128)(2,1)S(1)}, bf16[1024,64]{0,1:T(8,128)(2,1)S(1)}, u32[]{:S(2)}, u32[]{:S(2)}) collective-permute-start(bf16[1024,64]{0,1:T(8,128)(2,1)S(1)} %get-tuple-element.10), channel_id=1, source_target_pairs={{2,0},{3,1},{0,2},{1,3},{6,4},{7,5},{4,6},{5,7},{10,8},{11,9},{8,1... | collective-permute-start | bytes 393224 | tf_op jit(solution)/shard_map/ppermute | solution.py:25
  49.7 2.8 %fusion.60 = f32[1024,256]{1,0:T(8,128)} fusion(f32[1024,256]{0,1:T(8,128)S(1)} %fusion.35, f32[256,256]{1,0:T(8,128)S(1)} %copy-done.1), kind=kOutput, calls=%fused_computation.81 | convolution fusion | flops 805306368 | bytes 2359296 | tf_op jit(solution)/shard_map/dot_general | solution.py:198
  52.7 3.2 %collective-permute-done.3 = bf16[1024,64]{0,1:T(8,128)(2,1)S(1)} collective-permute-done((bf16[1024,64]{0,1:T(8,128)(2,1)S(1)}, bf16[1024,64]{0,1:T(8,128)(2,1)S(1)}, u32[]{:S(2)}, u32[]{:S(2)}) %collective-permute-start.3) | collective-permute-done | bytes 131104 | tf_op jit(solution)/shard_map/ppermute | solution.py:25
  55.9 0.4 collective-permute-start.9
  56.3 1.3 %collective-permute-start.5 = (bf16[1024,64]{0,1:T(8,128)(2,1)S(1)}, bf16[1024,64]{0,1:T(8,128)(2,1)S(1)}, u32[]{:S(2)}, u32[]{:S(2)}) collective-permute-start(bf16[1024,64]{0,1:T(8,128)(2,1)S(1)} %collective-permute-done.1), channel_id=1, source_target_pairs={{28,0},{5,1},{30,2},{7,3},{0,4},{9,5},{2,6},{11,7},{4,8},{13,9},{6... | collective-permute-start | bytes 393224 | tf_op jit(solution)/shard_map/ppermute | solution.py:171
  57.6 1.7 %fusion.43 = f32[1024,64]{0,1:T(8,128)S(1)} fusion(f32[1024,64]{0,1:T(8,128)S(1)} %fusion.24, bf16[1024,64]{0,1:T(8,128)(2,1)S(1)} %collective-permute-done.1, bf16[1024,64]{0,1:T(8,128)(2,1)S(1)} %collective-permute-done, bf16[1024,64]{0,1:T(8,128)(2,1)S(1)} %copy-done.2, f32[1024]{0:T(1024)S(1)} %multiply_reduce_fusion.5, f32[1024]{0:T(1024)S(1)} %multiply_reduce_fusion.6), kind=kOutput, calls=%fused_computation.52 | convolution fusion | flops 274792448 | bytes 925696 | tf_op jit(solution)/shard_map/dot_general | solution.py:203
  59.2 1.7 %fusion.42 = f32[1024,64]{0,1:T(8,128)S(1)} fusion(f32[1024,64]{0,1:T(8,128)S(1)} %fusion.43, bf16[1024,64]{0,1:T(8,128)(2,1)S(1)} %collective-permute-done.3, bf16[1024,64]{0,1:T(8,128)(2,1)S(1)} %collective-permute-done.2, bf16[1024,64]{0,1:T(8,128)(2,1)S(1)} %copy-done.2, f32[1024]{0:T(1024)S(1)} %multiply_reduce_fusion.4, ...), kind=kOutput, calls=%fused_computation.51 | convolution fusion | flops 274792448 | bytes 925696 | tf_op jit(solution)/shard_map/dot_general | solution.py:203
  61.0 0.3 collective-permute-start.11
  61.2 1.6 %fusion.29 = f32[1024,64]{0,1:T(8,128)S(1)} fusion(bf16[1024,64]{0,1:T(8,128)(2,1)S(1)} %collective-permute-done.9, bf16[1024,64]{0,1:T(8,128)(2,1)S(1)} %collective-permute-done.8, bf16[1024,64]{0,1:T(8,128)(2,1)S(1)} %copy-done.2, f32[1024]{0:T(1024)S(1)} %multiply_reduce_fusion.1, f32[1024]{0:T(1024)S(1)} %multiply_reduce_fusion.6), kind=kOutput, calls=%fused_computation.36 | convolution fusion | flops 274726912 | bytes 663552 | tf_op jit(solution)/shard_map/dot_general | solution.py:203
  62.9 1.7 %fusion.28 = f32[1024,64]{0,1:T(8,128)S(1)} fusion(bf16[1024,64]{0,1:T(8,128)(2,1)S(1)} %collective-permute-done.7, bf16[1024,64]{0,1:T(8,128)(2,1)S(1)} %collective-permute-done.6, bf16[1024,64]{0,1:T(8,128)(2,1)S(1)} %copy-done.2, f32[1024]{0:T(1024)S(1)} %multiply_reduce_fusion.2, f32[1024]{0:T(1024)S(1)} %multiply_reduce_fusion.6), kind=kOutput, calls=%fused_computation.35 | convolution fusion | flops 274726912 | bytes 663552 | tf_op jit(solution)/shard_map/dot_general | solution.py:203
  64.6 1.7 %fusion.41 = f32[1024,64]{0,1:T(8,128)S(1)} fusion(f32[1024,64]{0,1:T(8,128)S(1)} %fusion.29, f32[1024,64]{0,1:T(8,128)S(1)} %fusion.28, f32[1024,64]{0,1:T(8,128)S(1)} %fusion.42, bf16[1024,64]{0,1:T(8,128)(2,1)S(1)} %collective-permute-done.5, bf16[1024,64]{0,1:T(8,128)(2,1)S(1)} %collective-permute-done.4, bf16[1024,64]{0,1:T(8,128)(2,1)S(1)} %copy-done.2, ...), kind=kOutput, calls=%fused_computation.50 | convolution fusion | flops 274923520 | bytes 1449984 | tf_op jit(solution)/shard_map/dot_general | solution.py:203
  66.2 0.3 collective-permute-done.11
  66.5 2.4 %fusion.38 = f32[1024,64]{0,1:T(8,128)} fusion(f32[1024,64]{0,1:T(8,128)S(1)} %fusion.41, bf16[1024,64]{0,1:T(8,128)(2,1)S(1)} %collective-permute-done.11, bf16[1024,64]{0,1:T(8,128)(2,1)S(1)} %collective-permute-done.10, bf16[1024,64]{0,1:T(8,128)(2,1)S(1)} %copy-done.2, f32[1024]{0:T(1024)S(1)} %multiply_reduce_fusion, ...), kind=kOutput, calls=%fused_computation.47 | convolution fusion | flops 274989056 | bytes 1187840 | tf_op jit(solution)/shard_map/dot_general | solution.py:203
  (31 shorter events, 0.6 us)
Async XLA Ops:
  0.6 15.0 %copy-start.2 = (bf16[1024,64]{0,1:T(8,128)(2,1)S(1)}, bf16[1024,64]{0,1:T(8,128)(2,1)}, u32[]{:S(2)}) copy-start(bf16[1024,64]{0,1:T(8,128)(2,1)} %param.5) | copy-start | bytes 393220
  0.6 17.1 %copy-start.3 = (f32[256,64]{0,1:T(8,128)S(1)}, f32[256,64]{0,1:T(8,128)}, u32[]{:S(2)}) copy-start(f32[256,64]{0,1:T(8,128)} %param.8) | copy-start | bytes 196612
  15.6 7.5 %collective-permute-start.2 = (bf16[1024,64]{0,1:T(8,128)(2,1)S(1)}, bf16[1024,64]{0,1:T(8,128)(2,1)S(1)}, u32[]{:S(2)}, u32[]{:S(2)}) collective-permute-start(bf16[1024,64]{0,1:T(8,128)(2,1)S(1)} %copy-done.2), channel_id=1, source_target_pairs={{2,0},{3,1},{0,2},{1,3},{6,4},{7,5},{4,6},{5,7},{10,8},{11,9},{8,1... | collective-permute-start | bytes 393224 | tf_op jit(solution)/shard_map/ppermute | solution.py:25
  16.5 7.5 %collective-permute-start = (bf16[1024,64]{0,1:T(8,128)(2,1)S(1)}, bf16[1024,64]{0,1:T(8,128)(2,1)S(1)}, u32[]{:S(2)}, u32[]{:S(2)}) collective-permute-start(bf16[1024,64]{0,1:T(8,128)(2,1)S(1)} %copy-done.2), channel_id=1, source_target_pairs={{1,0},{0,1},{3,2},{2,3},{5,4},{4,5},{7,6},{6,7},{9,8},{8,9},{11,10... | collective-permute-start | bytes 393224 | tf_op jit(solution)/shard_map/ppermute | solution.py:25
  19.2 11.1 %all-to-all-start.1 = ((bf16[8,256,64]{1,2,0:T(8,128)(2,1)}), bf16[8,256,64]{1,2,0:T(8,128)(2,1)S(1)}, u32[]{:S(2)}, u32[]{:S(2)}) async-start(bf16[8,256,64]{1,2,0:T(8,128)(2,1)} %broadcast_in_dim.19), calls=%async_computation.1 | async-start | bytes 524288 | tf_op jit(solution)/shard_map/all_to_all | solution.py:30
  23.1 29.4 %collective-permute-start.8 = (bf16[1024,64]{0,1:T(8,128)(2,1)S(1)}, bf16[1024,64]{0,1:T(8,128)(2,1)S(1)}, u32[]{:S(2)}, u32[]{:S(2)}) collective-permute-start(bf16[1024,64]{0,1:T(8,128)(2,1)S(1)} %collective-permute-done.2), channel_id=1, source_target_pairs={{1,0},{0,1},{3,2},{2,3},{5,4},{4,5},{7,6},{6,7},{9,8},{8,9},{11,10... | collective-permute-start | bytes 393224 | tf_op jit(solution)/shard_map/ppermute | solution.py:25
  23.8 28.8 %collective-permute-start.6 = (bf16[1024,64]{0,1:T(8,128)(2,1)S(1)}, bf16[1024,64]{0,1:T(8,128)(2,1)S(1)}, u32[]{:S(2)}, u32[]{:S(2)}) collective-permute-start(bf16[1024,64]{0,1:T(8,128)(2,1)S(1)} %collective-permute-done.2), channel_id=1, source_target_pairs={{28,0},{29,1},{6,2},{7,3},{0,4},{1,5},{10,6},{11,7},{4,8},{5,9},{1... | collective-permute-start | bytes 393224 | tf_op jit(solution)/shard_map/ppermute | solution.py:171
  24.0 28.7 %collective-permute-start.4 = (bf16[1024,64]{0,1:T(8,128)(2,1)S(1)}, bf16[1024,64]{0,1:T(8,128)(2,1)S(1)}, u32[]{:S(2)}, u32[]{:S(2)}) collective-permute-start(bf16[1024,64]{0,1:T(8,128)(2,1)S(1)} %collective-permute-done), channel_id=1, source_target_pairs={{28,0},{5,1},{30,2},{7,3},{0,4},{9,5},{2,6},{11,7},{4,8},{13,9},{6... | collective-permute-start | bytes 393224 | tf_op jit(solution)/shard_map/ppermute | solution.py:171
  30.4 13.4 %copy-start = (f32[1024,64]{0,1:T(8,128)S(1)}, f32[1024,64]{0,1:T(8,128)}, u32[]{:S(2)}) copy-start(f32[1024,64]{0,1:T(8,128)} %param.9) | copy-start | bytes 786436
  45.6 4.1 %copy-start.1 = (f32[256,256]{1,0:T(8,128)S(1)}, f32[256,256]{1,0:T(8,128)}, u32[]{:S(2)}) copy-start(f32[256,256]{1,0:T(8,128)} %get-tuple-element.9) | copy-start | bytes 786436
  47.1 9.1 %collective-permute-start.1 = (bf16[1024,64]{0,1:T(8,128)(2,1)S(1)}, bf16[1024,64]{0,1:T(8,128)(2,1)S(1)}, u32[]{:S(2)}, u32[]{:S(2)}) collective-permute-start(bf16[1024,64]{0,1:T(8,128)(2,1)S(1)} %get-tuple-element.10), channel_id=1, source_target_pairs={{1,0},{0,1},{3,2},{2,3},{5,4},{4,5},{7,6},{6,7},{9,8},{8,9},{11,10... | collective-permute-start | bytes 393224 | tf_op jit(solution)/shard_map/ppermute | solution.py:25
  48.0 7.9 %collective-permute-start.3 = (bf16[1024,64]{0,1:T(8,128)(2,1)S(1)}, bf16[1024,64]{0,1:T(8,128)(2,1)S(1)}, u32[]{:S(2)}, u32[]{:S(2)}) collective-permute-start(bf16[1024,64]{0,1:T(8,128)(2,1)S(1)} %get-tuple-element.10), channel_id=1, source_target_pairs={{2,0},{3,1},{0,2},{1,3},{6,4},{7,5},{4,6},{5,7},{10,8},{11,9},{8,1... | collective-permute-start | bytes 393224 | tf_op jit(solution)/shard_map/ppermute | solution.py:25
  52.5 8.4 %collective-permute-start.10 = (bf16[1024,64]{0,1:T(8,128)(2,1)S(1)}, bf16[1024,64]{0,1:T(8,128)(2,1)S(1)}, u32[]{:S(2)}, u32[]{:S(2)}) collective-permute-start(bf16[1024,64]{0,1:T(8,128)(2,1)S(1)} %collective-permute-done.8), channel_id=1, source_target_pairs={{28,0},{29,1},{6,2},{7,3},{0,4},{1,5},{10,6},{11,7},{4,8},{5,9},{1... | collective-permute-start | bytes 393224 | tf_op jit(solution)/shard_map/ppermute | solution.py:171
  55.9 5.1 %collective-permute-start.9 = (bf16[1024,64]{0,1:T(8,128)(2,1)S(1)}, bf16[1024,64]{0,1:T(8,128)(2,1)S(1)}, u32[]{:S(2)}, u32[]{:S(2)}) collective-permute-start(bf16[1024,64]{0,1:T(8,128)(2,1)S(1)} %collective-permute-done.3), channel_id=1, source_target_pairs={{1,0},{0,1},{3,2},{2,3},{5,4},{4,5},{7,6},{6,7},{9,8},{8,9},{11,10... | collective-permute-start | bytes 393224 | tf_op jit(solution)/shard_map/ppermute | solution.py:25
  56.3 6.6 %collective-permute-start.7 = (bf16[1024,64]{0,1:T(8,128)(2,1)S(1)}, bf16[1024,64]{0,1:T(8,128)(2,1)S(1)}, u32[]{:S(2)}, u32[]{:S(2)}) collective-permute-start(bf16[1024,64]{0,1:T(8,128)(2,1)S(1)} %collective-permute-done.3), channel_id=1, source_target_pairs={{28,0},{29,1},{6,2},{7,3},{0,4},{1,5},{10,6},{11,7},{4,8},{5,9},{1... | collective-permute-start | bytes 393224 | tf_op jit(solution)/shard_map/ppermute | solution.py:171
  56.3 8.3 %collective-permute-start.5 = (bf16[1024,64]{0,1:T(8,128)(2,1)S(1)}, bf16[1024,64]{0,1:T(8,128)(2,1)S(1)}, u32[]{:S(2)}, u32[]{:S(2)}) collective-permute-start(bf16[1024,64]{0,1:T(8,128)(2,1)S(1)} %collective-permute-done.1), channel_id=1, source_target_pairs={{28,0},{5,1},{30,2},{7,3},{0,4},{9,5},{2,6},{11,7},{4,8},{13,9},{6... | collective-permute-start | bytes 393224 | tf_op jit(solution)/shard_map/ppermute | solution.py:171
  61.0 5.5 %collective-permute-start.11 = (bf16[1024,64]{0,1:T(8,128)(2,1)S(1)}, bf16[1024,64]{0,1:T(8,128)(2,1)S(1)}, u32[]{:S(2)}, u32[]{:S(2)}) collective-permute-start(bf16[1024,64]{0,1:T(8,128)(2,1)S(1)} %collective-permute-done.9), channel_id=1, source_target_pairs={{28,0},{29,1},{6,2},{7,3},{0,4},{1,5},{10,6},{11,7},{4,8},{5,9},{1... | collective-permute-start | bytes 393224 | tf_op jit(solution)/shard_map/ppermute | solution.py:171

commit v6 on v1

v6 whole, which is shorter than its diff:
```python
import functools

import jax
import jax.numpy as jnp
from jax import lax
from jax.experimental import pallas as pl
from jax.experimental.pallas import tpu as pltpu
from jax.sharding import PartitionSpec as P

PIVOTS = 128
KERNEL_SCALE = 32
BAND = 3
STRIP = 8
LANES = 128
EXTRA = 16
CHUNK = 256


jitter = 0.1
noise_weight = 0.5


def shifted(value, axis, steps):
    count = lax.axis_size(axis)
    return lax.ppermute(value, axis, [((i + steps) % count, i) for i in range(count)])


def swapped(value, axis, bit):
    return lax.ppermute(value, axis, [(i ^ bit, i) for i in range(lax.axis_size(axis))])


def summed(value, axis):
    bit = 1
    while bit < lax.axis_size(axis):
        value = value + swapped(value, axis, bit)
        bit *= 2
    return value


def neighbours(value, tall):
    outer, inner = lax.axis_size("gx"), lax.axis_size("gy")
    if not tall:
        return [shifted(value, ("gx", "gy"), k) for k in range(-BAND, BAND + 1) if k != 0]

    def cross(piece, bits):
        pairs = []
        for x in range(outer):
            for z in range(inner):
                source = (x - 1 if z ^ bits > z else x + 1) % outer
                pairs.append((source * inner + z, x * inner + z))
        return lax.ppermute(piece, ("gx", "gy"), pairs)

    two = swapped(value, "gy", 2)
    one = swapped(value, "gy", 1)
    three = swapped(two, "gy", 1)
    return [one, two, cross(one, 1), cross(two, 2), three, cross(three, 3)]


def in_vmem(count):
    return [pl.BlockSpec(memory_space=pltpu.VMEM)] * count


def thirds(value):
    high = value.astype(jnp.bfloat16)
    rest = value - high.astype(jnp.float32)
    middle = rest.astype(jnp.bfloat16)
    return high, middle, (rest - middle.astype(jnp.float32)).astype(jnp.bfloat16)


def product(left, right, contract, precision=None):
    return lax.dot_general(
        left, right, (contract, ((), ())), precision=precision, preferred_element_type=jnp.float32
    )


def extended(columns, ones_first):
    wide = columns.astype(jnp.float32)
    half = -0.5 * jnp.sum(wide * wide, axis=0, keepdims=True)
    terms = [term.astype(jnp.float32) for term in thirds(half)]
    shape = (EXTRA, columns.shape[1])
    level = lax.broadcasted_iota(jnp.int32, shape, 0)
    first = 0 if ones_first else 3
    below = jnp.where((level >= first) & (level < first + 3), 1.0, 0.0)
    for i, term in enumerate(terms):
        below = jnp.where(level == 3 - first + i, jnp.broadcast_to(term, shape), below)
    return jnp.concatenate([wide, below], axis=0)


def kernel_of(product_of_extended):
    return jnp.exp(product_of_extended * (2.0 / KERNEL_SCALE))


def pick_kernel(owner_ref, pivot_ref, point_ref, out_ref):
    count = point_ref.shape[1]
    wanted = [jnp.where(owner_ref[r] == owner_ref[2], pivot_ref[r:r + 1, :], -1) for r in range(2)]
    wanted = jnp.concatenate(wanted, axis=1)
    place = lax.broadcasted_iota(jnp.int32, (count, wanted.shape[1]), 0)
    chosen = jnp.where(place == wanted, 1.0, 0.0).astype(jnp.bfloat16)
    out_ref[...] = product(point_ref[...], chosen, ((1,), (0,))).astype(jnp.bfloat16)


def pick(owners, pivots, points_t):
    return pl.pallas_call(
        pick_kernel,
        out_shape=jax.ShapeDtypeStruct((points_t.shape[0], 2 * PIVOTS), jnp.bfloat16),
        in_specs=[pl.BlockSpec(memory_space=pltpu.SMEM)] + in_vmem(2),
        out_specs=in_vmem(1)[0],
        name="pick",
    )(owners, pivots, points_t)


def column(strip, lane):
    return jnp.broadcast_to(strip[:, lane:lane + 1], strip.shape)


def row(strip, i):
    return jnp.broadcast_to(strip[i:i + 1, :], strip.shape)


def small_inverse(strip, start):
    columns = [column(strip, start + k) for k in range(STRIP)]
    a = [[row(columns[k], i) for k in range(i + 1)] for i in range(STRIP)]
    scale = [None] * STRIP
    for k in range(STRIP):
        scale[k] = lax.rsqrt(a[k][k])
        for i in range(k + 1, STRIP):
            a[i][k] = a[i][k] * scale[k]
        for i in range(k + 1, STRIP):
            for j in range(k + 1, i + 1):
                a[i][j] = a[i][j] - a[i][k] * a[j][k]
    t = [[None] * STRIP for _ in range(STRIP)]
    for j in range(STRIP):
        t[j][j] = scale[j]
        for i in range(j + 1, STRIP):
            total = a[i][j] * t[j][j]
            for q in range(j + 1, i):
                total = total + a[i][q] * t[q][j]
            t[i][j] = -scale[i] * total
    return t


def inverse_factor(strips):
    lane = lax.broadcasted_iota(jnp.int32, (STRIP, LANES), 1)
    level = lax.broadcasted_iota(jnp.int32, (STRIP, LANES), 0)
    strips = list(strips)
    result = []
    for p in range(len(strips)):
        start = p * STRIP
        t = small_inverse(strips[p], start)
        own = (lane >= start) & (lane < start + STRIP)
        entered = jnp.where(own, jnp.where(lane - start == level, 1.0, 0.0), strips[p])
        done = None
        for k in range(STRIP):
            t_column = t[STRIP - 1][k]
            for i in range(STRIP - 2, k - 1, -1):
                t_column = jnp.where(level == i, t[i][k], t_column)
            if k:
                t_column = jnp.where(level < k, 0.0, t_column)
            term = t_column * row(entered, k)
            done = term if done is None else done + term
        result.append(jnp.where(lane < start + STRIP, done, 0.0))
        rows = [row(done, k) for k in range(STRIP)]
        for r in range(p + 1, len(strips)):
            columns = [column(strips[r], start + j) for j in range(STRIP)]
            update = None
            for k in range(STRIP):
                l_column = columns[0] * t[k][0]
                for j in range(1, k + 1):
                    l_column = l_column + columns[j] * t[k][j]
                term = l_column * rows[k]
                update = term if update is None else update + term
            strips[r] = jnp.where(own, 0.0, strips[r]) - update
    return result


def probe_kernel(
    pivot_ref, point_ref, coeff_ref, noise_ref, inverse_ref, probe_ref, sent_ref, high_ref, middle_ref, little_ref
):
    hp = lax.Precision.HIGHEST
    size = pivot_ref.shape[1]
    half = size // 2
    pivots = extended(pivot_ref[...], True).astype(jnp.bfloat16)
    others = extended(pivot_ref[...], False).astype(jnp.bfloat16)
    points = extended(point_ref[...], False).astype(jnp.bfloat16)
    cols = kernel_of(product(pivots, points, ((0,), (0,))))
    high_ref[...], middle_ref[...], little_ref[...] = thirds(cols)

    gram = kernel_of(product(pivots, others, ((0,), (0,))))
    equal = lax.broadcasted_iota(jnp.int32, gram.shape, 0) == lax.broadcasted_iota(jnp.int32, gram.shape, 1)
    gram = gram + jnp.where(equal, jitter, 0.0)

    def inverted(block):
        strips = [block[s:s + STRIP, :] for s in range(0, half, STRIP)]
        return jnp.concatenate(inverse_factor(strips), axis=0)

    one = inverted(gram[:half, :half])
    below = product(gram[half:, :half], one, ((1,), (1,)), hp)
    back = product(below, one, ((1,), (0,)), hp)
    two = inverted(gram[half:, half:] - product(below, below, ((1,), (1,)), hp))
    coeffs = coeff_ref[...]
    start = product(coeffs[:, :half], one, ((1,), (0,)), hp)
    later = product(coeffs[:, half:], two, ((1,), (0,)), hp)
    weights = jnp.concatenate([start - product(later, back, ((1,), (0,)), hp), later], axis=1)

    rows = weights.shape[0]
    stacked = jnp.concatenate(thirds(weights), axis=0)
    by_high = product(stacked, high_ref[...], ((1,), (0,)))
    by_middle = product(stacked[:2 * rows], middle_ref[...], ((1,), (0,)))
    by_little = product(stacked[:rows], little_ref[...], ((1,), (0,)))
    small = by_high[2 * rows:] + by_middle[rows:] + by_little
    probes = by_high[:rows] + (by_high[rows:2 * rows] + by_middle[:rows] + small) + noise_ref[...]
    probe_ref[...] = probes
    sent_ref[...] = probes.astype(jnp.bfloat16)

    inverse_ref[:half, :half] = one
    inverse_ref[:half, half:] = jnp.zeros((half, half), jnp.float32)
    inverse_ref[half:, :half] = -product(two, back, ((1,), (0,)), hp)
    inverse_ref[half:, half:] = two


def probes_of(pivots_t, points_t, coeffs_t, noise_t):
    size = pivots_t.shape[1]
    count = points_t.shape[1]
    return pl.pallas_call(
        probe_kernel,
        out_shape=(
            jax.ShapeDtypeStruct((size, size), jnp.float32),
            jax.ShapeDtypeStruct(noise_t.shape, jnp.float32),
            jax.ShapeDtypeStruct(noise_t.shape, jnp.bfloat16),
        ),
        in_specs=in_vmem(4),
        out_specs=tuple(in_vmem(3)),
        scratch_shapes=[pltpu.VMEM((size, count), jnp.bfloat16)] * 3,
        compiler_params=pltpu.CompilerParams(vmem_limit_bytes=32 * 1024 * 1024),
        name="probes",
    )(pivots_t, points_t, coeffs_t, noise_t)


def factor_kernel(pivot_ref, point_ref, inverse_ref, factor_ref):
    pivots = extended(pivot_ref[...], True).astype(jnp.bfloat16)
    points = extended(point_ref[...], False).astype(jnp.bfloat16)
    cols = kernel_of(product(points, pivots, ((0,), (0,))))
    factor_ref[...] = product(cols, inverse_ref[...], ((1,), (1,)), lax.Precision.HIGHEST)


def factor_of(pivots_t, points_t, inverse):
    size = pivots_t.shape[1]
    count = points_t.shape[1]
    return pl.pallas_call(
        factor_kernel,
        out_shape=jax.ShapeDtypeStruct((count, size), jnp.float32),
        in_specs=in_vmem(3),
        out_specs=in_vmem(1)[0],
        compiler_params=pltpu.CompilerParams(vmem_limit_bytes=32 * 1024 * 1024),
        cost_estimate=pl.CostEstimate(flops=12 * count * size * size, bytes_accessed=4 * count * size, transcendentals=count * size),
        name="factor",
    )(pivots_t, points_t, inverse)


def band_kernel(pieces, first, last, *refs):
    own_ref = refs[0]
    piece_refs = refs[1:1 + 2 * pieces]
    at = 1 + 2 * pieces
    total_ref = out_ref = refs[-1]
    count = own_ref.shape[1]
    before_ref = None
    if not first:
        before_ref = refs[at]
        at += 1
    if last:
        probe_ref = refs[at]
    own = extended(own_ref[...], True)
    own = jnp.concatenate([own, jnp.zeros((LANES - own.shape[0], count), jnp.float32)], axis=0)
    own = jnp.transpose(own).astype(jnp.bfloat16)
    others = []
    for i in range(pieces):
        other = extended(piece_refs[2 * i][...], False)
        other = jnp.concatenate([other, jnp.zeros((LANES - other.shape[0], count), jnp.float32)], axis=0)
        others.append(other.astype(jnp.bfloat16))
    for s in range(0, count, CHUNK):
        total = None if first else before_ref[s:s + CHUNK, :]
        for i in range(pieces):
            tile = kernel_of(product(own[s:s + CHUNK, :], others[i], ((1,), (0,)))).astype(jnp.bfloat16)
            term = product(tile, piece_refs[2 * i + 1][...], ((1,), (1,)))
            total = term if total is None else total + term
        if last:
            scale = 1.0 / (count ** 0.5)
            out_ref[:, s:s + CHUNK] = jnp.transpose(total) * scale + noise_weight * probe_ref[:, s:s + CHUNK]
        else:
            total_ref[s:s + CHUNK, :] = total


def band_sum(own, pieces, before=None, probes=None):
    depth, count = own.shape
    width = pieces[0][1].shape[0]
    first, last = before is None, probes is not None
    operands = [own] + [array for piece in pieces for array in piece]
    operands += ([] if first else [before]) + ([probes] if last else [])
    return pl.pallas_call(
        functools.partial(band_kernel, len(pieces), first, last),
        out_shape=jax.ShapeDtypeStruct((width, count) if last else (count, width), jnp.float32),
        in_specs=in_vmem(len(operands)),
        out_specs=in_vmem(1)[0],
        compiler_params=pltpu.CompilerParams(vmem_limit_bytes=32 * 1024 * 1024),
        cost_estimate=pl.CostEstimate(
            flops=len(pieces) * 4 * count * count * LANES,
            bytes_accessed=4 * count * width * len(operands),
            transcendentals=len(pieces) * count * count,
        ),
        name="band_sum",
    )(*operands)


def shards(points, pivots, owners, coeffs, noise):
    tall = lax.axis_size("gy") == BAND + 1
    points = points.T
    me = lax.axis_index(("gx", "gy"))
    picked = pick(jnp.concatenate([owners, jnp.reshape(me, (1,))]), pivots, points)
    picked, settled = lax.optimization_barrier((summed(picked, "gy"), points))
    pivot_points = summed(picked, "gx")
    near_points = neighbours(settled, tall)

    inverse, probes, sent = probes_of(pivot_points, points, coeffs.T, noise.T)
    near_probes = neighbours(sent, tall)
    factor = factor_of(pivot_points, points, inverse)
    near = list(zip(near_points, near_probes))
    total = band_sum(points, [(points, sent)])
    total = band_sum(points, near[:2], total)
    total = band_sum(points, near[2:4], total)
    kernel_probes = band_sum(points, near[4:], total, probes).T
    return (kernel_probes, factor)


def solution(mesh):
    in_specs = (P(("gx", "gy"), None), P(), P(), P(), P(("gx", "gy"), None))
    out_specs = (P(("gx", "gy"), None), P(("gx", "gy"), None))
    return jax.shard_map(shards, mesh=mesh, in_specs=in_specs, out_specs=out_specs, check_vma=False)
```

time: 118 us -> 63 us (0.53)
  other arithmetic: 56.6 us -> 1.4 us
  Pallas kernels: 0 us -> 26.5 us
  matrix products: 19.3 us -> 0 us
  local copies, waits for them, and re-layouts: 4.43 us -> 0.66 us
  waiting for transfers between devices: 12.9 us -> 9.93 us
  between operations: 2.29 us -> 0.75 us
  starting transfers between devices: 22.3 us -> 23.5 us
    another operation x9 -> x0, other arithmetic: 53.7 us -> none  [the longest x6 34 us: shards(): jnp.linalg.cholesky(kern(pivot_points, pivot_points) + jitter * ident)]
    pallas_call x0 -> x7, Pallas kernels: none -> 26.5 us  [the longest x1 12.6 us: probes_of(): pl.pallas_call(probe_kernel, out_shape=(jax.ShapeDtypeStruct((size, size)...]
    dot_general x13 -> x0, matrix products: 17.9 us -> none  [the longest x7 11.9 us: shards(): total = total + jnp.dot(tile, probe, preferred_element_type=jnp.float32)]
    another operation x9 -> x0, local copies, waits for them, and re-layouts: 4.15 us -> none
    ppermute x22 -> x17, waiting for transfers between devices: 12.9 us -> 9.93 us  [the longest x11 9.54 us: swapped(): lax.ppermute(value, axis, [(i ^ bit, i) for i in range(lax.axis_size(axis...]
    eq x3 -> x0, other arithmetic: 1.47 us -> none  [the longest x1 0.75 us: shards(): index == wanted[:, :, None]]
    another operation x5 -> x0, matrix products: 1.31 us -> none  [the longest x3 0.84 us: shards(): inverse = solve(chol, ident, lower=True)]
    reduce_sum x8 -> x0, other arithmetic: 1.23 us -> none  [the longest x1 0.94 us: kern(): left_square_norm = jnp.sum(jnp.square(left.astype(jnp.float32)), axis=1)]
  transfers between devices with their start and end apart: 22 -> 17, of which waited for: 9 -> 10; matrix products, arithmetic and copies ran while one was open for 64% -> 0% of each run, Pallas kernels for 0% -> 34%
where the time goes in v6:
time: 63 us; the launch traced here: 62.8 us
  Pallas kernels  26.5 us (42%)
  starting transfers between devices  23.5 us (37%)
  waiting for transfers between devices  9.93 us (16%)
  other arithmetic  1.4 us (2%)
  between operations  0.75 us (1%)
  local copies, waits for them, and re-layouts  0.66 us (1%)
    ppermute x11, starting transfers between devices, swapped(): lax.ppermute(value, axis, [(i ^ bit, i) for i in range(lax.axis_size(axis...  20.6 us
    pallas_call x1, Pallas kernels, probes_of(): pl.pallas_call(probe_kernel, out_shape=(jax.ShapeDtypeStruct((size, size)...  12.6 us
    pallas_call x4, Pallas kernels, band_sum(): pl.pallas_call(functools.partial(band_kernel, len(pieces), first, last),...  9.78 us
    ppermute x11, waiting for transfers between devices, swapped(): lax.ppermute(value, axis, [(i ^ bit, i) for i in range(lax.axis_size(axis...  9.54 us
    ppermute x6, starting transfers between devices, cross(): return lax.ppermute(piece, ('gx', 'gy'), pairs)  2.96 us
    pallas_call x1, Pallas kernels, factor_of(): pl.pallas_call(factor_kernel, out_shape=jax.ShapeDtypeStruct((count, size...  2.39 us
    pallas_call x1, Pallas kernels, pick(): pl.pallas_call(pick_kernel, out_shape=jax.ShapeDtypeStruct((points_t.shap...  1.76 us
  transfers between devices with their start and end apart: 17, of which 10 were waited for; matrix products, arithmetic and copies ran while one was open for 0% of the time, Pallas kernels for 34%

profile of v6, /device:TPU:0, one launch (start us, length us, event | category | flops | bytes accessed | tf_op | source)
XLA Modules:
  0.0 62.8 jit_solution(13648683502523626830)
XLA Ops:
  0.6 0.6 %copy-done.3 = s32[2]{0:T(128)S(1)} copy-done((s32[2]{0:T(128)S(1)}, s32[2]{0:T(128)}, u32[]{:S(2)}) %copy-start.3) | copy-done | bytes 32
  1.3 0.6 pad_add_fusion.owner_ref
  1.9 1.8 %pick.1 = bf16[64,256]{1,0:T(8,128)(2,1)} custom-call(s32[3]{0:T(128)} %pad_add_fusion.owner_ref, s32[2,128]{1,0:T(2,128)} %pivot_ref.1, bf16[64,1024]{1,0:T(8,128)(2,1)} %bitcast.5), custom_call_target="tpu_custom_call" | custom-call | tf_op jit(solution)/shard_map/pick/pallas_call | solution.py:103
  3.6 3.0 %collective-permute-start = (bf16[64,256]{1,0:T(8,128)(2,1)}, bf16[64,256]{1,0:T(8,128)(2,1)S(1)}, u32[]{:S(2)}, u32[]{:S(2)}) collective-permute-start(bf16[64,256]{1,0:T(8,128)(2,1)} %pick.1), channel_id=1, source_target_pairs={{1,0},{0,1},{3,2},{2,3},{5,4},{4,5},{7,6},{6,7},{9,8},{8,9},{11,10... | collective-permute-start | bytes 98312 | tf_op jit(solution)/shard_map/ppermute | solution.py:29
  6.7 2.1 %collective-permute-done = bf16[64,256]{1,0:T(8,128)(2,1)S(1)} collective-permute-done((bf16[64,256]{1,0:T(8,128)(2,1)}, bf16[64,256]{1,0:T(8,128)(2,1)S(1)}, u32[]{:S(2)}, u32[]{:S(2)}) %collective-permute-start) | collective-permute-done | bytes 32800 | tf_op jit(solution)/shard_map/ppermute | solution.py:29
  8.8 0.8 %add.19 = bf16[64,256]{1,0:T(8,128)(2,1)S(1)} add(bf16[64,256]{1,0:T(8,128)(2,1)} %pick.1, bf16[64,256]{1,0:T(8,128)(2,1)S(1)} %collective-permute-done) | non-fusion elementwise | flops 16384 | bytes 98304 | tf_op jit(solution)/shard_map/add | solution.py:35
  9.5 3.1 %collective-permute-start.1 = (bf16[64,256]{1,0:T(8,128)(2,1)S(1)}, bf16[64,256]{1,0:T(8,128)(2,1)S(1)}, u32[]{:S(2)}, u32[]{:S(2)}) collective-permute-start(bf16[64,256]{1,0:T(8,128)(2,1)S(1)} %add.19), channel_id=1, source_target_pairs={{2,0},{3,1},{0,2},{1,3},{6,4},{7,5},{4,6},{5,7},{10,8},{11,9},{8,1... | collective-permute-start | bytes 98312 | tf_op jit(solution)/shard_map/ppermute | solution.py:29
  12.6 1.9 %collective-permute-done.1 = bf16[64,256]{1,0:T(8,128)(2,1)S(1)} collective-permute-done((bf16[64,256]{1,0:T(8,128)(2,1)S(1)}, bf16[64,256]{1,0:T(8,128)(2,1)S(1)}, u32[]{:S(2)}, u32[]{:S(2)}) %collective-permute-start.1) | collective-permute-done | bytes 32800 | tf_op jit(solution)/shard_map/ppermute | solution.py:29
  14.6 1.2 %collective-permute-done.4 = bf16[64,256]{1,0:T(8,128)(2,1)S(1)} collective-permute-done((bf16[64,256]{1,0:T(8,128)(2,1)S(1)}, bf16[64,256]{1,0:T(8,128)(2,1)S(1)}, u32[]{:S(2)}, u32[]{:S(2)}) %collective-permute-start.4) | collective-permute-done | bytes 32800 | tf_op jit(solution)/shard_map/ppermute | solution.py:29
  15.8 1.9 %collective-permute-start.5 = (bf16[64,256]{1,0:T(8,128)(2,1)S(1)}, bf16[64,256]{1,0:T(8,128)(2,1)S(1)}, u32[]{:S(2)}, u32[]{:S(2)}) collective-permute-start(bf16[64,256]{1,0:T(8,128)(2,1)S(1)} %add.21), channel_id=1, source_target_pairs={{8,0},{12,4},{0,8},{4,12},{24,16},{28,20},{16,24},{20,28},{9,1},{1... | collective-permute-start | bytes 98312 | tf_op jit(solution)/shard_map/ppermute | solution.py:29
  17.7 2.6 %collective-permute-start.2 = (bf16[64,1024]{1,0:T(8,128)(2,1)S(1)}, bf16[64,1024]{1,0:T(8,128)(2,1)S(1)}, u32[]{:S(2)}, u32[]{:S(2)}) collective-permute-start(bf16[64,1024]{1,0:T(8,128)(2,1)S(1)} %bitcast.6), channel_id=1, source_target_pairs={{2,0},{3,1},{0,2},{1,3},{6,4},{7,5},{4,6},{5,7},{10,8},{11,9},{8,1... | collective-permute-start | bytes 393224 | tf_op jit(solution)/shard_map/ppermute | solution.py:29
  20.4 1.6 %collective-permute-start.6 = (bf16[64,256]{1,0:T(8,128)(2,1)S(1)}, bf16[64,256]{1,0:T(8,128)(2,1)S(1)}, u32[]{:S(2)}, u32[]{:S(2)}) collective-permute-start(bf16[64,256]{1,0:T(8,128)(2,1)S(1)} %add.22), channel_id=1, source_target_pairs={{16,0},{20,4},{24,8},{28,12},{0,16},{4,20},{8,24},{12,28},{17,1},{... | collective-permute-start | bytes 98312 | tf_op jit(solution)/shard_map/ppermute | solution.py:29
  22.0 2.4 %collective-permute-done.6 = bf16[64,256]{1,0:T(8,128)(2,1)S(1)} collective-permute-done((bf16[64,256]{1,0:T(8,128)(2,1)S(1)}, bf16[64,256]{1,0:T(8,128)(2,1)S(1)}, u32[]{:S(2)}, u32[]{:S(2)}) %collective-permute-start.6) | collective-permute-done | bytes 32800 | tf_op jit(solution)/shard_map/ppermute | solution.py:29
  24.4 12.6 %probes.1 = (f32[256,256]{1,0:T(8,128)S(1)}, f32[64,1024]{1,0:T(8,128)S(1)}, bf16[64,1024]{1,0:T(8,128)(2,1)S(1)}) custom-call(bf16[64,256]{1,0:T(8,128)(2,1)S(1)} %add.23.pivot_ref, bf16[64,1024]{1,0:T(8,128)(2,1)S(1)} %bitcast.7, f32[64,256]{1,0:T(8,128)S(1)} %bitcast.16, f32[64,1024]{1,0:T(8,128)S(1)} %bitcast.15), custom_call_target="tpu_custom_call" | custom-call | tf_op jit(solution)/shard_map/probes/pallas_call | solution.py:224
  37.0 2.5 %collective-permute-start.7 = (bf16[64,1024]{1,0:T(8,128)(2,1)S(1)}, bf16[64,1024]{1,0:T(8,128)(2,1)S(1)}, u32[]{:S(2)}, u32[]{:S(2)}) collective-permute-start(bf16[64,1024]{1,0:T(8,128)(2,1)S(1)} %get-tuple-element.9.refs_2_), channel_id=1, source_target_pairs={{2,0},{3,1},{0,2},{1,3},{6,4},{7,5},{4,6},{5,7},{10,8},{11,9},{8,1... | collective-permute-start | bytes 393224 | tf_op jit(solution)/shard_map/ppermute | solution.py:29
  39.5 1.8 %collective-permute-start.11 = (bf16[64,1024]{1,0:T(8,128)(2,1)S(1)}, bf16[64,1024]{1,0:T(8,128)(2,1)S(1)}, u32[]{:S(2)}, u32[]{:S(2)}) collective-permute-start(bf16[64,1024]{1,0:T(8,128)(2,1)S(1)} %bitcast.8), channel_id=1, source_target_pairs={{1,0},{0,1},{3,2},{2,3},{5,4},{4,5},{7,6},{6,7},{9,8},{8,9},{11,10... | collective-permute-start | bytes 393224 | tf_op jit(solution)/shard_map/ppermute | solution.py:29
  41.3 0.2 collective-permute-start.13
  41.5 1.8 %collective-permute-start.3 = (bf16[64,1024]{1,0:T(8,128)(2,1)S(1)}, bf16[64,1024]{1,0:T(8,128)(2,1)S(1)}, u32[]{:S(2)}, u32[]{:S(2)}) collective-permute-start(bf16[64,1024]{1,0:T(8,128)(2,1)S(1)} %collective-permute-done.2.refs_3_), channel_id=1, source_target_pairs={{1,0},{0,1},{3,2},{2,3},{5,4},{4,5},{7,6},{6,7},{9,8},{8,9},{11,10... | collective-permute-start | bytes 393224 | tf_op jit(solution)/shard_map/ppermute | solution.py:29
  43.3 0.9 %collective-permute-done.7.refs_4_ = bf16[64,1024]{1,0:T(8,128)(2,1)S(1)} collective-permute-done((bf16[64,1024]{1,0:T(8,128)(2,1)S(1)}, bf16[64,1024]{1,0:T(8,128)(2,1)S(1)}, u32[]{:S(2)}, u32[]{:S(2)}) %collective-permute-start.7) | collective-permute-done | bytes 131104 | tf_op jit(solution)/shard_map/ppermute | solution.py:29
  44.2 2.0 %collective-permute-start.8 = (bf16[64,1024]{1,0:T(8,128)(2,1)S(1)}, bf16[64,1024]{1,0:T(8,128)(2,1)S(1)}, u32[]{:S(2)}, u32[]{:S(2)}) collective-permute-start(bf16[64,1024]{1,0:T(8,128)(2,1)S(1)} %collective-permute-done.7.refs_4_), channel_id=1, source_target_pairs={{1,0},{0,1},{3,2},{2,3},{5,4},{4,5},{7,6},{6,7},{9,8},{8,9},{11,10... | collective-permute-start | bytes 393224 | tf_op jit(solution)/shard_map/ppermute | solution.py:29
  46.2 2.4 %factor.1 = f32[1024,256]{1,0:T(8,128)} custom-call(bf16[64,256]{1,0:T(8,128)(2,1)S(1)} %add.23.pivot_ref, bf16[64,1024]{1,0:T(8,128)(2,1)S(1)} %bitcast.9, f32[256,256]{1,0:T(8,128)S(1)} %get-tuple-element.11.inverse_ref), custom_call_target="tpu_custom_call" | custom-call | flops 805306368 | bytes 1048576 | tf_op jit(solution)/shard_map/factor/pallas_call | solution.py:249
  48.6 0.7 %collective-permute-done.13.refs_2_ = bf16[64,1024]{1,0:T(8,128)(2,1)S(1)} collective-permute-done((bf16[64,1024]{1,0:T(8,128)(2,1)S(1)}, bf16[64,1024]{1,0:T(8,128)(2,1)S(1)}, u32[]{:S(2)}, u32[]{:S(2)}) %collective-permute-start.13) | collective-permute-done | bytes 131104 | tf_op jit(solution)/shard_map/ppermute | solution.py:29
  49.3 0.5 collective-permute-start.16
  49.8 0.5 collective-permute-start.14
  50.2 1.4 %band_sum.4.refs_5_ = f32[1024,64]{1,0:T(8,128)S(1)} custom-call(bf16[64,1024]{1,0:T(8,128)(2,1)S(1)} %bitcast.10, bf16[64,1024]{1,0:T(8,128)(2,1)S(1)} %bitcast.11, bf16[64,1024]{1,0:T(8,128)(2,1)S(1)} %get-tuple-element.9.refs_2_), custom_call_target="tpu_custom_call" | custom-call | flops 536870912 | bytes 786432 | tf_op jit(solution)/shard_map/band_sum/pallas_call | solution.py:299
  51.6 0.3 collective-permute-done.3.refs_1_
  51.9 1.4 %collective-permute-start.9 = (bf16[64,1024]{1,0:T(8,128)(2,1)S(1)}, bf16[64,1024]{1,0:T(8,128)(2,1)S(1)}, u32[]{:S(2)}, u32[]{:S(2)}) collective-permute-start(bf16[64,1024]{1,0:T(8,128)(2,1)S(1)} %collective-permute-done.3.refs_1_), channel_id=1, source_target_pairs={{28,0},{29,1},{6,2},{7,3},{0,4},{1,5},{10,6},{11,7},{4,8},{5,9},{1... | collective-permute-start | bytes 393224 | tf_op jit(solution)/shard_map/ppermute | solution.py:51
  53.3 0.7 %collective-permute-start.10 = (bf16[64,1024]{1,0:T(8,128)(2,1)S(1)}, bf16[64,1024]{1,0:T(8,128)(2,1)S(1)}, u32[]{:S(2)}, u32[]{:S(2)}) collective-permute-start(bf16[64,1024]{1,0:T(8,128)(2,1)S(1)} %collective-permute-done.8.refs_2_), channel_id=1, source_target_pairs={{28,0},{29,1},{6,2},{7,3},{0,4},{1,5},{10,6},{11,7},{4,8},{5,9},{1... | collective-permute-start | bytes 393224 | tf_op jit(solution)/shard_map/ppermute | solution.py:51
  54.0 2.5 %band_sum.5.refs_5_ = f32[1024,64]{1,0:T(8,128)S(1)} custom-call(bf16[64,1024]{1,0:T(8,128)(2,1)S(1)} %bitcast.12, bf16[64,1024]{1,0:T(8,128)(2,1)S(1)} %collective-permute-done.11.refs_1_, bf16[64,1024]{1,0:T(8,128)(2,1)S(1)} %collective-permute-done.13.refs_2_, bf16[64,1024]{1,0:T(8,128)(2,1)S(1)} %collective-permute-done.2.refs_3_, ...), custom_call_target="tpu_custom_call" | custom-call | flops 1073741824 | bytes 1572864 | tf_op jit(solution)/shard_map/band_sum/pallas_call | solution.py:299
  56.7 2.5 %band_sum.6.refs_5_ = f32[1024,64]{1,0:T(8,128)S(1)} custom-call(bf16[64,1024]{1,0:T(8,128)(2,1)S(1)} %bitcast.13, bf16[64,1024]{1,0:T(8,128)(2,1)S(1)} %collective-permute-done.12.refs_1_, bf16[64,1024]{1,0:T(8,128)(2,1)S(1)} %collective-permute-done.14.refs_2_, bf16[64,1024]{1,0:T(8,128)(2,1)S(1)} %collective-permute-done.15.refs_3_, ...), custom_call_target="tpu_custom_call" | custom-call | flops 1073741824 | bytes 1572864 | tf_op jit(solution)/shard_map/band_sum/pallas_call | solution.py:299
  59.2 0.3 collective-permute-done.10.refs_4_
  59.5 3.3 %band_sum.7 = f32[64,1024]{1,0:T(8,128)} custom-call(bf16[64,1024]{1,0:T(8,128)(2,1)S(1)} %bitcast.14, bf16[64,1024]{1,0:T(8,128)(2,1)S(1)} %collective-permute-done.3.refs_1_, bf16[64,1024]{1,0:T(8,128)(2,1)S(1)} %collective-permute-done.8.refs_2_, bf16[64,1024]{1,0:T(8,128)(2,1)S(1)} %collective-permute-done.9.refs_3_, ...), custom_call_target="tpu_custom_call" | custom-call | flops 1073741824 | bytes 1835008 | tf_op jit(solution)/shard_map/band_sum/pallas_call | solution.py:299
  (23 shorter events, 0.3 us)
Async XLA Ops:
  0.6 0.7 %copy-start.3 = (s32[2]{0:T(128)S(1)}, s32[2]{0:T(128)}, u32[]{:S(2)}) copy-start(s32[2]{0:T(128)} %param.7) | copy-start | bytes 28
  3.6 14.1 %copy-start = (bf16[1024,64]{0,1:T(8,128)(2,1)S(1)}, bf16[1024,64]{0,1:T(8,128)(2,1)}, u32[]{:S(2)}) copy-start(bf16[1024,64]{0,1:T(8,128)(2,1)} %param.5) | copy-start | bytes 393220
  3.6 20.7 %copy-start.1 = (f32[1024,64]{0,1:T(8,128)S(1)}, f32[1024,64]{0,1:T(8,128)}, u32[]{:S(2)}) copy-start(f32[1024,64]{0,1:T(8,128)} %param.9) | copy-start | bytes 786436
  3.6 5.1 %collective-permute-start = (bf16[64,256]{1,0:T(8,128)(2,1)}, bf16[64,256]{1,0:T(8,128)(2,1)S(1)}, u32[]{:S(2)}, u32[]{:S(2)}) collective-permute-start(bf16[64,256]{1,0:T(8,128)(2,1)} %pick.1), channel_id=1, source_target_pairs={{1,0},{0,1},{3,2},{2,3},{5,4},{4,5},{7,6},{6,7},{9,8},{8,9},{11,10... | collective-permute-start | bytes 98312 | tf_op jit(solution)/shard_map/ppermute | solution.py:29
  9.5 5.0 %collective-permute-start.1 = (bf16[64,256]{1,0:T(8,128)(2,1)S(1)}, bf16[64,256]{1,0:T(8,128)(2,1)S(1)}, u32[]{:S(2)}, u32[]{:S(2)}) collective-permute-start(bf16[64,256]{1,0:T(8,128)(2,1)S(1)} %add.19), channel_id=1, source_target_pairs={{2,0},{3,1},{0,2},{1,3},{6,4},{7,5},{4,6},{5,7},{10,8},{11,9},{8,1... | collective-permute-start | bytes 98312 | tf_op jit(solution)/shard_map/ppermute | solution.py:29
  14.6 1.3 %collective-permute-start.4 = (bf16[64,256]{1,0:T(8,128)(2,1)S(1)}, bf16[64,256]{1,0:T(8,128)(2,1)S(1)}, u32[]{:S(2)}, u32[]{:S(2)}) collective-permute-start(bf16[64,256]{1,0:T(8,128)(2,1)S(1)} %add.20), channel_id=1, source_target_pairs={{4,0},{0,4},{12,8},{8,12},{20,16},{16,20},{28,24},{24,28},{5,1},{1... | collective-permute-start | bytes 98312 | tf_op jit(solution)/shard_map/ppermute | solution.py:29
  15.8 4.5 %collective-permute-start.5 = (bf16[64,256]{1,0:T(8,128)(2,1)S(1)}, bf16[64,256]{1,0:T(8,128)(2,1)S(1)}, u32[]{:S(2)}, u32[]{:S(2)}) collective-permute-start(bf16[64,256]{1,0:T(8,128)(2,1)S(1)} %add.21), channel_id=1, source_target_pairs={{8,0},{12,4},{0,8},{4,12},{24,16},{28,20},{16,24},{20,28},{9,1},{1... | collective-permute-start | bytes 98312 | tf_op jit(solution)/shard_map/ppermute | solution.py:29
  17.7 23.8 %collective-permute-start.2 = (bf16[64,1024]{1,0:T(8,128)(2,1)S(1)}, bf16[64,1024]{1,0:T(8,128)(2,1)S(1)}, u32[]{:S(2)}, u32[]{:S(2)}) collective-permute-start(bf16[64,1024]{1,0:T(8,128)(2,1)S(1)} %bitcast.6), channel_id=1, source_target_pairs={{2,0},{3,1},{0,2},{1,3},{6,4},{7,5},{4,6},{5,7},{10,8},{11,9},{8,1... | collective-permute-start | bytes 393224 | tf_op jit(solution)/shard_map/ppermute | solution.py:29
  20.4 4.0 %copy-start.2 = (f32[256,64]{0,1:T(8,128)S(1)}, f32[256,64]{0,1:T(8,128)}, u32[]{:S(2)}) copy-start(f32[256,64]{0,1:T(8,128)} %param.8) | copy-start | bytes 196612
  20.4 4.0 %collective-permute-start.6 = (bf16[64,256]{1,0:T(8,128)(2,1)S(1)}, bf16[64,256]{1,0:T(8,128)(2,1)S(1)}, u32[]{:S(2)}, u32[]{:S(2)}) collective-permute-start(bf16[64,256]{1,0:T(8,128)(2,1)S(1)} %add.22), channel_id=1, source_target_pairs={{16,0},{20,4},{24,8},{28,12},{0,16},{4,20},{8,24},{12,28},{17,1},{... | collective-permute-start | bytes 98312 | tf_op jit(solution)/shard_map/ppermute | solution.py:29
  37.0 7.2 %collective-permute-start.7 = (bf16[64,1024]{1,0:T(8,128)(2,1)S(1)}, bf16[64,1024]{1,0:T(8,128)(2,1)S(1)}, u32[]{:S(2)}, u32[]{:S(2)}) collective-permute-start(bf16[64,1024]{1,0:T(8,128)(2,1)S(1)} %get-tuple-element.9.refs_2_), channel_id=1, source_target_pairs={{2,0},{3,1},{0,2},{1,3},{6,4},{7,5},{4,6},{5,7},{10,8},{11,9},{8,1... | collective-permute-start | bytes 393224 | tf_op jit(solution)/shard_map/ppermute | solution.py:29
  39.5 9.1 %collective-permute-start.11 = (bf16[64,1024]{1,0:T(8,128)(2,1)S(1)}, bf16[64,1024]{1,0:T(8,128)(2,1)S(1)}, u32[]{:S(2)}, u32[]{:S(2)}) collective-permute-start(bf16[64,1024]{1,0:T(8,128)(2,1)S(1)} %bitcast.8), channel_id=1, source_target_pairs={{1,0},{0,1},{3,2},{2,3},{5,4},{4,5},{7,6},{6,7},{9,8},{8,9},{11,10... | collective-permute-start | bytes 393224 | tf_op jit(solution)/shard_map/ppermute | solution.py:29
  41.3 8.0 %collective-permute-start.13 = (bf16[64,1024]{1,0:T(8,128)(2,1)S(1)}, bf16[64,1024]{1,0:T(8,128)(2,1)S(1)}, u32[]{:S(2)}, u32[]{:S(2)}) collective-permute-start(bf16[64,1024]{1,0:T(8,128)(2,1)S(1)} %get-tuple-element.9.refs_2_), channel_id=1, source_target_pairs={{1,0},{0,1},{3,2},{2,3},{5,4},{4,5},{7,6},{6,7},{9,8},{8,9},{11,10... | collective-permute-start | bytes 393224 | tf_op jit(solution)/shard_map/ppermute | solution.py:29
  41.5 8.3 %collective-permute-start.15 = (bf16[64,1024]{1,0:T(8,128)(2,1)S(1)}, bf16[64,1024]{1,0:T(8,128)(2,1)S(1)}, u32[]{:S(2)}, u32[]{:S(2)}) collective-permute-start(bf16[64,1024]{1,0:T(8,128)(2,1)S(1)} %collective-permute-done.2.refs_3_), channel_id=1, source_target_pairs={{28,0},{29,1},{6,2},{7,3},{0,4},{1,5},{10,6},{11,7},{4,8},{5,9},{1... | collective-permute-start | bytes 393224 | tf_op jit(solution)/shard_map/ppermute | solution.py:51
  41.5 10.4 %collective-permute-start.3 = (bf16[64,1024]{1,0:T(8,128)(2,1)S(1)}, bf16[64,1024]{1,0:T(8,128)(2,1)S(1)}, u32[]{:S(2)}, u32[]{:S(2)}) collective-permute-start(bf16[64,1024]{1,0:T(8,128)(2,1)S(1)} %collective-permute-done.2.refs_3_), channel_id=1, source_target_pairs={{1,0},{0,1},{3,2},{2,3},{5,4},{4,5},{7,6},{6,7},{9,8},{8,9},{11,10... | collective-permute-start | bytes 393224 | tf_op jit(solution)/shard_map/ppermute | solution.py:29
  44.2 9.1 %collective-permute-start.8 = (bf16[64,1024]{1,0:T(8,128)(2,1)S(1)}, bf16[64,1024]{1,0:T(8,128)(2,1)S(1)}, u32[]{:S(2)}, u32[]{:S(2)}) collective-permute-start(bf16[64,1024]{1,0:T(8,128)(2,1)S(1)} %collective-permute-done.7.refs_4_), channel_id=1, source_target_pairs={{1,0},{0,1},{3,2},{2,3},{5,4},{4,5},{7,6},{6,7},{9,8},{8,9},{11,10... | collective-permute-start | bytes 393224 | tf_op jit(solution)/shard_map/ppermute | solution.py:29
  48.6 8.0 %collective-permute-start.12 = (bf16[64,1024]{1,0:T(8,128)(2,1)S(1)}, bf16[64,1024]{1,0:T(8,128)(2,1)S(1)}, u32[]{:S(2)}, u32[]{:S(2)}) collective-permute-start(bf16[64,1024]{1,0:T(8,128)(2,1)S(1)} %collective-permute-done.11.refs_1_), channel_id=1, source_target_pairs={{28,0},{5,1},{30,2},{7,3},{0,4},{9,5},{2,6},{11,7},{4,8},{13,9},{6... | collective-permute-start | bytes 393224 | tf_op jit(solution)/shard_map/ppermute | solution.py:51
  49.3 7.4 %collective-permute-start.16 = (bf16[64,1024]{1,0:T(8,128)(2,1)S(1)}, bf16[64,1024]{1,0:T(8,128)(2,1)S(1)}, u32[]{:S(2)}, u32[]{:S(2)}) collective-permute-start(bf16[64,1024]{1,0:T(8,128)(2,1)S(1)} %collective-permute-done.7.refs_4_), channel_id=1, source_target_pairs={{28,0},{29,1},{6,2},{7,3},{0,4},{1,5},{10,6},{11,7},{4,8},{5,9},{1... | collective-permute-start | bytes 393224 | tf_op jit(solution)/shard_map/ppermute | solution.py:51
  49.8 6.9 %collective-permute-start.14 = (bf16[64,1024]{1,0:T(8,128)(2,1)S(1)}, bf16[64,1024]{1,0:T(8,128)(2,1)S(1)}, u32[]{:S(2)}, u32[]{:S(2)}) collective-permute-start(bf16[64,1024]{1,0:T(8,128)(2,1)S(1)} %collective-permute-done.13.refs_2_), channel_id=1, source_target_pairs={{28,0},{5,1},{30,2},{7,3},{0,4},{9,5},{2,6},{11,7},{4,8},{13,9},{6... | collective-permute-start | bytes 393224 | tf_op jit(solution)/shard_map/ppermute | solution.py:51
  51.9 7.3 %collective-permute-start.9 = (bf16[64,1024]{1,0:T(8,128)(2,1)S(1)}, bf16[64,1024]{1,0:T(8,128)(2,1)S(1)}, u32[]{:S(2)}, u32[]{:S(2)}) collective-permute-start(bf16[64,1024]{1,0:T(8,128)(2,1)S(1)} %collective-permute-done.3.refs_1_), channel_id=1, source_target_pairs={{28,0},{29,1},{6,2},{7,3},{0,4},{1,5},{10,6},{11,7},{4,8},{5,9},{1... | collective-permute-start | bytes 393224 | tf_op jit(solution)/shard_map/ppermute | solution.py:51
  53.3 6.1 %collective-permute-start.10 = (bf16[64,1024]{1,0:T(8,128)(2,1)S(1)}, bf16[64,1024]{1,0:T(8,128)(2,1)S(1)}, u32[]{:S(2)}, u32[]{:S(2)}) collective-permute-start(bf16[64,1024]{1,0:T(8,128)(2,1)S(1)} %collective-permute-done.8.refs_2_), channel_id=1, source_target_pairs={{28,0},{29,1},{6,2},{7,3},{0,4},{1,5},{10,6},{11,7},{4,8},{5,9},{1... | collective-permute-start | bytes 393224 | tf_op jit(solution)/shard_map/ppermute | solution.py:51

commit v7 on v6

--- a/solution.py
+++ b/solution.py
@@ -29,31 +29,42 @@
     return lax.ppermute(value, axis, [(i ^ bit, i) for i in range(lax.axis_size(axis))])
 
 
-def summed(value, axis):
-    bit = 1
-    while bit < lax.axis_size(axis):
-        value = value + swapped(value, axis, bit)
-        bit *= 2
-    return value
-
-
-def neighbours(value, tall):
+def after(value, *others):
+    return lax.optimization_barrier((value,) + others)[0]
+
+
+def spread(value):
+    sums = [value]
+    for axis in ("gx", "gy"):
+        bits = [1 << i for i in range(lax.axis_size(axis).bit_length() - 1)]
+        for bit in bits if axis == "gx" else bits[::-1]:
+            sums.append(sums[-1] + swapped(sums[-1], axis, bit))
+    return sums[1:]
+
+
+def cross(piece, bits):
     outer, inner = lax.axis_size("gx"), lax.axis_size("gy")
-    if not tall:
+    pairs = []
+    for x in range(outer):
+        for z in range(inner):
+            source = (x - 1 if z ^ bits > z else x + 1) % outer
+            pairs.append((source * inner + z, x * inner + z))
+    return lax.ppermute(piece, ("gx", "gy"), pairs)
+
+
+def neighbours(value, steps=()):
+    if lax.axis_size("gy") != BAND + 1:
         return [shifted(value, ("gx", "gy"), k) for k in range(-BAND, BAND + 1) if k != 0]
 
-    def cross(piece, bits):
-        pairs = []
-        for x in range(outer):
-            for z in range(inner):
-                source = (x - 1 if z ^ bits > z else x + 1) % outer
-                pairs.append((source * inner + z, x * inner + z))
-        return lax.ppermute(piece, ("gx", "gy"), pairs)
+    def at(piece, step):
+        return after(piece, steps[min(step, len(steps) - 1)]) if steps else piece
 
     two = swapped(value, "gy", 2)
-    one = swapped(value, "gy", 1)
-    three = swapped(two, "gy", 1)
-    return [one, two, cross(one, 1), cross(two, 2), three, cross(three, 3)]
+    one = swapped(at(value, 0), "gy", 1)
+    three = swapped(at(two, 1), "gy", 1)
+    cross_one = cross(at(one, 2), 1)
+    cross_two = cross(at(two, 3), 2)
+    return [one, two, cross_one, cross_two, three, cross(at(three, 4), 3)]
 
 
 def in_vmem(count):
@@ -92,7 +103,8 @@
 
 def pick_kernel(owner_ref, pivot_ref, point_ref, out_ref):
     count = point_ref.shape[1]
-    wanted = [jnp.where(owner_ref[r] == owner_ref[2], pivot_ref[r:r + 1, :], -1) for r in range(2)]
+    me = lax.axis_index(("gx", "gy"))
+    wanted = [jnp.where(owner_ref[r] == me, pivot_ref[r:r + 1, :], -1) for r in range(2)]
     wanted = jnp.concatenate(wanted, axis=1)
     place = lax.broadcasted_iota(jnp.int32, (count, wanted.shape[1]), 0)
     chosen = jnp.where(place == wanted, 1.0, 0.0).astype(jnp.bfloat16)
@@ -173,9 +185,8 @@
     return result
 
 
-def probe_kernel(
-    pivot_ref, point_ref, coeff_ref, noise_ref, inverse_ref, probe_ref, sent_ref, high_ref, middle_ref, little_ref
-):
+def probe_kernel(pivot_ref, point_ref, coeff_ref, noise_ref, *refs):
+    inverse_ref, probe_ref, sent_ref, high_ref, middle_ref, little_ref = refs[-6:]
     hp = lax.Precision.HIGHEST
     size = pivot_ref.shape[1]
     half = size // 2
@@ -218,7 +229,7 @@
     inverse_ref[half:, half:] = two
 
 
-def probes_of(pivots_t, points_t, coeffs_t, noise_t):
+def probes_of(pivots_t, points_t, coeffs_t, noise_t, awaited):
     size = pivots_t.shape[1]
     count = points_t.shape[1]
     return pl.pallas_call(
@@ -228,12 +239,12 @@
             jax.ShapeDtypeStruct(noise_t.shape, jnp.float32),
             jax.ShapeDtypeStruct(noise_t.shape, jnp.bfloat16),
         ),
-        in_specs=in_vmem(4),
+        in_specs=in_vmem(4) + [pl.BlockSpec(memory_space=pl.ANY)] * len(awaited),
         out_specs=tuple(in_vmem(3)),
         scratch_shapes=[pltpu.VMEM((size, count), jnp.bfloat16)] * 3,
         compiler_params=pltpu.CompilerParams(vmem_limit_bytes=32 * 1024 * 1024),
         name="probes",
-    )(pivots_t, points_t, coeffs_t, noise_t)
+    )(pivots_t, points_t, coeffs_t, noise_t, *awaited)
 
 
 def factor_kernel(pivot_ref, point_ref, inverse_ref, factor_ref):
@@ -312,16 +323,13 @@
 
 
 def shards(points, pivots, owners, coeffs, noise):
-    tall = lax.axis_size("gy") == BAND + 1
     points = points.T
-    me = lax.axis_index(("gx", "gy"))
-    picked = pick(jnp.concatenate([owners, jnp.reshape(me, (1,))]), pivots, points)
-    picked, settled = lax.optimization_barrier((summed(picked, "gy"), points))
-    pivot_points = summed(picked, "gx")
-    near_points = neighbours(settled, tall)
-
-    inverse, probes, sent = probes_of(pivot_points, points, coeffs.T, noise.T)
-    near_probes = neighbours(sent, tall)
+    rounds = spread(pick(owners, pivots, points))
+    pivot_points = rounds[-1]
+    near_points = neighbours(points, rounds)
+
+    inverse, probes, sent = probes_of(pivot_points, points, coeffs.T, noise.T, near_points[:5])
+    near_probes = neighbours(sent)
     factor = factor_of(pivot_points, points, inverse)
     near = list(zip(near_points, near_probes))
     total = band_sum(points, [(points, sent)])

time: 63 us -> 66.8 us (1.060)
  waiting for transfers between devices: 9.93 us -> 17.6 us
  starting transfers between devices: 23.5 us -> 20.7 us
    ppermute x11, waiting for transfers between devices: 9.54 us -> 17.5 us  [swapped(): lax.ppermute(value, axis, [(i ^ bit, i) for i in range(lax.axis_size(axis...]
    ppermute x11, starting transfers between devices: 20.6 us -> 16.1 us  [swapped(): lax.ppermute(value, axis, [(i ^ bit, i) for i in range(lax.axis_size(axis...]
    ppermute x6, starting transfers between devices: 2.96 us -> 4.62 us  [cross(): return lax.ppermute(piece, ('gx', 'gy'), pairs)]
  transfers between devices with their start and end apart: 17 -> 17, of which waited for: 10 -> 5; matrix products, arithmetic and copies ran while one was open for 0% -> 1% of each run, Pallas kernels for 34% -> 13%
where the time goes in v7:
time: 66.8 us; the launch traced here: 66.4 us
  Pallas kernels  26.6 us (40%)
  starting transfers between devices  20.7 us (31%)
  waiting for transfers between devices  17.6 us (26%)
  other arithmetic  0.81 us (1%)
  between operations  0.79 us (1%)
    ppermute x11, waiting for transfers between devices, swapped(): lax.ppermute(value, axis, [(i ^ bit, i) for i in range(lax.axis_size(axis...  17.5 us
    ppermute x11, starting transfers between devices, swapped(): lax.ppermute(value, axis, [(i ^ bit, i) for i in range(lax.axis_size(axis...  16.1 us
    pallas_call x1, Pallas kernels, probes_of(): pl.pallas_call(probe_kernel, out_shape=(jax.ShapeDtypeStruct((size, size)...  12.6 us
    pallas_call x4, Pallas kernels, band_sum(): pl.pallas_call(functools.partial(band_kernel, len(pieces), first, last),...  9.77 us
    ppermute x6, starting transfers between devices, cross(): return lax.ppermute(piece, ('gx', 'gy'), pairs)  4.62 us
    pallas_call x1, Pallas kernels, factor_of(): pl.pallas_call(factor_kernel, out_shape=jax.ShapeDtypeStruct((count, size...  2.39 us
    pallas_call x1, Pallas kernels, pick(): pl.pallas_call(pick_kernel, out_shape=jax.ShapeDtypeStruct((points_t.shap...  1.82 us
  transfers between devices with their start and end apart: 17, of which 5 were waited for; matrix products, arithmetic and copies ran while one was open for 1% of the time, Pallas kernels for 13%

profile of v7, /device:TPU:0, one launch (start us, length us, event | category | flops | bytes accessed | tf_op | source)
XLA Modules:
  0.0 66.4 jit_solution(10112512698218978901)
XLA Ops:
  0.6 1.8 %pick.1 = bf16[64,256]{1,0:T(8,128)(2,1)} custom-call(s32[2]{0:T(128)} %owner_ref.1, s32[2,128]{1,0:T(2,128)} %pivot_ref.1, bf16[64,1024]{1,0:T(8,128)(2,1)} %bitcast.4), custom_call_target="tpu_custom_call" | custom-call | tf_op jit(solution)/shard_map/pick/pallas_call | solution.py:115
  2.5 0.5 collective-permute-start.1
  2.9 3.7 %collective-permute-start = (bf16[64,1024]{1,0:T(8,128)(2,1)S(1)}, bf16[64,1024]{1,0:T(8,128)(2,1)S(1)}, u32[]{:S(2)}, u32[]{:S(2)}) collective-permute-start(bf16[64,1024]{1,0:T(8,128)(2,1)S(1)} %bitcast.5), channel_id=1, source_target_pairs={{2,0},{3,1},{0,2},{1,3},{6,4},{7,5},{4,6},{5,7},{10,8},{11,9},{8,1... | collective-permute-start | bytes 393224 | tf_op jit(solution)/shard_map/ppermute | solution.py:29
  6.6 0.8 %add.15 = bf16[64,256]{1,0:T(8,128)(2,1)S(1)} add(bf16[64,256]{1,0:T(8,128)(2,1)} %pick.1, bf16[64,256]{1,0:T(8,128)(2,1)S(1)} %collective-permute-done.1) | non-fusion elementwise | flops 16384 | bytes 98304 | tf_op jit(solution)/shard_map/add | solution.py:41
  7.3 1.6 %collective-permute-start.7 = (bf16[64,1024]{1,0:T(8,128)(2,1)S(1)}, bf16[64,1024]{1,0:T(8,128)(2,1)S(1)}, u32[]{:S(2)}, u32[]{:S(2)}) collective-permute-start(bf16[64,1024]{1,0:T(8,128)(2,1)S(1)} %bitcast.6), channel_id=1, source_target_pairs={{1,0},{0,1},{3,2},{2,3},{5,4},{4,5},{7,6},{6,7},{9,8},{8,9},{11,10... | collective-permute-start | bytes 393224 | tf_op jit(solution)/shard_map/ppermute | solution.py:29
  9.0 1.5 %collective-permute-start.2 = (bf16[64,256]{1,0:T(8,128)(2,1)S(1)}, bf16[64,256]{1,0:T(8,128)(2,1)S(1)}, u32[]{:S(2)}, u32[]{:S(2)}) collective-permute-start(bf16[64,256]{1,0:T(8,128)(2,1)S(1)} %add.15), channel_id=1, source_target_pairs={{8,0},{12,4},{0,8},{4,12},{24,16},{28,20},{16,24},{20,28},{9,1},{1... | collective-permute-start | bytes 98312 | tf_op jit(solution)/shard_map/ppermute | solution.py:29
  10.5 2.4 %collective-permute-done.2 = bf16[64,256]{1,0:T(8,128)(2,1)S(1)} collective-permute-done((bf16[64,256]{1,0:T(8,128)(2,1)S(1)}, bf16[64,256]{1,0:T(8,128)(2,1)S(1)}, u32[]{:S(2)}, u32[]{:S(2)}) %collective-permute-start.2) | collective-permute-done | bytes 32800 | tf_op jit(solution)/shard_map/ppermute | solution.py:29
  12.9 1.6 %collective-permute-start.4 = (bf16[64,256]{1,0:T(8,128)(2,1)S(1)}, bf16[64,256]{1,0:T(8,128)(2,1)S(1)}, u32[]{:S(2)}, u32[]{:S(2)}) collective-permute-start(bf16[64,256]{1,0:T(8,128)(2,1)S(1)} %add.16), channel_id=1, source_target_pairs={{16,0},{20,4},{24,8},{28,12},{0,16},{4,20},{8,24},{12,28},{17,1},{... | collective-permute-start | bytes 98312 | tf_op jit(solution)/shard_map/ppermute | solution.py:29
  14.5 2.4 %collective-permute-done.4 = bf16[64,256]{1,0:T(8,128)(2,1)S(1)} collective-permute-done((bf16[64,256]{1,0:T(8,128)(2,1)S(1)}, bf16[64,256]{1,0:T(8,128)(2,1)S(1)}, u32[]{:S(2)}, u32[]{:S(2)}) %collective-permute-start.4) | collective-permute-done | bytes 32800 | tf_op jit(solution)/shard_map/ppermute | solution.py:29
  16.9 1.4 %collective-permute-start.5 = (bf16[64,256]{1,0:T(8,128)(2,1)S(1)}, bf16[64,256]{1,0:T(8,128)(2,1)S(1)}, u32[]{:S(2)}, u32[]{:S(2)}) collective-permute-start(bf16[64,256]{1,0:T(8,128)(2,1)S(1)} %add.17), channel_id=1, source_target_pairs={{2,0},{3,1},{0,2},{1,3},{6,4},{7,5},{4,6},{5,7},{10,8},{11,9},{8,1... | collective-permute-start | bytes 98312 | tf_op jit(solution)/shard_map/ppermute | solution.py:29
  18.3 3.7 %collective-permute-done.5 = bf16[64,256]{1,0:T(8,128)(2,1)S(1)} collective-permute-done((bf16[64,256]{1,0:T(8,128)(2,1)S(1)}, bf16[64,256]{1,0:T(8,128)(2,1)S(1)}, u32[]{:S(2)}, u32[]{:S(2)}) %collective-permute-start.5) | collective-permute-done | bytes 32800 | tf_op jit(solution)/shard_map/ppermute | solution.py:29
  22.0 0.0 copy-start.2
  22.1 0.0 collective-permute-done.refs_1_.refs_3_
  22.1 0.1 collective-permute-start.9
  22.1 0.3 collective-permute-start.3
  22.4 1.3 %collective-permute-start.8 = (bf16[64,1024]{1,0:T(8,128)(2,1)S(1)}, bf16[64,1024]{1,0:T(8,128)(2,1)S(1)}, u32[]{:S(2)}, u32[]{:S(2)}) collective-permute-start(bf16[64,1024]{1,0:T(8,128)(2,1)S(1)} %collective-permute-done.7.refs_0_.refs_1_), channel_id=1, source_target_pairs={{28,0},{5,1},{30,2},{7,3},{0,4},{9,5},{2,6},{11,7},{4,8},{13,9},{6... | collective-permute-start | bytes 393224 | tf_op jit(solution)/shard_map/ppermute | solution.py:52
  23.7 2.8 %collective-permute-start.6 = (bf16[64,256]{1,0:T(8,128)(2,1)S(1)}, bf16[64,256]{1,0:T(8,128)(2,1)S(1)}, u32[]{:S(2)}, u32[]{:S(2)}) collective-permute-start(bf16[64,256]{1,0:T(8,128)(2,1)S(1)} %add.18), channel_id=1, source_target_pairs={{1,0},{0,1},{3,2},{2,3},{5,4},{4,5},{7,6},{6,7},{9,8},{8,9},{11,10... | collective-permute-start | bytes 98312 | tf_op jit(solution)/shard_map/ppermute | solution.py:29
  26.5 2.3 %collective-permute-done.6 = bf16[64,256]{1,0:T(8,128)(2,1)S(1)} collective-permute-done((bf16[64,256]{1,0:T(8,128)(2,1)S(1)}, bf16[64,256]{1,0:T(8,128)(2,1)S(1)}, u32[]{:S(2)}, u32[]{:S(2)}) %collective-permute-start.6) | collective-permute-done | bytes 32800 | tf_op jit(solution)/shard_map/ppermute | solution.py:29
  28.8 0.0 collective-permute-done.9.refs_3_
  28.8 12.6 %probes.1 = (f32[256,256]{1,0:T(8,128)S(1)}, f32[64,1024]{1,0:T(8,128)S(1)}, bf16[64,1024]{1,0:T(8,128)(2,1)S(1)}) custom-call(bf16[64,256]{1,0:T(8,128)(2,1)S(1)} %add.19.pivot_ref, bf16[64,1024]{1,0:T(8,128)(2,1)S(1)} %bitcast.7, f32[64,256]{1,0:T(8,128)S(1)} %bitcast.15, f32[64,1024]{1,0:T(8,128)S(1)} %bitcast.14, ...), custom_call_target="tpu_custom_call" | custom-call | tf_op jit(solution)/shard_map/probes/pallas_call | solution.py:235
  41.4 1.2 %collective-permute-start.10 = (bf16[64,1024]{1,0:T(8,128)(2,1)S(1)}, bf16[64,1024]{1,0:T(8,128)(2,1)S(1)}, u32[]{:S(2)}, u32[]{:S(2)}) collective-permute-start(bf16[64,1024]{1,0:T(8,128)(2,1)S(1)} %get-tuple-element.14.refs_2_), channel_id=1, source_target_pairs={{2,0},{3,1},{0,2},{1,3},{6,4},{7,5},{4,6},{5,7},{10,8},{11,9},{8,1... | collective-permute-start | bytes 393224 | tf_op jit(solution)/shard_map/ppermute | solution.py:29
  42.7 1.5 %collective-permute-start.14 = (bf16[64,1024]{1,0:T(8,128)(2,1)S(1)}, bf16[64,1024]{1,0:T(8,128)(2,1)S(1)}, u32[]{:S(2)}, u32[]{:S(2)}) collective-permute-start(bf16[64,1024]{1,0:T(8,128)(2,1)S(1)} %get-tuple-element.14.refs_2_), channel_id=1, source_target_pairs={{1,0},{0,1},{3,2},{2,3},{5,4},{4,5},{7,6},{6,7},{9,8},{8,9},{11,10... | collective-permute-start | bytes 393224 | tf_op jit(solution)/shard_map/ppermute | solution.py:29
  44.2 6.7 %collective-permute-done.10.refs_4_ = bf16[64,1024]{1,0:T(8,128)(2,1)S(1)} collective-permute-done((bf16[64,1024]{1,0:T(8,128)(2,1)S(1)}, bf16[64,1024]{1,0:T(8,128)(2,1)S(1)}, u32[]{:S(2)}, u32[]{:S(2)}) %collective-permute-start.10) | collective-permute-done | bytes 131104 | tf_op jit(solution)/shard_map/ppermute | solution.py:29
  50.9 0.0 collective-permute-start.12
  50.9 2.4 %factor.1 = f32[1024,256]{1,0:T(8,128)} custom-call(bf16[64,256]{1,0:T(8,128)(2,1)S(1)} %add.19.pivot_ref, bf16[64,1024]{1,0:T(8,128)(2,1)S(1)} %bitcast.8, f32[256,256]{1,0:T(8,128)S(1)} %get-tuple-element.17.inverse_ref), custom_call_target="tpu_custom_call" | custom-call | flops 805306368 | bytes 1048576 | tf_op jit(solution)/shard_map/factor/pallas_call | solution.py:260
  53.3 1.6 %collective-permute-start.16 = (bf16[64,1024]{1,0:T(8,128)(2,1)S(1)}, bf16[64,1024]{1,0:T(8,128)(2,1)S(1)}, u32[]{:S(2)}, u32[]{:S(2)}) collective-permute-start(bf16[64,1024]{1,0:T(8,128)(2,1)S(1)} %collective-permute-done.10.refs_4_), channel_id=1, source_target_pairs={{28,0},{29,1},{6,2},{7,3},{0,4},{1,5},{10,6},{11,7},{4,8},{5,9},{1... | collective-permute-start | bytes 393224 | tf_op jit(solution)/shard_map/ppermute | solution.py:52
  54.9 0.0 collective-permute-start.15
  54.9 1.4 %band_sum.4.refs_5_ = f32[1024,64]{1,0:T(8,128)S(1)} custom-call(bf16[64,1024]{1,0:T(8,128)(2,1)S(1)} %bitcast.9, bf16[64,1024]{1,0:T(8,128)(2,1)S(1)} %bitcast.10, bf16[64,1024]{1,0:T(8,128)(2,1)S(1)} %get-tuple-element.14.refs_2_), custom_call_target="tpu_custom_call" | custom-call | flops 536870912 | bytes 786432 | tf_op jit(solution)/shard_map/band_sum/pallas_call | solution.py:310
  56.4 1.7 %collective-permute-start.13 = (bf16[64,1024]{1,0:T(8,128)(2,1)S(1)}, bf16[64,1024]{1,0:T(8,128)(2,1)S(1)}, u32[]{:S(2)}, u32[]{:S(2)}) collective-permute-start(bf16[64,1024]{1,0:T(8,128)(2,1)S(1)} %collective-permute-done.11.refs_2_), channel_id=1, source_target_pairs={{28,0},{29,1},{6,2},{7,3},{0,4},{1,5},{10,6},{11,7},{4,8},{5,9},{1... | collective-permute-start | bytes 393224 | tf_op jit(solution)/shard_map/ppermute | solution.py:52
  58.0 2.5 %band_sum.5.refs_5_ = f32[1024,64]{1,0:T(8,128)S(1)} custom-call(bf16[64,1024]{1,0:T(8,128)(2,1)S(1)} %bitcast.11, bf16[64,1024]{1,0:T(8,128)(2,1)S(1)} %collective-permute-done.7.refs_0_.refs_1_, bf16[64,1024]{1,0:T(8,128)(2,1)S(1)} %collective-permute-done.14.refs_2_, bf16[64,1024]{1,0:T(8,128)(2,1)S(1)} %collective-permute-done.refs_1_.refs_3_, ...), custom_call_target="tpu_custom_call" | custom-call | flops 1073741824 | bytes 1572864 | tf_op jit(solution)/shard_map/band_sum/pallas_call | solution.py:310
  60.6 2.5 %band_sum.6.refs_5_ = f32[1024,64]{1,0:T(8,128)S(1)} custom-call(bf16[64,1024]{1,0:T(8,128)(2,1)S(1)} %bitcast.12, bf16[64,1024]{1,0:T(8,128)(2,1)S(1)} %collective-permute-done.8.refs_2_.refs_1_, bf16[64,1024]{1,0:T(8,128)(2,1)S(1)} %collective-permute-done.15.refs_2_, bf16[64,1024]{1,0:T(8,128)(2,1)S(1)} %collective-permute-done.9.refs_3_, ...), custom_call_target="tpu_custom_call" | custom-call | flops 1073741824 | bytes 1572864 | tf_op jit(solution)/shard_map/band_sum/pallas_call | solution.py:310
  63.1 3.3 %band_sum.7 = f32[64,1024]{1,0:T(8,128)} custom-call(bf16[64,1024]{1,0:T(8,128)(2,1)S(1)} %bitcast.13, bf16[64,1024]{1,0:T(8,128)(2,1)S(1)} %collective-permute-done.3.refs_4_.refs_1_, bf16[64,1024]{1,0:T(8,128)(2,1)S(1)} %collective-permute-done.11.refs_2_, bf16[64,1024]{1,0:T(8,128)(2,1)S(1)} %collective-permute-done.12.refs_3_, ...), custom_call_target="tpu_custom_call" | custom-call | flops 1073741824 | bytes 1835008 | tf_op jit(solution)/shard_map/band_sum/pallas_call | solution.py:310
  (20 shorter events, 0.1 us)
Async XLA Ops:
  0.6 2.3 %copy-start = (bf16[1024,64]{0,1:T(8,128)(2,1)S(1)}, bf16[1024,64]{0,1:T(8,128)(2,1)}, u32[]{:S(2)}) copy-start(bf16[1024,64]{0,1:T(8,128)(2,1)} %param.5) | copy-start | bytes 393220
  2.5 26.4 %copy-start.1 = (f32[1024,64]{0,1:T(8,128)S(1)}, f32[1024,64]{0,1:T(8,128)}, u32[]{:S(2)}) copy-start(f32[1024,64]{0,1:T(8,128)} %param.9) | copy-start | bytes 786436
  2.5 4.1 %collective-permute-start.1 = (bf16[64,256]{1,0:T(8,128)(2,1)}, bf16[64,256]{1,0:T(8,128)(2,1)S(1)}, u32[]{:S(2)}, u32[]{:S(2)}) collective-permute-start(bf16[64,256]{1,0:T(8,128)(2,1)} %pick.1), channel_id=1, source_target_pairs={{4,0},{0,4},{12,8},{8,12},{20,16},{16,20},{28,24},{24,28},{5,1},{1... | collective-permute-start | bytes 98312 | tf_op jit(solution)/shard_map/ppermute | solution.py:29
  2.9 19.1 %collective-permute-start = (bf16[64,1024]{1,0:T(8,128)(2,1)S(1)}, bf16[64,1024]{1,0:T(8,128)(2,1)S(1)}, u32[]{:S(2)}, u32[]{:S(2)}) collective-permute-start(bf16[64,1024]{1,0:T(8,128)(2,1)S(1)} %bitcast.5), channel_id=1, source_target_pairs={{2,0},{3,1},{0,2},{1,3},{6,4},{7,5},{4,6},{5,7},{10,8},{11,9},{8,1... | collective-permute-start | bytes 393224 | tf_op jit(solution)/shard_map/ppermute | solution.py:29
  7.3 15.1 %collective-permute-start.7 = (bf16[64,1024]{1,0:T(8,128)(2,1)S(1)}, bf16[64,1024]{1,0:T(8,128)(2,1)S(1)}, u32[]{:S(2)}, u32[]{:S(2)}) collective-permute-start(bf16[64,1024]{1,0:T(8,128)(2,1)S(1)} %bitcast.6), channel_id=1, source_target_pairs={{1,0},{0,1},{3,2},{2,3},{5,4},{4,5},{7,6},{6,7},{9,8},{8,9},{11,10... | collective-permute-start | bytes 393224 | tf_op jit(solution)/shard_map/ppermute | solution.py:29
  9.0 3.9 %collective-permute-start.2 = (bf16[64,256]{1,0:T(8,128)(2,1)S(1)}, bf16[64,256]{1,0:T(8,128)(2,1)S(1)}, u32[]{:S(2)}, u32[]{:S(2)}) collective-permute-start(bf16[64,256]{1,0:T(8,128)(2,1)S(1)} %add.15), channel_id=1, source_target_pairs={{8,0},{12,4},{0,8},{4,12},{24,16},{28,20},{16,24},{20,28},{9,1},{1... | collective-permute-start | bytes 98312 | tf_op jit(solution)/shard_map/ppermute | solution.py:29
  12.9 4.0 %collective-permute-start.4 = (bf16[64,256]{1,0:T(8,128)(2,1)S(1)}, bf16[64,256]{1,0:T(8,128)(2,1)S(1)}, u32[]{:S(2)}, u32[]{:S(2)}) collective-permute-start(bf16[64,256]{1,0:T(8,128)(2,1)S(1)} %add.16), channel_id=1, source_target_pairs={{16,0},{20,4},{24,8},{28,12},{0,16},{4,20},{8,24},{12,28},{17,1},{... | collective-permute-start | bytes 98312 | tf_op jit(solution)/shard_map/ppermute | solution.py:29
  16.9 5.1 %collective-permute-start.5 = (bf16[64,256]{1,0:T(8,128)(2,1)S(1)}, bf16[64,256]{1,0:T(8,128)(2,1)S(1)}, u32[]{:S(2)}, u32[]{:S(2)}) collective-permute-start(bf16[64,256]{1,0:T(8,128)(2,1)S(1)} %add.17), channel_id=1, source_target_pairs={{2,0},{3,1},{0,2},{1,3},{6,4},{7,5},{4,6},{5,7},{10,8},{11,9},{8,1... | collective-permute-start | bytes 98312 | tf_op jit(solution)/shard_map/ppermute | solution.py:29
  22.0 6.8 %copy-start.2 = (f32[256,64]{0,1:T(8,128)S(1)}, f32[256,64]{0,1:T(8,128)}, u32[]{:S(2)}) copy-start(f32[256,64]{0,1:T(8,128)} %param.8) | copy-start | bytes 196612
  22.1 6.7 %collective-permute-start.9 = (bf16[64,1024]{1,0:T(8,128)(2,1)S(1)}, bf16[64,1024]{1,0:T(8,128)(2,1)S(1)}, u32[]{:S(2)}, u32[]{:S(2)}) collective-permute-start(bf16[64,1024]{1,0:T(8,128)(2,1)S(1)} %collective-permute-done.refs_1_.refs_3_), channel_id=1, source_target_pairs={{28,0},{29,1},{6,2},{7,3},{0,4},{1,5},{10,6},{11,7},{4,8},{5,9},{1... | collective-permute-start | bytes 393224 | tf_op jit(solution)/shard_map/ppermute | solution.py:52
  22.1 6.7 %collective-permute-start.3 = (bf16[64,1024]{1,0:T(8,128)(2,1)S(1)}, bf16[64,1024]{1,0:T(8,128)(2,1)S(1)}, u32[]{:S(2)}, u32[]{:S(2)}) collective-permute-start(bf16[64,1024]{1,0:T(8,128)(2,1)S(1)} %collective-permute-done.refs_1_.refs_3_), channel_id=1, source_target_pairs={{1,0},{0,1},{3,2},{2,3},{5,4},{4,5},{7,6},{6,7},{9,8},{8,9},{11,10... | collective-permute-start | bytes 393224 | tf_op jit(solution)/shard_map/ppermute | solution.py:29
  22.4 6.4 %collective-permute-start.8 = (bf16[64,1024]{1,0:T(8,128)(2,1)S(1)}, bf16[64,1024]{1,0:T(8,128)(2,1)S(1)}, u32[]{:S(2)}, u32[]{:S(2)}) collective-permute-start(bf16[64,1024]{1,0:T(8,128)(2,1)S(1)} %collective-permute-done.7.refs_0_.refs_1_), channel_id=1, source_target_pairs={{28,0},{5,1},{30,2},{7,3},{0,4},{9,5},{2,6},{11,7},{4,8},{13,9},{6... | collective-permute-start | bytes 393224 | tf_op jit(solution)/shard_map/ppermute | solution.py:52
  23.7 5.0 %collective-permute-start.6 = (bf16[64,256]{1,0:T(8,128)(2,1)S(1)}, bf16[64,256]{1,0:T(8,128)(2,1)S(1)}, u32[]{:S(2)}, u32[]{:S(2)}) collective-permute-start(bf16[64,256]{1,0:T(8,128)(2,1)S(1)} %add.18), channel_id=1, source_target_pairs={{1,0},{0,1},{3,2},{2,3},{5,4},{4,5},{7,6},{6,7},{9,8},{8,9},{11,10... | collective-permute-start | bytes 98312 | tf_op jit(solution)/shard_map/ppermute | solution.py:29
  41.4 9.5 %collective-permute-start.10 = (bf16[64,1024]{1,0:T(8,128)(2,1)S(1)}, bf16[64,1024]{1,0:T(8,128)(2,1)S(1)}, u32[]{:S(2)}, u32[]{:S(2)}) collective-permute-start(bf16[64,1024]{1,0:T(8,128)(2,1)S(1)} %get-tuple-element.14.refs_2_), channel_id=1, source_target_pairs={{2,0},{3,1},{0,2},{1,3},{6,4},{7,5},{4,6},{5,7},{10,8},{11,9},{8,1... | collective-permute-start | bytes 393224 | tf_op jit(solution)/shard_map/ppermute | solution.py:29
  42.7 12.2 %collective-permute-start.14 = (bf16[64,1024]{1,0:T(8,128)(2,1)S(1)}, bf16[64,1024]{1,0:T(8,128)(2,1)S(1)}, u32[]{:S(2)}, u32[]{:S(2)}) collective-permute-start(bf16[64,1024]{1,0:T(8,128)(2,1)S(1)} %get-tuple-element.14.refs_2_), channel_id=1, source_target_pairs={{1,0},{0,1},{3,2},{2,3},{5,4},{4,5},{7,6},{6,7},{9,8},{8,9},{11,10... | collective-permute-start | bytes 393224 | tf_op jit(solution)/shard_map/ppermute | solution.py:29
  50.9 5.4 %collective-permute-start.11 = (bf16[64,1024]{1,0:T(8,128)(2,1)S(1)}, bf16[64,1024]{1,0:T(8,128)(2,1)S(1)}, u32[]{:S(2)}, u32[]{:S(2)}) collective-permute-start(bf16[64,1024]{1,0:T(8,128)(2,1)S(1)} %collective-permute-done.10.refs_4_), channel_id=1, source_target_pairs={{1,0},{0,1},{3,2},{2,3},{5,4},{4,5},{7,6},{6,7},{9,8},{8,9},{11,10... | collective-permute-start | bytes 393224 | tf_op jit(solution)/shard_map/ppermute | solution.py:29
  50.9 12.2 %collective-permute-start.12 = (bf16[64,1024]{1,0:T(8,128)(2,1)S(1)}, bf16[64,1024]{1,0:T(8,128)(2,1)S(1)}, u32[]{:S(2)}, u32[]{:S(2)}) collective-permute-start(bf16[64,1024]{1,0:T(8,128)(2,1)S(1)} %collective-permute-done.3.refs_4_.refs_1_), channel_id=1, source_target_pairs={{28,0},{29,1},{6,2},{7,3},{0,4},{1,5},{10,6},{11,7},{4,8},{5,9},{1... | collective-permute-start | bytes 393224 | tf_op jit(solution)/shard_map/ppermute | solution.py:52
  53.3 7.2 %collective-permute-start.16 = (bf16[64,1024]{1,0:T(8,128)(2,1)S(1)}, bf16[64,1024]{1,0:T(8,128)(2,1)S(1)}, u32[]{:S(2)}, u32[]{:S(2)}) collective-permute-start(bf16[64,1024]{1,0:T(8,128)(2,1)S(1)} %collective-permute-done.10.refs_4_), channel_id=1, source_target_pairs={{28,0},{29,1},{6,2},{7,3},{0,4},{1,5},{10,6},{11,7},{4,8},{5,9},{1... | collective-permute-start | bytes 393224 | tf_op jit(solution)/shard_map/ppermute | solution.py:52
  54.9 5.6 %collective-permute-start.15 = (bf16[64,1024]{1,0:T(8,128)(2,1)S(1)}, bf16[64,1024]{1,0:T(8,128)(2,1)S(1)}, u32[]{:S(2)}, u32[]{:S(2)}) collective-permute-start(bf16[64,1024]{1,0:T(8,128)(2,1)S(1)} %collective-permute-done.14.refs_2_), channel_id=1, source_target_pairs={{28,0},{5,1},{30,2},{7,3},{0,4},{9,5},{2,6},{11,7},{4,8},{13,9},{6... | collective-permute-start | bytes 393224 | tf_op jit(solution)/shard_map/ppermute | solution.py:52
  56.4 6.8 %collective-permute-start.13 = (bf16[64,1024]{1,0:T(8,128)(2,1)S(1)}, bf16[64,1024]{1,0:T(8,128)(2,1)S(1)}, u32[]{:S(2)}, u32[]{:S(2)}) collective-permute-start(bf16[64,1024]{1,0:T(8,128)(2,1)S(1)} %collective-permute-done.11.refs_2_), channel_id=1, source_target_pairs={{28,0},{29,1},{6,2},{7,3},{0,4},{1,5},{10,6},{11,7},{4,8},{5,9},{1... | collective-permute-start | bytes 393224 | tf_op jit(solution)/shard_map/ppermute | solution.py:52

commit v8 on v7

--- a/solution.py
+++ b/solution.py
@@ -52,7 +52,18 @@
     return lax.ppermute(piece, ("gx", "gy"), pairs)
 
 
-def neighbours(value, steps=()):
+def tied(value, *tokens):
+    return pl.pallas_call(
+        lambda *refs: None,
+        out_shape=jax.ShapeDtypeStruct(value.shape, value.dtype),
+        in_specs=[pl.BlockSpec(memory_space=pl.ANY)] * (1 + len(tokens)),
+        out_specs=pl.BlockSpec(memory_space=pl.ANY),
+        input_output_aliases={0: 0},
+        name="tied",
+    )(value, *tokens)
+
+
+def neighbours(value, steps=(), between=()):
     if lax.axis_size("gy") != BAND + 1:
         return [shifted(value, ("gx", "gy"), k) for k in range(-BAND, BAND + 1) if k != 0]
 
@@ -61,6 +72,8 @@
 
     two = swapped(value, "gy", 2)
     one = swapped(at(value, 0), "gy", 1)
+    if between:
+        two = tied(two, *between)
     three = swapped(at(two, 1), "gy", 1)
     cross_one = cross(at(one, 2), 1)
     cross_two = cross(at(two, 3), 2)
@@ -129,59 +142,111 @@
     return jnp.broadcast_to(strip[i:i + 1, :], strip.shape)
 
 
-def small_inverse(strip, start):
-    columns = [column(strip, start + k) for k in range(STRIP)]
+def total_of(terms):
+    while len(terms) > 1:
+        terms = [terms[i] + terms[i + 1] if i + 1 < len(terms) else terms[i] for i in range(0, len(terms), 2)]
+    return terms[0]
+
+
+def four_pivots(a):
+    rows = len(a)
+    x = [[None] * 4 for _ in range(4)]
+    scale = [None] * 4
+    product_so_far = None
+    for k in range(4):
+        pivot = a[k][k]
+        x[k][k] = product_so_far
+        product_so_far = pivot if k == 0 else product_so_far * pivot
+        scale[k] = lax.rsqrt(product_so_far)
+        for i in range(k + 1, rows):
+            for j in range(k + 1, min(i, 3) + 1):
+                a[i][j] = pivot * a[i][j] - a[i][k] * a[j][k]
+        for i in range(k + 1, 4):
+            for j in range(k):
+                x[i][j] = pivot * x[i][j] - a[i][k] * x[k][j]
+            x[i][k] = -a[i][k] if k == 0 else -a[i][k] * x[k][k]
+        yield
+    factor = [[a[i][k] * scale[k] for k in range(4)] for i in range(4, rows)]
+    inverse = [[scale[i] if x[i][j] is None else x[i][j] * scale[i] for j in range(i + 1)] for i in range(4)]
+    return factor, inverse
+
+
+def small_inverse(columns):
     a = [[row(columns[k], i) for k in range(i + 1)] for i in range(STRIP)]
-    scale = [None] * STRIP
-    for k in range(STRIP):
-        scale[k] = lax.rsqrt(a[k][k])
-        for i in range(k + 1, STRIP):
-            a[i][k] = a[i][k] * scale[k]
-        for i in range(k + 1, STRIP):
-            for j in range(k + 1, i + 1):
-                a[i][j] = a[i][j] - a[i][k] * a[j][k]
-    t = [[None] * STRIP for _ in range(STRIP)]
-    for j in range(STRIP):
-        t[j][j] = scale[j]
-        for i in range(j + 1, STRIP):
-            total = a[i][j] * t[j][j]
-            for q in range(j + 1, i):
-                total = total + a[i][q] * t[q][j]
-            t[i][j] = -scale[i] * total
-    return t
+    yield
+    below, one = yield from four_pivots([list(entries) for entries in a])
+    rest = [
+        [a[4 + i][4 + j] - total_of([below[i][k] * below[j][k] for k in range(4)]) for j in range(i + 1)]
+        for i in range(4)
+    ]
+    back = [[total_of([below[i][k] * one[k][j] for k in range(j, 4)]) for j in range(4)] for i in range(4)]
+    _, two = yield from four_pivots(rest)
+    corner = [[-total_of([two[i][m] * back[m][j] for m in range(i + 1)]) for j in range(4)] for i in range(4)]
+    return one + [corner[i] + two[i] for i in range(4)]
 
 
 def inverse_factor(strips):
     lane = lax.broadcasted_iota(jnp.int32, (STRIP, LANES), 1)
     level = lax.broadcasted_iota(jnp.int32, (STRIP, LANES), 0)
     strips = list(strips)
-    result = []
+    result = [None] * len(strips)
+    waiting = []
+
+    def factor_columns(r, start, t):
+        columns = [column(strips[r], start + j) for j in range(STRIP)]
+        return [total_of([columns[j] * t[k][j] for j in range(k + 1)]) for k in range(STRIP)]
+
+    def finish(p, t, found):
+        start = p * STRIP
+        own = (lane >= start) & (lane < start + STRIP)
+        rows = []
+
+        def scaled():
+            entered = jnp.where(own, jnp.where(lane - start == level, 1.0, 0.0), strips[p])
+            terms = []
+            for k in range(STRIP):
+                t_column = t[STRIP - 1][k]
+                for i in range(STRIP - 2, k - 1, -1):
+                    t_column = jnp.where(level == i, t[i][k], t_column)
+                if k:
+                    t_column = jnp.where(level < k, 0.0, t_column)
+                terms.append(t_column * row(entered, k))
+            done = total_of(terms)
+            result[p] = jnp.where(lane < start + STRIP, done, 0.0)
+            rows.extend(row(done, k) for k in range(STRIP))
+
+        def updated(r):
+            l_columns = found if r == p + 1 else factor_columns(r, start, t)
+            update = total_of([l_columns[k] * rows[k] for k in range(STRIP)])
+            strips[r] = jnp.where(own, 0.0, strips[r]) - update
+
+        return [scaled] + [functools.partial(updated, r) for r in range(p + 1, len(strips))]
+
+    columns = [column(strips[0], k) for k in range(STRIP)]
     for p in range(len(strips)):
-        start = p * STRIP
-        t = small_inverse(strips[p], start)
-        own = (lane >= start) & (lane < start + STRIP)
-        entered = jnp.where(own, jnp.where(lane - start == level, 1.0, 0.0), strips[p])
-        done = None
-        for k in range(STRIP):
-            t_column = t[STRIP - 1][k]
-            for i in range(STRIP - 2, k - 1, -1):
-                t_column = jnp.where(level == i, t[i][k], t_column)
-            if k:
-                t_column = jnp.where(level < k, 0.0, t_column)
-            term = t_column * row(entered, k)
-            done = term if done is None else done + term
-        result.append(jnp.where(lane < start + STRIP, done, 0.0))
-        rows = [row(done, k) for k in range(STRIP)]
-        for r in range(p + 1, len(strips)):
-            columns = [column(strips[r], start + j) for j in range(STRIP)]
-            update = None
-            for k in range(STRIP):
-                l_column = columns[0] * t[k][0]
-                for j in range(1, k + 1):
-                    l_column = l_column + columns[j] * t[k][j]
-                term = l_column * rows[k]
-                update = term if update is None else update + term
-            strips[r] = jnp.where(own, 0.0, strips[r]) - update
+        steps = small_inverse(columns)
+        while True:
+            try:
+                next(steps)
+            except StopIteration as ended:
+                t = ended.value
+                break
+            for _ in range(2):
+                if waiting:
+                    waiting.pop(0)()
+        while waiting:
+            waiting.pop(0)()
+        found = None
+        if p + 1 < len(strips):
+            start = p * STRIP
+            found = factor_columns(p + 1, start, t)
+            columns = [
+                column(strips[p + 1], start + STRIP + j) - total_of([found[k] * row(found[k], j) for k in range(STRIP)])
+                for j in range(STRIP)
+            ]
+        waiting = finish(p, t, found)
+    while waiting:
+        waiting.pop(0)()
     return result
 
 
@@ -329,10 +394,10 @@
     near_points = neighbours(points, rounds)
 
     inverse, probes, sent = probes_of(pivot_points, points, coeffs.T, noise.T, near_points[:5])
-    near_probes = neighbours(sent)
     factor = factor_of(pivot_points, points, inverse)
+    total = band_sum(points, [(points, sent)])
+    near_probes = neighbours(sent, between=(total, factor))
     near = list(zip(near_points, near_probes))
-    total = band_sum(points, [(points, sent)])
     total = band_sum(points, near[:2], total)
     total = band_sum(points, near[2:4], total)
     kernel_probes = band_sum(points, near[4:], total, probes).T

time: 66.8 us -> 63.4 us (0.949); the launches traced: 66.4 us -> 62.3 us
  Pallas kernels: 26.6 us -> 22.5 us
  local copies, waits for them, and re-layouts: 0.01 us -> 2.38 us
  starting transfers between devices: 20.7 us -> 19.1 us
  waiting for transfers between devices: 17.6 us -> 16.7 us
    pallas_call x1, Pallas kernels: 12.6 us -> 8.53 us  [probes_of(): pl.pallas_call(probe_kernel, out_shape=(jax.ShapeDtypeStruct((size, size)...]
    unnamed x6 -> x14, local copies, waits for them, and re-layouts: 0.01 us -> 2.38 us
    ppermute x6, starting transfers between devices: 4.62 us -> 3.03 us  [cross(): return lax.ppermute(piece, ('gx', 'gy'), pairs)]
    ppermute x11, waiting for transfers between devices: 17.5 us -> 16.7 us  [swapped(): lax.ppermute(value, axis, [(i ^ bit, i) for i in range(lax.axis_size(axis...]
  transfers between devices with their start and end apart: 17 -> 17, of which waited for: 5 -> 6; matrix products, arithmetic and copies ran while one was open for 1% -> 1% of each run, Pallas kernels for 13% -> 14%
where the time goes in v8:
time: 63.4 us; the launch traced here: 62.3 us
  Pallas kernels  22.5 us (35%)
  starting transfers between devices  19.1 us (30%)
  waiting for transfers between devices  16.7 us (26%)
  local copies, waits for them, and re-layouts  2.38 us (4%)
  other arithmetic  0.81 us (1%)
  between operations  0.81 us (1%)
    ppermute x11, waiting for transfers between devices, swapped(): lax.ppermute(value, axis, [(i ^ bit, i) for i in range(lax.axis_size(axis...  16.7 us
    ppermute x11, starting transfers between devices, swapped(): lax.ppermute(value, axis, [(i ^ bit, i) for i in range(lax.axis_size(axis...  16.1 us
    pallas_call x4, Pallas kernels, band_sum(): pl.pallas_call(functools.partial(band_kernel, len(pieces), first, last),...  9.78 us
    pallas_call x1, Pallas kernels, probes_of(): pl.pallas_call(probe_kernel, out_shape=(jax.ShapeDtypeStruct((size, size)...  8.53 us
    ppermute x6, starting transfers between devices, cross(): return lax.ppermute(piece, ('gx', 'gy'), pairs)  3.03 us
    pallas_call x1, Pallas kernels, factor_of(): pl.pallas_call(factor_kernel, out_shape=jax.ShapeDtypeStruct((count, size...  2.39 us
    unnamed x14, local copies, waits for them, and re-layouts  2.38 us
    pallas_call x1, Pallas kernels, pick(): pl.pallas_call(pick_kernel, out_shape=jax.ShapeDtypeStruct((points_t.shap...  1.82 us
  transfers between devices with their start and end apart: 17, of which 6 were waited for; matrix products, arithmetic and copies ran while one was open for 1% of the time, Pallas kernels for 14%

profile of v8, /device:TPU:0, one launch (start us, length us, event | category | flops | bytes accessed | tf_op | source)
XLA Modules:
  0.0 62.3 jit_solution(14820646193461080369)
XLA Ops:
  0.6 1.8 %pick.1 = bf16[64,256]{1,0:T(8,128)(2,1)} custom-call(s32[2]{0:T(128)} %owner_ref.1, s32[2,128]{1,0:T(2,128)} %pivot_ref.1, bf16[64,1024]{1,0:T(8,128)(2,1)} %bitcast.4), custom_call_target="tpu_custom_call" | custom-call | tf_op jit(solution)/shard_map/pick/pallas_call | solution.py:128
  2.5 0.5 collective-permute-start.1
  2.9 3.7 %collective-permute-start = (bf16[64,1024]{1,0:T(8,128)(2,1)S(1)}, bf16[64,1024]{1,0:T(8,128)(2,1)S(1)}, u32[]{:S(2)}, u32[]{:S(2)}) collective-permute-start(bf16[64,1024]{1,0:T(8,128)(2,1)S(1)} %bitcast.5), channel_id=1, source_target_pairs={{2,0},{3,1},{0,2},{1,3},{6,4},{7,5},{4,6},{5,7},{10,8},{11,9},{8,1... | collective-permute-start | bytes 393224 | tf_op jit(solution)/shard_map/ppermute | solution.py:29
  6.6 0.8 %add.15 = bf16[64,256]{1,0:T(8,128)(2,1)S(1)} add(bf16[64,256]{1,0:T(8,128)(2,1)} %pick.1, bf16[64,256]{1,0:T(8,128)(2,1)S(1)} %collective-permute-done.1) | non-fusion elementwise | flops 16384 | bytes 98304 | tf_op jit(solution)/shard_map/add | solution.py:41
  7.3 1.6 %collective-permute-start.7 = (bf16[64,1024]{1,0:T(8,128)(2,1)S(1)}, bf16[64,1024]{1,0:T(8,128)(2,1)S(1)}, u32[]{:S(2)}, u32[]{:S(2)}) collective-permute-start(bf16[64,1024]{1,0:T(8,128)(2,1)S(1)} %bitcast.6), channel_id=1, source_target_pairs={{1,0},{0,1},{3,2},{2,3},{5,4},{4,5},{7,6},{6,7},{9,8},{8,9},{11,10... | collective-permute-start | bytes 393224 | tf_op jit(solution)/shard_map/ppermute | solution.py:29
  9.0 1.5 %collective-permute-start.2 = (bf16[64,256]{1,0:T(8,128)(2,1)S(1)}, bf16[64,256]{1,0:T(8,128)(2,1)S(1)}, u32[]{:S(2)}, u32[]{:S(2)}) collective-permute-start(bf16[64,256]{1,0:T(8,128)(2,1)S(1)} %add.15), channel_id=1, source_target_pairs={{8,0},{12,4},{0,8},{4,12},{24,16},{28,20},{16,24},{20,28},{9,1},{1... | collective-permute-start | bytes 98312 | tf_op jit(solution)/shard_map/ppermute | solution.py:29
  10.5 2.4 %collective-permute-done.2 = bf16[64,256]{1,0:T(8,128)(2,1)S(1)} collective-permute-done((bf16[64,256]{1,0:T(8,128)(2,1)S(1)}, bf16[64,256]{1,0:T(8,128)(2,1)S(1)}, u32[]{:S(2)}, u32[]{:S(2)}) %collective-permute-start.2) | collective-permute-done | bytes 32800 | tf_op jit(solution)/shard_map/ppermute | solution.py:29
  12.9 1.6 %collective-permute-start.4 = (bf16[64,256]{1,0:T(8,128)(2,1)S(1)}, bf16[64,256]{1,0:T(8,128)(2,1)S(1)}, u32[]{:S(2)}, u32[]{:S(2)}) collective-permute-start(bf16[64,256]{1,0:T(8,128)(2,1)S(1)} %add.16), channel_id=1, source_target_pairs={{16,0},{20,4},{24,8},{28,12},{0,16},{4,20},{8,24},{12,28},{17,1},{... | collective-permute-start | bytes 98312 | tf_op jit(solution)/shard_map/ppermute | solution.py:29
  14.5 2.4 %collective-permute-done.4 = bf16[64,256]{1,0:T(8,128)(2,1)S(1)} collective-permute-done((bf16[64,256]{1,0:T(8,128)(2,1)S(1)}, bf16[64,256]{1,0:T(8,128)(2,1)S(1)}, u32[]{:S(2)}, u32[]{:S(2)}) %collective-permute-start.4) | collective-permute-done | bytes 32800 | tf_op jit(solution)/shard_map/ppermute | solution.py:29
  16.9 1.4 %collective-permute-start.5 = (bf16[64,256]{1,0:T(8,128)(2,1)S(1)}, bf16[64,256]{1,0:T(8,128)(2,1)S(1)}, u32[]{:S(2)}, u32[]{:S(2)}) collective-permute-start(bf16[64,256]{1,0:T(8,128)(2,1)S(1)} %add.17), channel_id=1, source_target_pairs={{2,0},{3,1},{0,2},{1,3},{6,4},{7,5},{4,6},{5,7},{10,8},{11,9},{8,1... | collective-permute-start | bytes 98312 | tf_op jit(solution)/shard_map/ppermute | solution.py:29
  18.3 3.7 %collective-permute-done.5 = bf16[64,256]{1,0:T(8,128)(2,1)S(1)} collective-permute-done((bf16[64,256]{1,0:T(8,128)(2,1)S(1)}, bf16[64,256]{1,0:T(8,128)(2,1)S(1)}, u32[]{:S(2)}, u32[]{:S(2)}) %collective-permute-start.5) | collective-permute-done | bytes 32800 | tf_op jit(solution)/shard_map/ppermute | solution.py:29
  22.0 0.0 copy-start.6
  22.1 0.1 collective-permute-start.9
  22.1 0.3 collective-permute-start.3
  22.4 1.3 %collective-permute-start.8 = (bf16[64,1024]{1,0:T(8,128)(2,1)S(1)}, bf16[64,1024]{1,0:T(8,128)(2,1)S(1)}, u32[]{:S(2)}, u32[]{:S(2)}) collective-permute-start(bf16[64,1024]{1,0:T(8,128)(2,1)S(1)} %collective-permute-done.7.refs_0_.refs_1_), channel_id=1, source_target_pairs={{28,0},{5,1},{30,2},{7,3},{0,4},{9,5},{2,6},{11,7},{4,8},{13,9},{6... | collective-permute-start | bytes 393224 | tf_op jit(solution)/shard_map/ppermute | solution.py:52
  23.7 2.8 %collective-permute-start.6 = (bf16[64,256]{1,0:T(8,128)(2,1)S(1)}, bf16[64,256]{1,0:T(8,128)(2,1)S(1)}, u32[]{:S(2)}, u32[]{:S(2)}) collective-permute-start(bf16[64,256]{1,0:T(8,128)(2,1)S(1)} %add.18), channel_id=1, source_target_pairs={{1,0},{0,1},{3,2},{2,3},{5,4},{4,5},{7,6},{6,7},{9,8},{8,9},{11,10... | collective-permute-start | bytes 98312 | tf_op jit(solution)/shard_map/ppermute | solution.py:29
  26.5 2.3 %collective-permute-done.6 = bf16[64,256]{1,0:T(8,128)(2,1)S(1)} collective-permute-done((bf16[64,256]{1,0:T(8,128)(2,1)S(1)}, bf16[64,256]{1,0:T(8,128)(2,1)S(1)}, u32[]{:S(2)}, u32[]{:S(2)}) %collective-permute-start.6) | collective-permute-done | bytes 32800 | tf_op jit(solution)/shard_map/ppermute | solution.py:29
  28.8 8.5 %probes.1 = (f32[256,256]{1,0:T(8,128)S(1)}, f32[64,1024]{1,0:T(8,128)S(1)}, bf16[64,1024]{1,0:T(8,128)(2,1)S(1)}) custom-call(bf16[64,256]{1,0:T(8,128)(2,1)S(1)} %add.19.pivot_ref, bf16[64,1024]{1,0:T(8,128)(2,1)S(1)} %bitcast.7, f32[64,256]{1,0:T(8,128)S(1)} %bitcast.15, f32[64,1024]{1,0:T(8,128)S(1)} %bitcast.14, ...), custom_call_target="tpu_custom_call" | custom-call | tf_op jit(solution)/shard_map/probes/pallas_call | solution.py:300
  37.4 1.2 %collective-permute-start.10 = (bf16[64,1024]{1,0:T(8,128)(2,1)S(1)}, bf16[64,1024]{1,0:T(8,128)(2,1)S(1)}, u32[]{:S(2)}, u32[]{:S(2)}) collective-permute-start(bf16[64,1024]{1,0:T(8,128)(2,1)S(1)} %get-tuple-element.14.refs_2_), channel_id=1, source_target_pairs={{2,0},{3,1},{0,2},{1,3},{6,4},{7,5},{4,6},{5,7},{10,8},{11,9},{8,1... | collective-permute-start | bytes 393224 | tf_op jit(solution)/shard_map/ppermute | solution.py:29
  38.6 1.5 %collective-permute-start.14 = (bf16[64,1024]{1,0:T(8,128)(2,1)S(1)}, bf16[64,1024]{1,0:T(8,128)(2,1)S(1)}, u32[]{:S(2)}, u32[]{:S(2)}) collective-permute-start(bf16[64,1024]{1,0:T(8,128)(2,1)S(1)} %get-tuple-element.14.refs_2_), channel_id=1, source_target_pairs={{1,0},{0,1},{3,2},{2,3},{5,4},{4,5},{7,6},{6,7},{9,8},{8,9},{11,10... | collective-permute-start | bytes 393224 | tf_op jit(solution)/shard_map/ppermute | solution.py:29
  40.1 2.4 %factor.1.refs_2_ = f32[1024,256]{1,0:T(8,128)} custom-call(bf16[64,256]{1,0:T(8,128)(2,1)S(1)} %add.19.pivot_ref, bf16[64,1024]{1,0:T(8,128)(2,1)S(1)} %bitcast.8, f32[256,256]{1,0:T(8,128)S(1)} %get-tuple-element.15.inverse_ref), custom_call_target="tpu_custom_call" | custom-call | flops 805306368 | bytes 1048576 | tf_op jit(solution)/shard_map/factor/pallas_call | solution.py:325
  42.5 1.4 %band_sum.4.refs_1_.refs_5_ = f32[1024,64]{1,0:T(8,128)S(1)} custom-call(bf16[64,1024]{1,0:T(8,128)(2,1)S(1)} %bitcast.9, bf16[64,1024]{1,0:T(8,128)(2,1)S(1)} %bitcast.10, bf16[64,1024]{1,0:T(8,128)(2,1)S(1)} %get-tuple-element.14.refs_2_), custom_call_target="tpu_custom_call" | custom-call | flops 536870912 | bytes 786432 | tf_op jit(solution)/shard_map/band_sum/pallas_call | solution.py:375
  44.0 0.8 %copy-done = f32[1024,64]{1,0:T(8,128)} copy-done((f32[1024,64]{1,0:T(8,128)}, f32[1024,64]{1,0:T(8,128)S(1)}, u32[]{:S(2)}) %copy-start) | copy-done | bytes 262168
  44.8 2.1 %collective-permute-done.10.refs_0_ = bf16[64,1024]{1,0:T(8,128)(2,1)S(1)} collective-permute-done((bf16[64,1024]{1,0:T(8,128)(2,1)S(1)}, bf16[64,1024]{1,0:T(8,128)(2,1)S(1)}, u32[]{:S(2)}, u32[]{:S(2)}) %collective-permute-start.10) | collective-permute-done | bytes 131104 | tf_op jit(solution)/shard_map/ppermute | solution.py:29
  46.9 0.7 %copy-done.4 = bf16[64,1024]{1,0:T(8,128)(2,1)} copy-done((bf16[64,1024]{1,0:T(8,128)(2,1)}, bf16[64,1024]{1,0:T(8,128)(2,1)S(1)}, u32[]{:S(2)}) %copy-start.4) | copy-done | bytes 131096
  47.5 1.6 %collective-permute-start.15 = (bf16[64,1024]{1,0:T(8,128)(2,1)S(1)}, bf16[64,1024]{1,0:T(8,128)(2,1)S(1)}, u32[]{:S(2)}, u32[]{:S(2)}) collective-permute-start(bf16[64,1024]{1,0:T(8,128)(2,1)S(1)} %collective-permute-done.14.refs_2_), channel_id=1, source_target_pairs={{28,0},{5,1},{30,2},{7,3},{0,4},{9,5},{2,6},{11,7},{4,8},{13,9},{6... | collective-permute-start | bytes 393224 | tf_op jit(solution)/shard_map/ppermute | solution.py:52
  49.1 0.1 collective-permute-start.12
  49.2 3.8 %collective-permute-done.11.refs_2_ = bf16[64,1024]{1,0:T(8,128)(2,1)S(1)} collective-permute-done((bf16[64,1024]{1,0:T(8,128)(2,1)}, bf16[64,1024]{1,0:T(8,128)(2,1)S(1)}, u32[]{:S(2)}, u32[]{:S(2)}) %collective-permute-start.11) | collective-permute-done | bytes 131104 | tf_op jit(solution)/shard_map/ppermute | solution.py:29
  53.0 0.9 %copy-done.5 = bf16[64,1024]{1,0:T(8,128)(2,1)S(1)} copy-done((bf16[64,1024]{1,0:T(8,128)(2,1)S(1)}, bf16[64,1024]{1,0:T(8,128)(2,1)}, u32[]{:S(2)}) %copy-start.5) | copy-done | bytes 131096
  53.9 2.5 %band_sum.5.refs_5_ = f32[1024,64]{1,0:T(8,128)S(1)} custom-call(bf16[64,1024]{1,0:T(8,128)(2,1)S(1)} %bitcast.11, bf16[64,1024]{1,0:T(8,128)(2,1)S(1)} %collective-permute-done.7.refs_0_.refs_1_, bf16[64,1024]{1,0:T(8,128)(2,1)S(1)} %collective-permute-done.14.refs_2_, bf16[64,1024]{1,0:T(8,128)(2,1)S(1)} %collective-permute-done.refs_1_.refs_3_, ...), custom_call_target="tpu_custom_call" | custom-call | flops 1073741824 | bytes 1572864 | tf_op jit(solution)/shard_map/band_sum/pallas_call | solution.py:375
  56.5 2.5 %band_sum.6.refs_5_ = f32[1024,64]{1,0:T(8,128)S(1)} custom-call(bf16[64,1024]{1,0:T(8,128)(2,1)S(1)} %bitcast.12, bf16[64,1024]{1,0:T(8,128)(2,1)S(1)} %collective-permute-done.8.refs_2_.refs_1_, bf16[64,1024]{1,0:T(8,128)(2,1)S(1)} %collective-permute-done.15.refs_2_, bf16[64,1024]{1,0:T(8,128)(2,1)S(1)} %collective-permute-done.9.refs_3_, ...), custom_call_target="tpu_custom_call" | custom-call | flops 1073741824 | bytes 1572864 | tf_op jit(solution)/shard_map/band_sum/pallas_call | solution.py:375
  59.0 3.3 %band_sum.7 = f32[64,1024]{1,0:T(8,128)} custom-call(bf16[64,1024]{1,0:T(8,128)(2,1)S(1)} %bitcast.13, bf16[64,1024]{1,0:T(8,128)(2,1)S(1)} %collective-permute-done.3.refs_4_.refs_1_, bf16[64,1024]{1,0:T(8,128)(2,1)S(1)} %collective-permute-done.11.refs_2_, bf16[64,1024]{1,0:T(8,128)(2,1)S(1)} %collective-permute-done.12.refs_3_, ...), custom_call_target="tpu_custom_call" | custom-call | flops 1073741824 | bytes 1835008 | tf_op jit(solution)/shard_map/band_sum/pallas_call | solution.py:375
  (29 shorter events, 0.1 us)
Async XLA Ops:
  0.6 2.3 %copy-start.2 = (bf16[1024,64]{0,1:T(8,128)(2,1)S(1)}, bf16[1024,64]{0,1:T(8,128)(2,1)}, u32[]{:S(2)}) copy-start(bf16[1024,64]{0,1:T(8,128)(2,1)} %param.5) | copy-start | bytes 393220
  2.5 26.4 %copy-start.3 = (f32[1024,64]{0,1:T(8,128)S(1)}, f32[1024,64]{0,1:T(8,128)}, u32[]{:S(2)}) copy-start(f32[1024,64]{0,1:T(8,128)} %param.9) | copy-start | bytes 786436
  2.5 4.1 %collective-permute-start.1 = (bf16[64,256]{1,0:T(8,128)(2,1)}, bf16[64,256]{1,0:T(8,128)(2,1)S(1)}, u32[]{:S(2)}, u32[]{:S(2)}) collective-permute-start(bf16[64,256]{1,0:T(8,128)(2,1)} %pick.1), channel_id=1, source_target_pairs={{4,0},{0,4},{12,8},{8,12},{20,16},{16,20},{28,24},{24,28},{5,1},{1... | collective-permute-start | bytes 98312 | tf_op jit(solution)/shard_map/ppermute | solution.py:29
  2.9 19.1 %collective-permute-start = (bf16[64,1024]{1,0:T(8,128)(2,1)S(1)}, bf16[64,1024]{1,0:T(8,128)(2,1)S(1)}, u32[]{:S(2)}, u32[]{:S(2)}) collective-permute-start(bf16[64,1024]{1,0:T(8,128)(2,1)S(1)} %bitcast.5), channel_id=1, source_target_pairs={{2,0},{3,1},{0,2},{1,3},{6,4},{7,5},{4,6},{5,7},{10,8},{11,9},{8,1... | collective-permute-start | bytes 393224 | tf_op jit(solution)/shard_map/ppermute | solution.py:29
  7.3 15.1 %collective-permute-start.7 = (bf16[64,1024]{1,0:T(8,128)(2,1)S(1)}, bf16[64,1024]{1,0:T(8,128)(2,1)S(1)}, u32[]{:S(2)}, u32[]{:S(2)}) collective-permute-start(bf16[64,1024]{1,0:T(8,128)(2,1)S(1)} %bitcast.6), channel_id=1, source_target_pairs={{1,0},{0,1},{3,2},{2,3},{5,4},{4,5},{7,6},{6,7},{9,8},{8,9},{11,10... | collective-permute-start | bytes 393224 | tf_op jit(solution)/shard_map/ppermute | solution.py:29
  9.0 3.9 %collective-permute-start.2 = (bf16[64,256]{1,0:T(8,128)(2,1)S(1)}, bf16[64,256]{1,0:T(8,128)(2,1)S(1)}, u32[]{:S(2)}, u32[]{:S(2)}) collective-permute-start(bf16[64,256]{1,0:T(8,128)(2,1)S(1)} %add.15), channel_id=1, source_target_pairs={{8,0},{12,4},{0,8},{4,12},{24,16},{28,20},{16,24},{20,28},{9,1},{1... | collective-permute-start | bytes 98312 | tf_op jit(solution)/shard_map/ppermute | solution.py:29
  12.9 4.0 %collective-permute-start.4 = (bf16[64,256]{1,0:T(8,128)(2,1)S(1)}, bf16[64,256]{1,0:T(8,128)(2,1)S(1)}, u32[]{:S(2)}, u32[]{:S(2)}) collective-permute-start(bf16[64,256]{1,0:T(8,128)(2,1)S(1)} %add.16), channel_id=1, source_target_pairs={{16,0},{20,4},{24,8},{28,12},{0,16},{4,20},{8,24},{12,28},{17,1},{... | collective-permute-start | bytes 98312 | tf_op jit(solution)/shard_map/ppermute | solution.py:29
  16.9 5.1 %collective-permute-start.5 = (bf16[64,256]{1,0:T(8,128)(2,1)S(1)}, bf16[64,256]{1,0:T(8,128)(2,1)S(1)}, u32[]{:S(2)}, u32[]{:S(2)}) collective-permute-start(bf16[64,256]{1,0:T(8,128)(2,1)S(1)} %add.17), channel_id=1, source_target_pairs={{2,0},{3,1},{0,2},{1,3},{6,4},{7,5},{4,6},{5,7},{10,8},{11,9},{8,1... | collective-permute-start | bytes 98312 | tf_op jit(solution)/shard_map/ppermute | solution.py:29
  22.0 6.8 %copy-start.6 = (f32[256,64]{0,1:T(8,128)S(1)}, f32[256,64]{0,1:T(8,128)}, u32[]{:S(2)}) copy-start(f32[256,64]{0,1:T(8,128)} %param.8) | copy-start | bytes 196612
  22.1 6.7 %collective-permute-start.9 = (bf16[64,1024]{1,0:T(8,128)(2,1)S(1)}, bf16[64,1024]{1,0:T(8,128)(2,1)S(1)}, u32[]{:S(2)}, u32[]{:S(2)}) collective-permute-start(bf16[64,1024]{1,0:T(8,128)(2,1)S(1)} %collective-permute-done.refs_1_.refs_3_), channel_id=1, source_target_pairs={{28,0},{29,1},{6,2},{7,3},{0,4},{1,5},{10,6},{11,7},{4,8},{5,9},{1... | collective-permute-start | bytes 393224 | tf_op jit(solution)/shard_map/ppermute | solution.py:52
  22.1 6.7 %collective-permute-start.3 = (bf16[64,1024]{1,0:T(8,128)(2,1)S(1)}, bf16[64,1024]{1,0:T(8,128)(2,1)S(1)}, u32[]{:S(2)}, u32[]{:S(2)}) collective-permute-start(bf16[64,1024]{1,0:T(8,128)(2,1)S(1)} %collective-permute-done.refs_1_.refs_3_), channel_id=1, source_target_pairs={{1,0},{0,1},{3,2},{2,3},{5,4},{4,5},{7,6},{6,7},{9,8},{8,9},{11,10... | collective-permute-start | bytes 393224 | tf_op jit(solution)/shard_map/ppermute | solution.py:29
  22.4 6.4 %collective-permute-start.8 = (bf16[64,1024]{1,0:T(8,128)(2,1)S(1)}, bf16[64,1024]{1,0:T(8,128)(2,1)S(1)}, u32[]{:S(2)}, u32[]{:S(2)}) collective-permute-start(bf16[64,1024]{1,0:T(8,128)(2,1)S(1)} %collective-permute-done.7.refs_0_.refs_1_), channel_id=1, source_target_pairs={{28,0},{5,1},{30,2},{7,3},{0,4},{9,5},{2,6},{11,7},{4,8},{13,9},{6... | collective-permute-start | bytes 393224 | tf_op jit(solution)/shard_map/ppermute | solution.py:52
  23.7 5.0 %collective-permute-start.6 = (bf16[64,256]{1,0:T(8,128)(2,1)S(1)}, bf16[64,256]{1,0:T(8,128)(2,1)S(1)}, u32[]{:S(2)}, u32[]{:S(2)}) collective-permute-start(bf16[64,256]{1,0:T(8,128)(2,1)S(1)} %add.18), channel_id=1, source_target_pairs={{1,0},{0,1},{3,2},{2,3},{5,4},{4,5},{7,6},{6,7},{9,8},{8,9},{11,10... | collective-permute-start | bytes 98312 | tf_op jit(solution)/shard_map/ppermute | solution.py:29
  37.4 9.5 %collective-permute-start.10 = (bf16[64,1024]{1,0:T(8,128)(2,1)S(1)}, bf16[64,1024]{1,0:T(8,128)(2,1)S(1)}, u32[]{:S(2)}, u32[]{:S(2)}) collective-permute-start(bf16[64,1024]{1,0:T(8,128)(2,1)S(1)} %get-tuple-element.14.refs_2_), channel_id=1, source_target_pairs={{2,0},{3,1},{0,2},{1,3},{6,4},{7,5},{4,6},{5,7},{10,8},{11,9},{8,1... | collective-permute-start | bytes 393224 | tf_op jit(solution)/shard_map/ppermute | solution.py:29
  38.6 8.9 %collective-permute-start.14 = (bf16[64,1024]{1,0:T(8,128)(2,1)S(1)}, bf16[64,1024]{1,0:T(8,128)(2,1)S(1)}, u32[]{:S(2)}, u32[]{:S(2)}) collective-permute-start(bf16[64,1024]{1,0:T(8,128)(2,1)S(1)} %get-tuple-element.14.refs_2_), channel_id=1, source_target_pairs={{1,0},{0,1},{3,2},{2,3},{5,4},{4,5},{7,6},{6,7},{9,8},{8,9},{11,10... | collective-permute-start | bytes 393224 | tf_op jit(solution)/shard_map/ppermute | solution.py:29
  43.9 0.8 %copy-start = (f32[1024,64]{1,0:T(8,128)}, f32[1024,64]{1,0:T(8,128)S(1)}, u32[]{:S(2)}) copy-start(f32[1024,64]{1,0:T(8,128)S(1)} %band_sum.4.refs_1_.refs_5_) | copy-start | bytes 786436
  46.9 0.7 %copy-start.4 = (bf16[64,1024]{1,0:T(8,128)(2,1)}, bf16[64,1024]{1,0:T(8,128)(2,1)S(1)}, u32[]{:S(2)}) copy-start(bf16[64,1024]{1,0:T(8,128)(2,1)S(1)} %collective-permute-done.10.refs_0_) | copy-start | bytes 393220
  47.5 5.5 %copy-start.1 = (f32[1024,64]{1,0:T(8,128)S(1)}, f32[1024,64]{1,0:T(8,128)}, u32[]{:S(2)}) copy-start(f32[1024,64]{1,0:T(8,128)} %copy-done) | copy-start | bytes 786436
  47.5 5.5 %collective-permute-start.11 = (bf16[64,1024]{1,0:T(8,128)(2,1)}, bf16[64,1024]{1,0:T(8,128)(2,1)S(1)}, u32[]{:S(2)}, u32[]{:S(2)}) collective-permute-start(bf16[64,1024]{1,0:T(8,128)(2,1)} %tied.1.refs_4_), channel_id=1, source_target_pairs={{1,0},{0,1},{3,2},{2,3},{5,4},{4,5},{7,6},{6,7},{9,8},{8,9},{11,10... | collective-permute-start | bytes 393224 | tf_op jit(solution)/shard_map/ppermute | solution.py:29
  47.5 8.9 %collective-permute-start.16 = (bf16[64,1024]{1,0:T(8,128)(2,1)}, bf16[64,1024]{1,0:T(8,128)(2,1)S(1)}, u32[]{:S(2)}, u32[]{:S(2)}) collective-permute-start(bf16[64,1024]{1,0:T(8,128)(2,1)} %tied.1.refs_4_), channel_id=1, source_target_pairs={{28,0},{29,1},{6,2},{7,3},{0,4},{1,5},{10,6},{11,7},{4,8},{5,9},{1... | collective-permute-start | bytes 393224 | tf_op jit(solution)/shard_map/ppermute | solution.py:52
  47.5 8.9 %collective-permute-start.15 = (bf16[64,1024]{1,0:T(8,128)(2,1)S(1)}, bf16[64,1024]{1,0:T(8,128)(2,1)S(1)}, u32[]{:S(2)}, u32[]{:S(2)}) collective-permute-start(bf16[64,1024]{1,0:T(8,128)(2,1)S(1)} %collective-permute-done.14.refs_2_), channel_id=1, source_target_pairs={{28,0},{5,1},{30,2},{7,3},{0,4},{9,5},{2,6},{11,7},{4,8},{13,9},{6... | collective-permute-start | bytes 393224 | tf_op jit(solution)/shard_map/ppermute | solution.py:52
  49.1 9.9 %collective-permute-start.12 = (bf16[64,1024]{1,0:T(8,128)(2,1)S(1)}, bf16[64,1024]{1,0:T(8,128)(2,1)S(1)}, u32[]{:S(2)}, u32[]{:S(2)}) collective-permute-start(bf16[64,1024]{1,0:T(8,128)(2,1)S(1)} %collective-permute-done.3.refs_4_.refs_1_), channel_id=1, source_target_pairs={{28,0},{29,1},{6,2},{7,3},{0,4},{1,5},{10,6},{11,7},{4,8},{5,9},{1... | collective-permute-start | bytes 393224 | tf_op jit(solution)/shard_map/ppermute | solution.py:52
  53.0 6.0 %collective-permute-start.13 = (bf16[64,1024]{1,0:T(8,128)(2,1)S(1)}, bf16[64,1024]{1,0:T(8,128)(2,1)S(1)}, u32[]{:S(2)}, u32[]{:S(2)}) collective-permute-start(bf16[64,1024]{1,0:T(8,128)(2,1)S(1)} %collective-permute-done.11.refs_2_), channel_id=1, source_target_pairs={{28,0},{29,1},{6,2},{7,3},{0,4},{1,5},{10,6},{11,7},{4,8},{5,9},{1... | collective-permute-start | bytes 393224 | tf_op jit(solution)/shard_map/ppermute | solution.py:52
  53.0 0.9 %copy-start.5 = (bf16[64,1024]{1,0:T(8,128)(2,1)S(1)}, bf16[64,1024]{1,0:T(8,128)(2,1)}, u32[]{:S(2)}) copy-start(bf16[64,1024]{1,0:T(8,128)(2,1)} %tied.1.refs_4_) | copy-start | bytes 393220

commit v9 on v8

--- a/solution.py
+++ b/solution.py
@@ -1,4 +1,5 @@
 import functools
+import math
 
 import jax
 import jax.numpy as jnp
@@ -27,10 +28,6 @@
 
 def swapped(value, axis, bit):
     return lax.ppermute(value, axis, [(i ^ bit, i) for i in range(lax.axis_size(axis))])
-
-
-def after(value, *others):
-    return lax.optimization_barrier((value,) + others)[0]
 
 
 def spread(value):
@@ -53,31 +50,18 @@
 
 
 def tied(value, *tokens):
-    return pl.pallas_call(
-        lambda *refs: None,
-        out_shape=jax.ShapeDtypeStruct(value.shape, value.dtype),
-        in_specs=[pl.BlockSpec(memory_space=pl.ANY)] * (1 + len(tokens)),
-        out_specs=pl.BlockSpec(memory_space=pl.ANY),
-        input_output_aliases={0: 0},
-        name="tied",
-    )(value, *tokens)
-
-
-def neighbours(value, steps=(), between=()):
-    if lax.axis_size("gy") != BAND + 1:
-        return [shifted(value, ("gx", "gy"), k) for k in range(-BAND, BAND + 1) if k != 0]
-
-    def at(piece, step):
-        return after(piece, steps[min(step, len(steps) - 1)]) if steps else piece
-
+    for token in tokens:
+        value = jnp.where(token[0, 0] == jnp.inf, jnp.zeros_like(value), value)
+    return value
+
+
+def column_blocks(value):
     two = swapped(value, "gy", 2)
-    one = swapped(at(value, 0), "gy", 1)
-    if between:
-        two = tied(two, *between)
-    three = swapped(at(two, 1), "gy", 1)
-    cross_one = cross(at(one, 2), 1)
-    cross_two = cross(at(two, 3), 2)
-    return [one, two, cross_one, cross_two, three, cross(at(three, 4), 3)]
+    return swapped(value, "gy", 1), two, swapped(two, "gy", 1)
+
+
+def direct_blocks(value):
+    return [shifted(value, ("gx", "gy"), k) for k in range(-BAND, BAND + 1) if k != 0]
 
 
 def in_vmem(count):
@@ -111,7 +95,7 @@
 
 
 def kernel_of(product_of_extended):
-    return jnp.exp(product_of_extended * (2.0 / KERNEL_SCALE))
+    return jnp.exp2(product_of_extended * (2.0 / KERNEL_SCALE * math.log2(math.e)))
 
 
 def pick_kernel(owner_ref, pivot_ref, point_ref, out_ref):
@@ -127,7 +111,7 @@
 def pick(owners, pivots, points_t):
     return pl.pallas_call(
         pick_kernel,
-        out_shape=jax.ShapeDtypeStruct((points_t.shape[0], 2 * PIVOTS), jnp.bfloat16),
+        out_shape=pltpu.VMEM((points_t.shape[0], 2 * PIVOTS), jnp.bfloat16),
         in_specs=[pl.BlockSpec(memory_space=pltpu.SMEM)] + in_vmem(2),
         out_specs=in_vmem(1)[0],
         name="pick",
@@ -302,7 +286,7 @@
         out_shape=(
             jax.ShapeDtypeStruct((size, size), jnp.float32),
             jax.ShapeDtypeStruct(noise_t.shape, jnp.float32),
-            jax.ShapeDtypeStruct(noise_t.shape, jnp.bfloat16),
+            pltpu.VMEM(noise_t.shape, jnp.bfloat16),
         ),
         in_specs=in_vmem(4) + [pl.BlockSpec(memory_space=pl.ANY)] * len(awaited),
         out_specs=tuple(in_vmem(3)),
@@ -333,47 +317,46 @@
     )(pivots_t, points_t, inverse)
 
 
-def band_kernel(pieces, first, last, *refs):
-    own_ref = refs[0]
-    piece_refs = refs[1:1 + 2 * pieces]
-    at = 1 + 2 * pieces
-    total_ref = out_ref = refs[-1]
+def band_kernel(parts, first, last, *refs):
+    refs = list(refs)
+    out_ref = refs.pop()
+    own_ref = refs.pop(0)
     count = own_ref.shape[1]
-    before_ref = None
-    if not first:
-        before_ref = refs[at]
-        at += 1
-    if last:
-        probe_ref = refs[at]
-    own = extended(own_ref[...], True)
-    own = jnp.concatenate([own, jnp.zeros((LANES - own.shape[0], count), jnp.float32)], axis=0)
-    own = jnp.transpose(own).astype(jnp.bfloat16)
-    others = []
-    for i in range(pieces):
-        other = extended(piece_refs[2 * i][...], False)
-        other = jnp.concatenate([other, jnp.zeros((LANES - other.shape[0], count), jnp.float32)], axis=0)
-        others.append(other.astype(jnp.bfloat16))
+    pieces = []
+    for part in parts:
+        if part == 2:
+            pieces.append((refs.pop(0)[...], refs.pop(0)[...]))
+        else:
+            stacked = refs.pop(0)
+            pieces.append((stacked[:own_ref.shape[0], :], stacked[own_ref.shape[0]:, :]))
+    before_ref = None if first else refs.pop(0)
+
+    def padded(value):
+        return jnp.concatenate([value, jnp.zeros((LANES - value.shape[0], count), jnp.float32)], axis=0)
+
+    own = jnp.transpose(padded(extended(own_ref[...], True))).astype(jnp.bfloat16)
+    others = [padded(extended(block, False)).astype(jnp.bfloat16) for block, _ in pieces]
     for s in range(0, count, CHUNK):
         total = None if first else before_ref[s:s + CHUNK, :]
-        for i in range(pieces):
-            tile = kernel_of(product(own[s:s + CHUNK, :], others[i], ((1,), (0,)))).astype(jnp.bfloat16)
-            term = product(tile, piece_refs[2 * i + 1][...], ((1,), (1,)))
+        for other, (_, probes) in zip(others, pieces):
+            tile = kernel_of(product(own[s:s + CHUNK, :], other, ((1,), (0,)))).astype(jnp.bfloat16)
+            term = product(tile, probes, ((1,), (1,)))
             total = term if total is None else total + term
         if last:
             scale = 1.0 / (count ** 0.5)
-            out_ref[:, s:s + CHUNK] = jnp.transpose(total) * scale + noise_weight * probe_ref[:, s:s + CHUNK]
+            out_ref[:, s:s + CHUNK] = jnp.transpose(total) * scale + noise_weight * refs[0][:, s:s + CHUNK]
         else:
-            total_ref[s:s + CHUNK, :] = total
+            out_ref[s:s + CHUNK, :] = total
 
 
 def band_sum(own, pieces, before=None, probes=None):
     depth, count = own.shape
-    width = pieces[0][1].shape[0]
+    width = pieces[0][1].shape[0] if len(pieces[0]) == 2 else pieces[0][0].shape[0] - depth
     first, last = before is None, probes is not None
     operands = [own] + [array for piece in pieces for array in piece]
     operands += ([] if first else [before]) + ([probes] if last else [])
     return pl.pallas_call(
-        functools.partial(band_kernel, len(pieces), first, last),
+        functools.partial(band_kernel, tuple(len(piece) for piece in pieces), first, last),
         out_shape=jax.ShapeDtypeStruct((width, count) if last else (count, width), jnp.float32),
         in_specs=in_vmem(len(operands)),
         out_specs=in_vmem(1)[0],
@@ -388,20 +371,28 @@
 
 
 def shards(points, pivots, owners, coeffs, noise):
+    tall = lax.axis_size("gy") == BAND + 1
     points = points.T
-    rounds = spread(pick(owners, pivots, points))
-    pivot_points = rounds[-1]
-    near_points = neighbours(points, rounds)
-
-    inverse, probes, sent = probes_of(pivot_points, points, coeffs.T, noise.T, near_points[:5])
+    pivot_points = spread(pick(owners, pivots, points))[-1]
+    near = column_blocks(points) if tall else direct_blocks(points)
+
+    inverse, probes, sent = probes_of(pivot_points, points, coeffs.T, noise.T, near)
     factor = factor_of(pivot_points, points, inverse)
     total = band_sum(points, [(points, sent)])
-    near_probes = neighbours(sent, between=(total, factor))
-    near = list(zip(near_points, near_probes))
-    total = band_sum(points, near[:2], total)
-    total = band_sum(points, near[2:4], total)
-    kernel_probes = band_sum(points, near[4:], total, probes).T
-    return (kernel_probes, factor)
+    if tall:
+        two = tied(swapped(sent, "gy", 2), total, factor)
+        one = tied(swapped(sent, "gy", 1), total, factor)
+        three = swapped(two, "gy", 1)
+        crossed = [cross(jnp.concatenate([near[i], probe], axis=0), i + 1) for i, probe in enumerate((one, two))]
+        total = band_sum(points, [(near[0], one), (near[1], two)], total)
+        crossed.append(cross(jnp.concatenate([near[2], tied(three, total)], axis=0), 3))
+        total = band_sum(points, [(crossed[0],), (crossed[1],), (near[2], three)], total)
+        kernel_probes = band_sum(points, [(crossed[2],)], total, probes)
+    else:
+        pieces = list(zip(near, direct_blocks(sent)))
+        total = band_sum(points, pieces[:3], total)
+        kernel_probes = band_sum(points, pieces[3:], total, probes)
+    return (kernel_probes.T, factor)
 
 
 def solution(mesh):

time: 63.4 us -> 59.8 us (0.943); the launches traced: 62.3 us -> 59.6 us
  waiting for transfers between devices: 16.7 us -> 12.1 us
  between operations: 0.81 us -> 2.83 us
  starting transfers between devices: 19.1 us -> 20.4 us
  Pallas kernels: 22.5 us -> 21.7 us
  other arithmetic: 0.81 us -> 0.16 us
    ppermute x11, waiting for transfers between devices: 16.7 us -> 10.2 us  [swapped(): lax.ppermute(value, axis, [(i ^ bit, i) for i in range(lax.axis_size(axis...]
    ppermute x11, starting transfers between devices: 16.1 us -> 18.5 us  [swapped(): lax.ppermute(value, axis, [(i ^ bit, i) for i in range(lax.axis_size(axis...]
    unnamed x14 -> x6, local copies, waits for them, and re-layouts: 2.38 us -> 0.02 us
    slice x0 -> x3, local copies, waits for them, and re-layouts: none -> 2.31 us  [tied(): value = jnp.where(token[0, 0] == jnp.inf, jnp.zeros_like(value), value)]
    ppermute x6 -> x3, waiting for transfers between devices: 0.02 us -> 1.95 us  [cross(): return lax.ppermute(piece, ('gx', 'gy'), pairs)]
    ppermute x6 -> x3, starting transfers between devices: 3.03 us -> 1.95 us  [cross(): return lax.ppermute(piece, ('gx', 'gy'), pairs)]
    pallas_call x6 -> x5, Pallas kernels: 11.6 us -> 10.8 us  [the longest x4 9.65 us: band_sum(): pl.pallas_call(functools.partial(band_kernel, tuple((len(piece) for piece...]
    add x5, other arithmetic: 0.81 us -> 0.06 us  [spread(): sums.append(sums[-1] + swapped(sums[-1], axis, bit))]
  transfers between devices with their start and end apart: 17 -> 14, of which waited for: 6 -> 6; matrix products, arithmetic and copies ran while one was open for 1% -> 4% of each run, Pallas kernels for 14% -> 19%
where the time goes in v9:
time: 59.8 us; the launch traced here: 59.6 us
  Pallas kernels  21.7 us (36%)
  starting transfers between devices  20.4 us (34%)
  waiting for transfers between devices  12.1 us (20%)
  between operations  2.83 us (5%)
  local copies, waits for them, and re-layouts  2.32 us (4%)
    ppermute x11, starting transfers between devices, swapped(): lax.ppermute(value, axis, [(i ^ bit, i) for i in range(lax.axis_size(axis...  18.5 us
    ppermute x11, waiting for transfers between devices, swapped(): lax.ppermute(value, axis, [(i ^ bit, i) for i in range(lax.axis_size(axis...  10.2 us
    pallas_call x4, Pallas kernels, band_sum(): pl.pallas_call(functools.partial(band_kernel, tuple((len(piece) for piece...  9.65 us
    pallas_call x1, Pallas kernels, probes_of(): pl.pallas_call(probe_kernel, out_shape=(jax.ShapeDtypeStruct((size, size)...  8.51 us
    pallas_call x1, Pallas kernels, factor_of(): pl.pallas_call(factor_kernel, out_shape=jax.ShapeDtypeStruct((count, size...  2.38 us
    slice x3, local copies, waits for them, and re-layouts, tied(): value = jnp.where(token[0, 0] == jnp.inf, jnp.zeros_like(value), value)  2.31 us
    ppermute x3, starting transfers between devices, cross(): return lax.ppermute(piece, ('gx', 'gy'), pairs)  1.95 us
    ppermute x3, waiting for transfers between devices, cross(): return lax.ppermute(piece, ('gx', 'gy'), pairs)  1.95 us
  transfers between devices with their start and end apart: 14, of which 6 were waited for; matrix products, arithmetic and copies ran while one was open for 4% of the time, Pallas kernels for 19%

profile of v9, /device:TPU:0, one launch (start us, length us, event | category | flops | bytes accessed | tf_op | source)
XLA Modules:
  0.0 59.6 jit_solution(103052328775203890)
XLA Ops:
  0.6 4.1 %collective-permute-start = (bf16[64,1024]{1,0:T(8,128)(2,1)}, bf16[64,1024]{1,0:T(8,128)(2,1)S(1)}, u32[]{:S(2)}, u32[]{:S(2)}) collective-permute-start(bf16[64,1024]{1,0:T(8,128)(2,1)} %bitcast.7), channel_id=1, source_target_pairs={{2,0},{3,1},{0,2},{1,3},{6,4},{7,5},{4,6},{5,7},{10,8},{11,9},{8,1... | collective-permute-start | bytes 393224 | tf_op jit(solution)/shard_map/ppermute | solution.py:30
  4.7 1.2 %pick.1 = bf16[64,256]{1,0:T(8,128)(2,1)S(1)} custom-call(s32[2]{0:T(128)} %owner_ref.1, s32[2,128]{1,0:T(2,128)} %pivot_ref.1, bf16[64,1024]{1,0:T(8,128)(2,1)} %bitcast.8), custom_call_target="tpu_custom_call" | custom-call | tf_op jit(solution)/shard_map/pick/pallas_call | solution.py:112
  5.9 0.0 copy-start.1
  5.9 0.1 collective-permute-start.3
  6.0 1.2 %collective-permute-done.3 = bf16[64,256]{1,0:T(8,128)(2,1)S(1)} collective-permute-done((bf16[64,256]{1,0:T(8,128)(2,1)S(1)}, bf16[64,256]{1,0:T(8,128)(2,1)S(1)}, u32[]{:S(2)}, u32[]{:S(2)}) %collective-permute-start.3) | collective-permute-done | bytes 32800 | tf_op jit(solution)/shard_map/ppermute | solution.py:30
  7.2 1.6 %collective-permute-start.4 = (bf16[64,256]{1,0:T(8,128)(2,1)S(1)}, bf16[64,256]{1,0:T(8,128)(2,1)S(1)}, u32[]{:S(2)}, u32[]{:S(2)}) collective-permute-start(bf16[64,256]{1,0:T(8,128)(2,1)S(1)} %add.15), channel_id=1, source_target_pairs={{8,0},{12,4},{0,8},{4,12},{24,16},{28,20},{16,24},{20,28},{9,1},{1... | collective-permute-start | bytes 98312 | tf_op jit(solution)/shard_map/ppermute | solution.py:30
  8.8 1.6 %collective-permute-start.2 = (bf16[64,1024]{1,0:T(8,128)(2,1)S(1)}, bf16[64,1024]{1,0:T(8,128)(2,1)S(1)}, u32[]{:S(2)}, u32[]{:S(2)}) collective-permute-start(bf16[64,1024]{1,0:T(8,128)(2,1)S(1)} %bitcast.9), channel_id=1, source_target_pairs={{1,0},{0,1},{3,2},{2,3},{5,4},{4,5},{7,6},{6,7},{9,8},{8,9},{11,10... | collective-permute-start | bytes 393224 | tf_op jit(solution)/shard_map/ppermute | solution.py:30
  10.4 0.9 %collective-permute-done.refs_1_.refs_3_ = bf16[64,1024]{1,0:T(8,128)(2,1)S(1)} collective-permute-done((bf16[64,1024]{1,0:T(8,128)(2,1)}, bf16[64,1024]{1,0:T(8,128)(2,1)S(1)}, u32[]{:S(2)}, u32[]{:S(2)}) %collective-permute-start) | collective-permute-done | bytes 131104 | tf_op jit(solution)/shard_map/ppermute | solution.py:30
  11.3 0.9 %collective-permute-start.1 = (bf16[64,1024]{1,0:T(8,128)(2,1)S(1)}, bf16[64,1024]{1,0:T(8,128)(2,1)S(1)}, u32[]{:S(2)}, u32[]{:S(2)}) collective-permute-start(bf16[64,1024]{1,0:T(8,128)(2,1)S(1)} %collective-permute-done.refs_1_.refs_3_), channel_id=1, source_target_pairs={{1,0},{0,1},{3,2},{2,3},{5,4},{4,5},{7,6},{6,7},{9,8},{8,9},{11,10... | collective-permute-start | bytes 393224 | tf_op jit(solution)/shard_map/ppermute | solution.py:30
  12.1 1.6 %collective-permute-start.5 = (bf16[64,256]{1,0:T(8,128)(2,1)S(1)}, bf16[64,256]{1,0:T(8,128)(2,1)S(1)}, u32[]{:S(2)}, u32[]{:S(2)}) collective-permute-start(bf16[64,256]{1,0:T(8,128)(2,1)S(1)} %add.16), channel_id=1, source_target_pairs={{16,0},{20,4},{24,8},{28,12},{0,16},{4,20},{8,24},{12,28},{17,1},{... | collective-permute-start | bytes 98312 | tf_op jit(solution)/shard_map/ppermute | solution.py:30
  13.7 2.4 %collective-permute-done.5 = bf16[64,256]{1,0:T(8,128)(2,1)S(1)} collective-permute-done((bf16[64,256]{1,0:T(8,128)(2,1)S(1)}, bf16[64,256]{1,0:T(8,128)(2,1)S(1)}, u32[]{:S(2)}, u32[]{:S(2)}) %collective-permute-start.5) | collective-permute-done | bytes 32800 | tf_op jit(solution)/shard_map/ppermute | solution.py:30
  16.1 3.4 %collective-permute-start.6 = (bf16[64,256]{1,0:T(8,128)(2,1)S(1)}, bf16[64,256]{1,0:T(8,128)(2,1)S(1)}, u32[]{:S(2)}, u32[]{:S(2)}) collective-permute-start(bf16[64,256]{1,0:T(8,128)(2,1)S(1)} %add.17), channel_id=1, source_target_pairs={{2,0},{3,1},{0,2},{1,3},{6,4},{7,5},{4,6},{5,7},{10,8},{11,9},{8,1... | collective-permute-start | bytes 98312 | tf_op jit(solution)/shard_map/ppermute | solution.py:30
  19.5 2.2 %collective-permute-done.6 = bf16[64,256]{1,0:T(8,128)(2,1)S(1)} collective-permute-done((bf16[64,256]{1,0:T(8,128)(2,1)S(1)}, bf16[64,256]{1,0:T(8,128)(2,1)S(1)}, u32[]{:S(2)}, u32[]{:S(2)}) %collective-permute-start.6) | collective-permute-done | bytes 32800 | tf_op jit(solution)/shard_map/ppermute | solution.py:30
  21.8 0.0 copy-start.2
  21.8 0.6 collective-permute-start.7
  22.4 3.4 %collective-permute-done.7 = bf16[64,256]{1,0:T(8,128)(2,1)S(1)} collective-permute-done((bf16[64,256]{1,0:T(8,128)(2,1)S(1)}, bf16[64,256]{1,0:T(8,128)(2,1)S(1)}, u32[]{:S(2)}, u32[]{:S(2)}) %collective-permute-start.7) | collective-permute-done | bytes 32800 | tf_op jit(solution)/shard_map/ppermute | solution.py:30
  25.9 8.5 %probes.1 = (f32[256,256]{1,0:T(8,128)S(1)}, f32[64,1024]{1,0:T(8,128)S(1)}, bf16[64,1024]{1,0:T(8,128)(2,1)S(1)}) custom-call(bf16[64,256]{1,0:T(8,128)(2,1)S(1)} %add.19.pivot_ref, bf16[64,1024]{1,0:T(8,128)(2,1)S(1)} %bitcast.10, f32[64,256]{1,0:T(8,128)S(1)} %bitcast.18, f32[64,1024]{1,0:T(8,128)S(1)} %bitcast.17, ...), custom_call_target="tpu_custom_call" | custom-call | tf_op jit(solution)/shard_map/probes/pallas_call | solution.py:284
  34.4 0.6 collective-permute-start.8
  34.9 2.2 %collective-permute-start.9 = (bf16[64,1024]{1,0:T(8,128)(2,1)S(1)}, bf16[64,1024]{1,0:T(8,128)(2,1)S(1)}, u32[]{:S(2)}, u32[]{:S(2)}) collective-permute-start(bf16[64,1024]{1,0:T(8,128)(2,1)S(1)} %get-tuple-element.6.refs_2_), channel_id=1, source_target_pairs={{2,0},{3,1},{0,2},{1,3},{6,4},{7,5},{4,6},{5,7},{10,8},{11,9},{8,1... | collective-permute-start | bytes 393224 | tf_op jit(solution)/shard_map/ppermute | solution.py:30
  37.1 2.4 %factor.1 = f32[1024,256]{1,0:T(8,128)} custom-call(bf16[64,256]{1,0:T(8,128)(2,1)S(1)} %add.19.pivot_ref, bf16[64,1024]{1,0:T(8,128)(2,1)S(1)} %bitcast.11, f32[256,256]{1,0:T(8,128)S(1)} %get-tuple-element.5.inverse_ref), custom_call_target="tpu_custom_call" | custom-call | flops 805306368 | bytes 1048576 | tf_op jit(solution)/shard_map/factor/pallas_call | solution.py:309
  39.5 1.3 %slice.14 = f32[1,1]{1,0:T(1,128)} slice(f32[1024,256]{1,0:T(8,128)} %factor.1), slice={[0:1], [0:1]} | slice | bytes 8 | tf_op jit(solution)/shard_map/slice | solution.py:54
  40.8 1.4 %band_sum.4.refs_5_ = f32[1024,64]{1,0:T(8,128)S(1)} custom-call(bf16[64,1024]{1,0:T(8,128)(2,1)S(1)} %bitcast.12, bf16[64,1024]{1,0:T(8,128)(2,1)S(1)} %bitcast.13, bf16[64,1024]{1,0:T(8,128)(2,1)S(1)} %get-tuple-element.6.refs_2_), custom_call_target="tpu_custom_call" | custom-call | flops 536870912 | bytes 786432 | tf_op jit(solution)/shard_map/band_sum/pallas_call | solution.py:358
  42.2 0.5 slice.15
  44.1 0.2 collective-permute-start.12
  44.4 2.0 %collective-permute-start.10 = (bf16[64,1024]{1,0:T(8,128)(2,1)S(1)}, bf16[64,1024]{1,0:T(8,128)(2,1)S(1)}, u32[]{:S(2)}, u32[]{:S(2)}) collective-permute-start(bf16[64,1024]{1,0:T(8,128)(2,1)S(1)} %select_select_fusion.refs_4_), channel_id=1, source_target_pairs={{1,0},{0,1},{3,2},{2,3},{5,4},{4,5},{7,6},{6,7},{9,8},{8,9},{11,10... | collective-permute-start | bytes 393224 | tf_op jit(solution)/shard_map/ppermute | solution.py:30
  46.4 0.3 collective-permute-start.13
  46.7 2.5 %band_sum.5.refs_5_ = f32[1024,64]{1,0:T(8,128)S(1)} custom-call(bf16[64,1024]{1,0:T(8,128)(2,1)S(1)} %bitcast.14, bf16[64,1024]{1,0:T(8,128)(2,1)S(1)} %collective-permute-done.2.refs_0_.refs_1_, bf16[64,1024]{1,0:T(8,128)(2,1)S(1)} %select_select_fusion.1.refs_2_, bf16[64,1024]{1,0:T(8,128)(2,1)S(1)} %collective-permute-done.refs_1_.refs_3_, ...), custom_call_target="tpu_custom_call" | custom-call | flops 1073741824 | bytes 1572864 | tf_op jit(solution)/shard_map/band_sum/pallas_call | solution.py:358
  49.2 0.5 slice.16
  50.4 1.5 %collective-permute-start.11 = (bf16[128,1024]{1,0:T(8,128)(2,1)S(1)}, bf16[128,1024]{1,0:T(8,128)(2,1)S(1)}, u32[]{:S(2)}, u32[]{:S(2)}) collective-permute-start(bf16[128,1024]{1,0:T(8,128)(2,1)S(1)} %pad_maximum_fusion), channel_id=1, source_target_pairs={{28,0},{29,1},{6,2},{7,3},{0,4},{1,5},{10,6},{11,7},{4,8},{5,9},{1... | collective-permute-start | bytes 786440 | tf_op jit(solution)/shard_map/ppermute | solution.py:49
  51.9 1.9 %collective-permute-done.13.refs_2_ = bf16[128,1024]{1,0:T(8,128)(2,1)S(1)} collective-permute-done((bf16[128,1024]{1,0:T(8,128)(2,1)S(1)}, bf16[128,1024]{1,0:T(8,128)(2,1)S(1)}, u32[]{:S(2)}, u32[]{:S(2)}) %collective-permute-start.13) | collective-permute-done | bytes 262176 | tf_op jit(solution)/shard_map/ppermute | solution.py:49
  53.8 3.6 %band_sum.6.refs_2_ = f32[1024,64]{1,0:T(8,128)S(1)} custom-call(bf16[64,1024]{1,0:T(8,128)(2,1)S(1)} %bitcast.15, bf16[128,1024]{1,0:T(8,128)(2,1)S(1)} %collective-permute-done.12.refs_1_, bf16[128,1024]{1,0:T(8,128)(2,1)S(1)} %collective-permute-done.13.refs_2_, bf16[64,1024]{1,0:T(8,128)(2,1)S(1)} %collective-permute-done.1.refs_2_.refs_3_, ...), custom_call_target="tpu_custom_call" | custom-call | flops 1610612736 | bytes 1572864 | tf_op jit(solution)/shard_map/band_sum/pallas_call | solution.py:358
  57.5 2.1 %band_sum.7 = f32[64,1024]{1,0:T(8,128)} custom-call(bf16[64,1024]{1,0:T(8,128)(2,1)S(1)} %bitcast.16, bf16[128,1024]{1,0:T(8,128)(2,1)S(1)} %collective-permute-done.11.refs_1_, f32[1024,64]{1,0:T(8,128)S(1)} %band_sum.6.refs_2_, f32[64,1024]{1,0:T(8,128)S(1)} %get-tuple-element.7.refs_3_), custom_call_target="tpu_custom_call" | custom-call | flops 536870912 | bytes 1048576 | tf_op jit(solution)/shard_map/band_sum/pallas_call | solution.py:358
  (23 shorter events, 0.2 us)
Async XLA Ops:
  0.6 8.1 %copy-start = (bf16[1024,64]{0,1:T(8,128)(2,1)S(1)}, bf16[1024,64]{0,1:T(8,128)(2,1)}, u32[]{:S(2)}) copy-start(bf16[1024,64]{0,1:T(8,128)(2,1)} %param.5) | copy-start | bytes 393220
  0.6 10.6 %collective-permute-start = (bf16[64,1024]{1,0:T(8,128)(2,1)}, bf16[64,1024]{1,0:T(8,128)(2,1)S(1)}, u32[]{:S(2)}, u32[]{:S(2)}) collective-permute-start(bf16[64,1024]{1,0:T(8,128)(2,1)} %bitcast.7), channel_id=1, source_target_pairs={{2,0},{3,1},{0,2},{1,3},{6,4},{7,5},{4,6},{5,7},{10,8},{11,9},{8,1... | collective-permute-start | bytes 393224 | tf_op jit(solution)/shard_map/ppermute | solution.py:30
  5.9 19.9 %copy-start.1 = (f32[1024,64]{0,1:T(8,128)S(1)}, f32[1024,64]{0,1:T(8,128)}, u32[]{:S(2)}) copy-start(f32[1024,64]{0,1:T(8,128)} %param.9) | copy-start | bytes 786436
  5.9 1.3 %collective-permute-start.3 = (bf16[64,256]{1,0:T(8,128)(2,1)S(1)}, bf16[64,256]{1,0:T(8,128)(2,1)S(1)}, u32[]{:S(2)}, u32[]{:S(2)}) collective-permute-start(bf16[64,256]{1,0:T(8,128)(2,1)S(1)} %pick.1), channel_id=1, source_target_pairs={{4,0},{0,4},{12,8},{8,12},{20,16},{16,20},{28,24},{24,28},{5,1},{1... | collective-permute-start | bytes 98312 | tf_op jit(solution)/shard_map/ppermute | solution.py:30
  7.2 4.9 %collective-permute-start.4 = (bf16[64,256]{1,0:T(8,128)(2,1)S(1)}, bf16[64,256]{1,0:T(8,128)(2,1)S(1)}, u32[]{:S(2)}, u32[]{:S(2)}) collective-permute-start(bf16[64,256]{1,0:T(8,128)(2,1)S(1)} %add.15), channel_id=1, source_target_pairs={{8,0},{12,4},{0,8},{4,12},{24,16},{28,20},{16,24},{20,28},{9,1},{1... | collective-permute-start | bytes 98312 | tf_op jit(solution)/shard_map/ppermute | solution.py:30
  8.8 17.0 %collective-permute-start.2 = (bf16[64,1024]{1,0:T(8,128)(2,1)S(1)}, bf16[64,1024]{1,0:T(8,128)(2,1)S(1)}, u32[]{:S(2)}, u32[]{:S(2)}) collective-permute-start(bf16[64,1024]{1,0:T(8,128)(2,1)S(1)} %bitcast.9), channel_id=1, source_target_pairs={{1,0},{0,1},{3,2},{2,3},{5,4},{4,5},{7,6},{6,7},{9,8},{8,9},{11,10... | collective-permute-start | bytes 393224 | tf_op jit(solution)/shard_map/ppermute | solution.py:30
  11.3 14.6 %collective-permute-start.1 = (bf16[64,1024]{1,0:T(8,128)(2,1)S(1)}, bf16[64,1024]{1,0:T(8,128)(2,1)S(1)}, u32[]{:S(2)}, u32[]{:S(2)}) collective-permute-start(bf16[64,1024]{1,0:T(8,128)(2,1)S(1)} %collective-permute-done.refs_1_.refs_3_), channel_id=1, source_target_pairs={{1,0},{0,1},{3,2},{2,3},{5,4},{4,5},{7,6},{6,7},{9,8},{8,9},{11,10... | collective-permute-start | bytes 393224 | tf_op jit(solution)/shard_map/ppermute | solution.py:30
  12.1 4.0 %collective-permute-start.5 = (bf16[64,256]{1,0:T(8,128)(2,1)S(1)}, bf16[64,256]{1,0:T(8,128)(2,1)S(1)}, u32[]{:S(2)}, u32[]{:S(2)}) collective-permute-start(bf16[64,256]{1,0:T(8,128)(2,1)S(1)} %add.16), channel_id=1, source_target_pairs={{16,0},{20,4},{24,8},{28,12},{0,16},{4,20},{8,24},{12,28},{17,1},{... | collective-permute-start | bytes 98312 | tf_op jit(solution)/shard_map/ppermute | solution.py:30
  16.1 5.6 %collective-permute-start.6 = (bf16[64,256]{1,0:T(8,128)(2,1)S(1)}, bf16[64,256]{1,0:T(8,128)(2,1)S(1)}, u32[]{:S(2)}, u32[]{:S(2)}) collective-permute-start(bf16[64,256]{1,0:T(8,128)(2,1)S(1)} %add.17), channel_id=1, source_target_pairs={{2,0},{3,1},{0,2},{1,3},{6,4},{7,5},{4,6},{5,7},{10,8},{11,9},{8,1... | collective-permute-start | bytes 98312 | tf_op jit(solution)/shard_map/ppermute | solution.py:30
  21.8 4.0 %copy-start.2 = (f32[256,64]{0,1:T(8,128)S(1)}, f32[256,64]{0,1:T(8,128)}, u32[]{:S(2)}) copy-start(f32[256,64]{0,1:T(8,128)} %param.8) | copy-start | bytes 196612
  21.8 4.0 %collective-permute-start.7 = (bf16[64,256]{1,0:T(8,128)(2,1)S(1)}, bf16[64,256]{1,0:T(8,128)(2,1)S(1)}, u32[]{:S(2)}, u32[]{:S(2)}) collective-permute-start(bf16[64,256]{1,0:T(8,128)(2,1)S(1)} %add.18), channel_id=1, source_target_pairs={{1,0},{0,1},{3,2},{2,3},{5,4},{4,5},{7,6},{6,7},{9,8},{8,9},{11,10... | collective-permute-start | bytes 98312 | tf_op jit(solution)/shard_map/ppermute | solution.py:30
  34.4 9.7 %collective-permute-start.8 = (bf16[64,1024]{1,0:T(8,128)(2,1)S(1)}, bf16[64,1024]{1,0:T(8,128)(2,1)S(1)}, u32[]{:S(2)}, u32[]{:S(2)}) collective-permute-start(bf16[64,1024]{1,0:T(8,128)(2,1)S(1)} %get-tuple-element.6.refs_2_), channel_id=1, source_target_pairs={{1,0},{0,1},{3,2},{2,3},{5,4},{4,5},{7,6},{6,7},{9,8},{8,9},{11,10... | collective-permute-start | bytes 393224 | tf_op jit(solution)/shard_map/ppermute | solution.py:30
  34.9 9.4 %collective-permute-start.9 = (bf16[64,1024]{1,0:T(8,128)(2,1)S(1)}, bf16[64,1024]{1,0:T(8,128)(2,1)S(1)}, u32[]{:S(2)}, u32[]{:S(2)}) collective-permute-start(bf16[64,1024]{1,0:T(8,128)(2,1)S(1)} %get-tuple-element.6.refs_2_), channel_id=1, source_target_pairs={{2,0},{3,1},{0,2},{1,3},{6,4},{7,5},{4,6},{5,7},{10,8},{11,9},{8,1... | collective-permute-start | bytes 393224 | tf_op jit(solution)/shard_map/ppermute | solution.py:30
  44.1 7.8 %collective-permute-start.12 = (bf16[128,1024]{1,0:T(8,128)(2,1)S(1)}, bf16[128,1024]{1,0:T(8,128)(2,1)S(1)}, u32[]{:S(2)}, u32[]{:S(2)}) collective-permute-start(bf16[128,1024]{1,0:T(8,128)(2,1)S(1)} %pad_maximum_fusion.1), channel_id=1, source_target_pairs={{28,0},{5,1},{30,2},{7,3},{0,4},{9,5},{2,6},{11,7},{4,8},{13,9},{6... | collective-permute-start | bytes 786440 | tf_op jit(solution)/shard_map/ppermute | solution.py:49
  44.4 6.0 %collective-permute-start.10 = (bf16[64,1024]{1,0:T(8,128)(2,1)S(1)}, bf16[64,1024]{1,0:T(8,128)(2,1)S(1)}, u32[]{:S(2)}, u32[]{:S(2)}) collective-permute-start(bf16[64,1024]{1,0:T(8,128)(2,1)S(1)} %select_select_fusion.refs_4_), channel_id=1, source_target_pairs={{1,0},{0,1},{3,2},{2,3},{5,4},{4,5},{7,6},{6,7},{9,8},{8,9},{11,10... | collective-permute-start | bytes 393224 | tf_op jit(solution)/shard_map/ppermute | solution.py:30
  46.4 7.4 %collective-permute-start.13 = (bf16[128,1024]{1,0:T(8,128)(2,1)S(1)}, bf16[128,1024]{1,0:T(8,128)(2,1)S(1)}, u32[]{:S(2)}, u32[]{:S(2)}) collective-permute-start(bf16[128,1024]{1,0:T(8,128)(2,1)S(1)} %pad_maximum_fusion.2), channel_id=1, source_target_pairs={{28,0},{29,1},{6,2},{7,3},{0,4},{1,5},{10,6},{11,7},{4,8},{5,9},{1... | collective-permute-start | bytes 786440 | tf_op jit(solution)/shard_map/ppermute | solution.py:49
  50.4 7.0 %collective-permute-start.11 = (bf16[128,1024]{1,0:T(8,128)(2,1)S(1)}, bf16[128,1024]{1,0:T(8,128)(2,1)S(1)}, u32[]{:S(2)}, u32[]{:S(2)}) collective-permute-start(bf16[128,1024]{1,0:T(8,128)(2,1)S(1)} %pad_maximum_fusion), channel_id=1, source_target_pairs={{28,0},{29,1},{6,2},{7,3},{0,4},{1,5},{10,6},{11,7},{4,8},{5,9},{1... | collective-permute-start | bytes 786440 | tf_op jit(solution)/shard_map/ppermute | solution.py:49

commit v10 on v9

--- a/solution.py
+++ b/solution.py
@@ -47,12 +47,6 @@
             source = (x - 1 if z ^ bits > z else x + 1) % outer
             pairs.append((source * inner + z, x * inner + z))
     return lax.ppermute(piece, ("gx", "gy"), pairs)
-
-
-def tied(value, *tokens):
-    for token in tokens:
-        value = jnp.where(token[0, 0] == jnp.inf, jnp.zeros_like(value), value)
-    return value
 
 
 def column_blocks(value):
@@ -296,70 +290,94 @@
     )(pivots_t, points_t, coeffs_t, noise_t, *awaited)
 
 
-def factor_kernel(pivot_ref, point_ref, inverse_ref, factor_ref):
-    pivots = extended(pivot_ref[...], True).astype(jnp.bfloat16)
-    points = extended(point_ref[...], False).astype(jnp.bfloat16)
-    cols = kernel_of(product(points, pivots, ((0,), (0,))))
-    factor_ref[...] = product(cols, inverse_ref[...], ((1,), (1,)), lax.Precision.HIGHEST)
-
-
-def factor_of(pivots_t, points_t, inverse):
+def padded(value):
+    return jnp.concatenate([value, jnp.zeros((LANES - value.shape[0], value.shape[1]), value.dtype)], axis=0)
+
+
+def tile_terms(own, other, probes):
+    return product(kernel_of(product(own, other, ((1,), (0,)))).astype(jnp.bfloat16), probes, ((1,), (1,)))
+
+
+def factor_kernel(pivot_ref, point_ref, inverse_ref, sent_ref, factor_ref, total_ref, zero_ref):
+    count = point_ref.shape[1]
+    own = jnp.transpose(padded(extended(point_ref[...], True))).astype(jnp.bfloat16)
+    pivots = padded(extended(pivot_ref[...], False)).astype(jnp.bfloat16)
+    other = padded(extended(point_ref[...], False)).astype(jnp.bfloat16)
+    high, middle, _ = thirds(inverse_ref[...])
+    for s in range(0, count, CHUNK):
+        rows = own[s:s + CHUNK, :]
+        cols_high, cols_middle, _ = thirds(kernel_of(product(rows, pivots, ((1,), (0,)))))
+        factor_ref[s:s + CHUNK, :] = (
+            product(cols_high, middle, ((1,), (1,))) + product(cols_middle, high, ((1,), (1,)))
+        ) + product(cols_high, high, ((1,), (1,)))
+        total_ref[s:s + CHUNK, :] = tile_terms(rows, other, sent_ref[...])
+    zero_ref[...] = jnp.zeros_like(zero_ref)
+
+
+def factor_of(pivots_t, points_t, inverse, sent_t):
     size = pivots_t.shape[1]
     count = points_t.shape[1]
     return pl.pallas_call(
         factor_kernel,
-        out_shape=jax.ShapeDtypeStruct((count, size), jnp.float32),
-        in_specs=in_vmem(3),
-        out_specs=in_vmem(1)[0],
+        out_shape=(
+            jax.ShapeDtypeStruct((count, size), jnp.float32),
+            jax.ShapeDtypeStruct((count, sent_t.shape[0]), jnp.float32),
+            pltpu.VMEM(sent_t.shape, sent_t.dtype),
+        ),
+        in_specs=in_vmem(4),
+        out_specs=tuple(in_vmem(3)),
         compiler_params=pltpu.CompilerParams(vmem_limit_bytes=32 * 1024 * 1024),
-        cost_estimate=pl.CostEstimate(flops=12 * count * size * size, bytes_accessed=4 * count * size, transcendentals=count * size),
+        cost_estimate=pl.CostEstimate(
+            flops=6 * count * size * size + 4 * count * count * LANES,
+            bytes_accessed=6 * count * size,
+            transcendentals=count * (size + count),
+        ),
         name="factor",
-    )(pivots_t, points_t, inverse)
-
-
-def band_kernel(parts, first, last, *refs):
+    )(pivots_t, points_t, inverse, sent_t)
+
+
+def band_kernel(parts, last, *refs):
     refs = list(refs)
-    out_ref = refs.pop()
     own_ref = refs.pop(0)
-    count = own_ref.shape[1]
+    depth, count = own_ref.shape
     pieces = []
     for part in parts:
         if part == 2:
             pieces.append((refs.pop(0)[...], refs.pop(0)[...]))
         else:
             stacked = refs.pop(0)
-            pieces.append((stacked[:own_ref.shape[0], :], stacked[own_ref.shape[0]:, :]))
-    before_ref = None if first else refs.pop(0)
-
-    def padded(value):
-        return jnp.concatenate([value, jnp.zeros((LANES - value.shape[0], count), jnp.float32)], axis=0)
-
+            pieces.append((stacked[:depth, :], stacked[depth:, :]))
+    before_ref = refs.pop(0)
     own = jnp.transpose(padded(extended(own_ref[...], True))).astype(jnp.bfloat16)
     others = [padded(extended(block, False)).astype(jnp.bfloat16) for block, _ in pieces]
     for s in range(0, count, CHUNK):
-        total = None if first else before_ref[s:s + CHUNK, :]
+        total = before_ref[s:s + CHUNK, :]
         for other, (_, probes) in zip(others, pieces):
-            tile = kernel_of(product(own[s:s + CHUNK, :], other, ((1,), (0,)))).astype(jnp.bfloat16)
-            term = product(tile, probes, ((1,), (1,)))
-            total = term if total is None else total + term
+            total = total + tile_terms(own[s:s + CHUNK, :], other, probes)
         if last:
+            probe_ref, out_ref = refs
             scale = 1.0 / (count ** 0.5)
-            out_ref[:, s:s + CHUNK] = jnp.transpose(total) * scale + noise_weight * refs[0][:, s:s + CHUNK]
+            out_ref[:, s:s + CHUNK] = jnp.transpose(total) * scale + noise_weight * probe_ref[:, s:s + CHUNK]
         else:
-            out_ref[s:s + CHUNK, :] = total
-
-
-def band_sum(own, pieces, before=None, probes=None):
+            refs[0][s:s + CHUNK, :] = total
+    if not last:
+        refs[1][...] = jnp.zeros_like(refs[1])
+
+
+def band_sum(own, pieces, before, probes=None):
     depth, count = own.shape
-    width = pieces[0][1].shape[0] if len(pieces[0]) == 2 else pieces[0][0].shape[0] - depth
-    first, last = before is None, probes is not None
-    operands = [own] + [array for piece in pieces for array in piece]
-    operands += ([] if first else [before]) + ([probes] if last else [])
+    width = before.shape[1]
+    last = probes is not None
+    operands = [own] + [array for piece in pieces for array in piece] + [before] + ([probes] if last else [])
+    if last:
+        out_shape = jax.ShapeDtypeStruct((width, count), jnp.float32)
+    else:
+        out_shape = (jax.ShapeDtypeStruct(before.shape, jnp.float32), pltpu.VMEM((width, count), jnp.bfloat16))
     return pl.pallas_call(
-        functools.partial(band_kernel, tuple(len(piece) for piece in pieces), first, last),
-        out_shape=jax.ShapeDtypeStruct((width, count) if last else (count, width), jnp.float32),
+        functools.partial(band_kernel, tuple(len(piece) for piece in pieces), last),
+        out_shape=out_shape,
         in_specs=in_vmem(len(operands)),
-        out_specs=in_vmem(1)[0],
+        out_specs=in_vmem(1)[0] if last else tuple(in_vmem(2)),
         compiler_params=pltpu.CompilerParams(vmem_limit_bytes=32 * 1024 * 1024),
         cost_estimate=pl.CostEstimate(
             flops=len(pieces) * 4 * count * count * LANES,
@@ -377,20 +395,19 @@
     near = column_blocks(points) if tall else direct_blocks(points)
 
     inverse, probes, sent = probes_of(pivot_points, points, coeffs.T, noise.T, near)
-    factor = factor_of(pivot_points, points, inverse)
-    total = band_sum(points, [(points, sent)])
+    factor, total, zeros = factor_of(pivot_points, points, inverse, sent)
     if tall:
-        two = tied(swapped(sent, "gy", 2), total, factor)
-        one = tied(swapped(sent, "gy", 1), total, factor)
+        two = swapped(sent, "gy", 2) + zeros
+        one = swapped(sent, "gy", 1) + zeros
         three = swapped(two, "gy", 1)
         crossed = [cross(jnp.concatenate([near[i], probe], axis=0), i + 1) for i, probe in enumerate((one, two))]
-        total = band_sum(points, [(near[0], one), (near[1], two)], total)
-        crossed.append(cross(jnp.concatenate([near[2], tied(three, total)], axis=0), 3))
-        total = band_sum(points, [(crossed[0],), (crossed[1],), (near[2], three)], total)
+        total, zeros = band_sum(points, [(near[0], one), (near[1], two)], total)
+        crossed.append(cross(jnp.concatenate([near[2], three + zeros], axis=0), 3))
+        total, _ = band_sum(points, [(crossed[0],), (crossed[1],), (near[2], three)], total)
         kernel_probes = band_sum(points, [(crossed[2],)], total, probes)
     else:
         pieces = list(zip(near, direct_blocks(sent)))
-        total = band_sum(points, pieces[:3], total)
+        total, _ = band_sum(points, pieces[:3], total)
         kernel_probes = band_sum(points, pieces[3:], total, probes)
     return (kernel_probes.T, factor)
 

time: 59.8 us -> 56.9 us (0.952)
  waiting for transfers between devices: 12.1 us -> 15.1 us
  local copies, waits for them, and re-layouts: 2.32 us -> 0.02 us
  between operations: 2.83 us -> 0.78 us
  Pallas kernels: 21.7 us -> 20.9 us
  starting transfers between devices: 20.4 us -> 19.8 us
    slice x3 -> x0, local copies, waits for them, and re-layouts: 2.31 us -> none  [tied(): value = jnp.where(token[0, 0] == jnp.inf, jnp.zeros_like(value), value)]
    ppermute x11, waiting for transfers between devices: 10.2 us -> 12.2 us  [swapped(): lax.ppermute(value, axis, [(i ^ bit, i) for i in range(lax.axis_size(axis...]
    pallas_call x4 -> x3, Pallas kernels: 9.65 us -> 8.21 us  [band_sum(): pl.pallas_call(functools.partial(band_kernel, tuple((len(piece) for piece...]
    ppermute x3, starting transfers between devices: 1.95 us -> 0.69 us  [cross(): return lax.ppermute(piece, ('gx', 'gy'), pairs)]
    ppermute x3, waiting for transfers between devices: 1.95 us -> 2.89 us  [cross(): return lax.ppermute(piece, ('gx', 'gy'), pairs)]
    pallas_call x1, Pallas kernels: 2.38 us -> 3.03 us  [factor_of(): pl.pallas_call(factor_kernel, out_shape=(jax.ShapeDtypeStruct((count, siz...]
    ppermute x11, starting transfers between devices: 18.5 us -> 19.1 us  [swapped(): lax.ppermute(value, axis, [(i ^ bit, i) for i in range(lax.axis_size(axis...]
  transfers between devices with their start and end apart: 14 -> 14, of which waited for: 6 -> 9; matrix products, arithmetic and copies ran while one was open for 4% -> 0% of each run, Pallas kernels for 19% -> 18%
where the time goes in v10:
time: 56.9 us; the launch traced here: 56.7 us
  Pallas kernels  20.9 us (37%)
  starting transfers between devices  19.8 us (35%)
  waiting for transfers between devices  15.1 us (27%)
  between operations  0.78 us (1%)
    ppermute x11, starting transfers between devices, swapped(): lax.ppermute(value, axis, [(i ^ bit, i) for i in range(lax.axis_size(axis...  19.1 us
    ppermute x11, waiting for transfers between devices, swapped(): lax.ppermute(value, axis, [(i ^ bit, i) for i in range(lax.axis_size(axis...  12.2 us
    pallas_call x1, Pallas kernels, probes_of(): pl.pallas_call(probe_kernel, out_shape=(jax.ShapeDtypeStruct((size, size)...  8.51 us
    pallas_call x3, Pallas kernels, band_sum(): pl.pallas_call(functools.partial(band_kernel, tuple((len(piece) for piece...  8.21 us
    pallas_call x1, Pallas kernels, factor_of(): pl.pallas_call(factor_kernel, out_shape=(jax.ShapeDtypeStruct((count, siz...  3.03 us
    ppermute x3, waiting for transfers between devices, cross(): return lax.ppermute(piece, ('gx', 'gy'), pairs)  2.89 us
    pallas_call x1, Pallas kernels, pick(): pl.pallas_call(pick_kernel, out_shape=pltpu.VMEM((points_t.shape[0], 2 *...  1.17 us
  transfers between devices with their start and end apart: 14, of which 9 were waited for; matrix products, arithmetic and copies ran while one was open for 0% of the time, Pallas kernels for 18%

profile of v10, /device:TPU:0, one launch (start us, length us, event | category | flops | bytes accessed | tf_op | source)
XLA Modules:
  0.0 56.7 jit_solution(11994782726630398539)
XLA Ops:
  0.6 4.1 %collective-permute-start = (bf16[64,1024]{1,0:T(8,128)(2,1)}, bf16[64,1024]{1,0:T(8,128)(2,1)S(1)}, u32[]{:S(2)}, u32[]{:S(2)}) collective-permute-start(bf16[64,1024]{1,0:T(8,128)(2,1)} %bitcast.4), channel_id=1, source_target_pairs={{2,0},{3,1},{0,2},{1,3},{6,4},{7,5},{4,6},{5,7},{10,8},{11,9},{8,1... | collective-permute-start | bytes 393224 | tf_op jit(solution)/shard_map/ppermute | solution.py:30
  4.7 1.2 %pick.1 = bf16[64,256]{1,0:T(8,128)(2,1)S(1)} custom-call(s32[2]{0:T(128)} %owner_ref.1, s32[2,128]{1,0:T(2,128)} %pivot_ref.1, bf16[64,1024]{1,0:T(8,128)(2,1)} %bitcast.5), custom_call_target="tpu_custom_call" | custom-call | tf_op jit(solution)/shard_map/pick/pallas_call | solution.py:106
  5.9 0.0 copy-start.1
  5.9 0.1 collective-permute-start.2
  6.0 1.2 %collective-permute-done.2 = bf16[64,256]{1,0:T(8,128)(2,1)S(1)} collective-permute-done((bf16[64,256]{1,0:T(8,128)(2,1)S(1)}, bf16[64,256]{1,0:T(8,128)(2,1)S(1)}, u32[]{:S(2)}, u32[]{:S(2)}) %collective-permute-start.2) | collective-permute-done | bytes 32800 | tf_op jit(solution)/shard_map/ppermute | solution.py:30
  7.2 1.6 %collective-permute-start.3 = (bf16[64,256]{1,0:T(8,128)(2,1)S(1)}, bf16[64,256]{1,0:T(8,128)(2,1)S(1)}, u32[]{:S(2)}, u32[]{:S(2)}) collective-permute-start(bf16[64,256]{1,0:T(8,128)(2,1)S(1)} %add.24), channel_id=1, source_target_pairs={{8,0},{12,4},{0,8},{4,12},{24,16},{28,20},{16,24},{20,28},{9,1},{1... | collective-permute-start | bytes 98312 | tf_op jit(solution)/shard_map/ppermute | solution.py:30
  8.8 1.6 %collective-permute-start.7 = (bf16[64,1024]{1,0:T(8,128)(2,1)S(1)}, bf16[64,1024]{1,0:T(8,128)(2,1)S(1)}, u32[]{:S(2)}, u32[]{:S(2)}) collective-permute-start(bf16[64,1024]{1,0:T(8,128)(2,1)S(1)} %bitcast.6), channel_id=1, source_target_pairs={{1,0},{0,1},{3,2},{2,3},{5,4},{4,5},{7,6},{6,7},{9,8},{8,9},{11,10... | collective-permute-start | bytes 393224 | tf_op jit(solution)/shard_map/ppermute | solution.py:30
  10.4 0.9 %collective-permute-done.refs_1_.refs_3_ = bf16[64,1024]{1,0:T(8,128)(2,1)S(1)} collective-permute-done((bf16[64,1024]{1,0:T(8,128)(2,1)}, bf16[64,1024]{1,0:T(8,128)(2,1)S(1)}, u32[]{:S(2)}, u32[]{:S(2)}) %collective-permute-start) | collective-permute-done | bytes 131104 | tf_op jit(solution)/shard_map/ppermute | solution.py:30
  11.3 0.9 %collective-permute-start.1 = (bf16[64,1024]{1,0:T(8,128)(2,1)S(1)}, bf16[64,1024]{1,0:T(8,128)(2,1)S(1)}, u32[]{:S(2)}, u32[]{:S(2)}) collective-permute-start(bf16[64,1024]{1,0:T(8,128)(2,1)S(1)} %collective-permute-done.refs_1_.refs_3_), channel_id=1, source_target_pairs={{1,0},{0,1},{3,2},{2,3},{5,4},{4,5},{7,6},{6,7},{9,8},{8,9},{11,10... | collective-permute-start | bytes 393224 | tf_op jit(solution)/shard_map/ppermute | solution.py:30
  12.1 0.0 collective-permute-done.3
  12.1 1.6 %collective-permute-start.4 = (bf16[64,256]{1,0:T(8,128)(2,1)S(1)}, bf16[64,256]{1,0:T(8,128)(2,1)S(1)}, u32[]{:S(2)}, u32[]{:S(2)}) collective-permute-start(bf16[64,256]{1,0:T(8,128)(2,1)S(1)} %add.25), channel_id=1, source_target_pairs={{16,0},{20,4},{24,8},{28,12},{0,16},{4,20},{8,24},{12,28},{17,1},{... | collective-permute-start | bytes 98312 | tf_op jit(solution)/shard_map/ppermute | solution.py:30
  13.7 2.4 %collective-permute-done.4 = bf16[64,256]{1,0:T(8,128)(2,1)S(1)} collective-permute-done((bf16[64,256]{1,0:T(8,128)(2,1)S(1)}, bf16[64,256]{1,0:T(8,128)(2,1)S(1)}, u32[]{:S(2)}, u32[]{:S(2)}) %collective-permute-start.4) | collective-permute-done | bytes 32800 | tf_op jit(solution)/shard_map/ppermute | solution.py:30
  16.1 3.4 %collective-permute-start.5 = (bf16[64,256]{1,0:T(8,128)(2,1)S(1)}, bf16[64,256]{1,0:T(8,128)(2,1)S(1)}, u32[]{:S(2)}, u32[]{:S(2)}) collective-permute-start(bf16[64,256]{1,0:T(8,128)(2,1)S(1)} %add.26), channel_id=1, source_target_pairs={{2,0},{3,1},{0,2},{1,3},{6,4},{7,5},{4,6},{5,7},{10,8},{11,9},{8,1... | collective-permute-start | bytes 98312 | tf_op jit(solution)/shard_map/ppermute | solution.py:30
  19.5 2.2 %collective-permute-done.5 = bf16[64,256]{1,0:T(8,128)(2,1)S(1)} collective-permute-done((bf16[64,256]{1,0:T(8,128)(2,1)S(1)}, bf16[64,256]{1,0:T(8,128)(2,1)S(1)}, u32[]{:S(2)}, u32[]{:S(2)}) %collective-permute-start.5) | collective-permute-done | bytes 32800 | tf_op jit(solution)/shard_map/ppermute | solution.py:30
  21.8 0.0 copy-start.2
  21.8 0.6 collective-permute-start.6
  22.4 3.4 %collective-permute-done.6 = bf16[64,256]{1,0:T(8,128)(2,1)S(1)} collective-permute-done((bf16[64,256]{1,0:T(8,128)(2,1)S(1)}, bf16[64,256]{1,0:T(8,128)(2,1)S(1)}, u32[]{:S(2)}, u32[]{:S(2)}) %collective-permute-start.6) | collective-permute-done | bytes 32800 | tf_op jit(solution)/shard_map/ppermute | solution.py:30
  25.9 8.5 %probes.1 = (f32[256,256]{1,0:T(8,128)S(1)}, f32[64,1024]{1,0:T(8,128)S(1)}, bf16[64,1024]{1,0:T(8,128)(2,1)S(1)}) custom-call(bf16[64,256]{1,0:T(8,128)(2,1)S(1)} %add.28.pivot_ref, bf16[64,1024]{1,0:T(8,128)(2,1)S(1)} %bitcast.7, f32[64,256]{1,0:T(8,128)S(1)} %bitcast.13, f32[64,1024]{1,0:T(8,128)S(1)} %bitcast.12, ...), custom_call_target="tpu_custom_call" | custom-call | tf_op jit(solution)/shard_map/probes/pallas_call | solution.py:278
  34.4 0.6 collective-permute-start.10
  34.9 2.2 %collective-permute-start.8 = (bf16[64,1024]{1,0:T(8,128)(2,1)S(1)}, bf16[64,1024]{1,0:T(8,128)(2,1)S(1)}, u32[]{:S(2)}, u32[]{:S(2)}) collective-permute-start(bf16[64,1024]{1,0:T(8,128)(2,1)S(1)} %get-tuple-element.11.sent_ref), channel_id=1, source_target_pairs={{2,0},{3,1},{0,2},{1,3},{6,4},{7,5},{4,6},{5,7},{10,8},{11,9},{8,1... | collective-permute-start | bytes 393224 | tf_op jit(solution)/shard_map/ppermute | solution.py:30
  37.1 3.0 %factor.1 = (f32[1024,256]{1,0:T(8,128)}, f32[1024,64]{1,0:T(8,128)S(1)}, bf16[64,1024]{1,0:T(8,128)(2,1)S(1)}) custom-call(bf16[64,256]{1,0:T(8,128)(2,1)S(1)} %add.28.pivot_ref, bf16[64,1024]{1,0:T(8,128)(2,1)S(1)} %bitcast.8, f32[256,256]{1,0:T(8,128)S(1)} %get-tuple-element.12.inverse_ref, bf16[64,1024]{1,0:T(8,128)(2,1)S(1)} %get-tuple-element.11.sent_ref), custom_call_target="tpu_custom_call" | custom-call | flops 939524096 | bytes 1572864 | tf_op jit(solution)/shard_map/factor/pallas_call | solution.py:320
  40.1 0.7 %collective-permute-done.8 = bf16[64,1024]{1,0:T(8,128)(2,1)S(1)} collective-permute-done((bf16[64,1024]{1,0:T(8,128)(2,1)S(1)}, bf16[64,1024]{1,0:T(8,128)(2,1)S(1)}, u32[]{:S(2)}, u32[]{:S(2)}) %collective-permute-start.8) | collective-permute-done | bytes 131104 | tf_op jit(solution)/shard_map/ppermute | solution.py:30
  40.9 0.1 collective-permute-start.12
  40.9 2.6 %collective-permute-start.9 = (bf16[64,1024]{1,0:T(8,128)(2,1)S(1)}, bf16[64,1024]{1,0:T(8,128)(2,1)S(1)}, u32[]{:S(2)}, u32[]{:S(2)}) collective-permute-start(bf16[64,1024]{1,0:T(8,128)(2,1)S(1)} %get-tuple-element.21.refs_4_), channel_id=1, source_target_pairs={{1,0},{0,1},{3,2},{2,3},{5,4},{4,5},{7,6},{6,7},{9,8},{8,9},{11,10... | collective-permute-start | bytes 393224 | tf_op jit(solution)/shard_map/ppermute | solution.py:30
  43.6 0.4 collective-permute-start.13
  44.0 2.5 %band_sum.3 = (f32[1024,64]{1,0:T(8,128)S(1)}, bf16[64,1024]{1,0:T(8,128)(2,1)S(1)}) custom-call(bf16[64,1024]{1,0:T(8,128)(2,1)S(1)} %bitcast.9, bf16[64,1024]{1,0:T(8,128)(2,1)S(1)} %collective-permute-done.7.refs_0_.refs_1_, bf16[64,1024]{1,0:T(8,128)(2,1)S(1)} %get-tuple-element.20.refs_2_, bf16[64,1024]{1,0:T(8,128)(2,1)S(1)} %collective-permute-done.refs_1_.refs_3_, ...), custom_call_target="tpu_custom_call" | custom-call | flops 1073741824 | bytes 1572864 | tf_op jit(solution)/shard_map/band_sum/pallas_call | solution.py:376
  46.5 1.3 %collective-permute-done.9.refs_4_ = bf16[64,1024]{1,0:T(8,128)(2,1)S(1)} collective-permute-done((bf16[64,1024]{1,0:T(8,128)(2,1)S(1)}, bf16[64,1024]{1,0:T(8,128)(2,1)S(1)}, u32[]{:S(2)}, u32[]{:S(2)}) %collective-permute-start.9) | collective-permute-done | bytes 131104 | tf_op jit(solution)/shard_map/ppermute | solution.py:30
  47.9 0.2 collective-permute-start.11
  48.2 2.4 %collective-permute-done.13.refs_2_ = bf16[128,1024]{1,0:T(8,128)(2,1)S(1)} collective-permute-done((bf16[128,1024]{1,0:T(8,128)(2,1)S(1)}, bf16[128,1024]{1,0:T(8,128)(2,1)S(1)}, u32[]{:S(2)}, u32[]{:S(2)}) %collective-permute-start.13) | collective-permute-done | bytes 262176 | tf_op jit(solution)/shard_map/ppermute | solution.py:49
  50.5 3.6 %band_sum.4 = (f32[1024,64]{1,0:T(8,128)S(1)}, bf16[64,1024]{1,0:T(8,128)(2,1)}) custom-call(bf16[64,1024]{1,0:T(8,128)(2,1)S(1)} %bitcast.10, bf16[128,1024]{1,0:T(8,128)(2,1)S(1)} %collective-permute-done.12.refs_1_, bf16[128,1024]{1,0:T(8,128)(2,1)S(1)} %collective-permute-done.13.refs_2_, bf16[64,1024]{1,0:T(8,128)(2,1)S(1)} %collective-permute-done.1.refs_2_.refs_3_, ...), custom_call_target="tpu_custom_call" | custom-call | flops 1610612736 | bytes 1572864 | tf_op jit(solution)/shard_map/band_sum/pallas_call | solution.py:376
  54.2 0.5 collective-permute-done.11.refs_1_
  54.7 2.1 %band_sum.5 = f32[64,1024]{1,0:T(8,128)} custom-call(bf16[64,1024]{1,0:T(8,128)(2,1)S(1)} %bitcast.11, bf16[128,1024]{1,0:T(8,128)(2,1)S(1)} %collective-permute-done.11.refs_1_, f32[1024,64]{1,0:T(8,128)S(1)} %get-tuple-element.17.refs_2_, f32[64,1024]{1,0:T(8,128)S(1)} %get-tuple-element.18.refs_3_), custom_call_target="tpu_custom_call" | custom-call | flops 536870912 | bytes 1048576 | tf_op jit(solution)/shard_map/band_sum/pallas_call | solution.py:376
  (18 shorter events, 0.2 us)
Async XLA Ops:
  0.6 8.1 %copy-start = (bf16[1024,64]{0,1:T(8,128)(2,1)S(1)}, bf16[1024,64]{0,1:T(8,128)(2,1)}, u32[]{:S(2)}) copy-start(bf16[1024,64]{0,1:T(8,128)(2,1)} %param.5) | copy-start | bytes 393220
  0.6 10.6 %collective-permute-start = (bf16[64,1024]{1,0:T(8,128)(2,1)}, bf16[64,1024]{1,0:T(8,128)(2,1)S(1)}, u32[]{:S(2)}, u32[]{:S(2)}) collective-permute-start(bf16[64,1024]{1,0:T(8,128)(2,1)} %bitcast.4), channel_id=1, source_target_pairs={{2,0},{3,1},{0,2},{1,3},{6,4},{7,5},{4,6},{5,7},{10,8},{11,9},{8,1... | collective-permute-start | bytes 393224 | tf_op jit(solution)/shard_map/ppermute | solution.py:30
  5.9 19.9 %copy-start.1 = (f32[1024,64]{0,1:T(8,128)S(1)}, f32[1024,64]{0,1:T(8,128)}, u32[]{:S(2)}) copy-start(f32[1024,64]{0,1:T(8,128)} %param.9) | copy-start | bytes 786436
  5.9 1.3 %collective-permute-start.2 = (bf16[64,256]{1,0:T(8,128)(2,1)S(1)}, bf16[64,256]{1,0:T(8,128)(2,1)S(1)}, u32[]{:S(2)}, u32[]{:S(2)}) collective-permute-start(bf16[64,256]{1,0:T(8,128)(2,1)S(1)} %pick.1), channel_id=1, source_target_pairs={{4,0},{0,4},{12,8},{8,12},{20,16},{16,20},{28,24},{24,28},{5,1},{1... | collective-permute-start | bytes 98312 | tf_op jit(solution)/shard_map/ppermute | solution.py:30
  7.2 4.9 %collective-permute-start.3 = (bf16[64,256]{1,0:T(8,128)(2,1)S(1)}, bf16[64,256]{1,0:T(8,128)(2,1)S(1)}, u32[]{:S(2)}, u32[]{:S(2)}) collective-permute-start(bf16[64,256]{1,0:T(8,128)(2,1)S(1)} %add.24), channel_id=1, source_target_pairs={{8,0},{12,4},{0,8},{4,12},{24,16},{28,20},{16,24},{20,28},{9,1},{1... | collective-permute-start | bytes 98312 | tf_op jit(solution)/shard_map/ppermute | solution.py:30
  8.8 17.0 %collective-permute-start.7 = (bf16[64,1024]{1,0:T(8,128)(2,1)S(1)}, bf16[64,1024]{1,0:T(8,128)(2,1)S(1)}, u32[]{:S(2)}, u32[]{:S(2)}) collective-permute-start(bf16[64,1024]{1,0:T(8,128)(2,1)S(1)} %bitcast.6), channel_id=1, source_target_pairs={{1,0},{0,1},{3,2},{2,3},{5,4},{4,5},{7,6},{6,7},{9,8},{8,9},{11,10... | collective-permute-start | bytes 393224 | tf_op jit(solution)/shard_map/ppermute | solution.py:30
  11.3 14.6 %collective-permute-start.1 = (bf16[64,1024]{1,0:T(8,128)(2,1)S(1)}, bf16[64,1024]{1,0:T(8,128)(2,1)S(1)}, u32[]{:S(2)}, u32[]{:S(2)}) collective-permute-start(bf16[64,1024]{1,0:T(8,128)(2,1)S(1)} %collective-permute-done.refs_1_.refs_3_), channel_id=1, source_target_pairs={{1,0},{0,1},{3,2},{2,3},{5,4},{4,5},{7,6},{6,7},{9,8},{8,9},{11,10... | collective-permute-start | bytes 393224 | tf_op jit(solution)/shard_map/ppermute | solution.py:30
  12.1 4.0 %collective-permute-start.4 = (bf16[64,256]{1,0:T(8,128)(2,1)S(1)}, bf16[64,256]{1,0:T(8,128)(2,1)S(1)}, u32[]{:S(2)}, u32[]{:S(2)}) collective-permute-start(bf16[64,256]{1,0:T(8,128)(2,1)S(1)} %add.25), channel_id=1, source_target_pairs={{16,0},{20,4},{24,8},{28,12},{0,16},{4,20},{8,24},{12,28},{17,1},{... | collective-permute-start | bytes 98312 | tf_op jit(solution)/shard_map/ppermute | solution.py:30
  16.1 5.6 %collective-permute-start.5 = (bf16[64,256]{1,0:T(8,128)(2,1)S(1)}, bf16[64,256]{1,0:T(8,128)(2,1)S(1)}, u32[]{:S(2)}, u32[]{:S(2)}) collective-permute-start(bf16[64,256]{1,0:T(8,128)(2,1)S(1)} %add.26), channel_id=1, source_target_pairs={{2,0},{3,1},{0,2},{1,3},{6,4},{7,5},{4,6},{5,7},{10,8},{11,9},{8,1... | collective-permute-start | bytes 98312 | tf_op jit(solution)/shard_map/ppermute | solution.py:30
  21.8 4.0 %copy-start.2 = (f32[256,64]{0,1:T(8,128)S(1)}, f32[256,64]{0,1:T(8,128)}, u32[]{:S(2)}) copy-start(f32[256,64]{0,1:T(8,128)} %param.8) | copy-start | bytes 196612
  21.8 4.0 %collective-permute-start.6 = (bf16[64,256]{1,0:T(8,128)(2,1)S(1)}, bf16[64,256]{1,0:T(8,128)(2,1)S(1)}, u32[]{:S(2)}, u32[]{:S(2)}) collective-permute-start(bf16[64,256]{1,0:T(8,128)(2,1)S(1)} %add.27), channel_id=1, source_target_pairs={{1,0},{0,1},{3,2},{2,3},{5,4},{4,5},{7,6},{6,7},{9,8},{8,9},{11,10... | collective-permute-start | bytes 98312 | tf_op jit(solution)/shard_map/ppermute | solution.py:30
  34.4 5.8 %collective-permute-start.10 = (bf16[64,1024]{1,0:T(8,128)(2,1)S(1)}, bf16[64,1024]{1,0:T(8,128)(2,1)S(1)}, u32[]{:S(2)}, u32[]{:S(2)}) collective-permute-start(bf16[64,1024]{1,0:T(8,128)(2,1)S(1)} %get-tuple-element.11.sent_ref), channel_id=1, source_target_pairs={{1,0},{0,1},{3,2},{2,3},{5,4},{4,5},{7,6},{6,7},{9,8},{8,9},{11,10... | collective-permute-start | bytes 393224 | tf_op jit(solution)/shard_map/ppermute | solution.py:30
  34.9 5.9 %collective-permute-start.8 = (bf16[64,1024]{1,0:T(8,128)(2,1)S(1)}, bf16[64,1024]{1,0:T(8,128)(2,1)S(1)}, u32[]{:S(2)}, u32[]{:S(2)}) collective-permute-start(bf16[64,1024]{1,0:T(8,128)(2,1)S(1)} %get-tuple-element.11.sent_ref), channel_id=1, source_target_pairs={{2,0},{3,1},{0,2},{1,3},{6,4},{7,5},{4,6},{5,7},{10,8},{11,9},{8,1... | collective-permute-start | bytes 393224 | tf_op jit(solution)/shard_map/ppermute | solution.py:30
  40.9 7.3 %collective-permute-start.12 = (bf16[128,1024]{1,0:T(8,128)(2,1)S(1)}, bf16[128,1024]{1,0:T(8,128)(2,1)S(1)}, u32[]{:S(2)}, u32[]{:S(2)}) collective-permute-start(bf16[128,1024]{1,0:T(8,128)(2,1)S(1)} %pad_maximum_fusion.1), channel_id=1, source_target_pairs={{28,0},{5,1},{30,2},{7,3},{0,4},{9,5},{2,6},{11,7},{4,8},{13,9},{6... | collective-permute-start | bytes 786440 | tf_op jit(solution)/shard_map/ppermute | solution.py:49
  40.9 6.9 %collective-permute-start.9 = (bf16[64,1024]{1,0:T(8,128)(2,1)S(1)}, bf16[64,1024]{1,0:T(8,128)(2,1)S(1)}, u32[]{:S(2)}, u32[]{:S(2)}) collective-permute-start(bf16[64,1024]{1,0:T(8,128)(2,1)S(1)} %get-tuple-element.21.refs_4_), channel_id=1, source_target_pairs={{1,0},{0,1},{3,2},{2,3},{5,4},{4,5},{7,6},{6,7},{9,8},{8,9},{11,10... | collective-permute-start | bytes 393224 | tf_op jit(solution)/shard_map/ppermute | solution.py:30
  43.6 6.9 %collective-permute-start.13 = (bf16[128,1024]{1,0:T(8,128)(2,1)S(1)}, bf16[128,1024]{1,0:T(8,128)(2,1)S(1)}, u32[]{:S(2)}, u32[]{:S(2)}) collective-permute-start(bf16[128,1024]{1,0:T(8,128)(2,1)S(1)} %pad_maximum_fusion.2), channel_id=1, source_target_pairs={{28,0},{29,1},{6,2},{7,3},{0,4},{1,5},{10,6},{11,7},{4,8},{5,9},{1... | collective-permute-start | bytes 786440 | tf_op jit(solution)/shard_map/ppermute | solution.py:49
  47.9 6.7 %collective-permute-start.11 = (bf16[128,1024]{1,0:T(8,128)(2,1)S(1)}, bf16[128,1024]{1,0:T(8,128)(2,1)S(1)}, u32[]{:S(2)}, u32[]{:S(2)}) collective-permute-start(bf16[128,1024]{1,0:T(8,128)(2,1)S(1)} %pad_maximum_fusion), channel_id=1, source_target_pairs={{28,0},{29,1},{6,2},{7,3},{0,4},{1,5},{10,6},{11,7},{4,8},{5,9},{1... | collective-permute-start | bytes 786440 | tf_op jit(solution)/shard_map/ppermute | solution.py:49

commit v11 on v10

--- a/solution.py
+++ b/solution.py
@@ -31,12 +31,14 @@
 
 
 def spread(value):
-    sums = [value]
     for axis in ("gx", "gy"):
-        bits = [1 << i for i in range(lax.axis_size(axis).bit_length() - 1)]
-        for bit in bits if axis == "gx" else bits[::-1]:
-            sums.append(sums[-1] + swapped(sums[-1], axis, bit))
-    return sums[1:]
+        count = lax.axis_size(axis)
+        bit = 1
+        while bit < count:
+            wide = 2 if (count // bit).bit_length() % 2 == 0 else 4
+            value = sum((swapped(value, axis, bit * k) for k in range(1, wide)), value)
+            bit *= wide
+    return value
 
 
 def cross(piece, bits):
@@ -47,11 +49,6 @@
             source = (x - 1 if z ^ bits > z else x + 1) % outer
             pairs.append((source * inner + z, x * inner + z))
     return lax.ppermute(piece, ("gx", "gy"), pairs)
-
-
-def column_blocks(value):
-    two = swapped(value, "gy", 2)
-    return swapped(value, "gy", 1), two, swapped(two, "gy", 1)
 
 
 def direct_blocks(value):
@@ -298,11 +295,10 @@
     return product(kernel_of(product(own, other, ((1,), (0,)))).astype(jnp.bfloat16), probes, ((1,), (1,)))
 
 
-def factor_kernel(pivot_ref, point_ref, inverse_ref, sent_ref, factor_ref, total_ref, zero_ref):
+def factor_kernel(pivot_ref, point_ref, inverse_ref, awaited_ref, factor_ref, zero_ref):
     count = point_ref.shape[1]
     own = jnp.transpose(padded(extended(point_ref[...], True))).astype(jnp.bfloat16)
     pivots = padded(extended(pivot_ref[...], False)).astype(jnp.bfloat16)
-    other = padded(extended(point_ref[...], False)).astype(jnp.bfloat16)
     high, middle, _ = thirds(inverse_ref[...])
     for s in range(0, count, CHUNK):
         rows = own[s:s + CHUNK, :]
@@ -310,71 +306,77 @@
         factor_ref[s:s + CHUNK, :] = (
             product(cols_high, middle, ((1,), (1,))) + product(cols_middle, high, ((1,), (1,)))
         ) + product(cols_high, high, ((1,), (1,)))
-        total_ref[s:s + CHUNK, :] = tile_terms(rows, other, sent_ref[...])
     zero_ref[...] = jnp.zeros_like(zero_ref)
 
 
-def factor_of(pivots_t, points_t, inverse, sent_t):
+def factor_of(pivots_t, points_t, inverse, awaited):
     size = pivots_t.shape[1]
-    count = points_t.shape[1]
+    depth, count = points_t.shape
     return pl.pallas_call(
         factor_kernel,
         out_shape=(
             jax.ShapeDtypeStruct((count, size), jnp.float32),
-            jax.ShapeDtypeStruct((count, sent_t.shape[0]), jnp.float32),
-            pltpu.VMEM(sent_t.shape, sent_t.dtype),
+            pltpu.VMEM((depth, count), jnp.bfloat16),
         ),
-        in_specs=in_vmem(4),
-        out_specs=tuple(in_vmem(3)),
+        in_specs=in_vmem(3) + [pl.BlockSpec(memory_space=pl.ANY)],
+        out_specs=tuple(in_vmem(2)),
         compiler_params=pltpu.CompilerParams(vmem_limit_bytes=32 * 1024 * 1024),
         cost_estimate=pl.CostEstimate(
-            flops=6 * count * size * size + 4 * count * count * LANES,
+            flops=6 * count * size * size,
             bytes_accessed=6 * count * size,
-            transcendentals=count * (size + count),
+            transcendentals=count * size,
         ),
         name="factor",
-    )(pivots_t, points_t, inverse, sent_t)
-
-
-def band_kernel(parts, last, *refs):
-    refs = list(refs)
-    own_ref = refs.pop(0)
+    )(pivots_t, points_t, inverse, awaited)
+
+
+def band_kernel(pieces, first, last, *refs):
+    own_ref = refs[0]
     depth, count = own_ref.shape
-    pieces = []
-    for part in parts:
-        if part == 2:
-            pieces.append((refs.pop(0)[...], refs.pop(0)[...]))
-        else:
-            stacked = refs.pop(0)
-            pieces.append((stacked[:depth, :], stacked[depth:, :]))
-    before_ref = refs.pop(0)
+    rest = list(refs[1 + max(place for piece in pieces for place, _ in piece):])
+    before_ref = None if first else rest.pop(0)
     own = jnp.transpose(padded(extended(own_ref[...], True))).astype(jnp.bfloat16)
-    others = [padded(extended(block, False)).astype(jnp.bfloat16) for block, _ in pieces]
+    blocks = []
+    for (point_at, point_row), (probe_at, probe_row) in pieces:
+        points = refs[point_at][point_row:point_row + depth, :]
+        blocks.append((padded(extended(points, False)).astype(jnp.bfloat16), refs[probe_at], probe_row))
     for s in range(0, count, CHUNK):
-        total = before_ref[s:s + CHUNK, :]
-        for other, (_, probes) in zip(others, pieces):
-            total = total + tile_terms(own[s:s + CHUNK, :], other, probes)
+        total = None if first else before_ref[s:s + CHUNK, :]
+        for other, probe_ref, probe_row in blocks:
+            term = tile_terms(own[s:s + CHUNK, :], other, probe_ref[probe_row:, :])
+            total = term if total is None else total + term
         if last:
-            probe_ref, out_ref = refs
+            probe_ref, out_ref = rest
             scale = 1.0 / (count ** 0.5)
             out_ref[:, s:s + CHUNK] = jnp.transpose(total) * scale + noise_weight * probe_ref[:, s:s + CHUNK]
         else:
-            refs[0][s:s + CHUNK, :] = total
+            rest[0][s:s + CHUNK, :] = total
     if not last:
-        refs[1][...] = jnp.zeros_like(refs[1])
-
-
-def band_sum(own, pieces, before, probes=None):
+        rest[1][...] = jnp.zeros_like(rest[1])
+
+
+def band_sum(own, pieces, before=None, probes=None):
     depth, count = own.shape
-    width = before.shape[1]
-    last = probes is not None
-    operands = [own] + [array for piece in pieces for array in piece] + [before] + ([probes] if last else [])
+    first, last = before is None, probes is not None
+    operands = [own]
+    places = []
+    for piece in pieces:
+        place = []
+        for array, start in piece:
+            known = [i for i, operand in enumerate(operands) if operand is array]
+            if not known:
+                operands.append(array)
+            place.append((known[0] if known else len(operands) - 1, start))
+        places.append(tuple(place))
+    array, start = pieces[0][1]
+    width = array.shape[0] - start
+    operands += ([] if first else [before]) + ([probes] if last else [])
     if last:
         out_shape = jax.ShapeDtypeStruct((width, count), jnp.float32)
     else:
-        out_shape = (jax.ShapeDtypeStruct(before.shape, jnp.float32), pltpu.VMEM((width, count), jnp.bfloat16))
+        out_shape = (jax.ShapeDtypeStruct((count, width), jnp.float32), pltpu.VMEM((width, count), jnp.bfloat16))
     return pl.pallas_call(
-        functools.partial(band_kernel, tuple(len(piece) for piece in pieces), last),
+        functools.partial(band_kernel, tuple(places), first, last),
         out_shape=out_shape,
         in_specs=in_vmem(len(operands)),
         out_specs=in_vmem(1)[0] if last else tuple(in_vmem(2)),
@@ -391,22 +393,33 @@
 def shards(points, pivots, owners, coeffs, noise):
     tall = lax.axis_size("gy") == BAND + 1
     points = points.T
-    pivot_points = spread(pick(owners, pivots, points))[-1]
-    near = column_blocks(points) if tall else direct_blocks(points)
+    depth = points.shape[0]
+    pivot_points = spread(pick(owners, pivots, points))
+    if tall:
+        far = swapped(points, "gy", 2)
+        pair = swapped(jnp.concatenate([points, far], axis=0), "gy", 1)
+        near = [far, pair]
+    else:
+        near = direct_blocks(points)
 
     inverse, probes, sent = probes_of(pivot_points, points, coeffs.T, noise.T, near)
-    factor, total, zeros = factor_of(pivot_points, points, inverse, sent)
+    total, zeros = band_sum(points, [((points, 0), (sent, 0))])
     if tall:
-        two = swapped(sent, "gy", 2) + zeros
+        two = swapped(sent, "gy", 2)
         one = swapped(sent, "gy", 1) + zeros
+        factor, zeros = factor_of(pivot_points, points, inverse, one)
+        two = two + zeros
+        cross_one = cross(jnp.concatenate([pair[:depth], one], axis=0), 1)
         three = swapped(two, "gy", 1)
-        crossed = [cross(jnp.concatenate([near[i], probe], axis=0), i + 1) for i, probe in enumerate((one, two))]
-        total, zeros = band_sum(points, [(near[0], one), (near[1], two)], total)
-        crossed.append(cross(jnp.concatenate([near[2], three + zeros], axis=0), 3))
-        total, _ = band_sum(points, [(crossed[0],), (crossed[1],), (near[2], three)], total)
-        kernel_probes = band_sum(points, [(crossed[2],)], total, probes)
+        cross_two = cross(jnp.concatenate([far, two], axis=0), 2)
+        total, zeros = band_sum(points, [((pair, 0), (one, 0)), ((far, 0), (two, 0))], total)
+        cross_three = cross(jnp.concatenate([pair[depth:], three + zeros], axis=0), 3)
+        crossed = [((stacked, 0), (stacked, depth)) for stacked in (cross_one, cross_two, cross_three)]
+        total, _ = band_sum(points, crossed[:2] + [((pair, depth), (three, 0))], total)
+        kernel_probes = band_sum(points, crossed[2:], total, probes)
     else:
-        pieces = list(zip(near, direct_blocks(sent)))
+        factor, _ = factor_of(pivot_points, points, inverse, zeros)
+        pieces = [((block, 0), (probe, 0)) for block, probe in zip(near, direct_blocks(sent))]
         total, _ = band_sum(points, pieces[:3], total)
         kernel_probes = band_sum(points, pieces[3:], total, probes)
     return (kernel_probes.T, factor)

time: 56.9 us -> 55.4 us (0.974)
  starting transfers between devices: 19.8 us -> 18.4 us
  waiting for transfers between devices: 15.1 us -> 14.5 us
    ppermute x11 -> x12, starting transfers between devices: 19.1 us -> 17.2 us  [swapped(): lax.ppermute(value, axis, [(i ^ bit, i) for i in range(lax.axis_size(axis...]
    pallas_call x3 -> x4, Pallas kernels: 8.21 us -> 9.64 us  [band_sum(): pl.pallas_call(functools.partial(band_kernel, tuple(places), first, last)...]
    pallas_call x1, Pallas kernels: 3.03 us -> 1.91 us  [factor_of(): pl.pallas_call(factor_kernel, out_shape=(jax.ShapeDtypeStruct((count, siz...]
    ppermute x11 -> x12, waiting for transfers between devices: 12.2 us -> 11.8 us  [swapped(): lax.ppermute(value, axis, [(i ^ bit, i) for i in range(lax.axis_size(axis...]
  transfers between devices with their start and end apart: 14 -> 15, of which waited for: 9 -> 10; matrix products, arithmetic and copies ran while one was open for 0% -> 0% of each run, Pallas kernels for 18% -> 19%
where the time goes in v11:
time: 55.4 us; the launch traced here: 55.2 us
  Pallas kernels  21.2 us (38%)
  starting transfers between devices  18.4 us (33%)
  waiting for transfers between devices  14.5 us (26%)
  between operations  0.79 us (1%)
    ppermute x12, starting transfers between devices, swapped(): lax.ppermute(value, axis, [(i ^ bit, i) for i in range(lax.axis_size(axis...  17.2 us
    ppermute x12, waiting for transfers between devices, swapped(): lax.ppermute(value, axis, [(i ^ bit, i) for i in range(lax.axis_size(axis...  11.8 us
    pallas_call x4, Pallas kernels, band_sum(): pl.pallas_call(functools.partial(band_kernel, tuple(places), first, last)...  9.64 us
    pallas_call x1, Pallas kernels, probes_of(): pl.pallas_call(probe_kernel, out_shape=(jax.ShapeDtypeStruct((size, size)...  8.52 us
    ppermute x3, waiting for transfers between devices, cross(): return lax.ppermute(piece, ('gx', 'gy'), pairs)  2.74 us
    pallas_call x1, Pallas kernels, factor_of(): pl.pallas_call(factor_kernel, out_shape=(jax.ShapeDtypeStruct((count, siz...  1.91 us
    ppermute x3, starting transfers between devices, cross(): return lax.ppermute(piece, ('gx', 'gy'), pairs)  1.18 us
    pallas_call x1, Pallas kernels, pick(): pl.pallas_call(pick_kernel, out_shape=pltpu.VMEM((points_t.shape[0], 2 *...  1.17 us
  transfers between devices with their start and end apart: 15, of which 10 were waited for; matrix products, arithmetic and copies ran while one was open for 0% of the time, Pallas kernels for 19%

profile of v11, /device:TPU:0, one launch (start us, length us, event | category | flops | bytes accessed | tf_op | source)
XLA Modules:
  0.0 55.2 jit_solution(11652066104199519994)
XLA Ops:
  0.6 4.1 %collective-permute-start = (bf16[64,1024]{1,0:T(8,128)(2,1)}, bf16[64,1024]{1,0:T(8,128)(2,1)S(1)}, u32[]{:S(2)}, u32[]{:S(2)}) collective-permute-start(bf16[64,1024]{1,0:T(8,128)(2,1)} %bitcast.4), channel_id=1, source_target_pairs={{2,0},{3,1},{0,2},{1,3},{6,4},{7,5},{4,6},{5,7},{10,8},{11,9},{8,1... | collective-permute-start | bytes 393224 | tf_op jit(solution)/shard_map/ppermute | solution.py:30
  4.7 1.2 %pick.1 = bf16[64,256]{1,0:T(8,128)(2,1)S(1)} custom-call(s32[2]{0:T(128)} %owner_ref.1, s32[2,128]{1,0:T(2,128)} %pivot_ref.1, bf16[64,1024]{1,0:T(8,128)(2,1)} %bitcast.5), custom_call_target="tpu_custom_call" | custom-call | tf_op jit(solution)/shard_map/pick/pallas_call | solution.py:103
  5.9 0.1 collective-permute-start.2
  6.0 1.2 %collective-permute-done.2 = bf16[64,256]{1,0:T(8,128)(2,1)S(1)} collective-permute-done((bf16[64,256]{1,0:T(8,128)(2,1)S(1)}, bf16[64,256]{1,0:T(8,128)(2,1)S(1)}, u32[]{:S(2)}, u32[]{:S(2)}) %collective-permute-start.2) | collective-permute-done | bytes 32800 | tf_op jit(solution)/shard_map/ppermute | solution.py:30
  7.2 2.5 %collective-permute-start.5 = (bf16[64,256]{1,0:T(8,128)(2,1)S(1)}, bf16[64,256]{1,0:T(8,128)(2,1)S(1)}, u32[]{:S(2)}, u32[]{:S(2)}) collective-permute-start(bf16[64,256]{1,0:T(8,128)(2,1)S(1)} %add.30), channel_id=1, source_target_pairs={{24,0},{28,4},{16,8},{20,12},{8,16},{12,20},{0,24},{4,28},{25,1},{... | collective-permute-start | bytes 98312 | tf_op jit(solution)/shard_map/ppermute | solution.py:30
  9.7 0.5 collective-permute-start.4
  10.2 0.5 collective-permute-start.3
  10.8 0.5 collective-permute-done.refs_0_.refs_3_
  11.3 1.1 %collective-permute-start.1 = (bf16[128,1024]{1,0:T(8,128)(2,1)S(1)}, bf16[128,1024]{1,0:T(8,128)(2,1)S(1)}, u32[]{:S(2)}, u32[]{:S(2)}) collective-permute-start(bf16[128,1024]{1,0:T(8,128)(2,1)S(1)} %pad_maximum_fusion), channel_id=1, source_target_pairs={{1,0},{0,1},{3,2},{2,3},{5,4},{4,5},{7,6},{6,7},{9,8},{8,9},{11,10... | collective-permute-start | bytes 786440 | tf_op jit(solution)/shard_map/ppermute | solution.py:30
  12.4 1.2 %collective-permute-done.4 = bf16[64,256]{1,0:T(8,128)(2,1)S(1)} collective-permute-done((bf16[64,256]{1,0:T(8,128)(2,1)S(1)}, bf16[64,256]{1,0:T(8,128)(2,1)S(1)}, u32[]{:S(2)}, u32[]{:S(2)}) %collective-permute-start.4) | collective-permute-done | bytes 32800 | tf_op jit(solution)/shard_map/ppermute | solution.py:30
  13.6 0.5 collective-permute-done.3
  14.2 1.4 %collective-permute-start.8 = (bf16[64,256]{1,0:T(8,128)(2,1)S(1)}, bf16[64,256]{1,0:T(8,128)(2,1)S(1)}, u32[]{:S(2)}, u32[]{:S(2)}) collective-permute-start(bf16[64,256]{1,0:T(8,128)(2,1)S(1)} %add_add_fusion.1), channel_id=1, source_target_pairs={{3,0},{2,1},{1,2},{0,3},{7,4},{6,5},{5,6},{4,7},{11,8},{10,9},{9,1... | collective-permute-start | bytes 98312 | tf_op jit(solution)/shard_map/ppermute | solution.py:30
  15.6 1.7 %collective-permute-start.7 = (bf16[64,256]{1,0:T(8,128)(2,1)S(1)}, bf16[64,256]{1,0:T(8,128)(2,1)S(1)}, u32[]{:S(2)}, u32[]{:S(2)}) collective-permute-start(bf16[64,256]{1,0:T(8,128)(2,1)S(1)} %add_add_fusion.1), channel_id=1, source_target_pairs={{2,0},{3,1},{0,2},{1,3},{6,4},{7,5},{4,6},{5,7},{10,8},{11,9},{8,1... | collective-permute-start | bytes 98312 | tf_op jit(solution)/shard_map/ppermute | solution.py:30
  17.3 1.3 %collective-permute-start.6 = (bf16[64,256]{1,0:T(8,128)(2,1)S(1)}, bf16[64,256]{1,0:T(8,128)(2,1)S(1)}, u32[]{:S(2)}, u32[]{:S(2)}) collective-permute-start(bf16[64,256]{1,0:T(8,128)(2,1)S(1)} %add_add_fusion.1), channel_id=1, source_target_pairs={{1,0},{0,1},{3,2},{2,3},{5,4},{4,5},{7,6},{6,7},{9,8},{8,9},{11,10... | collective-permute-start | bytes 98312 | tf_op jit(solution)/shard_map/ppermute | solution.py:30
  18.6 4.1 %collective-permute-done.8 = bf16[64,256]{1,0:T(8,128)(2,1)S(1)} collective-permute-done((bf16[64,256]{1,0:T(8,128)(2,1)S(1)}, bf16[64,256]{1,0:T(8,128)(2,1)S(1)}, u32[]{:S(2)}, u32[]{:S(2)}) %collective-permute-start.8) | collective-permute-done | bytes 32800 | tf_op jit(solution)/shard_map/ppermute | solution.py:30
  22.8 8.5 %probes.1 = (f32[256,256]{1,0:T(8,128)S(1)}, f32[64,1024]{1,0:T(8,128)S(1)}, bf16[64,1024]{1,0:T(8,128)(2,1)S(1)}) custom-call(bf16[64,256]{1,0:T(8,128)(2,1)S(1)} %add_add_fusion.pivot_ref, bf16[64,1024]{1,0:T(8,128)(2,1)S(1)} %bitcast.7, f32[64,256]{1,0:T(8,128)S(1)} %bitcast.14, f32[64,1024]{1,0:T(8,128)S(1)} %bitcast.13, ...), custom_call_target="tpu_custom_call" | custom-call | tf_op jit(solution)/shard_map/probes/pallas_call | solution.py:275
  31.3 1.1 %collective-permute-start.10 = (bf16[64,1024]{1,0:T(8,128)(2,1)S(1)}, bf16[64,1024]{1,0:T(8,128)(2,1)S(1)}, u32[]{:S(2)}, u32[]{:S(2)}) collective-permute-start(bf16[64,1024]{1,0:T(8,128)(2,1)S(1)} %get-tuple-element.12.refs_1_), channel_id=1, source_target_pairs={{1,0},{0,1},{3,2},{2,3},{5,4},{4,5},{7,6},{6,7},{9,8},{8,9},{11,10... | collective-permute-start | bytes 393224 | tf_op jit(solution)/shard_map/ppermute | solution.py:30
  32.3 2.1 %collective-permute-start.9 = (bf16[64,1024]{1,0:T(8,128)(2,1)S(1)}, bf16[64,1024]{1,0:T(8,128)(2,1)S(1)}, u32[]{:S(2)}, u32[]{:S(2)}) collective-permute-start(bf16[64,1024]{1,0:T(8,128)(2,1)S(1)} %get-tuple-element.12.refs_1_), channel_id=1, source_target_pairs={{2,0},{3,1},{0,2},{1,3},{6,4},{7,5},{4,6},{5,7},{10,8},{11,9},{8,1... | collective-permute-start | bytes 393224 | tf_op jit(solution)/shard_map/ppermute | solution.py:30
  34.5 1.4 %band_sum.4 = (f32[1024,64]{1,0:T(8,128)S(1)}, bf16[64,1024]{1,0:T(8,128)(2,1)S(1)}) custom-call(bf16[64,1024]{1,0:T(8,128)(2,1)S(1)} %bitcast.8, bf16[64,1024]{1,0:T(8,128)(2,1)S(1)} %get-tuple-element.12.refs_1_), custom_call_target="tpu_custom_call" | custom-call | flops 536870912 | bytes 524288 | tf_op jit(solution)/shard_map/band_sum/pallas_call | solution.py:378
  35.9 1.7 %collective-permute-done.10 = bf16[64,1024]{1,0:T(8,128)(2,1)S(1)} collective-permute-done((bf16[64,1024]{1,0:T(8,128)(2,1)S(1)}, bf16[64,1024]{1,0:T(8,128)(2,1)S(1)}, u32[]{:S(2)}, u32[]{:S(2)}) %collective-permute-start.10) | collective-permute-done | bytes 131104 | tf_op jit(solution)/shard_map/ppermute | solution.py:30
  37.7 0.1 collective-permute-start.13
  37.7 1.9 %factor.1 = (f32[1024,256]{1,0:T(8,128)}, bf16[64,1024]{1,0:T(8,128)(2,1)S(1)}) custom-call(bf16[64,256]{1,0:T(8,128)(2,1)S(1)} %add_add_fusion.pivot_ref, bf16[64,1024]{1,0:T(8,128)(2,1)S(1)} %bitcast.9, f32[256,256]{1,0:T(8,128)S(1)} %get-tuple-element.13.inverse_ref, bf16[64,1024]{1,0:T(8,128)(2,1)S(1)} %add.37.awaited_ref.refs_2_), custom_call_target="tpu_custom_call" | custom-call | flops 402653184 | bytes 1572864 | tf_op jit(solution)/shard_map/factor/pallas_call | solution.py:315
  39.7 0.4 collective-permute-done.9
  40.1 0.8 %collective-permute-start.11 = (bf16[64,1024]{1,0:T(8,128)(2,1)S(1)}, bf16[64,1024]{1,0:T(8,128)(2,1)S(1)}, u32[]{:S(2)}, u32[]{:S(2)}) collective-permute-start(bf16[64,1024]{1,0:T(8,128)(2,1)S(1)} %add.38.refs_4_), channel_id=1, source_target_pairs={{1,0},{0,1},{3,2},{2,3},{5,4},{4,5},{7,6},{6,7},{9,8},{8,9},{11,10... | collective-permute-start | bytes 393224 | tf_op jit(solution)/shard_map/ppermute | solution.py:30
  40.9 0.7 %collective-permute-start.14 = (bf16[128,1024]{1,0:T(8,128)(2,1)S(1)}, bf16[128,1024]{1,0:T(8,128)(2,1)S(1)}, u32[]{:S(2)}, u32[]{:S(2)}) collective-permute-start(bf16[128,1024]{1,0:T(8,128)(2,1)S(1)} %pad_maximum_fusion.3), channel_id=1, source_target_pairs={{28,0},{29,1},{6,2},{7,3},{0,4},{1,5},{10,6},{11,7},{4,8},{5,9},{1... | collective-permute-start | bytes 786440 | tf_op jit(solution)/shard_map/ppermute | solution.py:51
  41.6 2.5 %band_sum.5 = (f32[1024,64]{1,0:T(8,128)S(1)}, bf16[64,1024]{1,0:T(8,128)(2,1)S(1)}) custom-call(bf16[64,1024]{1,0:T(8,128)(2,1)S(1)} %bitcast.10, bf16[128,1024]{1,0:T(8,128)(2,1)S(1)} %collective-permute-done.1.refs_1_.refs_3_, bf16[64,1024]{1,0:T(8,128)(2,1)S(1)} %add.37.awaited_ref.refs_2_, bf16[64,1024]{1,0:T(8,128)(2,1)S(1)} %collective-permute-done.refs_0_.refs_3_, ...), custom_call_target="tpu_custom_call" | custom-call | flops 1073741824 | bytes 1572864 | tf_op jit(solution)/shard_map/band_sum/pallas_call | solution.py:378
  44.2 2.2 %collective-permute-done.11.refs_4_ = bf16[64,1024]{1,0:T(8,128)(2,1)S(1)} collective-permute-done((bf16[64,1024]{1,0:T(8,128)(2,1)S(1)}, bf16[64,1024]{1,0:T(8,128)(2,1)S(1)}, u32[]{:S(2)}, u32[]{:S(2)}) %collective-permute-start.11) | collective-permute-done | bytes 131104 | tf_op jit(solution)/shard_map/ppermute | solution.py:30
  46.4 0.4 collective-permute-start.12
  46.8 1.0 %collective-permute-done.14.refs_2_ = bf16[128,1024]{1,0:T(8,128)(2,1)S(1)} collective-permute-done((bf16[128,1024]{1,0:T(8,128)(2,1)S(1)}, bf16[128,1024]{1,0:T(8,128)(2,1)S(1)}, u32[]{:S(2)}, u32[]{:S(2)}) %collective-permute-start.14) | collective-permute-done | bytes 262176 | tf_op jit(solution)/shard_map/ppermute | solution.py:51
  47.8 3.6 %band_sum.6 = (f32[1024,64]{1,0:T(8,128)S(1)}, bf16[64,1024]{1,0:T(8,128)(2,1)}) custom-call(bf16[64,1024]{1,0:T(8,128)(2,1)S(1)} %bitcast.11, bf16[128,1024]{1,0:T(8,128)(2,1)S(1)} %collective-permute-done.13.refs_1_, bf16[128,1024]{1,0:T(8,128)(2,1)S(1)} %collective-permute-done.14.refs_2_, bf16[128,1024]{1,0:T(8,128)(2,1)S(1)} %collective-permute-done.1.refs_1_.refs_3_, ...), custom_call_target="tpu_custom_call" | custom-call | flops 1610612736 | bytes 1572864 | tf_op jit(solution)/shard_map/band_sum/pallas_call | solution.py:378
  51.4 1.7 %collective-permute-done.12.refs_1_ = bf16[128,1024]{1,0:T(8,128)(2,1)S(1)} collective-permute-done((bf16[128,1024]{1,0:T(8,128)(2,1)S(1)}, bf16[128,1024]{1,0:T(8,128)(2,1)S(1)}, u32[]{:S(2)}, u32[]{:S(2)}) %collective-permute-start.12) | collective-permute-done | bytes 262176 | tf_op jit(solution)/shard_map/ppermute | solution.py:51
  53.1 2.1 %band_sum.7 = f32[64,1024]{1,0:T(8,128)} custom-call(bf16[64,1024]{1,0:T(8,128)(2,1)S(1)} %bitcast.12, bf16[128,1024]{1,0:T(8,128)(2,1)S(1)} %collective-permute-done.12.refs_1_, f32[1024,64]{1,0:T(8,128)S(1)} %get-tuple-element.19.refs_2_, f32[64,1024]{1,0:T(8,128)S(1)} %get-tuple-element.20.refs_3_), custom_call_target="tpu_custom_call" | custom-call | flops 536870912 | bytes 1048576 | tf_op jit(solution)/shard_map/band_sum/pallas_call | solution.py:378
  (22 shorter events, 0.3 us)
Async XLA Ops:
  0.6 10.6 %copy-start = (bf16[1024,64]{0,1:T(8,128)(2,1)S(1)}, bf16[1024,64]{0,1:T(8,128)(2,1)}, u32[]{:S(2)}) copy-start(bf16[1024,64]{0,1:T(8,128)(2,1)} %param.5) | copy-start | bytes 393220
  0.6 10.6 %collective-permute-start = (bf16[64,1024]{1,0:T(8,128)(2,1)}, bf16[64,1024]{1,0:T(8,128)(2,1)S(1)}, u32[]{:S(2)}, u32[]{:S(2)}) collective-permute-start(bf16[64,1024]{1,0:T(8,128)(2,1)} %bitcast.4), channel_id=1, source_target_pairs={{2,0},{3,1},{0,2},{1,3},{6,4},{7,5},{4,6},{5,7},{10,8},{11,9},{8,1... | collective-permute-start | bytes 393224 | tf_op jit(solution)/shard_map/ppermute | solution.py:30
  5.9 1.3 %collective-permute-start.2 = (bf16[64,256]{1,0:T(8,128)(2,1)S(1)}, bf16[64,256]{1,0:T(8,128)(2,1)S(1)}, u32[]{:S(2)}, u32[]{:S(2)}) collective-permute-start(bf16[64,256]{1,0:T(8,128)(2,1)S(1)} %pick.1), channel_id=1, source_target_pairs={{4,0},{0,4},{12,8},{8,12},{20,16},{16,20},{28,24},{24,28},{5,1},{1... | collective-permute-start | bytes 98312 | tf_op jit(solution)/shard_map/ppermute | solution.py:30
  7.2 5.2 %collective-permute-start.5 = (bf16[64,256]{1,0:T(8,128)(2,1)S(1)}, bf16[64,256]{1,0:T(8,128)(2,1)S(1)}, u32[]{:S(2)}, u32[]{:S(2)}) collective-permute-start(bf16[64,256]{1,0:T(8,128)(2,1)S(1)} %add.30), channel_id=1, source_target_pairs={{24,0},{28,4},{16,8},{20,12},{8,16},{12,20},{0,24},{4,28},{25,1},{... | collective-permute-start | bytes 98312 | tf_op jit(solution)/shard_map/ppermute | solution.py:30
  9.7 3.9 %collective-permute-start.4 = (bf16[64,256]{1,0:T(8,128)(2,1)S(1)}, bf16[64,256]{1,0:T(8,128)(2,1)S(1)}, u32[]{:S(2)}, u32[]{:S(2)}) collective-permute-start(bf16[64,256]{1,0:T(8,128)(2,1)S(1)} %add.30), channel_id=1, source_target_pairs={{16,0},{20,4},{24,8},{28,12},{0,16},{4,20},{8,24},{12,28},{17,1},{... | collective-permute-start | bytes 98312 | tf_op jit(solution)/shard_map/ppermute | solution.py:30
  10.2 3.9 %collective-permute-start.3 = (bf16[64,256]{1,0:T(8,128)(2,1)S(1)}, bf16[64,256]{1,0:T(8,128)(2,1)S(1)}, u32[]{:S(2)}, u32[]{:S(2)}) collective-permute-start(bf16[64,256]{1,0:T(8,128)(2,1)S(1)} %add.30), channel_id=1, source_target_pairs={{8,0},{12,4},{0,8},{4,12},{24,16},{28,20},{16,24},{20,28},{9,1},{1... | collective-permute-start | bytes 98312 | tf_op jit(solution)/shard_map/ppermute | solution.py:30
  11.3 11.5 %copy-start.1 = (f32[1024,64]{0,1:T(8,128)S(1)}, f32[1024,64]{0,1:T(8,128)}, u32[]{:S(2)}) copy-start(f32[1024,64]{0,1:T(8,128)} %param.9) | copy-start | bytes 786436
  11.3 11.4 %collective-permute-start.1 = (bf16[128,1024]{1,0:T(8,128)(2,1)S(1)}, bf16[128,1024]{1,0:T(8,128)(2,1)S(1)}, u32[]{:S(2)}, u32[]{:S(2)}) collective-permute-start(bf16[128,1024]{1,0:T(8,128)(2,1)S(1)} %pad_maximum_fusion), channel_id=1, source_target_pairs={{1,0},{0,1},{3,2},{2,3},{5,4},{4,5},{7,6},{6,7},{9,8},{8,9},{11,10... | collective-permute-start | bytes 786440 | tf_op jit(solution)/shard_map/ppermute | solution.py:30
  14.2 8.6 %copy-start.2 = (f32[256,64]{0,1:T(8,128)S(1)}, f32[256,64]{0,1:T(8,128)}, u32[]{:S(2)}) copy-start(f32[256,64]{0,1:T(8,128)} %param.8) | copy-start | bytes 196612
  14.2 8.5 %collective-permute-start.8 = (bf16[64,256]{1,0:T(8,128)(2,1)S(1)}, bf16[64,256]{1,0:T(8,128)(2,1)S(1)}, u32[]{:S(2)}, u32[]{:S(2)}) collective-permute-start(bf16[64,256]{1,0:T(8,128)(2,1)S(1)} %add_add_fusion.1), channel_id=1, source_target_pairs={{3,0},{2,1},{1,2},{0,3},{7,4},{6,5},{5,6},{4,7},{11,8},{10,9},{9,1... | collective-permute-start | bytes 98312 | tf_op jit(solution)/shard_map/ppermute | solution.py:30
  15.6 7.1 %collective-permute-start.7 = (bf16[64,256]{1,0:T(8,128)(2,1)S(1)}, bf16[64,256]{1,0:T(8,128)(2,1)S(1)}, u32[]{:S(2)}, u32[]{:S(2)}) collective-permute-start(bf16[64,256]{1,0:T(8,128)(2,1)S(1)} %add_add_fusion.1), channel_id=1, source_target_pairs={{2,0},{3,1},{0,2},{1,3},{6,4},{7,5},{4,6},{5,7},{10,8},{11,9},{8,1... | collective-permute-start | bytes 98312 | tf_op jit(solution)/shard_map/ppermute | solution.py:30
  17.3 5.4 %collective-permute-start.6 = (bf16[64,256]{1,0:T(8,128)(2,1)S(1)}, bf16[64,256]{1,0:T(8,128)(2,1)S(1)}, u32[]{:S(2)}, u32[]{:S(2)}) collective-permute-start(bf16[64,256]{1,0:T(8,128)(2,1)S(1)} %add_add_fusion.1), channel_id=1, source_target_pairs={{1,0},{0,1},{3,2},{2,3},{5,4},{4,5},{7,6},{6,7},{9,8},{8,9},{11,10... | collective-permute-start | bytes 98312 | tf_op jit(solution)/shard_map/ppermute | solution.py:30
  31.3 6.3 %collective-permute-start.10 = (bf16[64,1024]{1,0:T(8,128)(2,1)S(1)}, bf16[64,1024]{1,0:T(8,128)(2,1)S(1)}, u32[]{:S(2)}, u32[]{:S(2)}) collective-permute-start(bf16[64,1024]{1,0:T(8,128)(2,1)S(1)} %get-tuple-element.12.refs_1_), channel_id=1, source_target_pairs={{1,0},{0,1},{3,2},{2,3},{5,4},{4,5},{7,6},{6,7},{9,8},{8,9},{11,10... | collective-permute-start | bytes 393224 | tf_op jit(solution)/shard_map/ppermute | solution.py:30
  32.3 7.7 %collective-permute-start.9 = (bf16[64,1024]{1,0:T(8,128)(2,1)S(1)}, bf16[64,1024]{1,0:T(8,128)(2,1)S(1)}, u32[]{:S(2)}, u32[]{:S(2)}) collective-permute-start(bf16[64,1024]{1,0:T(8,128)(2,1)S(1)} %get-tuple-element.12.refs_1_), channel_id=1, source_target_pairs={{2,0},{3,1},{0,2},{1,3},{6,4},{7,5},{4,6},{5,7},{10,8},{11,9},{8,1... | collective-permute-start | bytes 393224 | tf_op jit(solution)/shard_map/ppermute | solution.py:30
  37.7 9.1 %collective-permute-start.13 = (bf16[128,1024]{1,0:T(8,128)(2,1)S(1)}, bf16[128,1024]{1,0:T(8,128)(2,1)S(1)}, u32[]{:S(2)}, u32[]{:S(2)}) collective-permute-start(bf16[128,1024]{1,0:T(8,128)(2,1)S(1)} %pad_maximum_fusion.2), channel_id=1, source_target_pairs={{28,0},{5,1},{30,2},{7,3},{0,4},{9,5},{2,6},{11,7},{4,8},{13,9},{6... | collective-permute-start | bytes 786440 | tf_op jit(solution)/shard_map/ppermute | solution.py:51
  40.1 6.2 %collective-permute-start.11 = (bf16[64,1024]{1,0:T(8,128)(2,1)S(1)}, bf16[64,1024]{1,0:T(8,128)(2,1)S(1)}, u32[]{:S(2)}, u32[]{:S(2)}) collective-permute-start(bf16[64,1024]{1,0:T(8,128)(2,1)S(1)} %add.38.refs_4_), channel_id=1, source_target_pairs={{1,0},{0,1},{3,2},{2,3},{5,4},{4,5},{7,6},{6,7},{9,8},{8,9},{11,10... | collective-permute-start | bytes 393224 | tf_op jit(solution)/shard_map/ppermute | solution.py:30
  40.9 6.9 %collective-permute-start.14 = (bf16[128,1024]{1,0:T(8,128)(2,1)S(1)}, bf16[128,1024]{1,0:T(8,128)(2,1)S(1)}, u32[]{:S(2)}, u32[]{:S(2)}) collective-permute-start(bf16[128,1024]{1,0:T(8,128)(2,1)S(1)} %pad_maximum_fusion.3), channel_id=1, source_target_pairs={{28,0},{29,1},{6,2},{7,3},{0,4},{1,5},{10,6},{11,7},{4,8},{5,9},{1... | collective-permute-start | bytes 786440 | tf_op jit(solution)/shard_map/ppermute | solution.py:51
  46.4 6.7 %collective-permute-start.12 = (bf16[128,1024]{1,0:T(8,128)(2,1)S(1)}, bf16[128,1024]{1,0:T(8,128)(2,1)S(1)}, u32[]{:S(2)}, u32[]{:S(2)}) collective-permute-start(bf16[128,1024]{1,0:T(8,128)(2,1)S(1)} %pad_maximum_fusion.1), channel_id=1, source_target_pairs={{28,0},{29,1},{6,2},{7,3},{0,4},{1,5},{10,6},{11,7},{4,8},{5,9},{1... | collective-permute-start | bytes 786440 | tf_op jit(solution)/shard_map/ppermute | solution.py:51

commit v12 on v11

--- a/solution.py
+++ b/solution.py
@@ -15,6 +15,8 @@
 LANES = 128
 EXTRA = 16
 CHUNK = 256
+SHORT = pl.CostEstimate(flops=1, bytes_accessed=1, transcendentals=0)
+LONG = pl.CostEstimate(flops=1 << 34, bytes_accessed=1, transcendentals=0)
 
 
 jitter = 0.1
@@ -31,7 +33,7 @@
 
 
 def spread(value):
-    for axis in ("gx", "gy"):
+    for axis in ("gy", "gx"):
         count = lax.axis_size(axis)
         bit = 1
         while bit < count:
@@ -39,6 +41,10 @@
             value = sum((swapped(value, axis, bit * k) for k in range(1, wide)), value)
             bit *= wide
     return value
+
+
+def zero_like(value):
+    return jnp.minimum(jnp.abs(value), 0)
 
 
 def cross(piece, bits):
@@ -282,6 +288,7 @@
         in_specs=in_vmem(4) + [pl.BlockSpec(memory_space=pl.ANY)] * len(awaited),
         out_specs=tuple(in_vmem(3)),
         scratch_shapes=[pltpu.VMEM((size, count), jnp.bfloat16)] * 3,
+        cost_estimate=LONG,
         compiler_params=pltpu.CompilerParams(vmem_limit_bytes=32 * 1024 * 1024),
         name="probes",
     )(pivots_t, points_t, coeffs_t, noise_t, *awaited)
@@ -321,11 +328,7 @@
         in_specs=in_vmem(3) + [pl.BlockSpec(memory_space=pl.ANY)],
         out_specs=tuple(in_vmem(2)),
         compiler_params=pltpu.CompilerParams(vmem_limit_bytes=32 * 1024 * 1024),
-        cost_estimate=pl.CostEstimate(
-            flops=6 * count * size * size,
-            bytes_accessed=6 * count * size,
-            transcendentals=count * size,
-        ),
+        cost_estimate=SHORT,
         name="factor",
     )(pivots_t, points_t, inverse, awaited)
 
@@ -381,11 +384,7 @@
         in_specs=in_vmem(len(operands)),
         out_specs=in_vmem(1)[0] if last else tuple(in_vmem(2)),
         compiler_params=pltpu.CompilerParams(vmem_limit_bytes=32 * 1024 * 1024),
-        cost_estimate=pl.CostEstimate(
-            flops=len(pieces) * 4 * count * count * LANES,
-            bytes_accessed=4 * count * width * len(operands),
-            transcendentals=len(pieces) * count * count,
-        ),
+        cost_estimate=SHORT,
         name="band_sum",
     )(*operands)
 
@@ -398,6 +397,8 @@
     if tall:
         far = swapped(points, "gy", 2)
         pair = swapped(jnp.concatenate([points, far], axis=0), "gy", 1)
+        crossing_one = cross(pair[:depth], 1)
+        crossing_pair = cross(jnp.concatenate([far, pair[depth:]], axis=0), 2)
         near = [far, pair]
     else:
         near = direct_blocks(points)
@@ -405,18 +406,19 @@
     inverse, probes, sent = probes_of(pivot_points, points, coeffs.T, noise.T, near)
     total, zeros = band_sum(points, [((points, 0), (sent, 0))])
     if tall:
-        two = swapped(sent, "gy", 2)
-        one = swapped(sent, "gy", 1) + zeros
+        leaving = sent + zero_like(crossing_one) + zero_like(crossing_pair[:depth])
+        two = swapped(leaving, "gy", 2)
+        one = swapped(leaving, "gy", 1) + zeros
         factor, zeros = factor_of(pivot_points, points, inverse, one)
         two = two + zeros
-        cross_one = cross(jnp.concatenate([pair[:depth], one], axis=0), 1)
         three = swapped(two, "gy", 1)
-        cross_two = cross(jnp.concatenate([far, two], axis=0), 2)
+        cross_one, cross_two = cross(one, 1), cross(two, 2)
         total, zeros = band_sum(points, [((pair, 0), (one, 0)), ((far, 0), (two, 0))], total)
-        cross_three = cross(jnp.concatenate([pair[depth:], three + zeros], axis=0), 3)
-        crossed = [((stacked, 0), (stacked, depth)) for stacked in (cross_one, cross_two, cross_three)]
-        total, _ = band_sum(points, crossed[:2] + [((pair, depth), (three, 0))], total)
-        kernel_probes = band_sum(points, crossed[2:], total, probes)
+        three = three + zeros
+        cross_three = cross(three, 3)
+        pieces = [((crossing_one, 0), (cross_one, 0)), ((crossing_pair, 0), (cross_two, 0)), ((pair, depth), (three, 0))]
+        total, _ = band_sum(points, pieces, total)
+        kernel_probes = band_sum(points, [((crossing_pair, depth), (cross_three, 0))], total, probes)
     else:
         factor, _ = factor_of(pivot_points, points, inverse, zeros)
         pieces = [((block, 0), (probe, 0)) for block, probe in zip(near, direct_blocks(sent))]

time: 55.4 us -> 59 us (1.065)
  waiting for transfers between devices: 14.5 us -> 18.3 us
    ppermute x12, waiting for transfers between devices: 11.8 us -> 16.6 us  [swapped(): lax.ppermute(value, axis, [(i ^ bit, i) for i in range(lax.axis_size(axis...]
    ppermute x12, starting transfers between devices: 17.2 us -> 16 us  [swapped(): lax.ppermute(value, axis, [(i ^ bit, i) for i in range(lax.axis_size(axis...]
    ppermute x3 -> x5, waiting for transfers between devices: 2.74 us -> 1.7 us  [cross(): return lax.ppermute(piece, ('gx', 'gy'), pairs)]
    ppermute x3 -> x5, starting transfers between devices: 1.18 us -> 2.12 us  [cross(): return lax.ppermute(piece, ('gx', 'gy'), pairs)]
  transfers between devices with their start and end apart: 15 -> 17, of which waited for: 10 -> 11; matrix products, arithmetic and copies ran while one was open for 0% -> 0% of each run, Pallas kernels for 19% -> 31%
where the time goes in v12:
time: 59 us; the launch traced here: 58.8 us
  Pallas kernels  21.3 us (36%)
  waiting for transfers between devices  18.3 us (31%)
  starting transfers between devices  18.1 us (31%)
  between operations  0.84 us (1%)
    ppermute x12, waiting for transfers between devices, swapped(): lax.ppermute(value, axis, [(i ^ bit, i) for i in range(lax.axis_size(axis...  16.6 us
    ppermute x12, starting transfers between devices, swapped(): lax.ppermute(value, axis, [(i ^ bit, i) for i in range(lax.axis_size(axis...  16 us
    pallas_call x4, Pallas kernels, band_sum(): pl.pallas_call(functools.partial(band_kernel, tuple(places), first, last)...  9.64 us
    pallas_call x1, Pallas kernels, probes_of(): pl.pallas_call(probe_kernel, out_shape=(jax.ShapeDtypeStruct((size, size)...  8.52 us
    ppermute x5, starting transfers between devices, cross(): return lax.ppermute(piece, ('gx', 'gy'), pairs)  2.12 us
    pallas_call x1, Pallas kernels, factor_of(): pl.pallas_call(factor_kernel, out_shape=(jax.ShapeDtypeStruct((count, siz...  1.91 us
    ppermute x5, waiting for transfers between devices, cross(): return lax.ppermute(piece, ('gx', 'gy'), pairs)  1.7 us
    pallas_call x1, Pallas kernels, pick(): pl.pallas_call(pick_kernel, out_shape=pltpu.VMEM((points_t.shape[0], 2 *...  1.2 us
  transfers between devices with their start and end apart: 17, of which 11 were waited for; matrix products, arithmetic and copies ran while one was open for 0% of the time, Pallas kernels for 31%

profile of v12, /device:TPU:0, one launch (start us, length us, event | category | flops | bytes accessed | tf_op | source)
XLA Modules:
  0.0 58.8 jit_solution(5845026214715172364)
XLA Ops:
  0.6 1.2 %pick.1 = bf16[64,256]{1,0:T(8,128)(2,1)S(1)} custom-call(s32[2]{0:T(128)} %owner_ref.1, s32[2,128]{1,0:T(2,128)} %pivot_ref.1, bf16[64,1024]{1,0:T(8,128)(2,1)} %bitcast.4), custom_call_target="tpu_custom_call" | custom-call | tf_op jit(solution)/shard_map/pick/pallas_call | solution.py:109
  1.8 3.1 %collective-permute-start.3 = (bf16[64,256]{1,0:T(8,128)(2,1)S(1)}, bf16[64,256]{1,0:T(8,128)(2,1)S(1)}, u32[]{:S(2)}, u32[]{:S(2)}) collective-permute-start(bf16[64,256]{1,0:T(8,128)(2,1)S(1)} %pick.1), channel_id=1, source_target_pairs={{1,0},{0,1},{3,2},{2,3},{5,4},{4,5},{7,6},{6,7},{9,8},{8,9},{11,10... | collective-permute-start | bytes 98312 | tf_op jit(solution)/shard_map/ppermute | solution.py:32
  4.9 2.6 %collective-permute-start.4 = (bf16[64,256]{1,0:T(8,128)(2,1)S(1)}, bf16[64,256]{1,0:T(8,128)(2,1)S(1)}, u32[]{:S(2)}, u32[]{:S(2)}) collective-permute-start(bf16[64,256]{1,0:T(8,128)(2,1)S(1)} %pick.1), channel_id=1, source_target_pairs={{2,0},{3,1},{0,2},{1,3},{6,4},{7,5},{4,6},{5,7},{10,8},{11,9},{8,1... | collective-permute-start | bytes 98312 | tf_op jit(solution)/shard_map/ppermute | solution.py:32
  7.5 1.9 %collective-permute-start = (bf16[64,1024]{1,0:T(8,128)(2,1)S(1)}, bf16[64,1024]{1,0:T(8,128)(2,1)S(1)}, u32[]{:S(2)}, u32[]{:S(2)}) collective-permute-start(bf16[64,1024]{1,0:T(8,128)(2,1)S(1)} %bitcast.5), channel_id=1, source_target_pairs={{2,0},{3,1},{0,2},{1,3},{6,4},{7,5},{4,6},{5,7},{10,8},{11,9},{8,1... | collective-permute-start | bytes 393224 | tf_op jit(solution)/shard_map/ppermute | solution.py:32
  9.4 0.9 %collective-permute-done.4 = bf16[64,256]{1,0:T(8,128)(2,1)S(1)} collective-permute-done((bf16[64,256]{1,0:T(8,128)(2,1)S(1)}, bf16[64,256]{1,0:T(8,128)(2,1)S(1)}, u32[]{:S(2)}, u32[]{:S(2)}) %collective-permute-start.4) | collective-permute-done | bytes 32800 | tf_op jit(solution)/shard_map/ppermute | solution.py:32
  10.4 3.0 %collective-permute-done.5 = bf16[64,256]{1,0:T(8,128)(2,1)S(1)} collective-permute-done((bf16[64,256]{1,0:T(8,128)(2,1)S(1)}, bf16[64,256]{1,0:T(8,128)(2,1)S(1)}, u32[]{:S(2)}, u32[]{:S(2)}) %collective-permute-start.5) | collective-permute-done | bytes 32800 | tf_op jit(solution)/shard_map/ppermute | solution.py:32
  13.4 0.1 collective-permute-start.6
  13.5 3.5 %collective-permute-done.refs_0_.refs_3_ = bf16[64,1024]{1,0:T(8,128)(2,1)S(1)} collective-permute-done((bf16[64,1024]{1,0:T(8,128)(2,1)S(1)}, bf16[64,1024]{1,0:T(8,128)(2,1)S(1)}, u32[]{:S(2)}, u32[]{:S(2)}) %collective-permute-start) | collective-permute-done | bytes 131104 | tf_op jit(solution)/shard_map/ppermute | solution.py:32
  17.0 0.1 collective-permute-start.1
  17.1 1.6 %collective-permute-start.7 = (bf16[64,256]{1,0:T(8,128)(2,1)S(1)}, bf16[64,256]{1,0:T(8,128)(2,1)S(1)}, u32[]{:S(2)}, u32[]{:S(2)}) collective-permute-start(bf16[64,256]{1,0:T(8,128)(2,1)S(1)} %add.39), channel_id=1, source_target_pairs={{8,0},{12,4},{0,8},{4,12},{24,16},{28,20},{16,24},{20,28},{9,1},{1... | collective-permute-start | bytes 98312 | tf_op jit(solution)/shard_map/ppermute | solution.py:32
  18.7 1.5 %collective-permute-start.8 = (bf16[64,256]{1,0:T(8,128)(2,1)S(1)}, bf16[64,256]{1,0:T(8,128)(2,1)S(1)}, u32[]{:S(2)}, u32[]{:S(2)}) collective-permute-start(bf16[64,256]{1,0:T(8,128)(2,1)S(1)} %add.39), channel_id=1, source_target_pairs={{16,0},{20,4},{24,8},{28,12},{0,16},{4,20},{8,24},{12,28},{17,1},{... | collective-permute-start | bytes 98312 | tf_op jit(solution)/shard_map/ppermute | solution.py:32
  20.2 0.5 collective-permute-start.9
  20.7 0.4 collective-permute-done.7
  21.1 1.8 %collective-permute-done.8 = bf16[64,256]{1,0:T(8,128)(2,1)S(1)} collective-permute-done((bf16[64,256]{1,0:T(8,128)(2,1)S(1)}, bf16[64,256]{1,0:T(8,128)(2,1)S(1)}, u32[]{:S(2)}, u32[]{:S(2)}) %collective-permute-start.8) | collective-permute-done | bytes 32800 | tf_op jit(solution)/shard_map/ppermute | solution.py:32
  23.0 2.1 %collective-permute-done.9 = bf16[64,256]{1,0:T(8,128)(2,1)S(1)} collective-permute-done((bf16[64,256]{1,0:T(8,128)(2,1)S(1)}, bf16[64,256]{1,0:T(8,128)(2,1)S(1)}, u32[]{:S(2)}, u32[]{:S(2)}) %collective-permute-start.9) | collective-permute-done | bytes 32800 | tf_op jit(solution)/shard_map/ppermute | solution.py:32
  25.1 0.1 collective-permute-start.2
  25.2 1.0 %collective-permute-start.10 = (bf16[64,1024]{1,0:T(8,128)(2,1)S(1)}, bf16[64,1024]{1,0:T(8,128)(2,1)S(1)}, u32[]{:S(2)}, u32[]{:S(2)}) collective-permute-start(bf16[64,1024]{1,0:T(8,128)(2,1)S(1)} %get-tuple-element.22), channel_id=1, source_target_pairs={{28,0},{5,1},{30,2},{7,3},{0,4},{9,5},{2,6},{11,7},{4,8},{13,9},{6... | collective-permute-start | bytes 393224 | tf_op jit(solution)/shard_map/ppermute | solution.py:57
  26.2 8.5 %probes.1 = (f32[256,256]{1,0:T(8,128)S(1)}, f32[64,1024]{1,0:T(8,128)S(1)}, bf16[64,1024]{1,0:T(8,128)(2,1)S(1)}) custom-call(bf16[64,256]{1,0:T(8,128)(2,1)S(1)} %add_add_fusion.pivot_ref, bf16[64,1024]{1,0:T(8,128)(2,1)S(1)} %bitcast.7, f32[64,256]{1,0:T(8,128)S(1)} %bitcast.14, f32[64,1024]{1,0:T(8,128)S(1)} %bitcast.13, ...), custom_call_target="tpu_custom_call" | custom-call | flops 17179869184 | bytes 1 | tf_op jit(solution)/shard_map/probes/pallas_call | solution.py:281
  34.8 3.7 %collective-permute-start.12 = (bf16[64,1024]{1,0:T(8,128)(2,1)S(1)}, bf16[64,1024]{1,0:T(8,128)(2,1)S(1)}, u32[]{:S(2)}, u32[]{:S(2)}) collective-permute-start(bf16[64,1024]{1,0:T(8,128)(2,1)S(1)} %fusion.1), channel_id=1, source_target_pairs={{1,0},{0,1},{3,2},{2,3},{5,4},{4,5},{7,6},{6,7},{9,8},{8,9},{11,10... | collective-permute-start | bytes 393224 | tf_op jit(solution)/shard_map/ppermute | solution.py:32
  38.5 1.0 %collective-permute-start.11 = (bf16[64,1024]{1,0:T(8,128)(2,1)S(1)}, bf16[64,1024]{1,0:T(8,128)(2,1)S(1)}, u32[]{:S(2)}, u32[]{:S(2)}) collective-permute-start(bf16[64,1024]{1,0:T(8,128)(2,1)S(1)} %fusion.1), channel_id=1, source_target_pairs={{2,0},{3,1},{0,2},{1,3},{6,4},{7,5},{4,6},{5,7},{10,8},{11,9},{8,1... | collective-permute-start | bytes 393224 | tf_op jit(solution)/shard_map/ppermute | solution.py:32
  39.5 1.4 %band_sum.4 = (f32[1024,64]{1,0:T(8,128)S(1)}, bf16[64,1024]{1,0:T(8,128)(2,1)S(1)}) custom-call(bf16[64,1024]{1,0:T(8,128)(2,1)S(1)} %bitcast.8, bf16[64,1024]{1,0:T(8,128)(2,1)S(1)} %get-tuple-element.12.refs_1_), custom_call_target="tpu_custom_call" | custom-call | flops 1 | bytes 1 | tf_op jit(solution)/shard_map/band_sum/pallas_call | solution.py:381
  40.9 1.6 %collective-permute-done.12 = bf16[64,1024]{1,0:T(8,128)(2,1)S(1)} collective-permute-done((bf16[64,1024]{1,0:T(8,128)(2,1)S(1)}, bf16[64,1024]{1,0:T(8,128)(2,1)S(1)}, u32[]{:S(2)}, u32[]{:S(2)}) %collective-permute-start.12) | collective-permute-done | bytes 131104 | tf_op jit(solution)/shard_map/ppermute | solution.py:32
  42.6 1.9 %factor.1 = (f32[1024,256]{1,0:T(8,128)}, bf16[64,1024]{1,0:T(8,128)(2,1)S(1)}) custom-call(bf16[64,256]{1,0:T(8,128)(2,1)S(1)} %add_add_fusion.pivot_ref, bf16[64,1024]{1,0:T(8,128)(2,1)S(1)} %bitcast.9, f32[256,256]{1,0:T(8,128)S(1)} %get-tuple-element.13.inverse_ref, bf16[64,1024]{1,0:T(8,128)(2,1)S(1)} %add.45.awaited_ref.refs_2_), custom_call_target="tpu_custom_call" | custom-call | flops 1 | bytes 1 | tf_op jit(solution)/shard_map/factor/pallas_call | solution.py:322
  44.5 1.8 %collective-permute-done.11 = bf16[64,1024]{1,0:T(8,128)(2,1)S(1)} collective-permute-done((bf16[64,1024]{1,0:T(8,128)(2,1)S(1)}, bf16[64,1024]{1,0:T(8,128)(2,1)S(1)}, u32[]{:S(2)}, u32[]{:S(2)}) %collective-permute-start.11) | collective-permute-done | bytes 131104 | tf_op jit(solution)/shard_map/ppermute | solution.py:32
  46.3 0.1 collective-permute-start.13
  46.4 0.9 %collective-permute-start.15 = (bf16[64,1024]{1,0:T(8,128)(2,1)S(1)}, bf16[64,1024]{1,0:T(8,128)(2,1)S(1)}, u32[]{:S(2)}, u32[]{:S(2)}) collective-permute-start(bf16[64,1024]{1,0:T(8,128)(2,1)S(1)} %add.45.awaited_ref.refs_2_), channel_id=1, source_target_pairs={{28,0},{5,1},{30,2},{7,3},{0,4},{9,5},{2,6},{11,7},{4,8},{13,9},{6... | collective-permute-start | bytes 393224 | tf_op jit(solution)/shard_map/ppermute | solution.py:57
  47.4 2.5 %band_sum.5 = (f32[1024,64]{1,0:T(8,128)S(1)}, bf16[64,1024]{1,0:T(8,128)(2,1)S(1)}) custom-call(bf16[64,1024]{1,0:T(8,128)(2,1)S(1)} %bitcast.10, bf16[128,1024]{1,0:T(8,128)(2,1)S(1)} %collective-permute-done.1.refs_1_.refs_5_, bf16[64,1024]{1,0:T(8,128)(2,1)S(1)} %add.45.awaited_ref.refs_2_, bf16[64,1024]{1,0:T(8,128)(2,1)S(1)} %collective-permute-done.refs_0_.refs_3_, ...), custom_call_target="tpu_custom_call" | custom-call | flops 1 | bytes 1 | tf_op jit(solution)/shard_map/band_sum/pallas_call | solution.py:381
  49.9 1.4 %collective-permute-done.13 = bf16[64,1024]{1,0:T(8,128)(2,1)S(1)} collective-permute-done((bf16[64,1024]{1,0:T(8,128)(2,1)S(1)}, bf16[64,1024]{1,0:T(8,128)(2,1)S(1)}, u32[]{:S(2)}, u32[]{:S(2)}) %collective-permute-start.13) | collective-permute-done | bytes 131104 | tf_op jit(solution)/shard_map/ppermute | solution.py:32
  51.4 0.3 collective-permute-done.16.refs_4_
  51.7 1.4 %collective-permute-done.15.refs_2_ = bf16[64,1024]{1,0:T(8,128)(2,1)S(1)} collective-permute-done((bf16[64,1024]{1,0:T(8,128)(2,1)S(1)}, bf16[64,1024]{1,0:T(8,128)(2,1)S(1)}, u32[]{:S(2)}, u32[]{:S(2)}) %collective-permute-start.15) | collective-permute-done | bytes 131104 | tf_op jit(solution)/shard_map/ppermute | solution.py:57
  53.1 3.6 %band_sum.6 = (f32[1024,64]{1,0:T(8,128)S(1)}, bf16[64,1024]{1,0:T(8,128)(2,1)}) custom-call(bf16[64,1024]{1,0:T(8,128)(2,1)S(1)} %bitcast.11, bf16[64,1024]{1,0:T(8,128)(2,1)S(1)} %collective-permute-done.10.refs_1_, bf16[64,1024]{1,0:T(8,128)(2,1)S(1)} %collective-permute-done.15.refs_2_, bf16[128,1024]{1,0:T(8,128)(2,1)S(1)} %collective-permute-done.2.refs_3_.refs_1_, ...), custom_call_target="tpu_custom_call" | custom-call | flops 1 | bytes 1 | tf_op jit(solution)/shard_map/band_sum/pallas_call | solution.py:381
  56.8 2.1 %band_sum.7 = f32[64,1024]{1,0:T(8,128)} custom-call(bf16[64,1024]{1,0:T(8,128)(2,1)S(1)} %bitcast.12, bf16[128,1024]{1,0:T(8,128)(2,1)S(1)} %collective-permute-done.2.refs_3_.refs_1_, bf16[64,1024]{1,0:T(8,128)(2,1)S(1)} %collective-permute-done.14.refs_2_, f32[1024,64]{1,0:T(8,128)S(1)} %get-tuple-element.19.refs_3_, f32[64,1024]{1,0:T(8,128)S(1)} %get-tuple-element.20.refs_4_), custom_call_target="tpu_custom_call" | custom-call | flops 1 | bytes 1 | tf_op jit(solution)/shard_map/band_sum/pallas_call | solution.py:381
  (25 shorter events, 0.4 us)
Async XLA Ops:
  0.6 6.9 %copy-start = (bf16[1024,64]{0,1:T(8,128)(2,1)S(1)}, bf16[1024,64]{0,1:T(8,128)(2,1)}, u32[]{:S(2)}) copy-start(bf16[1024,64]{0,1:T(8,128)(2,1)} %param.5) | copy-start | bytes 393220
  1.8 7.6 %collective-permute-start.3 = (bf16[64,256]{1,0:T(8,128)(2,1)S(1)}, bf16[64,256]{1,0:T(8,128)(2,1)S(1)}, u32[]{:S(2)}, u32[]{:S(2)}) collective-permute-start(bf16[64,256]{1,0:T(8,128)(2,1)S(1)} %pick.1), channel_id=1, source_target_pairs={{1,0},{0,1},{3,2},{2,3},{5,4},{4,5},{7,6},{6,7},{9,8},{8,9},{11,10... | collective-permute-start | bytes 98312 | tf_op jit(solution)/shard_map/ppermute | solution.py:32
  4.9 5.4 %collective-permute-start.4 = (bf16[64,256]{1,0:T(8,128)(2,1)S(1)}, bf16[64,256]{1,0:T(8,128)(2,1)S(1)}, u32[]{:S(2)}, u32[]{:S(2)}) collective-permute-start(bf16[64,256]{1,0:T(8,128)(2,1)S(1)} %pick.1), channel_id=1, source_target_pairs={{2,0},{3,1},{0,2},{1,3},{6,4},{7,5},{4,6},{5,7},{10,8},{11,9},{8,1... | collective-permute-start | bytes 98312 | tf_op jit(solution)/shard_map/ppermute | solution.py:32
  7.5 5.9 %collective-permute-start.5 = (bf16[64,256]{1,0:T(8,128)(2,1)S(1)}, bf16[64,256]{1,0:T(8,128)(2,1)S(1)}, u32[]{:S(2)}, u32[]{:S(2)}) collective-permute-start(bf16[64,256]{1,0:T(8,128)(2,1)S(1)} %pick.1), channel_id=1, source_target_pairs={{3,0},{2,1},{1,2},{0,3},{7,4},{6,5},{5,6},{4,7},{11,8},{10,9},{9,1... | collective-permute-start | bytes 98312 | tf_op jit(solution)/shard_map/ppermute | solution.py:32
  7.5 9.5 %collective-permute-start = (bf16[64,1024]{1,0:T(8,128)(2,1)S(1)}, bf16[64,1024]{1,0:T(8,128)(2,1)S(1)}, u32[]{:S(2)}, u32[]{:S(2)}) collective-permute-start(bf16[64,1024]{1,0:T(8,128)(2,1)S(1)} %bitcast.5), channel_id=1, source_target_pairs={{2,0},{3,1},{0,2},{1,3},{6,4},{7,5},{4,6},{5,7},{10,8},{11,9},{8,1... | collective-permute-start | bytes 393224 | tf_op jit(solution)/shard_map/ppermute | solution.py:32
  13.4 3.7 %collective-permute-start.6 = (bf16[64,256]{1,0:T(8,128)(2,1)S(1)}, bf16[64,256]{1,0:T(8,128)(2,1)S(1)}, u32[]{:S(2)}, u32[]{:S(2)}) collective-permute-start(bf16[64,256]{1,0:T(8,128)(2,1)S(1)} %add_add_fusion.1), channel_id=1, source_target_pairs={{4,0},{0,4},{12,8},{8,12},{20,16},{16,20},{28,24},{24,28},{5,1},{1... | collective-permute-start | bytes 98312 | tf_op jit(solution)/shard_map/ppermute | solution.py:32
  17.0 8.0 %collective-permute-start.1 = (bf16[128,1024]{1,0:T(8,128)(2,1)S(1)}, bf16[128,1024]{1,0:T(8,128)(2,1)S(1)}, u32[]{:S(2)}, u32[]{:S(2)}) collective-permute-start(bf16[128,1024]{1,0:T(8,128)(2,1)S(1)} %pad_maximum_fusion), channel_id=1, source_target_pairs={{1,0},{0,1},{3,2},{2,3},{5,4},{4,5},{7,6},{6,7},{9,8},{8,9},{11,10... | collective-permute-start | bytes 786440 | tf_op jit(solution)/shard_map/ppermute | solution.py:32
  17.1 4.0 %collective-permute-start.7 = (bf16[64,256]{1,0:T(8,128)(2,1)S(1)}, bf16[64,256]{1,0:T(8,128)(2,1)S(1)}, u32[]{:S(2)}, u32[]{:S(2)}) collective-permute-start(bf16[64,256]{1,0:T(8,128)(2,1)S(1)} %add.39), channel_id=1, source_target_pairs={{8,0},{12,4},{0,8},{4,12},{24,16},{28,20},{16,24},{20,28},{9,1},{1... | collective-permute-start | bytes 98312 | tf_op jit(solution)/shard_map/ppermute | solution.py:32
  18.7 4.3 %collective-permute-start.8 = (bf16[64,256]{1,0:T(8,128)(2,1)S(1)}, bf16[64,256]{1,0:T(8,128)(2,1)S(1)}, u32[]{:S(2)}, u32[]{:S(2)}) collective-permute-start(bf16[64,256]{1,0:T(8,128)(2,1)S(1)} %add.39), channel_id=1, source_target_pairs={{16,0},{20,4},{24,8},{28,12},{0,16},{4,20},{8,24},{12,28},{17,1},{... | collective-permute-start | bytes 98312 | tf_op jit(solution)/shard_map/ppermute | solution.py:32
  20.2 4.8 %collective-permute-start.9 = (bf16[64,256]{1,0:T(8,128)(2,1)S(1)}, bf16[64,256]{1,0:T(8,128)(2,1)S(1)}, u32[]{:S(2)}, u32[]{:S(2)}) collective-permute-start(bf16[64,256]{1,0:T(8,128)(2,1)S(1)} %add.39), channel_id=1, source_target_pairs={{24,0},{28,4},{16,8},{20,12},{8,16},{12,20},{0,24},{4,28},{25,1},{... | collective-permute-start | bytes 98312 | tf_op jit(solution)/shard_map/ppermute | solution.py:32
  25.1 1.1 %copy-start.1 = (f32[1024,64]{0,1:T(8,128)S(1)}, f32[1024,64]{0,1:T(8,128)}, u32[]{:S(2)}) copy-start(f32[1024,64]{0,1:T(8,128)} %param.9) | copy-start | bytes 786436
  25.1 1.1 %copy-start.2 = (f32[256,64]{0,1:T(8,128)S(1)}, f32[256,64]{0,1:T(8,128)}, u32[]{:S(2)}) copy-start(f32[256,64]{0,1:T(8,128)} %param.8) | copy-start | bytes 196612
  25.1 9.6 %collective-permute-start.2 = (bf16[128,1024]{1,0:T(8,128)(2,1)S(1)}, bf16[128,1024]{1,0:T(8,128)(2,1)S(1)}, u32[]{:S(2)}, u32[]{:S(2)}) collective-permute-start(bf16[128,1024]{1,0:T(8,128)(2,1)S(1)} %pad_maximum_fusion.1), channel_id=1, source_target_pairs={{28,0},{29,1},{6,2},{7,3},{0,4},{1,5},{10,6},{11,7},{4,8},{5,9},{1... | collective-permute-start | bytes 786440 | tf_op jit(solution)/shard_map/ppermute | solution.py:57
  25.2 9.5 %collective-permute-start.10 = (bf16[64,1024]{1,0:T(8,128)(2,1)S(1)}, bf16[64,1024]{1,0:T(8,128)(2,1)S(1)}, u32[]{:S(2)}, u32[]{:S(2)}) collective-permute-start(bf16[64,1024]{1,0:T(8,128)(2,1)S(1)} %get-tuple-element.22), channel_id=1, source_target_pairs={{28,0},{5,1},{30,2},{7,3},{0,4},{9,5},{2,6},{11,7},{4,8},{13,9},{6... | collective-permute-start | bytes 393224 | tf_op jit(solution)/shard_map/ppermute | solution.py:57
  34.8 7.7 %collective-permute-start.12 = (bf16[64,1024]{1,0:T(8,128)(2,1)S(1)}, bf16[64,1024]{1,0:T(8,128)(2,1)S(1)}, u32[]{:S(2)}, u32[]{:S(2)}) collective-permute-start(bf16[64,1024]{1,0:T(8,128)(2,1)S(1)} %fusion.1), channel_id=1, source_target_pairs={{1,0},{0,1},{3,2},{2,3},{5,4},{4,5},{7,6},{6,7},{9,8},{8,9},{11,10... | collective-permute-start | bytes 393224 | tf_op jit(solution)/shard_map/ppermute | solution.py:32
  38.5 7.8 %collective-permute-start.11 = (bf16[64,1024]{1,0:T(8,128)(2,1)S(1)}, bf16[64,1024]{1,0:T(8,128)(2,1)S(1)}, u32[]{:S(2)}, u32[]{:S(2)}) collective-permute-start(bf16[64,1024]{1,0:T(8,128)(2,1)S(1)} %fusion.1), channel_id=1, source_target_pairs={{2,0},{3,1},{0,2},{1,3},{6,4},{7,5},{4,6},{5,7},{10,8},{11,9},{8,1... | collective-permute-start | bytes 393224 | tf_op jit(solution)/shard_map/ppermute | solution.py:32
  46.3 5.0 %collective-permute-start.13 = (bf16[64,1024]{1,0:T(8,128)(2,1)S(1)}, bf16[64,1024]{1,0:T(8,128)(2,1)S(1)}, u32[]{:S(2)}, u32[]{:S(2)}) collective-permute-start(bf16[64,1024]{1,0:T(8,128)(2,1)S(1)} %add.46.refs_4_), channel_id=1, source_target_pairs={{1,0},{0,1},{3,2},{2,3},{5,4},{4,5},{7,6},{6,7},{9,8},{8,9},{11,10... | collective-permute-start | bytes 393224 | tf_op jit(solution)/shard_map/ppermute | solution.py:32
  46.4 5.3 %collective-permute-start.16 = (bf16[64,1024]{1,0:T(8,128)(2,1)S(1)}, bf16[64,1024]{1,0:T(8,128)(2,1)S(1)}, u32[]{:S(2)}, u32[]{:S(2)}) collective-permute-start(bf16[64,1024]{1,0:T(8,128)(2,1)S(1)} %add.46.refs_4_), channel_id=1, source_target_pairs={{28,0},{29,1},{6,2},{7,3},{0,4},{1,5},{10,6},{11,7},{4,8},{5,9},{1... | collective-permute-start | bytes 393224 | tf_op jit(solution)/shard_map/ppermute | solution.py:57
  46.4 6.7 %collective-permute-start.15 = (bf16[64,1024]{1,0:T(8,128)(2,1)S(1)}, bf16[64,1024]{1,0:T(8,128)(2,1)S(1)}, u32[]{:S(2)}, u32[]{:S(2)}) collective-permute-start(bf16[64,1024]{1,0:T(8,128)(2,1)S(1)} %add.45.awaited_ref.refs_2_), channel_id=1, source_target_pairs={{28,0},{5,1},{30,2},{7,3},{0,4},{9,5},{2,6},{11,7},{4,8},{13,9},{6... | collective-permute-start | bytes 393224 | tf_op jit(solution)/shard_map/ppermute | solution.py:57
  51.4 5.4 %collective-permute-start.14 = (bf16[64,1024]{1,0:T(8,128)(2,1)S(1)}, bf16[64,1024]{1,0:T(8,128)(2,1)S(1)}, u32[]{:S(2)}, u32[]{:S(2)}) collective-permute-start(bf16[64,1024]{1,0:T(8,128)(2,1)S(1)} %add.47.refs_6_), channel_id=1, source_target_pairs={{28,0},{29,1},{6,2},{7,3},{0,4},{1,5},{10,6},{11,7},{4,8},{5,9},{1... | collective-permute-start | bytes 393224 | tf_op jit(solution)/shard_map/ppermute | solution.py:57

commit v13 on v12

--- a/solution.py
+++ b/solution.py
@@ -32,14 +32,13 @@
     return lax.ppermute(value, axis, [(i ^ bit, i) for i in range(lax.axis_size(axis))])
 
 
-def spread(value):
-    for axis in ("gy", "gx"):
-        count = lax.axis_size(axis)
-        bit = 1
-        while bit < count:
-            wide = 2 if (count // bit).bit_length() % 2 == 0 else 4
-            value = sum((swapped(value, axis, bit * k) for k in range(1, wide)), value)
-            bit *= wide
+def spread(value, axis):
+    count = lax.axis_size(axis)
+    bit = 1
+    while bit < count:
+        wide = 2 if (count // bit).bit_length() % 2 == 0 else 4
+        value = sum((swapped(value, axis, bit * k) for k in range(1, wide)), value)
+        bit *= wide
     return value
 
 
@@ -166,7 +165,7 @@
     return one + [corner[i] + two[i] for i in range(4)]
 
 
-def inverse_factor(strips):
+def inverse_factor(strips, beside):
     lane = lax.broadcasted_iota(jnp.int32, (STRIP, LANES), 1)
     level = lax.broadcasted_iota(jnp.int32, (STRIP, LANES), 0)
     strips = list(strips)
@@ -205,6 +204,8 @@
 
     columns = [column(strips[0], k) for k in range(STRIP)]
     for p in range(len(strips)):
+        if beside:
+            waiting.append(beside.pop(0))
         steps = small_inverse(columns)
         while True:
             try:
@@ -231,29 +232,34 @@
     return result
 
 
-def probe_kernel(pivot_ref, point_ref, coeff_ref, noise_ref, *refs):
-    inverse_ref, probe_ref, sent_ref, high_ref, middle_ref, little_ref = refs[-6:]
+def probe_kernel(
+    pivot_ref, point_ref, coeff_ref, noise_ref, inverse_ref, probe_ref, sent_ref, high_ref, middle_ref, little_ref
+):
     hp = lax.Precision.HIGHEST
     size = pivot_ref.shape[1]
     half = size // 2
-    pivots = extended(pivot_ref[...], True).astype(jnp.bfloat16)
-    others = extended(pivot_ref[...], False).astype(jnp.bfloat16)
-    points = extended(point_ref[...], False).astype(jnp.bfloat16)
-    cols = kernel_of(product(pivots, points, ((0,), (0,))))
-    high_ref[...], middle_ref[...], little_ref[...] = thirds(cols)
-
-    gram = kernel_of(product(pivots, others, ((0,), (0,))))
+    pivots = jnp.transpose(padded(extended(pivot_ref[...], True))).astype(jnp.bfloat16)
+    others = padded(extended(pivot_ref[...], False)).astype(jnp.bfloat16)
+    points = padded(extended(point_ref[...], False)).astype(jnp.bfloat16)
+
+    def columns_at(start):
+        at = slice(start, start + LANES)
+        cols = kernel_of(product(pivots, points[:, at], ((1,), (0,))))
+        high_ref[:, at], middle_ref[:, at], little_ref[:, at] = thirds(cols)
+
+    gram = kernel_of(product(pivots, others, ((1,), (0,))))
     equal = lax.broadcasted_iota(jnp.int32, gram.shape, 0) == lax.broadcasted_iota(jnp.int32, gram.shape, 1)
     gram = gram + jnp.where(equal, jitter, 0.0)
 
-    def inverted(block):
+    def inverted(block, beside):
         strips = [block[s:s + STRIP, :] for s in range(0, half, STRIP)]
-        return jnp.concatenate(inverse_factor(strips), axis=0)
-
-    one = inverted(gram[:half, :half])
+        return jnp.concatenate(inverse_factor(strips, beside), axis=0)
+
+    beside = [functools.partial(columns_at, start) for start in range(0, points.shape[1], LANES)]
+    one = inverted(gram[:half, :half], beside)
     below = product(gram[half:, :half], one, ((1,), (1,)), hp)
     back = product(below, one, ((1,), (0,)), hp)
-    two = inverted(gram[half:, half:] - product(below, below, ((1,), (1,)), hp))
+    two = inverted(gram[half:, half:] - product(below, below, ((1,), (1,)), hp), beside)
     coeffs = coeff_ref[...]
     start = product(coeffs[:, :half], one, ((1,), (0,)), hp)
     later = product(coeffs[:, half:], two, ((1,), (0,)), hp)
@@ -275,23 +281,23 @@
     inverse_ref[half:, half:] = two
 
 
-def probes_of(pivots_t, points_t, coeffs_t, noise_t, awaited):
+def probes_of(pivots_t, points_t, coeffs_t, noise_t):
     size = pivots_t.shape[1]
     count = points_t.shape[1]
     return pl.pallas_call(
         probe_kernel,
         out_shape=(
-            jax.ShapeDtypeStruct((size, size), jnp.float32),
-            jax.ShapeDtypeStruct(noise_t.shape, jnp.float32),
+            pltpu.VMEM((size, size), jnp.float32),
+            pltpu.VMEM(noise_t.shape, jnp.float32),
             pltpu.VMEM(noise_t.shape, jnp.bfloat16),
         ),
-        in_specs=in_vmem(4) + [pl.BlockSpec(memory_space=pl.ANY)] * len(awaited),
+        in_specs=in_vmem(4),
         out_specs=tuple(in_vmem(3)),
         scratch_shapes=[pltpu.VMEM((size, count), jnp.bfloat16)] * 3,
         cost_estimate=LONG,
         compiler_params=pltpu.CompilerParams(vmem_limit_bytes=32 * 1024 * 1024),
         name="probes",
-    )(pivots_t, points_t, coeffs_t, noise_t, *awaited)
+    )(pivots_t, points_t, coeffs_t, noise_t)
 
 
 def padded(value):
@@ -377,7 +383,7 @@
     if last:
         out_shape = jax.ShapeDtypeStruct((width, count), jnp.float32)
     else:
-        out_shape = (jax.ShapeDtypeStruct((count, width), jnp.float32), pltpu.VMEM((width, count), jnp.bfloat16))
+        out_shape = (pltpu.VMEM((count, width), jnp.float32), pltpu.VMEM((width, count), jnp.bfloat16))
     return pl.pallas_call(
         functools.partial(band_kernel, tuple(places), first, last),
         out_shape=out_shape,
@@ -393,32 +399,31 @@
     tall = lax.axis_size("gy") == BAND + 1
     points = points.T
     depth = points.shape[0]
-    pivot_points = spread(pick(owners, pivots, points))
+    row_sum = spread(pick(owners, pivots, points), "gx")
     if tall:
         far = swapped(points, "gy", 2)
+        row_sum = row_sum + zero_like(far[:, :row_sum.shape[1]])
         pair = swapped(jnp.concatenate([points, far], axis=0), "gy", 1)
-        crossing_one = cross(pair[:depth], 1)
-        crossing_pair = cross(jnp.concatenate([far, pair[depth:]], axis=0), 2)
-        near = [far, pair]
     else:
         near = direct_blocks(points)
-
-    inverse, probes, sent = probes_of(pivot_points, points, coeffs.T, noise.T, near)
+    pivot_points = spread(row_sum, "gy")
+
+    inverse, probes, sent = probes_of(pivot_points, points, coeffs.T, noise.T)
     total, zeros = band_sum(points, [((points, 0), (sent, 0))])
     if tall:
-        leaving = sent + zero_like(crossing_one) + zero_like(crossing_pair[:depth])
+        leaving = sent + zero_like(pair[:depth])
         two = swapped(leaving, "gy", 2)
         one = swapped(leaving, "gy", 1) + zeros
         factor, zeros = factor_of(pivot_points, points, inverse, one)
         two = two + zeros
+        cross_one = cross(jnp.concatenate([pair[:depth], one], axis=0), 1)
         three = swapped(two, "gy", 1)
-        cross_one, cross_two = cross(one, 1), cross(two, 2)
+        cross_two = cross(jnp.concatenate([far, two], axis=0), 2)
         total, zeros = band_sum(points, [((pair, 0), (one, 0)), ((far, 0), (two, 0))], total)
-        three = three + zeros
-        cross_three = cross(three, 3)
-        pieces = [((crossing_one, 0), (cross_one, 0)), ((crossing_pair, 0), (cross_two, 0)), ((pair, depth), (three, 0))]
-        total, _ = band_sum(points, pieces, total)
-        kernel_probes = band_sum(points, [((crossing_pair, depth), (cross_three, 0))], total, probes)
+        cross_three = cross(jnp.concatenate([pair[depth:], three + zeros], axis=0), 3)
+        crossed = [((stacked, 0), (stacked, depth)) for stacked in (cross_one, cross_two, cross_three)]
+        total, _ = band_sum(points, crossed[:2] + [((pair, depth), (three, 0))], total)
+        kernel_probes = band_sum(points, crossed[2:], total, probes)
     else:
         factor, _ = factor_of(pivot_points, points, inverse, zeros)
         pieces = [((block, 0), (probe, 0)) for block, probe in zip(near, direct_blocks(sent))]

time: 59 us -> 54.7 us (0.927)
  waiting for transfers between devices: 18.3 us -> 16.1 us
  starting transfers between devices: 18.1 us -> 16 us
    ppermute x12, waiting for transfers between devices: 16.6 us -> 11.6 us  [swapped(): lax.ppermute(value, axis, [(i ^ bit, i) for i in range(lax.axis_size(axis...]
    ppermute x5 -> x3, waiting for transfers between devices: 1.7 us -> 4.5 us  [cross(): return lax.ppermute(piece, ('gx', 'gy'), pairs)]
    ppermute x5 -> x3, starting transfers between devices: 2.12 us -> 0.96 us  [cross(): return lax.ppermute(piece, ('gx', 'gy'), pairs)]
    ppermute x12, starting transfers between devices: 16 us -> 15.1 us  [swapped(): lax.ppermute(value, axis, [(i ^ bit, i) for i in range(lax.axis_size(axis...]
  transfers between devices with their start and end apart: 17 -> 15, of which waited for: 11 -> 12; matrix products, arithmetic and copies ran while one was open for 0% -> 0% of each run, Pallas kernels for 31% -> 35%
where the time goes in v13:
time: 54.7 us; the launch traced here: 54.5 us
  Pallas kernels  21.3 us (39%)
  waiting for transfers between devices  16.1 us (29%)
  starting transfers between devices  16 us (29%)
  between operations  0.82 us (1%)
    ppermute x12, starting transfers between devices, swapped(): lax.ppermute(value, axis, [(i ^ bit, i) for i in range(lax.axis_size(axis...  15.1 us
    ppermute x12, waiting for transfers between devices, swapped(): lax.ppermute(value, axis, [(i ^ bit, i) for i in range(lax.axis_size(axis...  11.6 us
    pallas_call x4, Pallas kernels, band_sum(): pl.pallas_call(functools.partial(band_kernel, tuple(places), first, last)...  9.64 us
    pallas_call x1, Pallas kernels, probes_of(): pl.pallas_call(probe_kernel, out_shape=(pltpu.VMEM((size, size), jnp.floa...  8.62 us
    ppermute x3, waiting for transfers between devices, cross(): return lax.ppermute(piece, ('gx', 'gy'), pairs)  4.5 us
    pallas_call x1, Pallas kernels, factor_of(): pl.pallas_call(factor_kernel, out_shape=(jax.ShapeDtypeStruct((count, siz...  1.91 us
    pallas_call x1, Pallas kernels, pick(): pl.pallas_call(pick_kernel, out_shape=pltpu.VMEM((points_t.shape[0], 2 *...  1.17 us
  transfers between devices with their start and end apart: 15, of which 12 were waited for; matrix products, arithmetic and copies ran while one was open for 0% of the time, Pallas kernels for 35%

profile of v13, /device:TPU:0, one launch (start us, length us, event | category | flops | bytes accessed | tf_op | source)
XLA Modules:
  0.0 54.5 jit_solution(15519119130696068879)
XLA Ops:
  0.6 4.1 %collective-permute-start = (bf16[64,1024]{1,0:T(8,128)(2,1)}, bf16[64,1024]{1,0:T(8,128)(2,1)S(1)}, u32[]{:S(2)}, u32[]{:S(2)}) collective-permute-start(bf16[64,1024]{1,0:T(8,128)(2,1)} %bitcast.4), channel_id=1, source_target_pairs={{2,0},{3,1},{0,2},{1,3},{6,4},{7,5},{4,6},{5,7},{10,8},{11,9},{8,1... | collective-permute-start | bytes 393224 | tf_op jit(solution)/shard_map/ppermute | solution.py:32
  4.7 1.2 %pick.1 = bf16[64,256]{1,0:T(8,128)(2,1)S(1)} custom-call(s32[2]{0:T(128)} %owner_ref.1, s32[2,128]{1,0:T(2,128)} %pivot_ref.1, bf16[64,1024]{1,0:T(8,128)(2,1)} %bitcast.5), custom_call_target="tpu_custom_call" | custom-call | tf_op jit(solution)/shard_map/pick/pallas_call | solution.py:108
  5.9 0.1 collective-permute-start.2
  6.0 1.2 %collective-permute-done.2 = bf16[64,256]{1,0:T(8,128)(2,1)S(1)} collective-permute-done((bf16[64,256]{1,0:T(8,128)(2,1)S(1)}, bf16[64,256]{1,0:T(8,128)(2,1)S(1)}, u32[]{:S(2)}, u32[]{:S(2)}) %collective-permute-start.2) | collective-permute-done | bytes 32800 | tf_op jit(solution)/shard_map/ppermute | solution.py:32
  7.2 2.5 %collective-permute-start.5 = (bf16[64,256]{1,0:T(8,128)(2,1)S(1)}, bf16[64,256]{1,0:T(8,128)(2,1)S(1)}, u32[]{:S(2)}, u32[]{:S(2)}) collective-permute-start(bf16[64,256]{1,0:T(8,128)(2,1)S(1)} %add.36), channel_id=1, source_target_pairs={{24,0},{28,4},{16,8},{20,12},{8,16},{12,20},{0,24},{4,28},{25,1},{... | collective-permute-start | bytes 98312 | tf_op jit(solution)/shard_map/ppermute | solution.py:32
  9.7 0.5 collective-permute-start.4
  10.2 0.5 collective-permute-start.3
  10.8 1.3 %collective-permute-done.5 = bf16[64,256]{1,0:T(8,128)(2,1)S(1)} collective-permute-done((bf16[64,256]{1,0:T(8,128)(2,1)S(1)}, bf16[64,256]{1,0:T(8,128)(2,1)S(1)}, u32[]{:S(2)}, u32[]{:S(2)}) %collective-permute-start.5) | collective-permute-done | bytes 32800 | tf_op jit(solution)/shard_map/ppermute | solution.py:32
  12.1 1.5 %collective-permute-done.4 = bf16[64,256]{1,0:T(8,128)(2,1)S(1)} collective-permute-done((bf16[64,256]{1,0:T(8,128)(2,1)S(1)}, bf16[64,256]{1,0:T(8,128)(2,1)S(1)}, u32[]{:S(2)}, u32[]{:S(2)}) %collective-permute-start.4) | collective-permute-done | bytes 32800 | tf_op jit(solution)/shard_map/ppermute | solution.py:32
  13.6 0.5 collective-permute-done.3
  14.2 1.4 %collective-permute-start.8 = (bf16[64,256]{1,0:T(8,128)(2,1)S(1)}, bf16[64,256]{1,0:T(8,128)(2,1)S(1)}, u32[]{:S(2)}, u32[]{:S(2)}) collective-permute-start(bf16[64,256]{1,0:T(8,128)(2,1)S(1)} %fusion.1), channel_id=1, source_target_pairs={{3,0},{2,1},{1,2},{0,3},{7,4},{6,5},{5,6},{4,7},{11,8},{10,9},{9,1... | collective-permute-start | bytes 98312 | tf_op jit(solution)/shard_map/ppermute | solution.py:32
  15.6 1.7 %collective-permute-start.7 = (bf16[64,256]{1,0:T(8,128)(2,1)S(1)}, bf16[64,256]{1,0:T(8,128)(2,1)S(1)}, u32[]{:S(2)}, u32[]{:S(2)}) collective-permute-start(bf16[64,256]{1,0:T(8,128)(2,1)S(1)} %fusion.1), channel_id=1, source_target_pairs={{2,0},{3,1},{0,2},{1,3},{6,4},{7,5},{4,6},{5,7},{10,8},{11,9},{8,1... | collective-permute-start | bytes 98312 | tf_op jit(solution)/shard_map/ppermute | solution.py:32
  17.3 1.3 %collective-permute-start.6 = (bf16[64,256]{1,0:T(8,128)(2,1)S(1)}, bf16[64,256]{1,0:T(8,128)(2,1)S(1)}, u32[]{:S(2)}, u32[]{:S(2)}) collective-permute-start(bf16[64,256]{1,0:T(8,128)(2,1)S(1)} %fusion.1), channel_id=1, source_target_pairs={{1,0},{0,1},{3,2},{2,3},{5,4},{4,5},{7,6},{6,7},{9,8},{8,9},{11,10... | collective-permute-start | bytes 98312 | tf_op jit(solution)/shard_map/ppermute | solution.py:32
  18.7 0.7 %collective-permute-start.1 = (bf16[128,1024]{1,0:T(8,128)(2,1)S(1)}, bf16[128,1024]{1,0:T(8,128)(2,1)S(1)}, u32[]{:S(2)}, u32[]{:S(2)}) collective-permute-start(bf16[128,1024]{1,0:T(8,128)(2,1)S(1)} %pad_maximum_fusion), channel_id=1, source_target_pairs={{1,0},{0,1},{3,2},{2,3},{5,4},{4,5},{7,6},{6,7},{9,8},{8,9},{11,10... | collective-permute-start | bytes 786440 | tf_op jit(solution)/shard_map/ppermute | solution.py:32
  19.4 1.0 %collective-permute-done.8 = bf16[64,256]{1,0:T(8,128)(2,1)S(1)} collective-permute-done((bf16[64,256]{1,0:T(8,128)(2,1)S(1)}, bf16[64,256]{1,0:T(8,128)(2,1)S(1)}, u32[]{:S(2)}, u32[]{:S(2)}) %collective-permute-start.8) | collective-permute-done | bytes 32800 | tf_op jit(solution)/shard_map/ppermute | solution.py:32
  20.4 0.3 collective-permute-done.7
  20.8 0.9 %collective-permute-done.6 = bf16[64,256]{1,0:T(8,128)(2,1)S(1)} collective-permute-done((bf16[64,256]{1,0:T(8,128)(2,1)S(1)}, bf16[64,256]{1,0:T(8,128)(2,1)S(1)}, u32[]{:S(2)}, u32[]{:S(2)}) %collective-permute-start.6) | collective-permute-done | bytes 32800 | tf_op jit(solution)/shard_map/ppermute | solution.py:32
  21.6 8.6 %probes.1 = (f32[256,256]{1,0:T(8,128)S(1)}, f32[64,1024]{1,0:T(8,128)S(1)}, bf16[64,1024]{1,0:T(8,128)(2,1)S(1)}) custom-call(bf16[64,256]{1,0:T(8,128)(2,1)S(1)} %add_add_fusion.pivot_ref, bf16[64,1024]{1,0:T(8,128)(2,1)S(1)} %bitcast.7, f32[64,256]{1,0:T(8,128)S(1)} %bitcast.14, f32[64,1024]{1,0:T(8,128)S(1)} %bitcast.13), custom_call_target="tpu_custom_call" | custom-call | flops 17179869184 | bytes 1 | tf_op jit(solution)/shard_map/probes/pallas_call | solution.py:287
  30.3 1.4 %collective-permute-start.10 = (bf16[64,1024]{1,0:T(8,128)(2,1)S(1)}, bf16[64,1024]{1,0:T(8,128)(2,1)S(1)}, u32[]{:S(2)}, u32[]{:S(2)}) collective-permute-start(bf16[64,1024]{1,0:T(8,128)(2,1)S(1)} %get-tuple-element.23), channel_id=1, source_target_pairs={{1,0},{0,1},{3,2},{2,3},{5,4},{4,5},{7,6},{6,7},{9,8},{8,9},{11,10... | collective-permute-start | bytes 393224 | tf_op jit(solution)/shard_map/ppermute | solution.py:32
  31.7 0.7 %collective-permute-start.9 = (bf16[64,1024]{1,0:T(8,128)(2,1)S(1)}, bf16[64,1024]{1,0:T(8,128)(2,1)S(1)}, u32[]{:S(2)}, u32[]{:S(2)}) collective-permute-start(bf16[64,1024]{1,0:T(8,128)(2,1)S(1)} %get-tuple-element.23), channel_id=1, source_target_pairs={{2,0},{3,1},{0,2},{1,3},{6,4},{7,5},{4,6},{5,7},{10,8},{11,9},{8,1... | collective-permute-start | bytes 393224 | tf_op jit(solution)/shard_map/ppermute | solution.py:32
  32.4 1.4 %band_sum.4 = (f32[1024,64]{1,0:T(8,128)S(1)}, bf16[64,1024]{1,0:T(8,128)(2,1)S(1)}) custom-call(bf16[64,1024]{1,0:T(8,128)(2,1)S(1)} %bitcast.8, bf16[64,1024]{1,0:T(8,128)(2,1)S(1)} %get-tuple-element.12.refs_1_), custom_call_target="tpu_custom_call" | custom-call | flops 1 | bytes 1 | tf_op jit(solution)/shard_map/band_sum/pallas_call | solution.py:387
  33.8 2.2 %collective-permute-done.10 = bf16[64,1024]{1,0:T(8,128)(2,1)S(1)} collective-permute-done((bf16[64,1024]{1,0:T(8,128)(2,1)S(1)}, bf16[64,1024]{1,0:T(8,128)(2,1)S(1)}, u32[]{:S(2)}, u32[]{:S(2)}) %collective-permute-start.10) | collective-permute-done | bytes 131104 | tf_op jit(solution)/shard_map/ppermute | solution.py:32
  36.1 1.9 %factor.1 = (f32[1024,256]{1,0:T(8,128)}, bf16[64,1024]{1,0:T(8,128)(2,1)S(1)}) custom-call(bf16[64,256]{1,0:T(8,128)(2,1)S(1)} %add_add_fusion.pivot_ref, bf16[64,1024]{1,0:T(8,128)(2,1)S(1)} %bitcast.9, f32[256,256]{1,0:T(8,128)S(1)} %get-tuple-element.13.inverse_ref, bf16[64,1024]{1,0:T(8,128)(2,1)S(1)} %add.45.awaited_ref.refs_2_), custom_call_target="tpu_custom_call" | custom-call | flops 1 | bytes 1 | tf_op jit(solution)/shard_map/factor/pallas_call | solution.py:328
  38.0 1.1 %collective-permute-done.9 = bf16[64,1024]{1,0:T(8,128)(2,1)S(1)} collective-permute-done((bf16[64,1024]{1,0:T(8,128)(2,1)S(1)}, bf16[64,1024]{1,0:T(8,128)(2,1)S(1)}, u32[]{:S(2)}, u32[]{:S(2)}) %collective-permute-start.9) | collective-permute-done | bytes 131104 | tf_op jit(solution)/shard_map/ppermute | solution.py:32
  39.2 0.1 collective-permute-start.11
  39.4 0.8 %collective-permute-start.14 = (bf16[128,1024]{1,0:T(8,128)(2,1)S(1)}, bf16[128,1024]{1,0:T(8,128)(2,1)S(1)}, u32[]{:S(2)}, u32[]{:S(2)}) collective-permute-start(bf16[128,1024]{1,0:T(8,128)(2,1)S(1)} %pad_maximum_fusion.3), channel_id=1, source_target_pairs={{28,0},{29,1},{6,2},{7,3},{0,4},{1,5},{10,6},{11,7},{4,8},{5,9},{1... | collective-permute-start | bytes 786440 | tf_op jit(solution)/shard_map/ppermute | solution.py:56
  40.2 2.5 %band_sum.5 = (f32[1024,64]{1,0:T(8,128)S(1)}, bf16[64,1024]{1,0:T(8,128)(2,1)S(1)}) custom-call(bf16[64,1024]{1,0:T(8,128)(2,1)S(1)} %bitcast.10, bf16[128,1024]{1,0:T(8,128)(2,1)S(1)} %collective-permute-done.1.refs_1_.refs_3_, bf16[64,1024]{1,0:T(8,128)(2,1)S(1)} %add.45.awaited_ref.refs_2_, bf16[64,1024]{1,0:T(8,128)(2,1)S(1)} %collective-permute-done.refs_3_, ...), custom_call_target="tpu_custom_call" | custom-call | flops 1 | bytes 1 | tf_op jit(solution)/shard_map/band_sum/pallas_call | solution.py:387
  42.7 1.5 %collective-permute-done.11.refs_4_ = bf16[64,1024]{1,0:T(8,128)(2,1)S(1)} collective-permute-done((bf16[64,1024]{1,0:T(8,128)(2,1)S(1)}, bf16[64,1024]{1,0:T(8,128)(2,1)S(1)}, u32[]{:S(2)}, u32[]{:S(2)}) %collective-permute-start.11) | collective-permute-done | bytes 131104 | tf_op jit(solution)/shard_map/ppermute | solution.py:32
  44.3 1.7 %collective-permute-done.13.refs_1_ = bf16[128,1024]{1,0:T(8,128)(2,1)S(1)} collective-permute-done((bf16[128,1024]{1,0:T(8,128)(2,1)S(1)}, bf16[128,1024]{1,0:T(8,128)(2,1)S(1)}, u32[]{:S(2)}, u32[]{:S(2)}) %collective-permute-start.13) | collective-permute-done | bytes 262176 | tf_op jit(solution)/shard_map/ppermute | solution.py:56
  46.0 2.8 %collective-permute-done.14.refs_2_ = bf16[128,1024]{1,0:T(8,128)(2,1)S(1)} collective-permute-done((bf16[128,1024]{1,0:T(8,128)(2,1)S(1)}, bf16[128,1024]{1,0:T(8,128)(2,1)S(1)}, u32[]{:S(2)}, u32[]{:S(2)}) %collective-permute-start.14) | collective-permute-done | bytes 262176 | tf_op jit(solution)/shard_map/ppermute | solution.py:56
  48.8 3.6 %band_sum.6 = (f32[1024,64]{1,0:T(8,128)S(1)}, bf16[64,1024]{1,0:T(8,128)(2,1)}) custom-call(bf16[64,1024]{1,0:T(8,128)(2,1)S(1)} %bitcast.11, bf16[128,1024]{1,0:T(8,128)(2,1)S(1)} %collective-permute-done.13.refs_1_, bf16[128,1024]{1,0:T(8,128)(2,1)S(1)} %collective-permute-done.14.refs_2_, bf16[128,1024]{1,0:T(8,128)(2,1)S(1)} %collective-permute-done.1.refs_1_.refs_3_, ...), custom_call_target="tpu_custom_call" | custom-call | flops 1 | bytes 1 | tf_op jit(solution)/shard_map/band_sum/pallas_call | solution.py:387
  52.5 2.1 %band_sum.7 = f32[64,1024]{1,0:T(8,128)} custom-call(bf16[64,1024]{1,0:T(8,128)(2,1)S(1)} %bitcast.12, bf16[128,1024]{1,0:T(8,128)(2,1)S(1)} %collective-permute-done.12.refs_1_, f32[1024,64]{1,0:T(8,128)S(1)} %get-tuple-element.19.refs_2_, f32[64,1024]{1,0:T(8,128)S(1)} %get-tuple-element.20.refs_3_), custom_call_target="tpu_custom_call" | custom-call | flops 1 | bytes 1 | tf_op jit(solution)/shard_map/band_sum/pallas_call | solution.py:387
  (22 shorter events, 0.4 us)
Async XLA Ops:
  0.6 13.5 %collective-permute-start = (bf16[64,1024]{1,0:T(8,128)(2,1)}, bf16[64,1024]{1,0:T(8,128)(2,1)S(1)}, u32[]{:S(2)}, u32[]{:S(2)}) collective-permute-start(bf16[64,1024]{1,0:T(8,128)(2,1)} %bitcast.4), channel_id=1, source_target_pairs={{2,0},{3,1},{0,2},{1,3},{6,4},{7,5},{4,6},{5,7},{10,8},{11,9},{8,1... | collective-permute-start | bytes 393224 | tf_op jit(solution)/shard_map/ppermute | solution.py:32
  5.9 12.7 %copy-start = (bf16[1024,64]{0,1:T(8,128)(2,1)S(1)}, bf16[1024,64]{0,1:T(8,128)(2,1)}, u32[]{:S(2)}) copy-start(bf16[1024,64]{0,1:T(8,128)(2,1)} %param.5) | copy-start | bytes 393220
  5.9 1.3 %collective-permute-start.2 = (bf16[64,256]{1,0:T(8,128)(2,1)S(1)}, bf16[64,256]{1,0:T(8,128)(2,1)S(1)}, u32[]{:S(2)}, u32[]{:S(2)}) collective-permute-start(bf16[64,256]{1,0:T(8,128)(2,1)S(1)} %pick.1), channel_id=1, source_target_pairs={{4,0},{0,4},{12,8},{8,12},{20,16},{16,20},{28,24},{24,28},{5,1},{1... | collective-permute-start | bytes 98312 | tf_op jit(solution)/shard_map/ppermute | solution.py:32
  7.2 4.9 %collective-permute-start.5 = (bf16[64,256]{1,0:T(8,128)(2,1)S(1)}, bf16[64,256]{1,0:T(8,128)(2,1)S(1)}, u32[]{:S(2)}, u32[]{:S(2)}) collective-permute-start(bf16[64,256]{1,0:T(8,128)(2,1)S(1)} %add.36), channel_id=1, source_target_pairs={{24,0},{28,4},{16,8},{20,12},{8,16},{12,20},{0,24},{4,28},{25,1},{... | collective-permute-start | bytes 98312 | tf_op jit(solution)/shard_map/ppermute | solution.py:32
  9.7 3.9 %collective-permute-start.4 = (bf16[64,256]{1,0:T(8,128)(2,1)S(1)}, bf16[64,256]{1,0:T(8,128)(2,1)S(1)}, u32[]{:S(2)}, u32[]{:S(2)}) collective-permute-start(bf16[64,256]{1,0:T(8,128)(2,1)S(1)} %add.36), channel_id=1, source_target_pairs={{16,0},{20,4},{24,8},{28,12},{0,16},{4,20},{8,24},{12,28},{17,1},{... | collective-permute-start | bytes 98312 | tf_op jit(solution)/shard_map/ppermute | solution.py:32
  10.2 3.9 %collective-permute-start.3 = (bf16[64,256]{1,0:T(8,128)(2,1)S(1)}, bf16[64,256]{1,0:T(8,128)(2,1)S(1)}, u32[]{:S(2)}, u32[]{:S(2)}) collective-permute-start(bf16[64,256]{1,0:T(8,128)(2,1)S(1)} %add.36), channel_id=1, source_target_pairs={{8,0},{12,4},{0,8},{4,12},{24,16},{28,20},{16,24},{20,28},{9,1},{1... | collective-permute-start | bytes 98312 | tf_op jit(solution)/shard_map/ppermute | solution.py:32
  14.2 7.5 %copy-start.1 = (f32[1024,64]{0,1:T(8,128)S(1)}, f32[1024,64]{0,1:T(8,128)}, u32[]{:S(2)}) copy-start(f32[1024,64]{0,1:T(8,128)} %param.9) | copy-start | bytes 786436
  14.2 6.2 %collective-permute-start.8 = (bf16[64,256]{1,0:T(8,128)(2,1)S(1)}, bf16[64,256]{1,0:T(8,128)(2,1)S(1)}, u32[]{:S(2)}, u32[]{:S(2)}) collective-permute-start(bf16[64,256]{1,0:T(8,128)(2,1)S(1)} %fusion.1), channel_id=1, source_target_pairs={{3,0},{2,1},{1,2},{0,3},{7,4},{6,5},{5,6},{4,7},{11,8},{10,9},{9,1... | collective-permute-start | bytes 98312 | tf_op jit(solution)/shard_map/ppermute | solution.py:32
  15.6 5.2 %collective-permute-start.7 = (bf16[64,256]{1,0:T(8,128)(2,1)S(1)}, bf16[64,256]{1,0:T(8,128)(2,1)S(1)}, u32[]{:S(2)}, u32[]{:S(2)}) collective-permute-start(bf16[64,256]{1,0:T(8,128)(2,1)S(1)} %fusion.1), channel_id=1, source_target_pairs={{2,0},{3,1},{0,2},{1,3},{6,4},{7,5},{4,6},{5,7},{10,8},{11,9},{8,1... | collective-permute-start | bytes 98312 | tf_op jit(solution)/shard_map/ppermute | solution.py:32
  17.3 4.3 %collective-permute-start.6 = (bf16[64,256]{1,0:T(8,128)(2,1)S(1)}, bf16[64,256]{1,0:T(8,128)(2,1)S(1)}, u32[]{:S(2)}, u32[]{:S(2)}) collective-permute-start(bf16[64,256]{1,0:T(8,128)(2,1)S(1)} %fusion.1), channel_id=1, source_target_pairs={{1,0},{0,1},{3,2},{2,3},{5,4},{4,5},{7,6},{6,7},{9,8},{8,9},{11,10... | collective-permute-start | bytes 98312 | tf_op jit(solution)/shard_map/ppermute | solution.py:32
  18.7 3.0 %copy-start.2 = (f32[256,64]{0,1:T(8,128)S(1)}, f32[256,64]{0,1:T(8,128)}, u32[]{:S(2)}) copy-start(f32[256,64]{0,1:T(8,128)} %param.8) | copy-start | bytes 196612
  18.7 11.6 %collective-permute-start.1 = (bf16[128,1024]{1,0:T(8,128)(2,1)S(1)}, bf16[128,1024]{1,0:T(8,128)(2,1)S(1)}, u32[]{:S(2)}, u32[]{:S(2)}) collective-permute-start(bf16[128,1024]{1,0:T(8,128)(2,1)S(1)} %pad_maximum_fusion), channel_id=1, source_target_pairs={{1,0},{0,1},{3,2},{2,3},{5,4},{4,5},{7,6},{6,7},{9,8},{8,9},{11,10... | collective-permute-start | bytes 786440 | tf_op jit(solution)/shard_map/ppermute | solution.py:32
  30.3 5.7 %collective-permute-start.10 = (bf16[64,1024]{1,0:T(8,128)(2,1)S(1)}, bf16[64,1024]{1,0:T(8,128)(2,1)S(1)}, u32[]{:S(2)}, u32[]{:S(2)}) collective-permute-start(bf16[64,1024]{1,0:T(8,128)(2,1)S(1)} %get-tuple-element.23), channel_id=1, source_target_pairs={{1,0},{0,1},{3,2},{2,3},{5,4},{4,5},{7,6},{6,7},{9,8},{8,9},{11,10... | collective-permute-start | bytes 393224 | tf_op jit(solution)/shard_map/ppermute | solution.py:32
  31.7 7.4 %collective-permute-start.9 = (bf16[64,1024]{1,0:T(8,128)(2,1)S(1)}, bf16[64,1024]{1,0:T(8,128)(2,1)S(1)}, u32[]{:S(2)}, u32[]{:S(2)}) collective-permute-start(bf16[64,1024]{1,0:T(8,128)(2,1)S(1)} %get-tuple-element.23), channel_id=1, source_target_pairs={{2,0},{3,1},{0,2},{1,3},{6,4},{7,5},{4,6},{5,7},{10,8},{11,9},{8,1... | collective-permute-start | bytes 393224 | tf_op jit(solution)/shard_map/ppermute | solution.py:32
  39.2 5.0 %collective-permute-start.11 = (bf16[64,1024]{1,0:T(8,128)(2,1)S(1)}, bf16[64,1024]{1,0:T(8,128)(2,1)S(1)}, u32[]{:S(2)}, u32[]{:S(2)}) collective-permute-start(bf16[64,1024]{1,0:T(8,128)(2,1)S(1)} %add.46.refs_4_), channel_id=1, source_target_pairs={{1,0},{0,1},{3,2},{2,3},{5,4},{4,5},{7,6},{6,7},{9,8},{8,9},{11,10... | collective-permute-start | bytes 393224 | tf_op jit(solution)/shard_map/ppermute | solution.py:32
  39.3 6.7 %collective-permute-start.13 = (bf16[128,1024]{1,0:T(8,128)(2,1)S(1)}, bf16[128,1024]{1,0:T(8,128)(2,1)S(1)}, u32[]{:S(2)}, u32[]{:S(2)}) collective-permute-start(bf16[128,1024]{1,0:T(8,128)(2,1)S(1)} %pad_maximum_fusion.2), channel_id=1, source_target_pairs={{28,0},{5,1},{30,2},{7,3},{0,4},{9,5},{2,6},{11,7},{4,8},{13,9},{6... | collective-permute-start | bytes 786440 | tf_op jit(solution)/shard_map/ppermute | solution.py:56
  39.4 9.5 %collective-permute-start.14 = (bf16[128,1024]{1,0:T(8,128)(2,1)S(1)}, bf16[128,1024]{1,0:T(8,128)(2,1)S(1)}, u32[]{:S(2)}, u32[]{:S(2)}) collective-permute-start(bf16[128,1024]{1,0:T(8,128)(2,1)S(1)} %pad_maximum_fusion.3), channel_id=1, source_target_pairs={{28,0},{29,1},{6,2},{7,3},{0,4},{1,5},{10,6},{11,7},{4,8},{5,9},{1... | collective-permute-start | bytes 786440 | tf_op jit(solution)/shard_map/ppermute | solution.py:56
  44.3 8.2 %collective-permute-start.12 = (bf16[128,1024]{1,0:T(8,128)(2,1)S(1)}, bf16[128,1024]{1,0:T(8,128)(2,1)S(1)}, u32[]{:S(2)}, u32[]{:S(2)}) collective-permute-start(bf16[128,1024]{1,0:T(8,128)(2,1)S(1)} %pad_maximum_fusion.1), channel_id=1, source_target_pairs={{28,0},{29,1},{6,2},{7,3},{0,4},{1,5},{10,6},{11,7},{4,8},{5,9},{1... | collective-permute-start | bytes 786440 | tf_op jit(solution)/shard_map/ppermute | solution.py:56

commit v14 on v13

--- a/solution.py
+++ b/solution.py
@@ -15,7 +15,6 @@
 LANES = 128
 EXTRA = 16
 CHUNK = 256
-SHORT = pl.CostEstimate(flops=1, bytes_accessed=1, transcendentals=0)
 LONG = pl.CostEstimate(flops=1 << 34, bytes_accessed=1, transcendentals=0)
 
 
@@ -130,7 +129,7 @@
 
 def four_pivots(a):
     rows = len(a)
-    x = [[None] * 4 for _ in range(4)]
+    x = [[None] * (i + 1) for i in range(4)]
     scale = [None] * 4
     product_so_far = None
     for k in range(4):
@@ -147,22 +146,43 @@
             x[i][k] = -a[i][k] if k == 0 else -a[i][k] * x[k][k]
         yield
     factor = [[a[i][k] * scale[k] for k in range(4)] for i in range(4, rows)]
-    inverse = [[scale[i] if x[i][j] is None else x[i][j] * scale[i] for j in range(i + 1)] for i in range(4)]
-    return factor, inverse
-
-
-def small_inverse(columns):
+    return factor, x, scale
+
+
+def combined(entries, columns):
+    return total_of([column if entry is None else entry * column for entry, column in zip(entries, columns)])
+
+
+def small_inverse(columns, fetch):
     a = [[row(columns[k], i) for k in range(i + 1)] for i in range(STRIP)]
     yield
-    below, one = yield from four_pivots([list(entries) for entries in a])
+    below, x, scale = yield from four_pivots([list(entries) for entries in a])
+    one = [[scale[i] if entry is None else entry * scale[i] for entry in x[i]] for i in range(4)]
     rest = [
         [a[4 + i][4 + j] - total_of([below[i][k] * below[j][k] for k in range(4)]) for j in range(i + 1)]
         for i in range(4)
     ]
     back = [[total_of([below[i][k] * one[k][j] for k in range(j, 4)]) for j in range(4)] for i in range(4)]
-    _, two = yield from four_pivots(rest)
+    coming = fetch()
+    if coming is not None:
+        lower, diagonal = coming
+        found = [combined(one[k], lower[:k + 1]) for k in range(4)]
+        diagonal = [
+            diagonal[j] - total_of([found[k] * row(found[k], j) for k in range(4)]) for j in range(STRIP)
+        ]
+        lower = [lower[4 + m] - total_of([found[j] * below[m][j] for j in range(4)]) for m in range(4)]
+    _, x, scale = yield from four_pivots(rest)
+    if coming is not None:
+        plain = [combined(x[k], lower[:k + 1]) for k in range(4)]
+        squares = [scale[k] * scale[k] for k in range(4)]
+        diagonal = [
+            diagonal[j] - total_of([plain[k] * row(plain[k], j) * squares[k] for k in range(4)])
+            for j in range(STRIP)
+        ]
+        coming = found + [plain[k] * scale[k] for k in range(4)], diagonal
+    two = [[scale[i] if entry is None else entry * scale[i] for entry in x[i]] for i in range(4)]
     corner = [[-total_of([two[i][m] * back[m][j] for m in range(i + 1)]) for j in range(4)] for i in range(4)]
-    return one + [corner[i] + two[i] for i in range(4)]
+    return one + [corner[i] + two[i] for i in range(4)], coming
 
 
 def inverse_factor(strips, beside):
@@ -202,16 +222,22 @@
 
         return [scaled] + [functools.partial(updated, r) for r in range(p + 1, len(strips))]
 
+    def coming_to(p):
+        if p + 1 == len(strips):
+            return None
+        start = p * STRIP
+        return tuple([column(strips[p + 1], first + j) for j in range(STRIP)] for first in (start, start + STRIP))
+
     columns = [column(strips[0], k) for k in range(STRIP)]
     for p in range(len(strips)):
         if beside:
             waiting.append(beside.pop(0))
-        steps = small_inverse(columns)
+        steps = small_inverse(columns, functools.partial(coming_to, p))
         while True:
             try:
                 next(steps)
             except StopIteration as ended:
-                t = ended.value
+                t, coming = ended.value
                 break
             for _ in range(2):
                 if waiting:
@@ -219,13 +245,8 @@
         while waiting:
             waiting.pop(0)()
         found = None
-        if p + 1 < len(strips):
-            start = p * STRIP
-            found = factor_columns(p + 1, start, t)
-            columns = [
-                column(strips[p + 1], start + STRIP + j) - total_of([found[k] * row(found[k], j) for k in range(STRIP)])
-                for j in range(STRIP)
-            ]
+        if coming is not None:
+            found, columns = coming
         waiting = finish(p, t, found)
     while waiting:
         waiting.pop(0)()
@@ -334,7 +355,11 @@
         in_specs=in_vmem(3) + [pl.BlockSpec(memory_space=pl.ANY)],
         out_specs=tuple(in_vmem(2)),
         compiler_params=pltpu.CompilerParams(vmem_limit_bytes=32 * 1024 * 1024),
-        cost_estimate=SHORT,
+        cost_estimate=pl.CostEstimate(
+            flops=6 * count * size * size // 8,
+            bytes_accessed=6 * count * size // 8,
+            transcendentals=count * size // 8,
+        ),
         name="factor",
     )(pivots_t, points_t, inverse, awaited)
 
@@ -390,7 +415,11 @@
         in_specs=in_vmem(len(operands)),
         out_specs=in_vmem(1)[0] if last else tuple(in_vmem(2)),
         compiler_params=pltpu.CompilerParams(vmem_limit_bytes=32 * 1024 * 1024),
-        cost_estimate=SHORT,
+        cost_estimate=pl.CostEstimate(
+            flops=1 if first else len(pieces) * 4 * count * count * LANES,
+            bytes_accessed=1 if first else 4 * count * width * len(operands),
+            transcendentals=0 if first else len(pieces) * count * count,
+        ),
         name="band_sum",
     )(*operands)
 
@@ -422,7 +451,8 @@
         total, zeros = band_sum(points, [((pair, 0), (one, 0)), ((far, 0), (two, 0))], total)
         cross_three = cross(jnp.concatenate([pair[depth:], three + zeros], axis=0), 3)
         crossed = [((stacked, 0), (stacked, depth)) for stacked in (cross_one, cross_two, cross_three)]
-        total, _ = band_sum(points, crossed[:2] + [((pair, depth), (three, 0))], total)
+        total, _ = band_sum(points, [((pair, depth), (three, 0)), crossed[0]], total)
+        total, _ = band_sum(points, crossed[1:2], total)
         kernel_probes = band_sum(points, crossed[2:], total, probes)
     else:
         factor, _ = factor_of(pivot_points, points, inverse, zeros)

time: 54.7 us -> 53.3 us (0.974)
  waiting for transfers between devices: 16.1 us -> 14.9 us
  starting transfers between devices: 16 us -> 15.4 us
    ppermute x3, waiting for transfers between devices: 4.5 us -> 2.82 us  [cross(): return lax.ppermute(piece, ('gx', 'gy'), pairs)]
    ppermute x3, starting transfers between devices: 0.96 us -> 0.35 us  [cross(): return lax.ppermute(piece, ('gx', 'gy'), pairs)]
    pallas_call x4 -> x5, Pallas kernels: 9.64 us -> 9.85 us  [band_sum(): pl.pallas_call(functools.partial(band_kernel, tuple(places), first, last)...]
  transfers between devices with their start and end apart: 15 -> 15, of which waited for: 12 -> 11; matrix products, arithmetic and copies ran while one was open for 0% -> 0% of each run, Pallas kernels for 35% -> 37%
where the time goes in v14:
time: 53.3 us; the launch traced here: 53.1 us
  Pallas kernels  21.7 us (41%)
  starting transfers between devices  15.4 us (29%)
  waiting for transfers between devices  14.9 us (28%)
  between operations  0.84 us (2%)
    ppermute x12, starting transfers between devices, swapped(): lax.ppermute(value, axis, [(i ^ bit, i) for i in range(lax.axis_size(axis...  15.1 us
    ppermute x12, waiting for transfers between devices, swapped(): lax.ppermute(value, axis, [(i ^ bit, i) for i in range(lax.axis_size(axis...  12.1 us
    pallas_call x5, Pallas kernels, band_sum(): pl.pallas_call(functools.partial(band_kernel, tuple(places), first, last)...  9.85 us
    pallas_call x1, Pallas kernels, probes_of(): pl.pallas_call(probe_kernel, out_shape=(pltpu.VMEM((size, size), jnp.floa...  8.79 us
    ppermute x3, waiting for transfers between devices, cross(): return lax.ppermute(piece, ('gx', 'gy'), pairs)  2.82 us
    pallas_call x1, Pallas kernels, factor_of(): pl.pallas_call(factor_kernel, out_shape=(jax.ShapeDtypeStruct((count, siz...  1.92 us
    pallas_call x1, Pallas kernels, pick(): pl.pallas_call(pick_kernel, out_shape=pltpu.VMEM((points_t.shape[0], 2 *...  1.17 us
  transfers between devices with their start and end apart: 15, of which 11 were waited for; matrix products, arithmetic and copies ran while one was open for 0% of the time, Pallas kernels for 37%

profile of v14, /device:TPU:0, one launch (start us, length us, event | category | flops | bytes accessed | tf_op | source)
XLA Modules:
  0.0 53.1 jit_solution(9346018679477617365)
XLA Ops:
  0.6 4.1 %collective-permute-start = (bf16[64,1024]{1,0:T(8,128)(2,1)}, bf16[64,1024]{1,0:T(8,128)(2,1)S(1)}, u32[]{:S(2)}, u32[]{:S(2)}) collective-permute-start(bf16[64,1024]{1,0:T(8,128)(2,1)} %bitcast.4), channel_id=1, source_target_pairs={{2,0},{3,1},{0,2},{1,3},{6,4},{7,5},{4,6},{5,7},{10,8},{11,9},{8,1... | collective-permute-start | bytes 393224 | tf_op jit(solution)/shard_map/ppermute | solution.py:31
  4.7 1.2 %pick.1 = bf16[64,256]{1,0:T(8,128)(2,1)S(1)} custom-call(s32[2]{0:T(128)} %owner_ref.1, s32[2,128]{1,0:T(2,128)} %pivot_ref.1, bf16[64,1024]{1,0:T(8,128)(2,1)} %bitcast.5), custom_call_target="tpu_custom_call" | custom-call | tf_op jit(solution)/shard_map/pick/pallas_call | solution.py:107
  5.9 0.1 collective-permute-start.2
  6.0 1.2 %collective-permute-done.2 = bf16[64,256]{1,0:T(8,128)(2,1)S(1)} collective-permute-done((bf16[64,256]{1,0:T(8,128)(2,1)S(1)}, bf16[64,256]{1,0:T(8,128)(2,1)S(1)}, u32[]{:S(2)}, u32[]{:S(2)}) %collective-permute-start.2) | collective-permute-done | bytes 32800 | tf_op jit(solution)/shard_map/ppermute | solution.py:31
  7.2 2.5 %collective-permute-start.5 = (bf16[64,256]{1,0:T(8,128)(2,1)S(1)}, bf16[64,256]{1,0:T(8,128)(2,1)S(1)}, u32[]{:S(2)}, u32[]{:S(2)}) collective-permute-start(bf16[64,256]{1,0:T(8,128)(2,1)S(1)} %add.36), channel_id=1, source_target_pairs={{24,0},{28,4},{16,8},{20,12},{8,16},{12,20},{0,24},{4,28},{25,1},{... | collective-permute-start | bytes 98312 | tf_op jit(solution)/shard_map/ppermute | solution.py:31
  9.7 0.5 collective-permute-start.4
  10.2 0.5 %collective-permute-start.3 = (bf16[64,256]{1,0:T(8,128)(2,1)S(1)}, bf16[64,256]{1,0:T(8,128)(2,1)S(1)}, u32[]{:S(2)}, u32[]{:S(2)}) collective-permute-start(bf16[64,256]{1,0:T(8,128)(2,1)S(1)} %add.36), channel_id=1, source_target_pairs={{8,0},{12,4},{0,8},{4,12},{24,16},{28,20},{16,24},{20,28},{9,1},{1... | collective-permute-start | bytes 98312 | tf_op jit(solution)/shard_map/ppermute | solution.py:31
  10.8 1.3 %collective-permute-done.5 = bf16[64,256]{1,0:T(8,128)(2,1)S(1)} collective-permute-done((bf16[64,256]{1,0:T(8,128)(2,1)S(1)}, bf16[64,256]{1,0:T(8,128)(2,1)S(1)}, u32[]{:S(2)}, u32[]{:S(2)}) %collective-permute-start.5) | collective-permute-done | bytes 32800 | tf_op jit(solution)/shard_map/ppermute | solution.py:31
  12.1 1.5 %collective-permute-done.4 = bf16[64,256]{1,0:T(8,128)(2,1)S(1)} collective-permute-done((bf16[64,256]{1,0:T(8,128)(2,1)S(1)}, bf16[64,256]{1,0:T(8,128)(2,1)S(1)}, u32[]{:S(2)}, u32[]{:S(2)}) %collective-permute-start.4) | collective-permute-done | bytes 32800 | tf_op jit(solution)/shard_map/ppermute | solution.py:31
  13.6 0.5 collective-permute-done.3
  14.2 1.4 %collective-permute-start.8 = (bf16[64,256]{1,0:T(8,128)(2,1)S(1)}, bf16[64,256]{1,0:T(8,128)(2,1)S(1)}, u32[]{:S(2)}, u32[]{:S(2)}) collective-permute-start(bf16[64,256]{1,0:T(8,128)(2,1)S(1)} %fusion.1), channel_id=1, source_target_pairs={{3,0},{2,1},{1,2},{0,3},{7,4},{6,5},{5,6},{4,7},{11,8},{10,9},{9,1... | collective-permute-start | bytes 98312 | tf_op jit(solution)/shard_map/ppermute | solution.py:31
  15.6 1.7 %collective-permute-start.7 = (bf16[64,256]{1,0:T(8,128)(2,1)S(1)}, bf16[64,256]{1,0:T(8,128)(2,1)S(1)}, u32[]{:S(2)}, u32[]{:S(2)}) collective-permute-start(bf16[64,256]{1,0:T(8,128)(2,1)S(1)} %fusion.1), channel_id=1, source_target_pairs={{2,0},{3,1},{0,2},{1,3},{6,4},{7,5},{4,6},{5,7},{10,8},{11,9},{8,1... | collective-permute-start | bytes 98312 | tf_op jit(solution)/shard_map/ppermute | solution.py:31
  17.3 1.3 %collective-permute-start.6 = (bf16[64,256]{1,0:T(8,128)(2,1)S(1)}, bf16[64,256]{1,0:T(8,128)(2,1)S(1)}, u32[]{:S(2)}, u32[]{:S(2)}) collective-permute-start(bf16[64,256]{1,0:T(8,128)(2,1)S(1)} %fusion.1), channel_id=1, source_target_pairs={{1,0},{0,1},{3,2},{2,3},{5,4},{4,5},{7,6},{6,7},{9,8},{8,9},{11,10... | collective-permute-start | bytes 98312 | tf_op jit(solution)/shard_map/ppermute | solution.py:31
  18.7 0.7 %collective-permute-start.1 = (bf16[128,1024]{1,0:T(8,128)(2,1)S(1)}, bf16[128,1024]{1,0:T(8,128)(2,1)S(1)}, u32[]{:S(2)}, u32[]{:S(2)}) collective-permute-start(bf16[128,1024]{1,0:T(8,128)(2,1)S(1)} %pad_maximum_fusion), channel_id=1, source_target_pairs={{1,0},{0,1},{3,2},{2,3},{5,4},{4,5},{7,6},{6,7},{9,8},{8,9},{11,10... | collective-permute-start | bytes 786440 | tf_op jit(solution)/shard_map/ppermute | solution.py:31
  19.4 1.0 %collective-permute-done.8 = bf16[64,256]{1,0:T(8,128)(2,1)S(1)} collective-permute-done((bf16[64,256]{1,0:T(8,128)(2,1)S(1)}, bf16[64,256]{1,0:T(8,128)(2,1)S(1)}, u32[]{:S(2)}, u32[]{:S(2)}) %collective-permute-start.8) | collective-permute-done | bytes 32800 | tf_op jit(solution)/shard_map/ppermute | solution.py:31
  20.4 0.3 collective-permute-done.7
  20.8 0.9 %collective-permute-done.6 = bf16[64,256]{1,0:T(8,128)(2,1)S(1)} collective-permute-done((bf16[64,256]{1,0:T(8,128)(2,1)S(1)}, bf16[64,256]{1,0:T(8,128)(2,1)S(1)}, u32[]{:S(2)}, u32[]{:S(2)}) %collective-permute-start.6) | collective-permute-done | bytes 32800 | tf_op jit(solution)/shard_map/ppermute | solution.py:31
  21.6 8.8 %probes.1 = (f32[256,256]{1,0:T(8,128)S(1)}, f32[64,1024]{1,0:T(8,128)S(1)}, bf16[64,1024]{1,0:T(8,128)(2,1)S(1)}) custom-call(bf16[64,256]{1,0:T(8,128)(2,1)S(1)} %add_add_fusion.pivot_ref, bf16[64,1024]{1,0:T(8,128)(2,1)S(1)} %bitcast.7, f32[64,256]{1,0:T(8,128)S(1)} %bitcast.15, f32[64,1024]{1,0:T(8,128)S(1)} %bitcast.14), custom_call_target="tpu_custom_call" | custom-call | flops 17179869184 | bytes 1 | tf_op jit(solution)/shard_map/probes/pallas_call | solution.py:308
  30.5 1.4 %collective-permute-start.10 = (bf16[64,1024]{1,0:T(8,128)(2,1)S(1)}, bf16[64,1024]{1,0:T(8,128)(2,1)S(1)}, u32[]{:S(2)}, u32[]{:S(2)}) collective-permute-start(bf16[64,1024]{1,0:T(8,128)(2,1)S(1)} %get-tuple-element.25), channel_id=1, source_target_pairs={{1,0},{0,1},{3,2},{2,3},{5,4},{4,5},{7,6},{6,7},{9,8},{8,9},{11,10... | collective-permute-start | bytes 393224 | tf_op jit(solution)/shard_map/ppermute | solution.py:31
  31.9 0.7 %collective-permute-start.9 = (bf16[64,1024]{1,0:T(8,128)(2,1)S(1)}, bf16[64,1024]{1,0:T(8,128)(2,1)S(1)}, u32[]{:S(2)}, u32[]{:S(2)}) collective-permute-start(bf16[64,1024]{1,0:T(8,128)(2,1)S(1)} %get-tuple-element.25), channel_id=1, source_target_pairs={{2,0},{3,1},{0,2},{1,3},{6,4},{7,5},{4,6},{5,7},{10,8},{11,9},{8,1... | collective-permute-start | bytes 393224 | tf_op jit(solution)/shard_map/ppermute | solution.py:31
  32.6 1.4 %band_sum.5 = (f32[1024,64]{1,0:T(8,128)S(1)}, bf16[64,1024]{1,0:T(8,128)(2,1)S(1)}) custom-call(bf16[64,1024]{1,0:T(8,128)(2,1)S(1)} %bitcast.8, bf16[64,1024]{1,0:T(8,128)(2,1)S(1)} %get-tuple-element.13.refs_1_), custom_call_target="tpu_custom_call" | custom-call | flops 1 | bytes 1 | tf_op jit(solution)/shard_map/band_sum/pallas_call | solution.py:412
  34.0 2.2 %collective-permute-done.10 = bf16[64,1024]{1,0:T(8,128)(2,1)S(1)} collective-permute-done((bf16[64,1024]{1,0:T(8,128)(2,1)S(1)}, bf16[64,1024]{1,0:T(8,128)(2,1)S(1)}, u32[]{:S(2)}, u32[]{:S(2)}) %collective-permute-start.10) | collective-permute-done | bytes 131104 | tf_op jit(solution)/shard_map/ppermute | solution.py:31
  36.4 1.9 %factor.1 = (f32[1024,256]{1,0:T(8,128)}, bf16[64,1024]{1,0:T(8,128)(2,1)S(1)}) custom-call(bf16[64,256]{1,0:T(8,128)(2,1)S(1)} %add_add_fusion.pivot_ref, bf16[64,1024]{1,0:T(8,128)(2,1)S(1)} %bitcast.9, f32[256,256]{1,0:T(8,128)S(1)} %get-tuple-element.14.inverse_ref, bf16[64,1024]{1,0:T(8,128)(2,1)S(1)} %add.45.awaited_ref.refs_2_), custom_call_target="tpu_custom_call" | custom-call | flops 50331648 | bytes 196608 | tf_op jit(solution)/shard_map/factor/pallas_call | solution.py:349
  38.3 0.9 %collective-permute-done.9 = bf16[64,1024]{1,0:T(8,128)(2,1)S(1)} collective-permute-done((bf16[64,1024]{1,0:T(8,128)(2,1)S(1)}, bf16[64,1024]{1,0:T(8,128)(2,1)S(1)}, u32[]{:S(2)}, u32[]{:S(2)}) %collective-permute-start.9) | collective-permute-done | bytes 131104 | tf_op jit(solution)/shard_map/ppermute | solution.py:31
  39.2 0.1 collective-permute-start.11
  39.3 0.2 collective-permute-start.13
  39.6 2.5 %band_sum.6 = (f32[1024,64]{1,0:T(8,128)S(1)}, bf16[64,1024]{1,0:T(8,128)(2,1)S(1)}) custom-call(bf16[64,1024]{1,0:T(8,128)(2,1)S(1)} %bitcast.10, bf16[128,1024]{1,0:T(8,128)(2,1)S(1)} %collective-permute-done.1.refs_1_, bf16[64,1024]{1,0:T(8,128)(2,1)S(1)} %add.45.awaited_ref.refs_2_, bf16[64,1024]{1,0:T(8,128)(2,1)S(1)} %collective-permute-done.refs_3_, ...), custom_call_target="tpu_custom_call" | custom-call | flops 1073741824 | bytes 1572864 | tf_op jit(solution)/shard_map/band_sum/pallas_call | solution.py:412
  42.1 2.1 %collective-permute-done.11.refs_2_ = bf16[64,1024]{1,0:T(8,128)(2,1)S(1)} collective-permute-done((bf16[64,1024]{1,0:T(8,128)(2,1)S(1)}, bf16[64,1024]{1,0:T(8,128)(2,1)S(1)}, u32[]{:S(2)}, u32[]{:S(2)}) %collective-permute-start.11) | collective-permute-done | bytes 131104 | tf_op jit(solution)/shard_map/ppermute | solution.py:31
  44.4 2.5 %band_sum.7 = (f32[1024,64]{1,0:T(8,128)S(1)}, bf16[64,1024]{1,0:T(8,128)(2,1)}) custom-call(bf16[64,1024]{1,0:T(8,128)(2,1)S(1)} %bitcast.11, bf16[128,1024]{1,0:T(8,128)(2,1)S(1)} %collective-permute-done.1.refs_1_, bf16[64,1024]{1,0:T(8,128)(2,1)S(1)} %collective-permute-done.11.refs_2_, bf16[128,1024]{1,0:T(8,128)(2,1)S(1)} %collective-permute-done.14.refs_3_, ...), custom_call_target="tpu_custom_call" | custom-call | flops 1073741824 | bytes 1310720 | tf_op jit(solution)/shard_map/band_sum/pallas_call | solution.py:412
  46.9 1.3 %band_sum.8 = (f32[1024,64]{1,0:T(8,128)S(1)}, bf16[64,1024]{1,0:T(8,128)(2,1)}) custom-call(bf16[64,1024]{1,0:T(8,128)(2,1)S(1)} %bitcast.12, bf16[128,1024]{1,0:T(8,128)(2,1)S(1)} %collective-permute-done.13.refs_1_, f32[1024,64]{1,0:T(8,128)S(1)} %get-tuple-element.20.refs_2_), custom_call_target="tpu_custom_call" | custom-call | flops 536870912 | bytes 786432 | tf_op jit(solution)/shard_map/band_sum/pallas_call | solution.py:412
  48.3 2.8 %collective-permute-done.12.refs_1_ = bf16[128,1024]{1,0:T(8,128)(2,1)S(1)} collective-permute-done((bf16[128,1024]{1,0:T(8,128)(2,1)S(1)}, bf16[128,1024]{1,0:T(8,128)(2,1)S(1)}, u32[]{:S(2)}, u32[]{:S(2)}) %collective-permute-start.12) | collective-permute-done | bytes 262176 | tf_op jit(solution)/shard_map/ppermute | solution.py:55
  51.1 2.1 %band_sum.9 = f32[64,1024]{1,0:T(8,128)} custom-call(bf16[64,1024]{1,0:T(8,128)(2,1)S(1)} %bitcast.13, bf16[128,1024]{1,0:T(8,128)(2,1)S(1)} %collective-permute-done.12.refs_1_, f32[1024,64]{1,0:T(8,128)S(1)} %get-tuple-element.21.refs_2_, f32[64,1024]{1,0:T(8,128)S(1)} %get-tuple-element.22.refs_3_), custom_call_target="tpu_custom_call" | custom-call | flops 536870912 | bytes 1048576 | tf_op jit(solution)/shard_map/band_sum/pallas_call | solution.py:412
  (23 shorter events, 0.4 us)
Async XLA Ops:
  0.6 13.5 %collective-permute-start = (bf16[64,1024]{1,0:T(8,128)(2,1)}, bf16[64,1024]{1,0:T(8,128)(2,1)S(1)}, u32[]{:S(2)}, u32[]{:S(2)}) collective-permute-start(bf16[64,1024]{1,0:T(8,128)(2,1)} %bitcast.4), channel_id=1, source_target_pairs={{2,0},{3,1},{0,2},{1,3},{6,4},{7,5},{4,6},{5,7},{10,8},{11,9},{8,1... | collective-permute-start | bytes 393224 | tf_op jit(solution)/shard_map/ppermute | solution.py:31
  5.9 12.7 %copy-start = (bf16[1024,64]{0,1:T(8,128)(2,1)S(1)}, bf16[1024,64]{0,1:T(8,128)(2,1)}, u32[]{:S(2)}) copy-start(bf16[1024,64]{0,1:T(8,128)(2,1)} %param.5) | copy-start | bytes 393220
  5.9 1.3 %collective-permute-start.2 = (bf16[64,256]{1,0:T(8,128)(2,1)S(1)}, bf16[64,256]{1,0:T(8,128)(2,1)S(1)}, u32[]{:S(2)}, u32[]{:S(2)}) collective-permute-start(bf16[64,256]{1,0:T(8,128)(2,1)S(1)} %pick.1), channel_id=1, source_target_pairs={{4,0},{0,4},{12,8},{8,12},{20,16},{16,20},{28,24},{24,28},{5,1},{1... | collective-permute-start | bytes 98312 | tf_op jit(solution)/shard_map/ppermute | solution.py:31
  7.2 4.9 %collective-permute-start.5 = (bf16[64,256]{1,0:T(8,128)(2,1)S(1)}, bf16[64,256]{1,0:T(8,128)(2,1)S(1)}, u32[]{:S(2)}, u32[]{:S(2)}) collective-permute-start(bf16[64,256]{1,0:T(8,128)(2,1)S(1)} %add.36), channel_id=1, source_target_pairs={{24,0},{28,4},{16,8},{20,12},{8,16},{12,20},{0,24},{4,28},{25,1},{... | collective-permute-start | bytes 98312 | tf_op jit(solution)/shard_map/ppermute | solution.py:31
  9.7 3.9 %collective-permute-start.4 = (bf16[64,256]{1,0:T(8,128)(2,1)S(1)}, bf16[64,256]{1,0:T(8,128)(2,1)S(1)}, u32[]{:S(2)}, u32[]{:S(2)}) collective-permute-start(bf16[64,256]{1,0:T(8,128)(2,1)S(1)} %add.36), channel_id=1, source_target_pairs={{16,0},{20,4},{24,8},{28,12},{0,16},{4,20},{8,24},{12,28},{17,1},{... | collective-permute-start | bytes 98312 | tf_op jit(solution)/shard_map/ppermute | solution.py:31
  10.2 3.9 %collective-permute-start.3 = (bf16[64,256]{1,0:T(8,128)(2,1)S(1)}, bf16[64,256]{1,0:T(8,128)(2,1)S(1)}, u32[]{:S(2)}, u32[]{:S(2)}) collective-permute-start(bf16[64,256]{1,0:T(8,128)(2,1)S(1)} %add.36), channel_id=1, source_target_pairs={{8,0},{12,4},{0,8},{4,12},{24,16},{28,20},{16,24},{20,28},{9,1},{1... | collective-permute-start | bytes 98312 | tf_op jit(solution)/shard_map/ppermute | solution.py:31
  14.2 7.5 %copy-start.1 = (f32[1024,64]{0,1:T(8,128)S(1)}, f32[1024,64]{0,1:T(8,128)}, u32[]{:S(2)}) copy-start(f32[1024,64]{0,1:T(8,128)} %param.9) | copy-start | bytes 786436
  14.2 6.2 %collective-permute-start.8 = (bf16[64,256]{1,0:T(8,128)(2,1)S(1)}, bf16[64,256]{1,0:T(8,128)(2,1)S(1)}, u32[]{:S(2)}, u32[]{:S(2)}) collective-permute-start(bf16[64,256]{1,0:T(8,128)(2,1)S(1)} %fusion.1), channel_id=1, source_target_pairs={{3,0},{2,1},{1,2},{0,3},{7,4},{6,5},{5,6},{4,7},{11,8},{10,9},{9,1... | collective-permute-start | bytes 98312 | tf_op jit(solution)/shard_map/ppermute | solution.py:31
  15.6 5.2 %collective-permute-start.7 = (bf16[64,256]{1,0:T(8,128)(2,1)S(1)}, bf16[64,256]{1,0:T(8,128)(2,1)S(1)}, u32[]{:S(2)}, u32[]{:S(2)}) collective-permute-start(bf16[64,256]{1,0:T(8,128)(2,1)S(1)} %fusion.1), channel_id=1, source_target_pairs={{2,0},{3,1},{0,2},{1,3},{6,4},{7,5},{4,6},{5,7},{10,8},{11,9},{8,1... | collective-permute-start | bytes 98312 | tf_op jit(solution)/shard_map/ppermute | solution.py:31
  17.3 4.3 %collective-permute-start.6 = (bf16[64,256]{1,0:T(8,128)(2,1)S(1)}, bf16[64,256]{1,0:T(8,128)(2,1)S(1)}, u32[]{:S(2)}, u32[]{:S(2)}) collective-permute-start(bf16[64,256]{1,0:T(8,128)(2,1)S(1)} %fusion.1), channel_id=1, source_target_pairs={{1,0},{0,1},{3,2},{2,3},{5,4},{4,5},{7,6},{6,7},{9,8},{8,9},{11,10... | collective-permute-start | bytes 98312 | tf_op jit(solution)/shard_map/ppermute | solution.py:31
  18.7 3.0 %copy-start.2 = (f32[256,64]{0,1:T(8,128)S(1)}, f32[256,64]{0,1:T(8,128)}, u32[]{:S(2)}) copy-start(f32[256,64]{0,1:T(8,128)} %param.8) | copy-start | bytes 196612
  18.7 11.8 %collective-permute-start.1 = (bf16[128,1024]{1,0:T(8,128)(2,1)S(1)}, bf16[128,1024]{1,0:T(8,128)(2,1)S(1)}, u32[]{:S(2)}, u32[]{:S(2)}) collective-permute-start(bf16[128,1024]{1,0:T(8,128)(2,1)S(1)} %pad_maximum_fusion), channel_id=1, source_target_pairs={{1,0},{0,1},{3,2},{2,3},{5,4},{4,5},{7,6},{6,7},{9,8},{8,9},{11,10... | collective-permute-start | bytes 786440 | tf_op jit(solution)/shard_map/ppermute | solution.py:31
  30.5 5.7 %collective-permute-start.10 = (bf16[64,1024]{1,0:T(8,128)(2,1)S(1)}, bf16[64,1024]{1,0:T(8,128)(2,1)S(1)}, u32[]{:S(2)}, u32[]{:S(2)}) collective-permute-start(bf16[64,1024]{1,0:T(8,128)(2,1)S(1)} %get-tuple-element.25), channel_id=1, source_target_pairs={{1,0},{0,1},{3,2},{2,3},{5,4},{4,5},{7,6},{6,7},{9,8},{8,9},{11,10... | collective-permute-start | bytes 393224 | tf_op jit(solution)/shard_map/ppermute | solution.py:31
  31.9 7.3 %collective-permute-start.9 = (bf16[64,1024]{1,0:T(8,128)(2,1)S(1)}, bf16[64,1024]{1,0:T(8,128)(2,1)S(1)}, u32[]{:S(2)}, u32[]{:S(2)}) collective-permute-start(bf16[64,1024]{1,0:T(8,128)(2,1)S(1)} %get-tuple-element.25), channel_id=1, source_target_pairs={{2,0},{3,1},{0,2},{1,3},{6,4},{7,5},{4,6},{5,7},{10,8},{11,9},{8,1... | collective-permute-start | bytes 393224 | tf_op jit(solution)/shard_map/ppermute | solution.py:31
  36.3 8.1 %collective-permute-start.14 = (bf16[128,1024]{1,0:T(8,128)(2,1)S(1)}, bf16[128,1024]{1,0:T(8,128)(2,1)S(1)}, u32[]{:S(2)}, u32[]{:S(2)}) collective-permute-start(bf16[128,1024]{1,0:T(8,128)(2,1)S(1)} %pad_maximum_fusion.3), channel_id=1, source_target_pairs={{28,0},{5,1},{30,2},{7,3},{0,4},{9,5},{2,6},{11,7},{4,8},{13,9},{6... | collective-permute-start | bytes 786440 | tf_op jit(solution)/shard_map/ppermute | solution.py:55
  39.2 5.0 %collective-permute-start.11 = (bf16[64,1024]{1,0:T(8,128)(2,1)S(1)}, bf16[64,1024]{1,0:T(8,128)(2,1)S(1)}, u32[]{:S(2)}, u32[]{:S(2)}) collective-permute-start(bf16[64,1024]{1,0:T(8,128)(2,1)S(1)} %add.46.refs_4_), channel_id=1, source_target_pairs={{1,0},{0,1},{3,2},{2,3},{5,4},{4,5},{7,6},{6,7},{9,8},{8,9},{11,10... | collective-permute-start | bytes 393224 | tf_op jit(solution)/shard_map/ppermute | solution.py:31
  39.3 7.6 %collective-permute-start.13 = (bf16[128,1024]{1,0:T(8,128)(2,1)S(1)}, bf16[128,1024]{1,0:T(8,128)(2,1)S(1)}, u32[]{:S(2)}, u32[]{:S(2)}) collective-permute-start(bf16[128,1024]{1,0:T(8,128)(2,1)S(1)} %pad_maximum_fusion.2), channel_id=1, source_target_pairs={{28,0},{29,1},{6,2},{7,3},{0,4},{1,5},{10,6},{11,7},{4,8},{5,9},{1... | collective-permute-start | bytes 786440 | tf_op jit(solution)/shard_map/ppermute | solution.py:55
  44.3 6.7 %collective-permute-start.12 = (bf16[128,1024]{1,0:T(8,128)(2,1)S(1)}, bf16[128,1024]{1,0:T(8,128)(2,1)S(1)}, u32[]{:S(2)}, u32[]{:S(2)}) collective-permute-start(bf16[128,1024]{1,0:T(8,128)(2,1)S(1)} %pad_maximum_fusion.1), channel_id=1, source_target_pairs={{28,0},{29,1},{6,2},{7,3},{0,4},{1,5},{10,6},{11,7},{4,8},{5,9},{1... | collective-permute-start | bytes 786440 | tf_op jit(solution)/shard_map/ppermute | solution.py:55

commit v15 on v14

--- a/solution.py
+++ b/solution.py
@@ -115,6 +115,10 @@
 
 def column(strip, lane):
     return jnp.broadcast_to(strip[:, lane:lane + 1], strip.shape)
+
+
+def column_of(square, lane):
+    return jnp.broadcast_to(square[:, lane:lane + 1], (STRIP, LANES))
 
 
 def row(strip, i):
@@ -153,7 +157,7 @@
     return total_of([column if entry is None else entry * column for entry, column in zip(entries, columns)])
 
 
-def small_inverse(columns, fetch):
+def block_rows(columns, entered, fetch):
     a = [[row(columns[k], i) for k in range(i + 1)] for i in range(STRIP)]
     yield
     below, x, scale = yield from four_pivots([list(entries) for entries in a])
@@ -162,95 +166,73 @@
         [a[4 + i][4 + j] - total_of([below[i][k] * below[j][k] for k in range(4)]) for j in range(i + 1)]
         for i in range(4)
     ]
-    back = [[total_of([below[i][k] * one[k][j] for k in range(j, 4)]) for j in range(4)] for i in range(4)]
-    coming = fetch()
-    if coming is not None:
-        lower, diagonal = coming
-        found = [combined(one[k], lower[:k + 1]) for k in range(4)]
-        diagonal = [
-            diagonal[j] - total_of([found[k] * row(found[k], j) for k in range(4)]) for j in range(STRIP)
-        ]
-        lower = [lower[4 + m] - total_of([found[j] * below[m][j] for j in range(4)]) for m in range(4)]
+
+    def halfway(values):
+        upper = [combined(one[k], values[:k + 1]) for k in range(4)]
+        return upper, [values[4 + m] - total_of([below[m][j] * upper[j] for j in range(4)]) for m in range(4)]
+
+    sides = [halfway(values) for values in (entered, fetch()) if values is not None]
     _, x, scale = yield from four_pivots(rest)
-    if coming is not None:
-        plain = [combined(x[k], lower[:k + 1]) for k in range(4)]
-        squares = [scale[k] * scale[k] for k in range(4)]
-        diagonal = [
-            diagonal[j] - total_of([plain[k] * row(plain[k], j) * squares[k] for k in range(4)])
-            for j in range(STRIP)
-        ]
-        coming = found + [plain[k] * scale[k] for k in range(4)], diagonal
     two = [[scale[i] if entry is None else entry * scale[i] for entry in x[i]] for i in range(4)]
-    corner = [[-total_of([two[i][m] * back[m][j] for m in range(i + 1)]) for j in range(4)] for i in range(4)]
-    return one + [corner[i] + two[i] for i in range(4)], coming
+    solved = [upper + [combined(two[k], lower[:k + 1]) for k in range(4)] for upper, lower in sides]
+    return solved[0], solved[1] if len(solved) > 1 else None
 
 
 def inverse_factor(strips, beside):
     lane = lax.broadcasted_iota(jnp.int32, (STRIP, LANES), 1)
     level = lax.broadcasted_iota(jnp.int32, (STRIP, LANES), 0)
     strips = list(strips)
-    result = [None] * len(strips)
+    result = []
     waiting = []
 
-    def factor_columns(r, start, t):
-        columns = [column(strips[r], start + j) for j in range(STRIP)]
-        return [total_of([columns[j] * t[k][j] for j in range(k + 1)]) for k in range(STRIP)]
-
-    def finish(p, t, found):
+    def finish(p, own, rows):
+        turned = []
+
+        def turn():
+            turned.append(jnp.transpose(result[p]))
+
+        def update(r):
+            factors = turned[0][r * STRIP:(r + 1) * STRIP, :]
+            terms = [column_of(factors, k) * rows[k] for k in range(STRIP)]
+            strips[r] = jnp.where(own, 0.0, strips[r]) - total_of(terms)
+
+        return [turn] + [functools.partial(update, r) for r in range(p + 2, len(strips))]
+
+    columns = [column(strips[0], k) for k in range(STRIP)]
+    for p in range(len(strips)):
         start = p * STRIP
         own = (lane >= start) & (lane < start + STRIP)
-        rows = []
-
-        def scaled():
-            entered = jnp.where(own, jnp.where(lane - start == level, 1.0, 0.0), strips[p])
-            terms = []
-            for k in range(STRIP):
-                t_column = t[STRIP - 1][k]
-                for i in range(STRIP - 2, k - 1, -1):
-                    t_column = jnp.where(level == i, t[i][k], t_column)
-                if k:
-                    t_column = jnp.where(level < k, 0.0, t_column)
-                terms.append(t_column * row(entered, k))
-            done = total_of(terms)
-            result[p] = jnp.where(lane < start + STRIP, done, 0.0)
-            rows.extend(row(done, k) for k in range(STRIP))
-
-        def updated(r):
-            l_columns = found if r == p + 1 else factor_columns(r, start, t)
-            update = total_of([l_columns[k] * rows[k] for k in range(STRIP)])
-            strips[r] = jnp.where(own, 0.0, strips[r]) - update
-
-        return [scaled] + [functools.partial(updated, r) for r in range(p + 1, len(strips))]
-
-    def coming_to(p):
-        if p + 1 == len(strips):
-            return None
-        start = p * STRIP
-        return tuple([column(strips[p + 1], first + j) for j in range(STRIP)] for first in (start, start + STRIP))
-
-    columns = [column(strips[0], k) for k in range(STRIP)]
-    for p in range(len(strips)):
         if beside:
             waiting.append(beside.pop(0))
-        steps = small_inverse(columns, functools.partial(coming_to, p))
+        entered = jnp.where(own, jnp.where(lane - start == level, 1.0, 0.0), strips[p])
+
+        def fetch():
+            if p + 1 == len(strips):
+                return None
+            return [column(strips[p + 1], start + j) for j in range(STRIP)]
+
+        steps = block_rows(columns, [row(entered, k) for k in range(STRIP)], fetch)
         while True:
             try:
                 next(steps)
             except StopIteration as ended:
-                t, coming = ended.value
+                rows, found = ended.value
                 break
             for _ in range(2):
                 if waiting:
                     waiting.pop(0)()
         while waiting:
             waiting.pop(0)()
-        found = None
-        if coming is not None:
-            found, columns = coming
-        waiting = finish(p, t, found)
-    while waiting:
-        waiting.pop(0)()
-    return result
+        done = rows[0]
+        for k in range(1, STRIP):
+            done = jnp.where(level == k, rows[k], done)
+        result.append(done)
+        if found is not None:
+            update = total_of([found[k] * rows[k] for k in range(STRIP)])
+            strips[p + 1] = jnp.where(own, 0.0, strips[p + 1]) - update
+            columns = [column(strips[p + 1], start + STRIP + k) for k in range(STRIP)]
+            waiting = finish(p, own, rows)
+    return [jnp.where(lane < (p + 1) * STRIP, done, 0.0) for p, done in enumerate(result)]
 
 
 def probe_kernel(

time: 53.3 us -> 56.3 us (1.056)
  Pallas kernels: 21.7 us -> 24.8 us
    pallas_call x1, Pallas kernels: 8.79 us -> 11.8 us  [probes_of(): pl.pallas_call(probe_kernel, out_shape=(pltpu.VMEM((size, size), jnp.floa...]
  transfers between devices with their start and end apart: 15 -> 15, of which waited for: 11 -> 11; matrix products, arithmetic and copies ran while one was open for 0% -> 0% of each run, Pallas kernels for 37% -> 40%
where the time goes in v15:
time: 56.3 us; the launch traced here: 56.2 us
  Pallas kernels  24.8 us (44%)
  starting transfers between devices  15.4 us (27%)
  waiting for transfers between devices  14.9 us (26%)
  between operations  0.84 us (1%)
    ppermute x12, starting transfers between devices, swapped(): lax.ppermute(value, axis, [(i ^ bit, i) for i in range(lax.axis_size(axis...  15.1 us
    ppermute x12, waiting for transfers between devices, swapped(): lax.ppermute(value, axis, [(i ^ bit, i) for i in range(lax.axis_size(axis...  12.1 us
    pallas_call x1, Pallas kernels, probes_of(): pl.pallas_call(probe_kernel, out_shape=(pltpu.VMEM((size, size), jnp.floa...  11.8 us
    pallas_call x5, Pallas kernels, band_sum(): pl.pallas_call(functools.partial(band_kernel, tuple(places), first, last)...  9.85 us
    ppermute x3, waiting for transfers between devices, cross(): return lax.ppermute(piece, ('gx', 'gy'), pairs)  2.82 us
    pallas_call x1, Pallas kernels, factor_of(): pl.pallas_call(factor_kernel, out_shape=(jax.ShapeDtypeStruct((count, siz...  1.91 us
    pallas_call x1, Pallas kernels, pick(): pl.pallas_call(pick_kernel, out_shape=pltpu.VMEM((points_t.shape[0], 2 *...  1.17 us
  transfers between devices with their start and end apart: 15, of which 11 were waited for; matrix products, arithmetic and copies ran while one was open for 0% of the time, Pallas kernels for 40%

profile of v15, /device:TPU:0, one launch (start us, length us, event | category | flops | bytes accessed | tf_op | source)
XLA Modules:
  0.0 56.2 jit_solution(10743954854102321968)
XLA Ops:
  0.6 4.1 %collective-permute-start = (bf16[64,1024]{1,0:T(8,128)(2,1)}, bf16[64,1024]{1,0:T(8,128)(2,1)S(1)}, u32[]{:S(2)}, u32[]{:S(2)}) collective-permute-start(bf16[64,1024]{1,0:T(8,128)(2,1)} %bitcast.4), channel_id=1, source_target_pairs={{2,0},{3,1},{0,2},{1,3},{6,4},{7,5},{4,6},{5,7},{10,8},{11,9},{8,1... | collective-permute-start | bytes 393224 | tf_op jit(solution)/shard_map/ppermute | solution.py:31
  4.7 1.2 %pick.1 = bf16[64,256]{1,0:T(8,128)(2,1)S(1)} custom-call(s32[2]{0:T(128)} %owner_ref.1, s32[2,128]{1,0:T(2,128)} %pivot_ref.1, bf16[64,1024]{1,0:T(8,128)(2,1)} %bitcast.5), custom_call_target="tpu_custom_call" | custom-call | tf_op jit(solution)/shard_map/pick/pallas_call | solution.py:107
  5.9 0.1 collective-permute-start.2
  6.0 1.2 %collective-permute-done.2 = bf16[64,256]{1,0:T(8,128)(2,1)S(1)} collective-permute-done((bf16[64,256]{1,0:T(8,128)(2,1)S(1)}, bf16[64,256]{1,0:T(8,128)(2,1)S(1)}, u32[]{:S(2)}, u32[]{:S(2)}) %collective-permute-start.2) | collective-permute-done | bytes 32800 | tf_op jit(solution)/shard_map/ppermute | solution.py:31
  7.2 2.5 %collective-permute-start.5 = (bf16[64,256]{1,0:T(8,128)(2,1)S(1)}, bf16[64,256]{1,0:T(8,128)(2,1)S(1)}, u32[]{:S(2)}, u32[]{:S(2)}) collective-permute-start(bf16[64,256]{1,0:T(8,128)(2,1)S(1)} %add.36), channel_id=1, source_target_pairs={{24,0},{28,4},{16,8},{20,12},{8,16},{12,20},{0,24},{4,28},{25,1},{... | collective-permute-start | bytes 98312 | tf_op jit(solution)/shard_map/ppermute | solution.py:31
  9.7 0.5 collective-permute-start.4
  10.2 0.5 collective-permute-start.3
  10.8 1.3 %collective-permute-done.5 = bf16[64,256]{1,0:T(8,128)(2,1)S(1)} collective-permute-done((bf16[64,256]{1,0:T(8,128)(2,1)S(1)}, bf16[64,256]{1,0:T(8,128)(2,1)S(1)}, u32[]{:S(2)}, u32[]{:S(2)}) %collective-permute-start.5) | collective-permute-done | bytes 32800 | tf_op jit(solution)/shard_map/ppermute | solution.py:31
  12.1 1.5 %collective-permute-done.4 = bf16[64,256]{1,0:T(8,128)(2,1)S(1)} collective-permute-done((bf16[64,256]{1,0:T(8,128)(2,1)S(1)}, bf16[64,256]{1,0:T(8,128)(2,1)S(1)}, u32[]{:S(2)}, u32[]{:S(2)}) %collective-permute-start.4) | collective-permute-done | bytes 32800 | tf_op jit(solution)/shard_map/ppermute | solution.py:31
  13.6 0.5 collective-permute-done.3
  14.2 1.4 %collective-permute-start.8 = (bf16[64,256]{1,0:T(8,128)(2,1)S(1)}, bf16[64,256]{1,0:T(8,128)(2,1)S(1)}, u32[]{:S(2)}, u32[]{:S(2)}) collective-permute-start(bf16[64,256]{1,0:T(8,128)(2,1)S(1)} %fusion.1), channel_id=1, source_target_pairs={{3,0},{2,1},{1,2},{0,3},{7,4},{6,5},{5,6},{4,7},{11,8},{10,9},{9,1... | collective-permute-start | bytes 98312 | tf_op jit(solution)/shard_map/ppermute | solution.py:31
  15.6 1.7 %collective-permute-start.7 = (bf16[64,256]{1,0:T(8,128)(2,1)S(1)}, bf16[64,256]{1,0:T(8,128)(2,1)S(1)}, u32[]{:S(2)}, u32[]{:S(2)}) collective-permute-start(bf16[64,256]{1,0:T(8,128)(2,1)S(1)} %fusion.1), channel_id=1, source_target_pairs={{2,0},{3,1},{0,2},{1,3},{6,4},{7,5},{4,6},{5,7},{10,8},{11,9},{8,1... | collective-permute-start | bytes 98312 | tf_op jit(solution)/shard_map/ppermute | solution.py:31
  17.3 1.3 %collective-permute-start.6 = (bf16[64,256]{1,0:T(8,128)(2,1)S(1)}, bf16[64,256]{1,0:T(8,128)(2,1)S(1)}, u32[]{:S(2)}, u32[]{:S(2)}) collective-permute-start(bf16[64,256]{1,0:T(8,128)(2,1)S(1)} %fusion.1), channel_id=1, source_target_pairs={{1,0},{0,1},{3,2},{2,3},{5,4},{4,5},{7,6},{6,7},{9,8},{8,9},{11,10... | collective-permute-start | bytes 98312 | tf_op jit(solution)/shard_map/ppermute | solution.py:31
  18.7 0.7 %collective-permute-start.1 = (bf16[128,1024]{1,0:T(8,128)(2,1)S(1)}, bf16[128,1024]{1,0:T(8,128)(2,1)S(1)}, u32[]{:S(2)}, u32[]{:S(2)}) collective-permute-start(bf16[128,1024]{1,0:T(8,128)(2,1)S(1)} %pad_maximum_fusion), channel_id=1, source_target_pairs={{1,0},{0,1},{3,2},{2,3},{5,4},{4,5},{7,6},{6,7},{9,8},{8,9},{11,10... | collective-permute-start | bytes 786440 | tf_op jit(solution)/shard_map/ppermute | solution.py:31
  19.4 1.0 %collective-permute-done.8 = bf16[64,256]{1,0:T(8,128)(2,1)S(1)} collective-permute-done((bf16[64,256]{1,0:T(8,128)(2,1)S(1)}, bf16[64,256]{1,0:T(8,128)(2,1)S(1)}, u32[]{:S(2)}, u32[]{:S(2)}) %collective-permute-start.8) | collective-permute-done | bytes 32800 | tf_op jit(solution)/shard_map/ppermute | solution.py:31
  20.4 0.3 collective-permute-done.7
  20.8 0.9 %collective-permute-done.6 = bf16[64,256]{1,0:T(8,128)(2,1)S(1)} collective-permute-done((bf16[64,256]{1,0:T(8,128)(2,1)S(1)}, bf16[64,256]{1,0:T(8,128)(2,1)S(1)}, u32[]{:S(2)}, u32[]{:S(2)}) %collective-permute-start.6) | collective-permute-done | bytes 32800 | tf_op jit(solution)/shard_map/ppermute | solution.py:31
  21.6 11.8 %probes.1 = (f32[256,256]{1,0:T(8,128)S(1)}, f32[64,1024]{1,0:T(8,128)S(1)}, bf16[64,1024]{1,0:T(8,128)(2,1)S(1)}) custom-call(bf16[64,256]{1,0:T(8,128)(2,1)S(1)} %add_add_fusion.pivot_ref, bf16[64,1024]{1,0:T(8,128)(2,1)S(1)} %bitcast.7, f32[64,256]{1,0:T(8,128)S(1)} %bitcast.15, f32[64,1024]{1,0:T(8,128)S(1)} %bitcast.14), custom_call_target="tpu_custom_call" | custom-call | flops 17179869184 | bytes 1 | tf_op jit(solution)/shard_map/probes/pallas_call | solution.py:290
  33.5 1.4 %collective-permute-start.10 = (bf16[64,1024]{1,0:T(8,128)(2,1)S(1)}, bf16[64,1024]{1,0:T(8,128)(2,1)S(1)}, u32[]{:S(2)}, u32[]{:S(2)}) collective-permute-start(bf16[64,1024]{1,0:T(8,128)(2,1)S(1)} %get-tuple-element.25), channel_id=1, source_target_pairs={{1,0},{0,1},{3,2},{2,3},{5,4},{4,5},{7,6},{6,7},{9,8},{8,9},{11,10... | collective-permute-start | bytes 393224 | tf_op jit(solution)/shard_map/ppermute | solution.py:31
  35.0 0.7 %collective-permute-start.9 = (bf16[64,1024]{1,0:T(8,128)(2,1)S(1)}, bf16[64,1024]{1,0:T(8,128)(2,1)S(1)}, u32[]{:S(2)}, u32[]{:S(2)}) collective-permute-start(bf16[64,1024]{1,0:T(8,128)(2,1)S(1)} %get-tuple-element.25), channel_id=1, source_target_pairs={{2,0},{3,1},{0,2},{1,3},{6,4},{7,5},{4,6},{5,7},{10,8},{11,9},{8,1... | collective-permute-start | bytes 393224 | tf_op jit(solution)/shard_map/ppermute | solution.py:31
  35.6 1.4 %band_sum.5 = (f32[1024,64]{1,0:T(8,128)S(1)}, bf16[64,1024]{1,0:T(8,128)(2,1)S(1)}) custom-call(bf16[64,1024]{1,0:T(8,128)(2,1)S(1)} %bitcast.8, bf16[64,1024]{1,0:T(8,128)(2,1)S(1)} %get-tuple-element.13.refs_1_), custom_call_target="tpu_custom_call" | custom-call | flops 1 | bytes 1 | tf_op jit(solution)/shard_map/band_sum/pallas_call | solution.py:394
  37.0 2.2 %collective-permute-done.10 = bf16[64,1024]{1,0:T(8,128)(2,1)S(1)} collective-permute-done((bf16[64,1024]{1,0:T(8,128)(2,1)S(1)}, bf16[64,1024]{1,0:T(8,128)(2,1)S(1)}, u32[]{:S(2)}, u32[]{:S(2)}) %collective-permute-start.10) | collective-permute-done | bytes 131104 | tf_op jit(solution)/shard_map/ppermute | solution.py:31
  39.4 1.9 %factor.1 = (f32[1024,256]{1,0:T(8,128)}, bf16[64,1024]{1,0:T(8,128)(2,1)S(1)}) custom-call(bf16[64,256]{1,0:T(8,128)(2,1)S(1)} %add_add_fusion.pivot_ref, bf16[64,1024]{1,0:T(8,128)(2,1)S(1)} %bitcast.9, f32[256,256]{1,0:T(8,128)S(1)} %get-tuple-element.14.inverse_ref, bf16[64,1024]{1,0:T(8,128)(2,1)S(1)} %add.45.awaited_ref.refs_2_), custom_call_target="tpu_custom_call" | custom-call | flops 50331648 | bytes 196608 | tf_op jit(solution)/shard_map/factor/pallas_call | solution.py:331
  41.3 0.9 %collective-permute-done.9 = bf16[64,1024]{1,0:T(8,128)(2,1)S(1)} collective-permute-done((bf16[64,1024]{1,0:T(8,128)(2,1)S(1)}, bf16[64,1024]{1,0:T(8,128)(2,1)S(1)}, u32[]{:S(2)}, u32[]{:S(2)}) %collective-permute-start.9) | collective-permute-done | bytes 131104 | tf_op jit(solution)/shard_map/ppermute | solution.py:31
  42.3 0.1 collective-permute-start.11
  42.4 0.2 collective-permute-start.13
  42.6 2.5 %band_sum.6 = (f32[1024,64]{1,0:T(8,128)S(1)}, bf16[64,1024]{1,0:T(8,128)(2,1)S(1)}) custom-call(bf16[64,1024]{1,0:T(8,128)(2,1)S(1)} %bitcast.10, bf16[128,1024]{1,0:T(8,128)(2,1)S(1)} %collective-permute-done.1.refs_1_, bf16[64,1024]{1,0:T(8,128)(2,1)S(1)} %add.45.awaited_ref.refs_2_, bf16[64,1024]{1,0:T(8,128)(2,1)S(1)} %collective-permute-done.refs_3_, ...), custom_call_target="tpu_custom_call" | custom-call | flops 1073741824 | bytes 1572864 | tf_op jit(solution)/shard_map/band_sum/pallas_call | solution.py:394
  45.2 2.1 %collective-permute-done.11.refs_2_ = bf16[64,1024]{1,0:T(8,128)(2,1)S(1)} collective-permute-done((bf16[64,1024]{1,0:T(8,128)(2,1)S(1)}, bf16[64,1024]{1,0:T(8,128)(2,1)S(1)}, u32[]{:S(2)}, u32[]{:S(2)}) %collective-permute-start.11) | collective-permute-done | bytes 131104 | tf_op jit(solution)/shard_map/ppermute | solution.py:31
  47.4 2.5 %band_sum.7 = (f32[1024,64]{1,0:T(8,128)S(1)}, bf16[64,1024]{1,0:T(8,128)(2,1)}) custom-call(bf16[64,1024]{1,0:T(8,128)(2,1)S(1)} %bitcast.11, bf16[128,1024]{1,0:T(8,128)(2,1)S(1)} %collective-permute-done.1.refs_1_, bf16[64,1024]{1,0:T(8,128)(2,1)S(1)} %collective-permute-done.11.refs_2_, bf16[128,1024]{1,0:T(8,128)(2,1)S(1)} %collective-permute-done.14.refs_3_, ...), custom_call_target="tpu_custom_call" | custom-call | flops 1073741824 | bytes 1310720 | tf_op jit(solution)/shard_map/band_sum/pallas_call | solution.py:394
  50.0 1.3 %band_sum.8 = (f32[1024,64]{1,0:T(8,128)S(1)}, bf16[64,1024]{1,0:T(8,128)(2,1)}) custom-call(bf16[64,1024]{1,0:T(8,128)(2,1)S(1)} %bitcast.12, bf16[128,1024]{1,0:T(8,128)(2,1)S(1)} %collective-permute-done.13.refs_1_, f32[1024,64]{1,0:T(8,128)S(1)} %get-tuple-element.20.refs_2_), custom_call_target="tpu_custom_call" | custom-call | flops 536870912 | bytes 786432 | tf_op jit(solution)/shard_map/band_sum/pallas_call | solution.py:394
  51.3 2.8 %collective-permute-done.12.refs_1_ = bf16[128,1024]{1,0:T(8,128)(2,1)S(1)} collective-permute-done((bf16[128,1024]{1,0:T(8,128)(2,1)S(1)}, bf16[128,1024]{1,0:T(8,128)(2,1)S(1)}, u32[]{:S(2)}, u32[]{:S(2)}) %collective-permute-start.12) | collective-permute-done | bytes 262176 | tf_op jit(solution)/shard_map/ppermute | solution.py:55
  54.1 2.1 %band_sum.9 = f32[64,1024]{1,0:T(8,128)} custom-call(bf16[64,1024]{1,0:T(8,128)(2,1)S(1)} %bitcast.13, bf16[128,1024]{1,0:T(8,128)(2,1)S(1)} %collective-permute-done.12.refs_1_, f32[1024,64]{1,0:T(8,128)S(1)} %get-tuple-element.21.refs_2_, f32[64,1024]{1,0:T(8,128)S(1)} %get-tuple-element.22.refs_3_), custom_call_target="tpu_custom_call" | custom-call | flops 536870912 | bytes 1048576 | tf_op jit(solution)/shard_map/band_sum/pallas_call | solution.py:394
  (23 shorter events, 0.4 us)
Async XLA Ops:
  0.6 13.5 %collective-permute-start = (bf16[64,1024]{1,0:T(8,128)(2,1)}, bf16[64,1024]{1,0:T(8,128)(2,1)S(1)}, u32[]{:S(2)}, u32[]{:S(2)}) collective-permute-start(bf16[64,1024]{1,0:T(8,128)(2,1)} %bitcast.4), channel_id=1, source_target_pairs={{2,0},{3,1},{0,2},{1,3},{6,4},{7,5},{4,6},{5,7},{10,8},{11,9},{8,1... | collective-permute-start | bytes 393224 | tf_op jit(solution)/shard_map/ppermute | solution.py:31
  5.9 12.7 %copy-start = (bf16[1024,64]{0,1:T(8,128)(2,1)S(1)}, bf16[1024,64]{0,1:T(8,128)(2,1)}, u32[]{:S(2)}) copy-start(bf16[1024,64]{0,1:T(8,128)(2,1)} %param.5) | copy-start | bytes 393220
  5.9 1.3 %collective-permute-start.2 = (bf16[64,256]{1,0:T(8,128)(2,1)S(1)}, bf16[64,256]{1,0:T(8,128)(2,1)S(1)}, u32[]{:S(2)}, u32[]{:S(2)}) collective-permute-start(bf16[64,256]{1,0:T(8,128)(2,1)S(1)} %pick.1), channel_id=1, source_target_pairs={{4,0},{0,4},{12,8},{8,12},{20,16},{16,20},{28,24},{24,28},{5,1},{1... | collective-permute-start | bytes 98312 | tf_op jit(solution)/shard_map/ppermute | solution.py:31
  7.2 4.9 %collective-permute-start.5 = (bf16[64,256]{1,0:T(8,128)(2,1)S(1)}, bf16[64,256]{1,0:T(8,128)(2,1)S(1)}, u32[]{:S(2)}, u32[]{:S(2)}) collective-permute-start(bf16[64,256]{1,0:T(8,128)(2,1)S(1)} %add.36), channel_id=1, source_target_pairs={{24,0},{28,4},{16,8},{20,12},{8,16},{12,20},{0,24},{4,28},{25,1},{... | collective-permute-start | bytes 98312 | tf_op jit(solution)/shard_map/ppermute | solution.py:31
  9.7 3.9 %collective-permute-start.4 = (bf16[64,256]{1,0:T(8,128)(2,1)S(1)}, bf16[64,256]{1,0:T(8,128)(2,1)S(1)}, u32[]{:S(2)}, u32[]{:S(2)}) collective-permute-start(bf16[64,256]{1,0:T(8,128)(2,1)S(1)} %add.36), channel_id=1, source_target_pairs={{16,0},{20,4},{24,8},{28,12},{0,16},{4,20},{8,24},{12,28},{17,1},{... | collective-permute-start | bytes 98312 | tf_op jit(solution)/shard_map/ppermute | solution.py:31
  10.2 3.9 %collective-permute-start.3 = (bf16[64,256]{1,0:T(8,128)(2,1)S(1)}, bf16[64,256]{1,0:T(8,128)(2,1)S(1)}, u32[]{:S(2)}, u32[]{:S(2)}) collective-permute-start(bf16[64,256]{1,0:T(8,128)(2,1)S(1)} %add.36), channel_id=1, source_target_pairs={{8,0},{12,4},{0,8},{4,12},{24,16},{28,20},{16,24},{20,28},{9,1},{1... | collective-permute-start | bytes 98312 | tf_op jit(solution)/shard_map/ppermute | solution.py:31
  14.2 7.5 %copy-start.1 = (f32[1024,64]{0,1:T(8,128)S(1)}, f32[1024,64]{0,1:T(8,128)}, u32[]{:S(2)}) copy-start(f32[1024,64]{0,1:T(8,128)} %param.9) | copy-start | bytes 786436
  14.2 6.2 %collective-permute-start.8 = (bf16[64,256]{1,0:T(8,128)(2,1)S(1)}, bf16[64,256]{1,0:T(8,128)(2,1)S(1)}, u32[]{:S(2)}, u32[]{:S(2)}) collective-permute-start(bf16[64,256]{1,0:T(8,128)(2,1)S(1)} %fusion.1), channel_id=1, source_target_pairs={{3,0},{2,1},{1,2},{0,3},{7,4},{6,5},{5,6},{4,7},{11,8},{10,9},{9,1... | collective-permute-start | bytes 98312 | tf_op jit(solution)/shard_map/ppermute | solution.py:31
  15.6 5.2 %collective-permute-start.7 = (bf16[64,256]{1,0:T(8,128)(2,1)S(1)}, bf16[64,256]{1,0:T(8,128)(2,1)S(1)}, u32[]{:S(2)}, u32[]{:S(2)}) collective-permute-start(bf16[64,256]{1,0:T(8,128)(2,1)S(1)} %fusion.1), channel_id=1, source_target_pairs={{2,0},{3,1},{0,2},{1,3},{6,4},{7,5},{4,6},{5,7},{10,8},{11,9},{8,1... | collective-permute-start | bytes 98312 | tf_op jit(solution)/shard_map/ppermute | solution.py:31
  17.3 4.3 %collective-permute-start.6 = (bf16[64,256]{1,0:T(8,128)(2,1)S(1)}, bf16[64,256]{1,0:T(8,128)(2,1)S(1)}, u32[]{:S(2)}, u32[]{:S(2)}) collective-permute-start(bf16[64,256]{1,0:T(8,128)(2,1)S(1)} %fusion.1), channel_id=1, source_target_pairs={{1,0},{0,1},{3,2},{2,3},{5,4},{4,5},{7,6},{6,7},{9,8},{8,9},{11,10... | collective-permute-start | bytes 98312 | tf_op jit(solution)/shard_map/ppermute | solution.py:31
  18.7 3.0 %copy-start.2 = (f32[256,64]{0,1:T(8,128)S(1)}, f32[256,64]{0,1:T(8,128)}, u32[]{:S(2)}) copy-start(f32[256,64]{0,1:T(8,128)} %param.8) | copy-start | bytes 196612
  18.7 14.8 %collective-permute-start.1 = (bf16[128,1024]{1,0:T(8,128)(2,1)S(1)}, bf16[128,1024]{1,0:T(8,128)(2,1)S(1)}, u32[]{:S(2)}, u32[]{:S(2)}) collective-permute-start(bf16[128,1024]{1,0:T(8,128)(2,1)S(1)} %pad_maximum_fusion), channel_id=1, source_target_pairs={{1,0},{0,1},{3,2},{2,3},{5,4},{4,5},{7,6},{6,7},{9,8},{8,9},{11,10... | collective-permute-start | bytes 786440 | tf_op jit(solution)/shard_map/ppermute | solution.py:31
  33.5 5.7 %collective-permute-start.10 = (bf16[64,1024]{1,0:T(8,128)(2,1)S(1)}, bf16[64,1024]{1,0:T(8,128)(2,1)S(1)}, u32[]{:S(2)}, u32[]{:S(2)}) collective-permute-start(bf16[64,1024]{1,0:T(8,128)(2,1)S(1)} %get-tuple-element.25), channel_id=1, source_target_pairs={{1,0},{0,1},{3,2},{2,3},{5,4},{4,5},{7,6},{6,7},{9,8},{8,9},{11,10... | collective-permute-start | bytes 393224 | tf_op jit(solution)/shard_map/ppermute | solution.py:31
  35.0 7.3 %collective-permute-start.9 = (bf16[64,1024]{1,0:T(8,128)(2,1)S(1)}, bf16[64,1024]{1,0:T(8,128)(2,1)S(1)}, u32[]{:S(2)}, u32[]{:S(2)}) collective-permute-start(bf16[64,1024]{1,0:T(8,128)(2,1)S(1)} %get-tuple-element.25), channel_id=1, source_target_pairs={{2,0},{3,1},{0,2},{1,3},{6,4},{7,5},{4,6},{5,7},{10,8},{11,9},{8,1... | collective-permute-start | bytes 393224 | tf_op jit(solution)/shard_map/ppermute | solution.py:31
  39.3 8.1 %collective-permute-start.14 = (bf16[128,1024]{1,0:T(8,128)(2,1)S(1)}, bf16[128,1024]{1,0:T(8,128)(2,1)S(1)}, u32[]{:S(2)}, u32[]{:S(2)}) collective-permute-start(bf16[128,1024]{1,0:T(8,128)(2,1)S(1)} %pad_maximum_fusion.3), channel_id=1, source_target_pairs={{28,0},{5,1},{30,2},{7,3},{0,4},{9,5},{2,6},{11,7},{4,8},{13,9},{6... | collective-permute-start | bytes 786440 | tf_op jit(solution)/shard_map/ppermute | solution.py:55
  42.3 5.0 %collective-permute-start.11 = (bf16[64,1024]{1,0:T(8,128)(2,1)S(1)}, bf16[64,1024]{1,0:T(8,128)(2,1)S(1)}, u32[]{:S(2)}, u32[]{:S(2)}) collective-permute-start(bf16[64,1024]{1,0:T(8,128)(2,1)S(1)} %add.46.refs_4_), channel_id=1, source_target_pairs={{1,0},{0,1},{3,2},{2,3},{5,4},{4,5},{7,6},{6,7},{9,8},{8,9},{11,10... | collective-permute-start | bytes 393224 | tf_op jit(solution)/shard_map/ppermute | solution.py:31
  42.4 7.6 %collective-permute-start.13 = (bf16[128,1024]{1,0:T(8,128)(2,1)S(1)}, bf16[128,1024]{1,0:T(8,128)(2,1)S(1)}, u32[]{:S(2)}, u32[]{:S(2)}) collective-permute-start(bf16[128,1024]{1,0:T(8,128)(2,1)S(1)} %pad_maximum_fusion.2), channel_id=1, source_target_pairs={{28,0},{29,1},{6,2},{7,3},{0,4},{1,5},{10,6},{11,7},{4,8},{5,9},{1... | collective-permute-start | bytes 786440 | tf_op jit(solution)/shard_map/ppermute | solution.py:55
  47.4 6.7 %collective-permute-start.12 = (bf16[128,1024]{1,0:T(8,128)(2,1)S(1)}, bf16[128,1024]{1,0:T(8,128)(2,1)S(1)}, u32[]{:S(2)}, u32[]{:S(2)}) collective-permute-start(bf16[128,1024]{1,0:T(8,128)(2,1)S(1)} %pad_maximum_fusion.1), channel_id=1, source_target_pairs={{28,0},{29,1},{6,2},{7,3},{0,4},{1,5},{10,6},{11,7},{4,8},{5,9},{1... | collective-permute-start | bytes 786440 | tf_op jit(solution)/shard_map/ppermute | solution.py:55

commit v16 on v15

--- a/solution.py
+++ b/solution.py
@@ -171,11 +171,29 @@
         upper = [combined(one[k], values[:k + 1]) for k in range(4)]
         return upper, [values[4 + m] - total_of([below[m][j] * upper[j] for j in range(4)]) for m in range(4)]
 
-    sides = [halfway(values) for values in (entered, fetch()) if values is not None]
+    def updated(diagonal, factors):
+        return [diagonal[j] - total_of([f * row(f, j) for f in factors]) for j in range(STRIP)]
+
+    upper, lower = halfway(entered)
+    coming = fetch()
+    if coming is not None:
+        found, left = halfway(coming[0])
+        diagonal = updated(coming[1], found)
     _, x, scale = yield from four_pivots(rest)
     two = [[scale[i] if entry is None else entry * scale[i] for entry in x[i]] for i in range(4)]
-    solved = [upper + [combined(two[k], lower[:k + 1]) for k in range(4)] for upper, lower in sides]
-    return solved[0], solved[1] if len(solved) > 1 else None
+
+    def rear(values):
+        return [combined(two[k], values[:k + 1]) for k in range(4)]
+
+    if coming is not None:
+        more = rear(left)
+        coming = found + more, updated(diagonal, more)
+
+    def solve(values):
+        front, values = halfway(values)
+        return front + rear(values)
+
+    return solve, upper + rear(lower), coming
 
 
 def inverse_factor(strips, beside):
@@ -185,18 +203,28 @@
     result = []
     waiting = []
 
-    def finish(p, own, rows):
+    def finish(p, own, solve, rows):
         turned = []
+
+        def subtract(r, factors):
+            terms = [factors[k] * rows[k] for k in range(STRIP)]
+            strips[r] = jnp.where(own, 0.0, strips[r]) - total_of(terms)
+
+        def second(r):
+            subtract(r, solve([column(strips[r], p * STRIP + j) for j in range(STRIP)]))
 
         def turn():
             turned.append(jnp.transpose(result[p]))
 
-        def update(r):
-            factors = turned[0][r * STRIP:(r + 1) * STRIP, :]
-            terms = [column_of(factors, k) * rows[k] for k in range(STRIP)]
-            strips[r] = jnp.where(own, 0.0, strips[r]) - total_of(terms)
-
-        return [turn] + [functools.partial(update, r) for r in range(p + 2, len(strips))]
+        def later(r):
+            square = turned[0][r * STRIP:(r + 1) * STRIP, :]
+            subtract(r, [column_of(square, k) for k in range(STRIP)])
+
+        count = len(strips)
+        steps = [functools.partial(second, p + 2)] if p + 2 < count else []
+        if p + 3 < count:
+            steps += [turn] + [functools.partial(later, r) for r in range(p + 3, count)]
+        return steps
 
     columns = [column(strips[0], k) for k in range(STRIP)]
     for p in range(len(strips)):
@@ -209,14 +237,14 @@
         def fetch():
             if p + 1 == len(strips):
                 return None
-            return [column(strips[p + 1], start + j) for j in range(STRIP)]
+            return [[column(strips[p + 1], at + j) for j in range(STRIP)] for at in (start, start + STRIP)]
 
         steps = block_rows(columns, [row(entered, k) for k in range(STRIP)], fetch)
         while True:
             try:
                 next(steps)
             except StopIteration as ended:
-                rows, found = ended.value
+                solve, rows, coming = ended.value
                 break
             for _ in range(2):
                 if waiting:
@@ -227,11 +255,11 @@
         for k in range(1, STRIP):
             done = jnp.where(level == k, rows[k], done)
         result.append(done)
-        if found is not None:
+        if coming is not None:
+            found, columns = coming
             update = total_of([found[k] * rows[k] for k in range(STRIP)])
             strips[p + 1] = jnp.where(own, 0.0, strips[p + 1]) - update
-            columns = [column(strips[p + 1], start + STRIP + k) for k in range(STRIP)]
-            waiting = finish(p, own, rows)
+            waiting = finish(p, own, solve, rows)
     return [jnp.where(lane < (p + 1) * STRIP, done, 0.0) for p, done in enumerate(result)]
 
 
@@ -311,7 +339,8 @@
     return product(kernel_of(product(own, other, ((1,), (0,)))).astype(jnp.bfloat16), probes, ((1,), (1,)))
 
 
-def factor_kernel(pivot_ref, point_ref, inverse_ref, awaited_ref, factor_ref, zero_ref):
+def factor_kernel(pivot_ref, point_ref, inverse_ref, *refs):
+    factor_ref, zero_ref = refs[-2:]
     count = point_ref.shape[1]
     own = jnp.transpose(padded(extended(point_ref[...], True))).astype(jnp.bfloat16)
     pivots = padded(extended(pivot_ref[...], False)).astype(jnp.bfloat16)
@@ -334,7 +363,7 @@
             jax.ShapeDtypeStruct((count, size), jnp.float32),
             pltpu.VMEM((depth, count), jnp.bfloat16),
         ),
-        in_specs=in_vmem(3) + [pl.BlockSpec(memory_space=pl.ANY)],
+        in_specs=in_vmem(3) + [pl.BlockSpec(memory_space=pl.ANY)] * len(awaited),
         out_specs=tuple(in_vmem(2)),
         compiler_params=pltpu.CompilerParams(vmem_limit_bytes=32 * 1024 * 1024),
         cost_estimate=pl.CostEstimate(
@@ -343,7 +372,49 @@
             transcendentals=count * size // 8,
         ),
         name="factor",
-    )(pivots_t, points_t, inverse, awaited)
+    )(pivots_t, points_t, inverse, *awaited)
+
+
+def tile_kernel(own_ref, other_ref, awaited_ref, tile_ref):
+    count = own_ref.shape[1]
+    own = jnp.transpose(padded(extended(own_ref[...], True))).astype(jnp.bfloat16)
+    other = padded(extended(other_ref[...], False)).astype(jnp.bfloat16)
+    for s in range(0, count, CHUNK):
+        tile_ref[s:s + CHUNK, :] = kernel_of(product(own[s:s + CHUNK, :], other, ((1,), (0,)))).astype(jnp.bfloat16)
+
+
+def tile_of(own, other, awaited):
+    count = own.shape[1]
+    return pl.pallas_call(
+        tile_kernel,
+        out_shape=pltpu.VMEM((count, count), jnp.bfloat16),
+        in_specs=in_vmem(2) + [pl.BlockSpec(memory_space=pl.ANY)],
+        out_specs=in_vmem(1)[0],
+        compiler_params=pltpu.CompilerParams(vmem_limit_bytes=32 * 1024 * 1024),
+        cost_estimate=pl.CostEstimate(
+            flops=2 * count * count * LANES, bytes_accessed=2 * count * count, transcendentals=count * count
+        ),
+        name="tile",
+    )(own, other, awaited)
+
+
+def last_kernel(tile_ref, block_probe_ref, before_ref, probe_ref, out_ref):
+    count = tile_ref.shape[0]
+    scale = 1.0 / (count ** 0.5)
+    for s in range(0, count, CHUNK):
+        total = before_ref[s:s + CHUNK, :] + product(tile_ref[s:s + CHUNK, :], block_probe_ref[...], ((1,), (1,)))
+        out_ref[:, s:s + CHUNK] = jnp.transpose(total) * scale + noise_weight * probe_ref[:, s:s + CHUNK]
+
+
+def last_sum(tile, block_probes, before, probes):
+    return pl.pallas_call(
+        last_kernel,
+        out_shape=jax.ShapeDtypeStruct(probes.shape, jnp.float32),
+        in_specs=in_vmem(4),
+        out_specs=in_vmem(1)[0],
+        compiler_params=pltpu.CompilerParams(vmem_limit_bytes=32 * 1024 * 1024),
+        name="last_sum",
+    )(tile, block_probes, before, probes)
 
 
 def band_kernel(pieces, first, last, *refs):
@@ -425,19 +496,20 @@
         leaving = sent + zero_like(pair[:depth])
         two = swapped(leaving, "gy", 2)
         one = swapped(leaving, "gy", 1) + zeros
-        factor, zeros = factor_of(pivot_points, points, inverse, one)
+        last_points = cross(pair[depth:] + zeros, 3)
+        factor, zeros = factor_of(pivot_points, points, inverse, [one, last_points])
         two = two + zeros
-        cross_one = cross(jnp.concatenate([pair[:depth], one], axis=0), 1)
         three = swapped(two, "gy", 1)
         cross_two = cross(jnp.concatenate([far, two], axis=0), 2)
+        cross_one = cross(jnp.concatenate([pair[:depth], one], axis=0), 1)
         total, zeros = band_sum(points, [((pair, 0), (one, 0)), ((far, 0), (two, 0))], total)
-        cross_three = cross(jnp.concatenate([pair[depth:], three + zeros], axis=0), 3)
-        crossed = [((stacked, 0), (stacked, depth)) for stacked in (cross_one, cross_two, cross_three)]
-        total, _ = band_sum(points, [((pair, depth), (three, 0)), crossed[0]], total)
-        total, _ = band_sum(points, crossed[1:2], total)
-        kernel_probes = band_sum(points, crossed[2:], total, probes)
+        three = three + zeros
+        cross_three = cross(three, 3)
+        total, _ = band_sum(points, [((pair, depth), (three, 0)), ((cross_one, 0), (cross_one, depth))], total)
+        total, _ = band_sum(points, [((cross_two, 0), (cross_two, depth))], total)
+        kernel_probes = last_sum(tile_of(points, last_points, total), cross_three, total, probes)
     else:
-        factor, _ = factor_of(pivot_points, points, inverse, zeros)
+        factor, _ = factor_of(pivot_points, points, inverse, [zeros])
         pieces = [((block, 0), (probe, 0)) for block, probe in zip(near, direct_blocks(sent))]
         total, _ = band_sum(points, pieces[:3], total)
         kernel_probes = band_sum(points, pieces[3:], total, probes)

time: 56.3 us -> 60.7 us (1.078)
  local copies, waits for them, and re-layouts: 0.02 us -> 2.69 us
  waiting for transfers between devices: 14.9 us -> 16.9 us
  Pallas kernels: 24.8 us -> 23.4 us
  other arithmetic: 0.25 us -> 1.13 us
    ppermute x12, waiting for transfers between devices: 12.1 us -> 14.8 us  [swapped(): lax.ppermute(value, axis, [(i ^ bit, i) for i in range(lax.axis_size(axis...]
    unnamed x6, local copies, waits for them, and re-layouts: 0.02 us -> 2.69 us
    pallas_call x0 -> x2, Pallas kernels: none -> 2.24 us  [the longest x1 1.46 us: last_sum(): pl.pallas_call(last_kernel, out_shape=jax.ShapeDtypeStruct(probes.shape,...]
    pallas_call x5 -> x4, Pallas kernels: 9.85 us -> 7.8 us  [band_sum(): pl.pallas_call(functools.partial(band_kernel, tuple(places), first, last)...]
    pallas_call x1, Pallas kernels: 11.8 us -> 10.3 us  [probes_of(): pl.pallas_call(probe_kernel, out_shape=(pltpu.VMEM((size, size), jnp.floa...]
    concatenate x1, other arithmetic: 0.02 us -> 0.92 us  [shards(): pair = swapped(jnp.concatenate([points, far], axis=0), 'gy', 1)]
    ppermute x3 -> x4, waiting for transfers between devices: 2.82 us -> 2.16 us  [cross(): return lax.ppermute(piece, ('gx', 'gy'), pairs)]
  transfers between devices with their start and end apart: 15 -> 16, of which waited for: 11 -> 11; matrix products, arithmetic and copies ran while one was open for 0% -> 2% of each run, Pallas kernels for 40% -> 36%
where the time goes in v16:
time: 60.7 us; the launch traced here: 60.5 us
  Pallas kernels  23.4 us (39%)
  waiting for transfers between devices  16.9 us (28%)
  starting transfers between devices  15.5 us (26%)
  local copies, waits for them, and re-layouts  2.69 us (4%)
  other arithmetic  1.13 us (2%)
  between operations  0.81 us (1%)
    ppermute x12, starting transfers between devices, swapped(): lax.ppermute(value, axis, [(i ^ bit, i) for i in range(lax.axis_size(axis...  15.2 us
    ppermute x12, waiting for transfers between devices, swapped(): lax.ppermute(value, axis, [(i ^ bit, i) for i in range(lax.axis_size(axis...  14.8 us
    pallas_call x1, Pallas kernels, probes_of(): pl.pallas_call(probe_kernel, out_shape=(pltpu.VMEM((size, size), jnp.floa...  10.3 us
    pallas_call x4, Pallas kernels, band_sum(): pl.pallas_call(functools.partial(band_kernel, tuple(places), first, last)...  7.8 us
    unnamed x6, local copies, waits for them, and re-layouts  2.69 us
    ppermute x4, waiting for transfers between devices, cross(): return lax.ppermute(piece, ('gx', 'gy'), pairs)  2.16 us
    pallas_call x1, Pallas kernels, factor_of(): pl.pallas_call(factor_kernel, out_shape=(jax.ShapeDtypeStruct((count, siz...  1.91 us
    pallas_call x1, Pallas kernels, last_sum(): pl.pallas_call(last_kernel, out_shape=jax.ShapeDtypeStruct(probes.shape,...  1.46 us
  transfers between devices with their start and end apart: 16, of which 11 were waited for; matrix products, arithmetic and copies ran while one was open for 2% of the time, Pallas kernels for 36%

profile of v16, /device:TPU:0, one launch (start us, length us, event | category | flops | bytes accessed | tf_op | source)
XLA Modules:
  0.0 60.5 jit_solution(9065139001301383990)
XLA Ops:
  0.6 4.1 %collective-permute-start = (bf16[64,1024]{1,0:T(8,128)(2,1)}, bf16[64,1024]{1,0:T(8,128)(2,1)S(1)}, u32[]{:S(2)}, u32[]{:S(2)}) collective-permute-start(bf16[64,1024]{1,0:T(8,128)(2,1)} %bitcast.4), channel_id=1, source_target_pairs={{2,0},{3,1},{0,2},{1,3},{6,4},{7,5},{4,6},{5,7},{10,8},{11,9},{8,1... | collective-permute-start | bytes 393224 | tf_op jit(solution)/shard_map/ppermute | solution.py:31
  4.7 1.2 %pick.1 = bf16[64,256]{1,0:T(8,128)(2,1)S(1)} custom-call(s32[2]{0:T(128)} %owner_ref.1, s32[2,128]{1,0:T(2,128)} %pivot_ref.1, bf16[64,1024]{1,0:T(8,128)(2,1)} %bitcast.5), custom_call_target="tpu_custom_call" | custom-call | tf_op jit(solution)/shard_map/pick/pallas_call | solution.py:107
  6.0 1.2 %collective-permute-done.2 = bf16[64,256]{1,0:T(8,128)(2,1)S(1)} collective-permute-done((bf16[64,256]{1,0:T(8,128)(2,1)S(1)}, bf16[64,256]{1,0:T(8,128)(2,1)S(1)}, u32[]{:S(2)}, u32[]{:S(2)}) %collective-permute-start.2) | collective-permute-done | bytes 32800 | tf_op jit(solution)/shard_map/ppermute | solution.py:31
  7.2 2.5 %collective-permute-start.5 = (bf16[64,256]{1,0:T(8,128)(2,1)S(1)}, bf16[64,256]{1,0:T(8,128)(2,1)S(1)}, u32[]{:S(2)}, u32[]{:S(2)}) collective-permute-start(bf16[64,256]{1,0:T(8,128)(2,1)S(1)} %add.39), channel_id=1, source_target_pairs={{24,0},{28,4},{16,8},{20,12},{8,16},{12,20},{0,24},{4,28},{25,1},{... | collective-permute-start | bytes 98312 | tf_op jit(solution)/shard_map/ppermute | solution.py:31
  10.2 0.5 collective-permute-start.3
  10.7 1.3 %collective-permute-done.5 = bf16[64,256]{1,0:T(8,128)(2,1)S(1)} collective-permute-done((bf16[64,256]{1,0:T(8,128)(2,1)S(1)}, bf16[64,256]{1,0:T(8,128)(2,1)S(1)}, u32[]{:S(2)}, u32[]{:S(2)}) %collective-permute-start.5) | collective-permute-done | bytes 32800 | tf_op jit(solution)/shard_map/ppermute | solution.py:31
  12.1 1.5 %collective-permute-done.4 = bf16[64,256]{1,0:T(8,128)(2,1)S(1)} collective-permute-done((bf16[64,256]{1,0:T(8,128)(2,1)S(1)}, bf16[64,256]{1,0:T(8,128)(2,1)S(1)}, u32[]{:S(2)}, u32[]{:S(2)}) %collective-permute-start.4) | collective-permute-done | bytes 32800 | tf_op jit(solution)/shard_map/ppermute | solution.py:31
  13.6 0.5 collective-permute-done.3
  14.1 1.4 %collective-permute-start.8 = (bf16[64,256]{1,0:T(8,128)(2,1)S(1)}, bf16[64,256]{1,0:T(8,128)(2,1)S(1)}, u32[]{:S(2)}, u32[]{:S(2)}) collective-permute-start(bf16[64,256]{1,0:T(8,128)(2,1)S(1)} %fusion.1), channel_id=1, source_target_pairs={{3,0},{2,1},{1,2},{0,3},{7,4},{6,5},{5,6},{4,7},{11,8},{10,9},{9,1... | collective-permute-start | bytes 98312 | tf_op jit(solution)/shard_map/ppermute | solution.py:31
  15.6 1.7 %collective-permute-start.7 = (bf16[64,256]{1,0:T(8,128)(2,1)S(1)}, bf16[64,256]{1,0:T(8,128)(2,1)S(1)}, u32[]{:S(2)}, u32[]{:S(2)}) collective-permute-start(bf16[64,256]{1,0:T(8,128)(2,1)S(1)} %fusion.1), channel_id=1, source_target_pairs={{2,0},{3,1},{0,2},{1,3},{6,4},{7,5},{4,6},{5,7},{10,8},{11,9},{8,1... | collective-permute-start | bytes 98312 | tf_op jit(solution)/shard_map/ppermute | solution.py:31
  17.3 1.3 %collective-permute-start.6 = (bf16[64,256]{1,0:T(8,128)(2,1)S(1)}, bf16[64,256]{1,0:T(8,128)(2,1)S(1)}, u32[]{:S(2)}, u32[]{:S(2)}) collective-permute-start(bf16[64,256]{1,0:T(8,128)(2,1)S(1)} %fusion.1), channel_id=1, source_target_pairs={{1,0},{0,1},{3,2},{2,3},{5,4},{4,5},{7,6},{6,7},{9,8},{8,9},{11,10... | collective-permute-start | bytes 98312 | tf_op jit(solution)/shard_map/ppermute | solution.py:31
  18.6 0.9 %pad_maximum_fusion = bf16[128,1024]{1,0:T(8,128)(2,1)S(1)} fusion(bf16[64,1024]{1,0:T(8,128)(2,1)S(1)} %collective-permute-done.refs_3_, bf16[64,1024]{1,0:T(8,128)(2,1)} %bitcast.6), kind=kLoop, calls=%fused_computation | loop fusion | flops 524288 | bytes 524288 | tf_op jit(solution)/shard_map/concatenate | solution.py:488
  19.5 0.7 %collective-permute-start.1 = (bf16[128,1024]{1,0:T(8,128)(2,1)S(1)}, bf16[128,1024]{1,0:T(8,128)(2,1)S(1)}, u32[]{:S(2)}, u32[]{:S(2)}) collective-permute-start(bf16[128,1024]{1,0:T(8,128)(2,1)S(1)} %pad_maximum_fusion), channel_id=1, source_target_pairs={{1,0},{0,1},{3,2},{2,3},{5,4},{4,5},{7,6},{6,7},{9,8},{8,9},{11,10... | collective-permute-start | bytes 786440 | tf_op jit(solution)/shard_map/ppermute | solution.py:31
  20.7 0.8 %collective-permute-done.6 = bf16[64,256]{1,0:T(8,128)(2,1)S(1)} collective-permute-done((bf16[64,256]{1,0:T(8,128)(2,1)S(1)}, bf16[64,256]{1,0:T(8,128)(2,1)S(1)}, u32[]{:S(2)}, u32[]{:S(2)}) %collective-permute-start.6) | collective-permute-done | bytes 32800 | tf_op jit(solution)/shard_map/ppermute | solution.py:31
  21.5 0.9 %copy-done = bf16[1024,64]{0,1:T(8,128)(2,1)S(1)} copy-done((bf16[1024,64]{0,1:T(8,128)(2,1)S(1)}, bf16[1024,64]{0,1:T(8,128)(2,1)}, u32[]{:S(2)}) %copy-start) | copy-done | bytes 131096
  22.4 0.9 %copy-done.1 = f32[1024,64]{0,1:T(8,128)S(1)} copy-done((f32[1024,64]{0,1:T(8,128)S(1)}, f32[1024,64]{0,1:T(8,128)}, u32[]{:S(2)}) %copy-start.1) | copy-done | bytes 262168
  23.4 0.8 %copy-done.2 = f32[256,64]{0,1:T(8,128)S(1)} copy-done((f32[256,64]{0,1:T(8,128)S(1)}, f32[256,64]{0,1:T(8,128)}, u32[]{:S(2)}) %copy-start.2) | copy-done | bytes 65560
  24.2 10.3 %probes.1 = (f32[256,256]{1,0:T(8,128)S(1)}, f32[64,1024]{1,0:T(8,128)S(1)}, bf16[64,1024]{1,0:T(8,128)(2,1)S(1)}) custom-call(bf16[64,256]{1,0:T(8,128)(2,1)S(1)} %add_add_fusion.pivot_ref, bf16[64,1024]{1,0:T(8,128)(2,1)S(1)} %bitcast.7, f32[64,256]{1,0:T(8,128)S(1)} %bitcast.15, f32[64,1024]{1,0:T(8,128)S(1)} %bitcast.14), custom_call_target="tpu_custom_call" | custom-call | flops 17179869184 | bytes 1 | tf_op jit(solution)/shard_map/probes/pallas_call | solution.py:318
  34.5 1.4 %band_sum.4 = (f32[1024,64]{1,0:T(8,128)S(1)}, bf16[64,1024]{1,0:T(8,128)(2,1)S(1)}) custom-call(bf16[64,1024]{1,0:T(8,128)(2,1)S(1)} %bitcast.8, bf16[64,1024]{1,0:T(8,128)(2,1)S(1)} %get-tuple-element.13.refs_1_), custom_call_target="tpu_custom_call" | custom-call | flops 1 | bytes 1 | tf_op jit(solution)/shard_map/band_sum/pallas_call | solution.py:465
  36.0 1.5 %collective-permute-start.11 = (bf16[64,1024]{1,0:T(8,128)(2,1)S(1)}, bf16[64,1024]{1,0:T(8,128)(2,1)S(1)}, u32[]{:S(2)}, u32[]{:S(2)}) collective-permute-start(bf16[64,1024]{1,0:T(8,128)(2,1)S(1)} %get-tuple-element.25), channel_id=1, source_target_pairs={{1,0},{0,1},{3,2},{2,3},{5,4},{4,5},{7,6},{6,7},{9,8},{8,9},{11,10... | collective-permute-start | bytes 393224 | tf_op jit(solution)/shard_map/ppermute | solution.py:31
  37.5 0.7 %collective-permute-start.10 = (bf16[64,1024]{1,0:T(8,128)(2,1)S(1)}, bf16[64,1024]{1,0:T(8,128)(2,1)S(1)}, u32[]{:S(2)}, u32[]{:S(2)}) collective-permute-start(bf16[64,1024]{1,0:T(8,128)(2,1)S(1)} %get-tuple-element.25), channel_id=1, source_target_pairs={{2,0},{3,1},{0,2},{1,3},{6,4},{7,5},{4,6},{5,7},{10,8},{11,9},{8,1... | collective-permute-start | bytes 393224 | tf_op jit(solution)/shard_map/ppermute | solution.py:31
  38.2 2.9 %collective-permute-done.11 = bf16[64,1024]{1,0:T(8,128)(2,1)S(1)} collective-permute-done((bf16[64,1024]{1,0:T(8,128)(2,1)S(1)}, bf16[64,1024]{1,0:T(8,128)(2,1)S(1)}, u32[]{:S(2)}, u32[]{:S(2)}) %collective-permute-start.11) | collective-permute-done | bytes 131104 | tf_op jit(solution)/shard_map/ppermute | solution.py:31
  41.2 1.5 %collective-permute-done.9.refs_1_.other_ref = bf16[64,1024]{1,0:T(8,128)(2,1)S(1)} collective-permute-done((bf16[64,1024]{1,0:T(8,128)(2,1)S(1)}, bf16[64,1024]{1,0:T(8,128)(2,1)S(1)}, u32[]{:S(2)}, u32[]{:S(2)}) %collective-permute-start.9) | collective-permute-done | bytes 131104 | tf_op jit(solution)/shard_map/ppermute | solution.py:55
  42.8 1.9 %factor.1 = (f32[1024,256]{1,0:T(8,128)}, bf16[64,1024]{1,0:T(8,128)(2,1)S(1)}) custom-call(bf16[64,256]{1,0:T(8,128)(2,1)S(1)} %add_add_fusion.pivot_ref, bf16[64,1024]{1,0:T(8,128)(2,1)S(1)} %bitcast.9, f32[256,256]{1,0:T(8,128)S(1)} %get-tuple-element.15.inverse_ref, bf16[64,1024]{1,0:T(8,128)(2,1)S(1)} %add.49.refs_0_.refs_2_, ...), custom_call_target="tpu_custom_call" | custom-call | flops 50331648 | bytes 196608 | tf_op jit(solution)/shard_map/factor/pallas_call | solution.py:360
  44.7 2.5 %collective-permute-done.10 = bf16[64,1024]{1,0:T(8,128)(2,1)S(1)} collective-permute-done((bf16[64,1024]{1,0:T(8,128)(2,1)S(1)}, bf16[64,1024]{1,0:T(8,128)(2,1)S(1)}, u32[]{:S(2)}, u32[]{:S(2)}) %collective-permute-start.10) | collective-permute-done | bytes 131104 | tf_op jit(solution)/shard_map/ppermute | solution.py:31
  47.6 2.5 %band_sum.5 = (f32[1024,64]{1,0:T(8,128)S(1)}, bf16[64,1024]{1,0:T(8,128)(2,1)S(1)}) custom-call(bf16[64,1024]{1,0:T(8,128)(2,1)S(1)} %bitcast.10, bf16[128,1024]{1,0:T(8,128)(2,1)S(1)} %collective-permute-done.1.refs_1_, bf16[64,1024]{1,0:T(8,128)(2,1)S(1)} %add.49.refs_0_.refs_2_, bf16[64,1024]{1,0:T(8,128)(2,1)S(1)} %collective-permute-done.refs_3_, ...), custom_call_target="tpu_custom_call" | custom-call | flops 1073741824 | bytes 1572864 | tf_op jit(solution)/shard_map/band_sum/pallas_call | solution.py:465
  50.1 3.5 %collective-permute-done.13 = bf16[64,1024]{1,0:T(8,128)(2,1)S(1)} collective-permute-done((bf16[64,1024]{1,0:T(8,128)(2,1)S(1)}, bf16[64,1024]{1,0:T(8,128)(2,1)S(1)}, u32[]{:S(2)}, u32[]{:S(2)}) %collective-permute-start.13) | collective-permute-done | bytes 131104 | tf_op jit(solution)/shard_map/ppermute | solution.py:31
  53.8 2.5 %band_sum.6 = (f32[1024,64]{1,0:T(8,128)S(1)}, bf16[64,1024]{1,0:T(8,128)(2,1)}) custom-call(bf16[64,1024]{1,0:T(8,128)(2,1)S(1)} %bitcast.11, bf16[128,1024]{1,0:T(8,128)(2,1)S(1)} %collective-permute-done.1.refs_1_, bf16[64,1024]{1,0:T(8,128)(2,1)S(1)} %add.51.refs_2_, bf16[128,1024]{1,0:T(8,128)(2,1)S(1)} %collective-permute-done.14.refs_3_, ...), custom_call_target="tpu_custom_call" | custom-call | flops 1073741824 | bytes 1310720 | tf_op jit(solution)/shard_map/band_sum/pallas_call | solution.py:465
  56.3 1.3 %band_sum.7 = (f32[1024,64]{1,0:T(8,128)S(1)}, bf16[64,1024]{1,0:T(8,128)(2,1)}) custom-call(bf16[64,1024]{1,0:T(8,128)(2,1)S(1)} %bitcast.12, bf16[128,1024]{1,0:T(8,128)(2,1)S(1)} %collective-permute-done.12.refs_1_, f32[1024,64]{1,0:T(8,128)S(1)} %get-tuple-element.20.refs_2_), custom_call_target="tpu_custom_call" | custom-call | flops 536870912 | bytes 786432 | tf_op jit(solution)/shard_map/band_sum/pallas_call | solution.py:465
  57.6 0.8 %tile.1.tile_ref = bf16[1024,1024]{1,0:T(8,128)(2,1)S(1)} custom-call(bf16[64,1024]{1,0:T(8,128)(2,1)S(1)} %bitcast.13, bf16[64,1024]{1,0:T(8,128)(2,1)S(1)} %collective-permute-done.9.refs_1_.other_ref, f32[1024,64]{1,0:T(8,128)S(1)} %get-tuple-element.21.awaited_ref.before_ref), custom_call_target="tpu_custom_call" | custom-call | flops 268435456 | bytes 2097152 | tf_op jit(solution)/shard_map/tile/pallas_call | solution.py:388
  58.4 0.6 %collective-permute-done.15.block_probe_ref = bf16[64,1024]{1,0:T(8,128)(2,1)S(1)} collective-permute-done((bf16[64,1024]{1,0:T(8,128)(2,1)S(1)}, bf16[64,1024]{1,0:T(8,128)(2,1)S(1)}, u32[]{:S(2)}, u32[]{:S(2)}) %collective-permute-start.15) | collective-permute-done | bytes 131104 | tf_op jit(solution)/shard_map/ppermute | solution.py:55
  59.0 1.5 %last_sum.1 = f32[64,1024]{1,0:T(8,128)} custom-call(bf16[1024,1024]{1,0:T(8,128)(2,1)S(1)} %tile.1.tile_ref, bf16[64,1024]{1,0:T(8,128)(2,1)S(1)} %collective-permute-done.15.block_probe_ref, f32[1024,64]{1,0:T(8,128)S(1)} %get-tuple-element.21.awaited_ref.before_ref, f32[64,1024]{1,0:T(8,128)S(1)} %get-tuple-element.22.probe_ref), custom_call_target="tpu_custom_call" | custom-call | tf_op jit(solution)/shard_map/last_sum/pallas_call | solution.py:410
  (25 shorter events, 1.7 us)
Async XLA Ops:
  0.6 13.5 %collective-permute-start = (bf16[64,1024]{1,0:T(8,128)(2,1)}, bf16[64,1024]{1,0:T(8,128)(2,1)S(1)}, u32[]{:S(2)}, u32[]{:S(2)}) collective-permute-start(bf16[64,1024]{1,0:T(8,128)(2,1)} %bitcast.4), channel_id=1, source_target_pairs={{2,0},{3,1},{0,2},{1,3},{6,4},{7,5},{4,6},{5,7},{10,8},{11,9},{8,1... | collective-permute-start | bytes 393224 | tf_op jit(solution)/shard_map/ppermute | solution.py:31
  5.9 1.3 %collective-permute-start.2 = (bf16[64,256]{1,0:T(8,128)(2,1)S(1)}, bf16[64,256]{1,0:T(8,128)(2,1)S(1)}, u32[]{:S(2)}, u32[]{:S(2)}) collective-permute-start(bf16[64,256]{1,0:T(8,128)(2,1)S(1)} %pick.1), channel_id=1, source_target_pairs={{4,0},{0,4},{12,8},{8,12},{20,16},{16,20},{28,24},{24,28},{5,1},{1... | collective-permute-start | bytes 98312 | tf_op jit(solution)/shard_map/ppermute | solution.py:31
  7.2 4.9 %collective-permute-start.5 = (bf16[64,256]{1,0:T(8,128)(2,1)S(1)}, bf16[64,256]{1,0:T(8,128)(2,1)S(1)}, u32[]{:S(2)}, u32[]{:S(2)}) collective-permute-start(bf16[64,256]{1,0:T(8,128)(2,1)S(1)} %add.39), channel_id=1, source_target_pairs={{24,0},{28,4},{16,8},{20,12},{8,16},{12,20},{0,24},{4,28},{25,1},{... | collective-permute-start | bytes 98312 | tf_op jit(solution)/shard_map/ppermute | solution.py:31
  9.7 3.9 %collective-permute-start.4 = (bf16[64,256]{1,0:T(8,128)(2,1)S(1)}, bf16[64,256]{1,0:T(8,128)(2,1)S(1)}, u32[]{:S(2)}, u32[]{:S(2)}) collective-permute-start(bf16[64,256]{1,0:T(8,128)(2,1)S(1)} %add.39), channel_id=1, source_target_pairs={{16,0},{20,4},{24,8},{28,12},{0,16},{4,20},{8,24},{12,28},{17,1},{... | collective-permute-start | bytes 98312 | tf_op jit(solution)/shard_map/ppermute | solution.py:31
  10.2 3.9 %collective-permute-start.3 = (bf16[64,256]{1,0:T(8,128)(2,1)S(1)}, bf16[64,256]{1,0:T(8,128)(2,1)S(1)}, u32[]{:S(2)}, u32[]{:S(2)}) collective-permute-start(bf16[64,256]{1,0:T(8,128)(2,1)S(1)} %add.39), channel_id=1, source_target_pairs={{8,0},{12,4},{0,8},{4,12},{24,16},{28,20},{16,24},{20,28},{9,1},{1... | collective-permute-start | bytes 98312 | tf_op jit(solution)/shard_map/ppermute | solution.py:31
  14.1 6.1 %collective-permute-start.8 = (bf16[64,256]{1,0:T(8,128)(2,1)S(1)}, bf16[64,256]{1,0:T(8,128)(2,1)S(1)}, u32[]{:S(2)}, u32[]{:S(2)}) collective-permute-start(bf16[64,256]{1,0:T(8,128)(2,1)S(1)} %fusion.1), channel_id=1, source_target_pairs={{3,0},{2,1},{1,2},{0,3},{7,4},{6,5},{5,6},{4,7},{11,8},{10,9},{9,1... | collective-permute-start | bytes 98312 | tf_op jit(solution)/shard_map/ppermute | solution.py:31
  15.6 5.1 %collective-permute-start.7 = (bf16[64,256]{1,0:T(8,128)(2,1)S(1)}, bf16[64,256]{1,0:T(8,128)(2,1)S(1)}, u32[]{:S(2)}, u32[]{:S(2)}) collective-permute-start(bf16[64,256]{1,0:T(8,128)(2,1)S(1)} %fusion.1), channel_id=1, source_target_pairs={{2,0},{3,1},{0,2},{1,3},{6,4},{7,5},{4,6},{5,7},{10,8},{11,9},{8,1... | collective-permute-start | bytes 98312 | tf_op jit(solution)/shard_map/ppermute | solution.py:31
  17.3 4.3 %collective-permute-start.6 = (bf16[64,256]{1,0:T(8,128)(2,1)S(1)}, bf16[64,256]{1,0:T(8,128)(2,1)S(1)}, u32[]{:S(2)}, u32[]{:S(2)}) collective-permute-start(bf16[64,256]{1,0:T(8,128)(2,1)S(1)} %fusion.1), channel_id=1, source_target_pairs={{1,0},{0,1},{3,2},{2,3},{5,4},{4,5},{7,6},{6,7},{9,8},{8,9},{11,10... | collective-permute-start | bytes 98312 | tf_op jit(solution)/shard_map/ppermute | solution.py:31
  19.5 16.4 %collective-permute-start.1 = (bf16[128,1024]{1,0:T(8,128)(2,1)S(1)}, bf16[128,1024]{1,0:T(8,128)(2,1)S(1)}, u32[]{:S(2)}, u32[]{:S(2)}) collective-permute-start(bf16[128,1024]{1,0:T(8,128)(2,1)S(1)} %pad_maximum_fusion), channel_id=1, source_target_pairs={{1,0},{0,1},{3,2},{2,3},{5,4},{4,5},{7,6},{6,7},{9,8},{8,9},{11,10... | collective-permute-start | bytes 786440 | tf_op jit(solution)/shard_map/ppermute | solution.py:31
  21.5 0.9 %copy-start = (bf16[1024,64]{0,1:T(8,128)(2,1)S(1)}, bf16[1024,64]{0,1:T(8,128)(2,1)}, u32[]{:S(2)}) copy-start(bf16[1024,64]{0,1:T(8,128)(2,1)} %param.5) | copy-start | bytes 393220
  22.4 0.9 %copy-start.1 = (f32[1024,64]{0,1:T(8,128)S(1)}, f32[1024,64]{0,1:T(8,128)}, u32[]{:S(2)}) copy-start(f32[1024,64]{0,1:T(8,128)} %param.9) | copy-start | bytes 786436
  23.4 0.8 %copy-start.2 = (f32[256,64]{0,1:T(8,128)S(1)}, f32[256,64]{0,1:T(8,128)}, u32[]{:S(2)}) copy-start(f32[256,64]{0,1:T(8,128)} %param.8) | copy-start | bytes 196612
  36.0 5.1 %collective-permute-start.11 = (bf16[64,1024]{1,0:T(8,128)(2,1)S(1)}, bf16[64,1024]{1,0:T(8,128)(2,1)S(1)}, u32[]{:S(2)}, u32[]{:S(2)}) collective-permute-start(bf16[64,1024]{1,0:T(8,128)(2,1)S(1)} %get-tuple-element.25), channel_id=1, source_target_pairs={{1,0},{0,1},{3,2},{2,3},{5,4},{4,5},{7,6},{6,7},{9,8},{8,9},{11,10... | collective-permute-start | bytes 393224 | tf_op jit(solution)/shard_map/ppermute | solution.py:31
  37.5 5.3 %collective-permute-start.9 = (bf16[64,1024]{1,0:T(8,128)(2,1)S(1)}, bf16[64,1024]{1,0:T(8,128)(2,1)S(1)}, u32[]{:S(2)}, u32[]{:S(2)}) collective-permute-start(bf16[64,1024]{1,0:T(8,128)(2,1)S(1)} %get-tuple-element.26), channel_id=1, source_target_pairs={{28,0},{29,1},{6,2},{7,3},{0,4},{1,5},{10,6},{11,7},{4,8},{5,9},{1... | collective-permute-start | bytes 393224 | tf_op jit(solution)/shard_map/ppermute | solution.py:55
  37.5 9.7 %collective-permute-start.10 = (bf16[64,1024]{1,0:T(8,128)(2,1)S(1)}, bf16[64,1024]{1,0:T(8,128)(2,1)S(1)}, u32[]{:S(2)}, u32[]{:S(2)}) collective-permute-start(bf16[64,1024]{1,0:T(8,128)(2,1)S(1)} %get-tuple-element.25), channel_id=1, source_target_pairs={{2,0},{3,1},{0,2},{1,3},{6,4},{7,5},{4,6},{5,7},{10,8},{11,9},{8,1... | collective-permute-start | bytes 393224 | tf_op jit(solution)/shard_map/ppermute | solution.py:31
  41.2 12.6 %collective-permute-start.14 = (bf16[128,1024]{1,0:T(8,128)(2,1)S(1)}, bf16[128,1024]{1,0:T(8,128)(2,1)S(1)}, u32[]{:S(2)}, u32[]{:S(2)}) collective-permute-start(bf16[128,1024]{1,0:T(8,128)(2,1)S(1)} %pad_maximum_fusion.2), channel_id=1, source_target_pairs={{28,0},{5,1},{30,2},{7,3},{0,4},{9,5},{2,6},{11,7},{4,8},{13,9},{6... | collective-permute-start | bytes 786440 | tf_op jit(solution)/shard_map/ppermute | solution.py:55
  47.3 9.0 %collective-permute-start.12 = (bf16[128,1024]{1,0:T(8,128)(2,1)S(1)}, bf16[128,1024]{1,0:T(8,128)(2,1)S(1)}, u32[]{:S(2)}, u32[]{:S(2)}) collective-permute-start(bf16[128,1024]{1,0:T(8,128)(2,1)S(1)} %pad_maximum_fusion.1), channel_id=1, source_target_pairs={{28,0},{29,1},{6,2},{7,3},{0,4},{1,5},{10,6},{11,7},{4,8},{5,9},{1... | collective-permute-start | bytes 786440 | tf_op jit(solution)/shard_map/ppermute | solution.py:55
  47.5 6.1 %collective-permute-start.13 = (bf16[64,1024]{1,0:T(8,128)(2,1)S(1)}, bf16[64,1024]{1,0:T(8,128)(2,1)S(1)}, u32[]{:S(2)}, u32[]{:S(2)}) collective-permute-start(bf16[64,1024]{1,0:T(8,128)(2,1)S(1)} %add.50.refs_4_), channel_id=1, source_target_pairs={{1,0},{0,1},{3,2},{2,3},{5,4},{4,5},{7,6},{6,7},{9,8},{8,9},{11,10... | collective-permute-start | bytes 393224 | tf_op jit(solution)/shard_map/ppermute | solution.py:31
  53.7 5.3 %collective-permute-start.15 = (bf16[64,1024]{1,0:T(8,128)(2,1)S(1)}, bf16[64,1024]{1,0:T(8,128)(2,1)S(1)}, u32[]{:S(2)}, u32[]{:S(2)}) collective-permute-start(bf16[64,1024]{1,0:T(8,128)(2,1)S(1)} %add.51.refs_2_), channel_id=1, source_target_pairs={{28,0},{29,1},{6,2},{7,3},{0,4},{1,5},{10,6},{11,7},{4,8},{5,9},{1... | collective-permute-start | bytes 393224 | tf_op jit(solution)/shard_map/ppermute | solution.py:55

commit v17 on v15

--- a/solution.py
+++ b/solution.py
@@ -115,10 +115,6 @@
 
 def column(strip, lane):
     return jnp.broadcast_to(strip[:, lane:lane + 1], strip.shape)
-
-
-def column_of(square, lane):
-    return jnp.broadcast_to(square[:, lane:lane + 1], (STRIP, LANES))
 
 
 def row(strip, i):
@@ -171,11 +167,29 @@
         upper = [combined(one[k], values[:k + 1]) for k in range(4)]
         return upper, [values[4 + m] - total_of([below[m][j] * upper[j] for j in range(4)]) for m in range(4)]
 
-    sides = [halfway(values) for values in (entered, fetch()) if values is not None]
+    def updated(diagonal, factors):
+        return [diagonal[j] - total_of([f * row(f, j) for f in factors]) for j in range(STRIP)]
+
+    upper, lower = halfway(entered)
+    coming = fetch()
+    if coming is not None:
+        found, left = halfway(coming[0])
+        diagonal = updated(coming[1], found)
     _, x, scale = yield from four_pivots(rest)
     two = [[scale[i] if entry is None else entry * scale[i] for entry in x[i]] for i in range(4)]
-    solved = [upper + [combined(two[k], lower[:k + 1]) for k in range(4)] for upper, lower in sides]
-    return solved[0], solved[1] if len(solved) > 1 else None
+
+    def rear(values):
+        return [combined(two[k], values[:k + 1]) for k in range(4)]
+
+    if coming is not None:
+        more = rear(left)
+        coming = found + more, updated(diagonal, more)
+
+    def solve(values):
+        front, values = halfway(values)
+        return front + rear(values)
+
+    return solve, upper + rear(lower), coming
 
 
 def inverse_factor(strips, beside):
@@ -185,18 +199,13 @@
     result = []
     waiting = []
 
-    def finish(p, own, rows):
-        turned = []
-
-        def turn():
-            turned.append(jnp.transpose(result[p]))
-
+    def finish(p, own, solve, rows):
         def update(r):
-            factors = turned[0][r * STRIP:(r + 1) * STRIP, :]
-            terms = [column_of(factors, k) * rows[k] for k in range(STRIP)]
+            factors = solve([column(strips[r], p * STRIP + j) for j in range(STRIP)])
+            terms = [factors[k] * rows[k] for k in range(STRIP)]
             strips[r] = jnp.where(own, 0.0, strips[r]) - total_of(terms)
 
-        return [turn] + [functools.partial(update, r) for r in range(p + 2, len(strips))]
+        return [functools.partial(update, r) for r in range(p + 2, len(strips))]
 
     columns = [column(strips[0], k) for k in range(STRIP)]
     for p in range(len(strips)):
@@ -209,14 +218,14 @@
         def fetch():
             if p + 1 == len(strips):
                 return None
-            return [column(strips[p + 1], start + j) for j in range(STRIP)]
+            return [[column(strips[p + 1], at + j) for j in range(STRIP)] for at in (start, start + STRIP)]
 
         steps = block_rows(columns, [row(entered, k) for k in range(STRIP)], fetch)
         while True:
             try:
                 next(steps)
             except StopIteration as ended:
-                rows, found = ended.value
+                solve, rows, coming = ended.value
                 break
             for _ in range(2):
                 if waiting:
@@ -227,11 +236,11 @@
         for k in range(1, STRIP):
             done = jnp.where(level == k, rows[k], done)
         result.append(done)
-        if found is not None:
+        if coming is not None:
+            found, columns = coming
             update = total_of([found[k] * rows[k] for k in range(STRIP)])
             strips[p + 1] = jnp.where(own, 0.0, strips[p + 1]) - update
-            columns = [column(strips[p + 1], start + STRIP + k) for k in range(STRIP)]
-            waiting = finish(p, own, rows)
+            waiting = finish(p, own, solve, rows)
     return [jnp.where(lane < (p + 1) * STRIP, done, 0.0) for p, done in enumerate(result)]
 
 

time: 56.3 us -> 52.4 us (0.931)
  Pallas kernels: 24.8 us -> 20.8 us
    pallas_call x1, Pallas kernels: 11.8 us -> 7.89 us  [probes_of(): pl.pallas_call(probe_kernel, out_shape=(pltpu.VMEM((size, size), jnp.floa...]
  transfers between devices with their start and end apart: 15 -> 15, of which waited for: 11 -> 11; matrix products, arithmetic and copies ran while one was open for 0% -> 0% of each run, Pallas kernels for 40% -> 36%
where the time goes in v17:
time: 52.4 us; the launch traced here: 52.2 us
  Pallas kernels  20.8 us (40%)
  starting transfers between devices  15.4 us (29%)
  waiting for transfers between devices  14.9 us (28%)
  between operations  0.84 us (2%)
    ppermute x12, starting transfers between devices, swapped(): lax.ppermute(value, axis, [(i ^ bit, i) for i in range(lax.axis_size(axis...  15.1 us
    ppermute x12, waiting for transfers between devices, swapped(): lax.ppermute(value, axis, [(i ^ bit, i) for i in range(lax.axis_size(axis...  12.1 us
    pallas_call x5, Pallas kernels, band_sum(): pl.pallas_call(functools.partial(band_kernel, tuple(places), first, last)...  9.85 us
    pallas_call x1, Pallas kernels, probes_of(): pl.pallas_call(probe_kernel, out_shape=(pltpu.VMEM((size, size), jnp.floa...  7.89 us
    ppermute x3, waiting for transfers between devices, cross(): return lax.ppermute(piece, ('gx', 'gy'), pairs)  2.82 us
    pallas_call x1, Pallas kernels, factor_of(): pl.pallas_call(factor_kernel, out_shape=(jax.ShapeDtypeStruct((count, siz...  1.92 us
    pallas_call x1, Pallas kernels, pick(): pl.pallas_call(pick_kernel, out_shape=pltpu.VMEM((points_t.shape[0], 2 *...  1.17 us
  transfers between devices with their start and end apart: 15, of which 11 were waited for; matrix products, arithmetic and copies ran while one was open for 0% of the time, Pallas kernels for 36%

profile of v17, /device:TPU:0, one launch (start us, length us, event | category | flops | bytes accessed | tf_op | source)
XLA Modules:
  0.0 52.2 jit_solution(7555149078601761412)
XLA Ops:
  0.6 4.1 %collective-permute-start = (bf16[64,1024]{1,0:T(8,128)(2,1)}, bf16[64,1024]{1,0:T(8,128)(2,1)S(1)}, u32[]{:S(2)}, u32[]{:S(2)}) collective-permute-start(bf16[64,1024]{1,0:T(8,128)(2,1)} %bitcast.4), channel_id=1, source_target_pairs={{2,0},{3,1},{0,2},{1,3},{6,4},{7,5},{4,6},{5,7},{10,8},{11,9},{8,1... | collective-permute-start | bytes 393224 | tf_op jit(solution)/shard_map/ppermute | solution.py:31
  4.7 1.2 %pick.1 = bf16[64,256]{1,0:T(8,128)(2,1)S(1)} custom-call(s32[2]{0:T(128)} %owner_ref.1, s32[2,128]{1,0:T(2,128)} %pivot_ref.1, bf16[64,1024]{1,0:T(8,128)(2,1)} %bitcast.5), custom_call_target="tpu_custom_call" | custom-call | tf_op jit(solution)/shard_map/pick/pallas_call | solution.py:107
  5.9 0.1 collective-permute-start.2
  6.0 1.2 %collective-permute-done.2 = bf16[64,256]{1,0:T(8,128)(2,1)S(1)} collective-permute-done((bf16[64,256]{1,0:T(8,128)(2,1)S(1)}, bf16[64,256]{1,0:T(8,128)(2,1)S(1)}, u32[]{:S(2)}, u32[]{:S(2)}) %collective-permute-start.2) | collective-permute-done | bytes 32800 | tf_op jit(solution)/shard_map/ppermute | solution.py:31
  7.2 2.5 %collective-permute-start.5 = (bf16[64,256]{1,0:T(8,128)(2,1)S(1)}, bf16[64,256]{1,0:T(8,128)(2,1)S(1)}, u32[]{:S(2)}, u32[]{:S(2)}) collective-permute-start(bf16[64,256]{1,0:T(8,128)(2,1)S(1)} %add.36), channel_id=1, source_target_pairs={{24,0},{28,4},{16,8},{20,12},{8,16},{12,20},{0,24},{4,28},{25,1},{... | collective-permute-start | bytes 98312 | tf_op jit(solution)/shard_map/ppermute | solution.py:31
  9.7 0.5 collective-permute-start.4
  10.2 0.5 %collective-permute-start.3 = (bf16[64,256]{1,0:T(8,128)(2,1)S(1)}, bf16[64,256]{1,0:T(8,128)(2,1)S(1)}, u32[]{:S(2)}, u32[]{:S(2)}) collective-permute-start(bf16[64,256]{1,0:T(8,128)(2,1)S(1)} %add.36), channel_id=1, source_target_pairs={{8,0},{12,4},{0,8},{4,12},{24,16},{28,20},{16,24},{20,28},{9,1},{1... | collective-permute-start | bytes 98312 | tf_op jit(solution)/shard_map/ppermute | solution.py:31
  10.8 1.3 %collective-permute-done.5 = bf16[64,256]{1,0:T(8,128)(2,1)S(1)} collective-permute-done((bf16[64,256]{1,0:T(8,128)(2,1)S(1)}, bf16[64,256]{1,0:T(8,128)(2,1)S(1)}, u32[]{:S(2)}, u32[]{:S(2)}) %collective-permute-start.5) | collective-permute-done | bytes 32800 | tf_op jit(solution)/shard_map/ppermute | solution.py:31
  12.1 1.5 %collective-permute-done.4 = bf16[64,256]{1,0:T(8,128)(2,1)S(1)} collective-permute-done((bf16[64,256]{1,0:T(8,128)(2,1)S(1)}, bf16[64,256]{1,0:T(8,128)(2,1)S(1)}, u32[]{:S(2)}, u32[]{:S(2)}) %collective-permute-start.4) | collective-permute-done | bytes 32800 | tf_op jit(solution)/shard_map/ppermute | solution.py:31
  13.6 0.5 collective-permute-done.3
  14.2 1.4 %collective-permute-start.8 = (bf16[64,256]{1,0:T(8,128)(2,1)S(1)}, bf16[64,256]{1,0:T(8,128)(2,1)S(1)}, u32[]{:S(2)}, u32[]{:S(2)}) collective-permute-start(bf16[64,256]{1,0:T(8,128)(2,1)S(1)} %fusion.1), channel_id=1, source_target_pairs={{3,0},{2,1},{1,2},{0,3},{7,4},{6,5},{5,6},{4,7},{11,8},{10,9},{9,1... | collective-permute-start | bytes 98312 | tf_op jit(solution)/shard_map/ppermute | solution.py:31
  15.6 1.7 %collective-permute-start.7 = (bf16[64,256]{1,0:T(8,128)(2,1)S(1)}, bf16[64,256]{1,0:T(8,128)(2,1)S(1)}, u32[]{:S(2)}, u32[]{:S(2)}) collective-permute-start(bf16[64,256]{1,0:T(8,128)(2,1)S(1)} %fusion.1), channel_id=1, source_target_pairs={{2,0},{3,1},{0,2},{1,3},{6,4},{7,5},{4,6},{5,7},{10,8},{11,9},{8,1... | collective-permute-start | bytes 98312 | tf_op jit(solution)/shard_map/ppermute | solution.py:31
  17.3 1.3 %collective-permute-start.6 = (bf16[64,256]{1,0:T(8,128)(2,1)S(1)}, bf16[64,256]{1,0:T(8,128)(2,1)S(1)}, u32[]{:S(2)}, u32[]{:S(2)}) collective-permute-start(bf16[64,256]{1,0:T(8,128)(2,1)S(1)} %fusion.1), channel_id=1, source_target_pairs={{1,0},{0,1},{3,2},{2,3},{5,4},{4,5},{7,6},{6,7},{9,8},{8,9},{11,10... | collective-permute-start | bytes 98312 | tf_op jit(solution)/shard_map/ppermute | solution.py:31
  18.7 0.7 %collective-permute-start.1 = (bf16[128,1024]{1,0:T(8,128)(2,1)S(1)}, bf16[128,1024]{1,0:T(8,128)(2,1)S(1)}, u32[]{:S(2)}, u32[]{:S(2)}) collective-permute-start(bf16[128,1024]{1,0:T(8,128)(2,1)S(1)} %pad_maximum_fusion), channel_id=1, source_target_pairs={{1,0},{0,1},{3,2},{2,3},{5,4},{4,5},{7,6},{6,7},{9,8},{8,9},{11,10... | collective-permute-start | bytes 786440 | tf_op jit(solution)/shard_map/ppermute | solution.py:31
  19.4 1.0 %collective-permute-done.8 = bf16[64,256]{1,0:T(8,128)(2,1)S(1)} collective-permute-done((bf16[64,256]{1,0:T(8,128)(2,1)S(1)}, bf16[64,256]{1,0:T(8,128)(2,1)S(1)}, u32[]{:S(2)}, u32[]{:S(2)}) %collective-permute-start.8) | collective-permute-done | bytes 32800 | tf_op jit(solution)/shard_map/ppermute | solution.py:31
  20.4 0.3 collective-permute-done.7
  20.8 0.9 %collective-permute-done.6 = bf16[64,256]{1,0:T(8,128)(2,1)S(1)} collective-permute-done((bf16[64,256]{1,0:T(8,128)(2,1)S(1)}, bf16[64,256]{1,0:T(8,128)(2,1)S(1)}, u32[]{:S(2)}, u32[]{:S(2)}) %collective-permute-start.6) | collective-permute-done | bytes 32800 | tf_op jit(solution)/shard_map/ppermute | solution.py:31
  21.6 7.9 %probes.1 = (f32[256,256]{1,0:T(8,128)S(1)}, f32[64,1024]{1,0:T(8,128)S(1)}, bf16[64,1024]{1,0:T(8,128)(2,1)S(1)}) custom-call(bf16[64,256]{1,0:T(8,128)(2,1)S(1)} %add_add_fusion.pivot_ref, bf16[64,1024]{1,0:T(8,128)(2,1)S(1)} %bitcast.7, f32[64,256]{1,0:T(8,128)S(1)} %bitcast.15, f32[64,1024]{1,0:T(8,128)S(1)} %bitcast.14), custom_call_target="tpu_custom_call" | custom-call | flops 17179869184 | bytes 1 | tf_op jit(solution)/shard_map/probes/pallas_call | solution.py:299
  29.6 1.4 %collective-permute-start.10 = (bf16[64,1024]{1,0:T(8,128)(2,1)S(1)}, bf16[64,1024]{1,0:T(8,128)(2,1)S(1)}, u32[]{:S(2)}, u32[]{:S(2)}) collective-permute-start(bf16[64,1024]{1,0:T(8,128)(2,1)S(1)} %get-tuple-element.25), channel_id=1, source_target_pairs={{1,0},{0,1},{3,2},{2,3},{5,4},{4,5},{7,6},{6,7},{9,8},{8,9},{11,10... | collective-permute-start | bytes 393224 | tf_op jit(solution)/shard_map/ppermute | solution.py:31
  31.0 0.7 %collective-permute-start.9 = (bf16[64,1024]{1,0:T(8,128)(2,1)S(1)}, bf16[64,1024]{1,0:T(8,128)(2,1)S(1)}, u32[]{:S(2)}, u32[]{:S(2)}) collective-permute-start(bf16[64,1024]{1,0:T(8,128)(2,1)S(1)} %get-tuple-element.25), channel_id=1, source_target_pairs={{2,0},{3,1},{0,2},{1,3},{6,4},{7,5},{4,6},{5,7},{10,8},{11,9},{8,1... | collective-permute-start | bytes 393224 | tf_op jit(solution)/shard_map/ppermute | solution.py:31
  31.7 1.4 %band_sum.5 = (f32[1024,64]{1,0:T(8,128)S(1)}, bf16[64,1024]{1,0:T(8,128)(2,1)S(1)}) custom-call(bf16[64,1024]{1,0:T(8,128)(2,1)S(1)} %bitcast.8, bf16[64,1024]{1,0:T(8,128)(2,1)S(1)} %get-tuple-element.13.refs_1_), custom_call_target="tpu_custom_call" | custom-call | flops 1 | bytes 1 | tf_op jit(solution)/shard_map/band_sum/pallas_call | solution.py:403
  33.1 2.2 %collective-permute-done.10 = bf16[64,1024]{1,0:T(8,128)(2,1)S(1)} collective-permute-done((bf16[64,1024]{1,0:T(8,128)(2,1)S(1)}, bf16[64,1024]{1,0:T(8,128)(2,1)S(1)}, u32[]{:S(2)}, u32[]{:S(2)}) %collective-permute-start.10) | collective-permute-done | bytes 131104 | tf_op jit(solution)/shard_map/ppermute | solution.py:31
  35.5 1.9 %factor.1 = (f32[1024,256]{1,0:T(8,128)}, bf16[64,1024]{1,0:T(8,128)(2,1)S(1)}) custom-call(bf16[64,256]{1,0:T(8,128)(2,1)S(1)} %add_add_fusion.pivot_ref, bf16[64,1024]{1,0:T(8,128)(2,1)S(1)} %bitcast.9, f32[256,256]{1,0:T(8,128)S(1)} %get-tuple-element.14.inverse_ref, bf16[64,1024]{1,0:T(8,128)(2,1)S(1)} %add.45.awaited_ref.refs_2_), custom_call_target="tpu_custom_call" | custom-call | flops 50331648 | bytes 196608 | tf_op jit(solution)/shard_map/factor/pallas_call | solution.py:340
  37.4 0.9 %collective-permute-done.9 = bf16[64,1024]{1,0:T(8,128)(2,1)S(1)} collective-permute-done((bf16[64,1024]{1,0:T(8,128)(2,1)S(1)}, bf16[64,1024]{1,0:T(8,128)(2,1)S(1)}, u32[]{:S(2)}, u32[]{:S(2)}) %collective-permute-start.9) | collective-permute-done | bytes 131104 | tf_op jit(solution)/shard_map/ppermute | solution.py:31
  38.3 0.1 collective-permute-start.11
  38.4 0.2 collective-permute-start.13
  38.7 2.5 %band_sum.6 = (f32[1024,64]{1,0:T(8,128)S(1)}, bf16[64,1024]{1,0:T(8,128)(2,1)S(1)}) custom-call(bf16[64,1024]{1,0:T(8,128)(2,1)S(1)} %bitcast.10, bf16[128,1024]{1,0:T(8,128)(2,1)S(1)} %collective-permute-done.1.refs_1_, bf16[64,1024]{1,0:T(8,128)(2,1)S(1)} %add.45.awaited_ref.refs_2_, bf16[64,1024]{1,0:T(8,128)(2,1)S(1)} %collective-permute-done.refs_3_, ...), custom_call_target="tpu_custom_call" | custom-call | flops 1073741824 | bytes 1572864 | tf_op jit(solution)/shard_map/band_sum/pallas_call | solution.py:403
  41.2 2.1 %collective-permute-done.11.refs_2_ = bf16[64,1024]{1,0:T(8,128)(2,1)S(1)} collective-permute-done((bf16[64,1024]{1,0:T(8,128)(2,1)S(1)}, bf16[64,1024]{1,0:T(8,128)(2,1)S(1)}, u32[]{:S(2)}, u32[]{:S(2)}) %collective-permute-start.11) | collective-permute-done | bytes 131104 | tf_op jit(solution)/shard_map/ppermute | solution.py:31
  43.5 2.5 %band_sum.7 = (f32[1024,64]{1,0:T(8,128)S(1)}, bf16[64,1024]{1,0:T(8,128)(2,1)}) custom-call(bf16[64,1024]{1,0:T(8,128)(2,1)S(1)} %bitcast.11, bf16[128,1024]{1,0:T(8,128)(2,1)S(1)} %collective-permute-done.1.refs_1_, bf16[64,1024]{1,0:T(8,128)(2,1)S(1)} %collective-permute-done.11.refs_2_, bf16[128,1024]{1,0:T(8,128)(2,1)S(1)} %collective-permute-done.14.refs_3_, ...), custom_call_target="tpu_custom_call" | custom-call | flops 1073741824 | bytes 1310720 | tf_op jit(solution)/shard_map/band_sum/pallas_call | solution.py:403
  46.0 1.3 %band_sum.8 = (f32[1024,64]{1,0:T(8,128)S(1)}, bf16[64,1024]{1,0:T(8,128)(2,1)}) custom-call(bf16[64,1024]{1,0:T(8,128)(2,1)S(1)} %bitcast.12, bf16[128,1024]{1,0:T(8,128)(2,1)S(1)} %collective-permute-done.13.refs_1_, f32[1024,64]{1,0:T(8,128)S(1)} %get-tuple-element.20.refs_2_), custom_call_target="tpu_custom_call" | custom-call | flops 536870912 | bytes 786432 | tf_op jit(solution)/shard_map/band_sum/pallas_call | solution.py:403
  47.4 2.8 %collective-permute-done.12.refs_1_ = bf16[128,1024]{1,0:T(8,128)(2,1)S(1)} collective-permute-done((bf16[128,1024]{1,0:T(8,128)(2,1)S(1)}, bf16[128,1024]{1,0:T(8,128)(2,1)S(1)}, u32[]{:S(2)}, u32[]{:S(2)}) %collective-permute-start.12) | collective-permute-done | bytes 262176 | tf_op jit(solution)/shard_map/ppermute | solution.py:55
  50.2 2.1 %band_sum.9 = f32[64,1024]{1,0:T(8,128)} custom-call(bf16[64,1024]{1,0:T(8,128)(2,1)S(1)} %bitcast.13, bf16[128,1024]{1,0:T(8,128)(2,1)S(1)} %collective-permute-done.12.refs_1_, f32[1024,64]{1,0:T(8,128)S(1)} %get-tuple-element.21.refs_2_, f32[64,1024]{1,0:T(8,128)S(1)} %get-tuple-element.22.refs_3_), custom_call_target="tpu_custom_call" | custom-call | flops 536870912 | bytes 1048576 | tf_op jit(solution)/shard_map/band_sum/pallas_call | solution.py:403
  (23 shorter events, 0.4 us)
Async XLA Ops:
  0.6 13.5 %collective-permute-start = (bf16[64,1024]{1,0:T(8,128)(2,1)}, bf16[64,1024]{1,0:T(8,128)(2,1)S(1)}, u32[]{:S(2)}, u32[]{:S(2)}) collective-permute-start(bf16[64,1024]{1,0:T(8,128)(2,1)} %bitcast.4), channel_id=1, source_target_pairs={{2,0},{3,1},{0,2},{1,3},{6,4},{7,5},{4,6},{5,7},{10,8},{11,9},{8,1... | collective-permute-start | bytes 393224 | tf_op jit(solution)/shard_map/ppermute | solution.py:31
  5.9 12.7 %copy-start = (bf16[1024,64]{0,1:T(8,128)(2,1)S(1)}, bf16[1024,64]{0,1:T(8,128)(2,1)}, u32[]{:S(2)}) copy-start(bf16[1024,64]{0,1:T(8,128)(2,1)} %param.5) | copy-start | bytes 393220
  5.9 1.3 %collective-permute-start.2 = (bf16[64,256]{1,0:T(8,128)(2,1)S(1)}, bf16[64,256]{1,0:T(8,128)(2,1)S(1)}, u32[]{:S(2)}, u32[]{:S(2)}) collective-permute-start(bf16[64,256]{1,0:T(8,128)(2,1)S(1)} %pick.1), channel_id=1, source_target_pairs={{4,0},{0,4},{12,8},{8,12},{20,16},{16,20},{28,24},{24,28},{5,1},{1... | collective-permute-start | bytes 98312 | tf_op jit(solution)/shard_map/ppermute | solution.py:31
  7.2 4.9 %collective-permute-start.5 = (bf16[64,256]{1,0:T(8,128)(2,1)S(1)}, bf16[64,256]{1,0:T(8,128)(2,1)S(1)}, u32[]{:S(2)}, u32[]{:S(2)}) collective-permute-start(bf16[64,256]{1,0:T(8,128)(2,1)S(1)} %add.36), channel_id=1, source_target_pairs={{24,0},{28,4},{16,8},{20,12},{8,16},{12,20},{0,24},{4,28},{25,1},{... | collective-permute-start | bytes 98312 | tf_op jit(solution)/shard_map/ppermute | solution.py:31
  9.7 3.9 %collective-permute-start.4 = (bf16[64,256]{1,0:T(8,128)(2,1)S(1)}, bf16[64,256]{1,0:T(8,128)(2,1)S(1)}, u32[]{:S(2)}, u32[]{:S(2)}) collective-permute-start(bf16[64,256]{1,0:T(8,128)(2,1)S(1)} %add.36), channel_id=1, source_target_pairs={{16,0},{20,4},{24,8},{28,12},{0,16},{4,20},{8,24},{12,28},{17,1},{... | collective-permute-start | bytes 98312 | tf_op jit(solution)/shard_map/ppermute | solution.py:31
  10.2 3.9 %collective-permute-start.3 = (bf16[64,256]{1,0:T(8,128)(2,1)S(1)}, bf16[64,256]{1,0:T(8,128)(2,1)S(1)}, u32[]{:S(2)}, u32[]{:S(2)}) collective-permute-start(bf16[64,256]{1,0:T(8,128)(2,1)S(1)} %add.36), channel_id=1, source_target_pairs={{8,0},{12,4},{0,8},{4,12},{24,16},{28,20},{16,24},{20,28},{9,1},{1... | collective-permute-start | bytes 98312 | tf_op jit(solution)/shard_map/ppermute | solution.py:31
  14.2 7.5 %copy-start.1 = (f32[1024,64]{0,1:T(8,128)S(1)}, f32[1024,64]{0,1:T(8,128)}, u32[]{:S(2)}) copy-start(f32[1024,64]{0,1:T(8,128)} %param.9) | copy-start | bytes 786436
  14.2 6.2 %collective-permute-start.8 = (bf16[64,256]{1,0:T(8,128)(2,1)S(1)}, bf16[64,256]{1,0:T(8,128)(2,1)S(1)}, u32[]{:S(2)}, u32[]{:S(2)}) collective-permute-start(bf16[64,256]{1,0:T(8,128)(2,1)S(1)} %fusion.1), channel_id=1, source_target_pairs={{3,0},{2,1},{1,2},{0,3},{7,4},{6,5},{5,6},{4,7},{11,8},{10,9},{9,1... | collective-permute-start | bytes 98312 | tf_op jit(solution)/shard_map/ppermute | solution.py:31
  15.6 5.2 %collective-permute-start.7 = (bf16[64,256]{1,0:T(8,128)(2,1)S(1)}, bf16[64,256]{1,0:T(8,128)(2,1)S(1)}, u32[]{:S(2)}, u32[]{:S(2)}) collective-permute-start(bf16[64,256]{1,0:T(8,128)(2,1)S(1)} %fusion.1), channel_id=1, source_target_pairs={{2,0},{3,1},{0,2},{1,3},{6,4},{7,5},{4,6},{5,7},{10,8},{11,9},{8,1... | collective-permute-start | bytes 98312 | tf_op jit(solution)/shard_map/ppermute | solution.py:31
  17.3 4.3 %collective-permute-start.6 = (bf16[64,256]{1,0:T(8,128)(2,1)S(1)}, bf16[64,256]{1,0:T(8,128)(2,1)S(1)}, u32[]{:S(2)}, u32[]{:S(2)}) collective-permute-start(bf16[64,256]{1,0:T(8,128)(2,1)S(1)} %fusion.1), channel_id=1, source_target_pairs={{1,0},{0,1},{3,2},{2,3},{5,4},{4,5},{7,6},{6,7},{9,8},{8,9},{11,10... | collective-permute-start | bytes 98312 | tf_op jit(solution)/shard_map/ppermute | solution.py:31
  18.7 3.0 %copy-start.2 = (f32[256,64]{0,1:T(8,128)S(1)}, f32[256,64]{0,1:T(8,128)}, u32[]{:S(2)}) copy-start(f32[256,64]{0,1:T(8,128)} %param.8) | copy-start | bytes 196612
  18.7 10.9 %collective-permute-start.1 = (bf16[128,1024]{1,0:T(8,128)(2,1)S(1)}, bf16[128,1024]{1,0:T(8,128)(2,1)S(1)}, u32[]{:S(2)}, u32[]{:S(2)}) collective-permute-start(bf16[128,1024]{1,0:T(8,128)(2,1)S(1)} %pad_maximum_fusion), channel_id=1, source_target_pairs={{1,0},{0,1},{3,2},{2,3},{5,4},{4,5},{7,6},{6,7},{9,8},{8,9},{11,10... | collective-permute-start | bytes 786440 | tf_op jit(solution)/shard_map/ppermute | solution.py:31
  29.6 5.7 %collective-permute-start.10 = (bf16[64,1024]{1,0:T(8,128)(2,1)S(1)}, bf16[64,1024]{1,0:T(8,128)(2,1)S(1)}, u32[]{:S(2)}, u32[]{:S(2)}) collective-permute-start(bf16[64,1024]{1,0:T(8,128)(2,1)S(1)} %get-tuple-element.25), channel_id=1, source_target_pairs={{1,0},{0,1},{3,2},{2,3},{5,4},{4,5},{7,6},{6,7},{9,8},{8,9},{11,10... | collective-permute-start | bytes 393224 | tf_op jit(solution)/shard_map/ppermute | solution.py:31
  31.0 7.3 %collective-permute-start.9 = (bf16[64,1024]{1,0:T(8,128)(2,1)S(1)}, bf16[64,1024]{1,0:T(8,128)(2,1)S(1)}, u32[]{:S(2)}, u32[]{:S(2)}) collective-permute-start(bf16[64,1024]{1,0:T(8,128)(2,1)S(1)} %get-tuple-element.25), channel_id=1, source_target_pairs={{2,0},{3,1},{0,2},{1,3},{6,4},{7,5},{4,6},{5,7},{10,8},{11,9},{8,1... | collective-permute-start | bytes 393224 | tf_op jit(solution)/shard_map/ppermute | solution.py:31
  35.4 8.1 %collective-permute-start.14 = (bf16[128,1024]{1,0:T(8,128)(2,1)S(1)}, bf16[128,1024]{1,0:T(8,128)(2,1)S(1)}, u32[]{:S(2)}, u32[]{:S(2)}) collective-permute-start(bf16[128,1024]{1,0:T(8,128)(2,1)S(1)} %pad_maximum_fusion.3), channel_id=1, source_target_pairs={{28,0},{5,1},{30,2},{7,3},{0,4},{9,5},{2,6},{11,7},{4,8},{13,9},{6... | collective-permute-start | bytes 786440 | tf_op jit(solution)/shard_map/ppermute | solution.py:55
  38.3 5.0 %collective-permute-start.11 = (bf16[64,1024]{1,0:T(8,128)(2,1)S(1)}, bf16[64,1024]{1,0:T(8,128)(2,1)S(1)}, u32[]{:S(2)}, u32[]{:S(2)}) collective-permute-start(bf16[64,1024]{1,0:T(8,128)(2,1)S(1)} %add.46.refs_4_), channel_id=1, source_target_pairs={{1,0},{0,1},{3,2},{2,3},{5,4},{4,5},{7,6},{6,7},{9,8},{8,9},{11,10... | collective-permute-start | bytes 393224 | tf_op jit(solution)/shard_map/ppermute | solution.py:31
  38.4 7.6 %collective-permute-start.13 = (bf16[128,1024]{1,0:T(8,128)(2,1)S(1)}, bf16[128,1024]{1,0:T(8,128)(2,1)S(1)}, u32[]{:S(2)}, u32[]{:S(2)}) collective-permute-start(bf16[128,1024]{1,0:T(8,128)(2,1)S(1)} %pad_maximum_fusion.2), channel_id=1, source_target_pairs={{28,0},{29,1},{6,2},{7,3},{0,4},{1,5},{10,6},{11,7},{4,8},{5,9},{1... | collective-permute-start | bytes 786440 | tf_op jit(solution)/shard_map/ppermute | solution.py:55
  43.4 6.7 %collective-permute-start.12 = (bf16[128,1024]{1,0:T(8,128)(2,1)S(1)}, bf16[128,1024]{1,0:T(8,128)(2,1)S(1)}, u32[]{:S(2)}, u32[]{:S(2)}) collective-permute-start(bf16[128,1024]{1,0:T(8,128)(2,1)S(1)} %pad_maximum_fusion.1), channel_id=1, source_target_pairs={{28,0},{29,1},{6,2},{7,3},{0,4},{1,5},{10,6},{11,7},{4,8},{5,9},{1... | collective-permute-start | bytes 786440 | tf_op jit(solution)/shard_map/ppermute | solution.py:55

commit v18 on v17

--- a/solution.py
+++ b/solution.py
@@ -438,13 +438,13 @@
         two = two + zeros
         cross_one = cross(jnp.concatenate([pair[:depth], one], axis=0), 1)
         three = swapped(two, "gy", 1)
-        cross_two = cross(jnp.concatenate([far, two], axis=0), 2)
-        total, zeros = band_sum(points, [((pair, 0), (one, 0)), ((far, 0), (two, 0))], total)
-        cross_three = cross(jnp.concatenate([pair[depth:], three + zeros], axis=0), 3)
-        crossed = [((stacked, 0), (stacked, depth)) for stacked in (cross_one, cross_two, cross_three)]
-        total, _ = band_sum(points, [((pair, depth), (three, 0)), crossed[0]], total)
-        total, _ = band_sum(points, crossed[1:2], total)
-        kernel_probes = band_sum(points, crossed[2:], total, probes)
+        cross_two = cross(jnp.concatenate([far, pair[depth:], two], axis=0), 2)
+        total, _ = band_sum(points, [((pair, 0), (one, 0)), ((far, 0), (two, 0))], total)
+        total, zeros = band_sum(points, [((cross_one, 0), (cross_one, depth))], total)
+        three = three + zeros
+        cross_three = cross(three, 3)
+        total, _ = band_sum(points, [((cross_two, 0), (cross_two, 2 * depth)), ((pair, depth), (three, 0))], total)
+        kernel_probes = band_sum(points, [((cross_two, depth), (cross_three, 0))], total, probes)
     else:
         factor, _ = factor_of(pivot_points, points, inverse, zeros)
         pieces = [((block, 0), (probe, 0)) for block, probe in zip(near, direct_blocks(sent))]

time: 52.4 us -> 59.6 us (1.14)
  waiting for transfers between devices: 14.9 us -> 18.8 us
  starting transfers between devices: 15.4 us -> 18.7 us
    ppermute x3, waiting for transfers between devices: 2.82 us -> 8.53 us  [cross(): return lax.ppermute(piece, ('gx', 'gy'), pairs)]
    ppermute x12, starting transfers between devices: 15.1 us -> 17.5 us  [swapped(): lax.ppermute(value, axis, [(i ^ bit, i) for i in range(lax.axis_size(axis...]
    ppermute x12, waiting for transfers between devices: 12.1 us -> 10.3 us  [swapped(): lax.ppermute(value, axis, [(i ^ bit, i) for i in range(lax.axis_size(axis...]
    ppermute x3, starting transfers between devices: 0.35 us -> 1.14 us  [cross(): return lax.ppermute(piece, ('gx', 'gy'), pairs)]
  transfers between devices with their start and end apart: 15 -> 15, of which waited for: 11 -> 9; matrix products, arithmetic and copies ran while one was open for 0% -> 0% of each run, Pallas kernels for 36% -> 32%
where the time goes in v18:
time: 59.6 us; the launch traced here: 59.4 us
  Pallas kernels  20.8 us (35%)
  waiting for transfers between devices  18.8 us (32%)
  starting transfers between devices  18.7 us (31%)
  between operations  0.83 us (1%)
    ppermute x12, starting transfers between devices, swapped(): lax.ppermute(value, axis, [(i ^ bit, i) for i in range(lax.axis_size(axis...  17.5 us
    ppermute x12, waiting for transfers between devices, swapped(): lax.ppermute(value, axis, [(i ^ bit, i) for i in range(lax.axis_size(axis...  10.3 us
    pallas_call x5, Pallas kernels, band_sum(): pl.pallas_call(functools.partial(band_kernel, tuple(places), first, last)...  9.85 us
    ppermute x3, waiting for transfers between devices, cross(): return lax.ppermute(piece, ('gx', 'gy'), pairs)  8.53 us
    pallas_call x1, Pallas kernels, probes_of(): pl.pallas_call(probe_kernel, out_shape=(pltpu.VMEM((size, size), jnp.floa...  7.9 us
    pallas_call x1, Pallas kernels, factor_of(): pl.pallas_call(factor_kernel, out_shape=(jax.ShapeDtypeStruct((count, siz...  1.91 us
  transfers between devices with their start and end apart: 15, of which 9 were waited for; matrix products, arithmetic and copies ran while one was open for 0% of the time, Pallas kernels for 32%

profile of v18, /device:TPU:0, one launch (start us, length us, event | category | flops | bytes accessed | tf_op | source)
XLA Modules:
  0.0 59.4 jit_solution(16727986770230153621)
XLA Ops:
  0.6 4.1 %collective-permute-start = (bf16[64,1024]{1,0:T(8,128)(2,1)}, bf16[64,1024]{1,0:T(8,128)(2,1)S(1)}, u32[]{:S(2)}, u32[]{:S(2)}) collective-permute-start(bf16[64,1024]{1,0:T(8,128)(2,1)} %bitcast.4), channel_id=1, source_target_pairs={{2,0},{3,1},{0,2},{1,3},{6,4},{7,5},{4,6},{5,7},{10,8},{11,9},{8,1... | collective-permute-start | bytes 393224 | tf_op jit(solution)/shard_map/ppermute | solution.py:31
  4.7 1.2 %pick.1 = bf16[64,256]{1,0:T(8,128)(2,1)S(1)} custom-call(s32[2]{0:T(128)} %owner_ref.1, s32[2,128]{1,0:T(2,128)} %pivot_ref.1, bf16[64,1024]{1,0:T(8,128)(2,1)} %bitcast.5), custom_call_target="tpu_custom_call" | custom-call | tf_op jit(solution)/shard_map/pick/pallas_call | solution.py:107
  5.9 0.1 collective-permute-start.2
  6.0 1.2 %collective-permute-done.2 = bf16[64,256]{1,0:T(8,128)(2,1)S(1)} collective-permute-done((bf16[64,256]{1,0:T(8,128)(2,1)S(1)}, bf16[64,256]{1,0:T(8,128)(2,1)S(1)}, u32[]{:S(2)}, u32[]{:S(2)}) %collective-permute-start.2) | collective-permute-done | bytes 32800 | tf_op jit(solution)/shard_map/ppermute | solution.py:31
  7.2 1.6 %collective-permute-start.3 = (bf16[64,256]{1,0:T(8,128)(2,1)S(1)}, bf16[64,256]{1,0:T(8,128)(2,1)S(1)}, u32[]{:S(2)}, u32[]{:S(2)}) collective-permute-start(bf16[64,256]{1,0:T(8,128)(2,1)S(1)} %add.36), channel_id=1, source_target_pairs={{8,0},{12,4},{0,8},{4,12},{24,16},{28,20},{16,24},{20,28},{9,1},{1... | collective-permute-start | bytes 98312 | tf_op jit(solution)/shard_map/ppermute | solution.py:31
  8.8 1.5 %collective-permute-start.4 = (bf16[64,256]{1,0:T(8,128)(2,1)S(1)}, bf16[64,256]{1,0:T(8,128)(2,1)S(1)}, u32[]{:S(2)}, u32[]{:S(2)}) collective-permute-start(bf16[64,256]{1,0:T(8,128)(2,1)S(1)} %add.36), channel_id=1, source_target_pairs={{16,0},{20,4},{24,8},{28,12},{0,16},{4,20},{8,24},{12,28},{17,1},{... | collective-permute-start | bytes 98312 | tf_op jit(solution)/shard_map/ppermute | solution.py:31
  10.3 0.5 collective-permute-start.5
  10.8 0.4 collective-permute-done.3
  11.2 1.5 %collective-permute-done.4 = bf16[64,256]{1,0:T(8,128)(2,1)S(1)} collective-permute-done((bf16[64,256]{1,0:T(8,128)(2,1)S(1)}, bf16[64,256]{1,0:T(8,128)(2,1)S(1)}, u32[]{:S(2)}, u32[]{:S(2)}) %collective-permute-start.4) | collective-permute-done | bytes 32800 | tf_op jit(solution)/shard_map/ppermute | solution.py:31
  12.7 2.4 %collective-permute-done.5 = bf16[64,256]{1,0:T(8,128)(2,1)S(1)} collective-permute-done((bf16[64,256]{1,0:T(8,128)(2,1)S(1)}, bf16[64,256]{1,0:T(8,128)(2,1)S(1)}, u32[]{:S(2)}, u32[]{:S(2)}) %collective-permute-start.5) | collective-permute-done | bytes 32800 | tf_op jit(solution)/shard_map/ppermute | solution.py:31
  15.1 1.6 %collective-permute-start.6 = (bf16[64,256]{1,0:T(8,128)(2,1)S(1)}, bf16[64,256]{1,0:T(8,128)(2,1)S(1)}, u32[]{:S(2)}, u32[]{:S(2)}) collective-permute-start(bf16[64,256]{1,0:T(8,128)(2,1)S(1)} %fusion.1), channel_id=1, source_target_pairs={{1,0},{0,1},{3,2},{2,3},{5,4},{4,5},{7,6},{6,7},{9,8},{8,9},{11,10... | collective-permute-start | bytes 98312 | tf_op jit(solution)/shard_map/ppermute | solution.py:31
  16.8 0.3 collective-permute-start.7
  17.1 2.5 %collective-permute-start.8 = (bf16[64,256]{1,0:T(8,128)(2,1)S(1)}, bf16[64,256]{1,0:T(8,128)(2,1)S(1)}, u32[]{:S(2)}, u32[]{:S(2)}) collective-permute-start(bf16[64,256]{1,0:T(8,128)(2,1)S(1)} %fusion.1), channel_id=1, source_target_pairs={{3,0},{2,1},{1,2},{0,3},{7,4},{6,5},{5,6},{4,7},{11,8},{10,9},{9,1... | collective-permute-start | bytes 98312 | tf_op jit(solution)/shard_map/ppermute | solution.py:31
  19.6 0.7 %collective-permute-start.1 = (bf16[128,1024]{1,0:T(8,128)(2,1)S(1)}, bf16[128,1024]{1,0:T(8,128)(2,1)S(1)}, u32[]{:S(2)}, u32[]{:S(2)}) collective-permute-start(bf16[128,1024]{1,0:T(8,128)(2,1)S(1)} %pad_maximum_fusion.1), channel_id=1, source_target_pairs={{1,0},{0,1},{3,2},{2,3},{5,4},{4,5},{7,6},{6,7},{9,8},{8,9},{11,10... | collective-permute-start | bytes 786440 | tf_op jit(solution)/shard_map/ppermute | solution.py:31
  20.4 1.6 %collective-permute-done.7 = bf16[64,256]{1,0:T(8,128)(2,1)S(1)} collective-permute-done((bf16[64,256]{1,0:T(8,128)(2,1)S(1)}, bf16[64,256]{1,0:T(8,128)(2,1)S(1)}, u32[]{:S(2)}, u32[]{:S(2)}) %collective-permute-start.7) | collective-permute-done | bytes 32800 | tf_op jit(solution)/shard_map/ppermute | solution.py:31
  22.0 1.2 %collective-permute-done.8 = bf16[64,256]{1,0:T(8,128)(2,1)S(1)} collective-permute-done((bf16[64,256]{1,0:T(8,128)(2,1)S(1)}, bf16[64,256]{1,0:T(8,128)(2,1)S(1)}, u32[]{:S(2)}, u32[]{:S(2)}) %collective-permute-start.8) | collective-permute-done | bytes 32800 | tf_op jit(solution)/shard_map/ppermute | solution.py:31
  23.3 7.9 %probes.1 = (f32[256,256]{1,0:T(8,128)S(1)}, f32[64,1024]{1,0:T(8,128)S(1)}, bf16[64,1024]{1,0:T(8,128)(2,1)S(1)}) custom-call(bf16[64,256]{1,0:T(8,128)(2,1)S(1)} %add_add_fusion.pivot_ref, bf16[64,1024]{1,0:T(8,128)(2,1)S(1)} %bitcast.7, f32[64,256]{1,0:T(8,128)S(1)} %bitcast.15, f32[64,1024]{1,0:T(8,128)S(1)} %bitcast.14), custom_call_target="tpu_custom_call" | custom-call | flops 17179869184 | bytes 1 | tf_op jit(solution)/shard_map/probes/pallas_call | solution.py:299
  31.2 0.1 collective-permute-start.10
  31.3 3.0 %collective-permute-start.9 = (bf16[64,1024]{1,0:T(8,128)(2,1)S(1)}, bf16[64,1024]{1,0:T(8,128)(2,1)S(1)}, u32[]{:S(2)}, u32[]{:S(2)}) collective-permute-start(bf16[64,1024]{1,0:T(8,128)(2,1)S(1)} %get-tuple-element.25), channel_id=1, source_target_pairs={{2,0},{3,1},{0,2},{1,3},{6,4},{7,5},{4,6},{5,7},{10,8},{11,9},{8,1... | collective-permute-start | bytes 393224 | tf_op jit(solution)/shard_map/ppermute | solution.py:31
  34.3 1.4 %band_sum.5 = (f32[1024,64]{1,0:T(8,128)S(1)}, bf16[64,1024]{1,0:T(8,128)(2,1)S(1)}) custom-call(bf16[64,1024]{1,0:T(8,128)(2,1)S(1)} %bitcast.8, bf16[64,1024]{1,0:T(8,128)(2,1)S(1)} %get-tuple-element.13.refs_1_), custom_call_target="tpu_custom_call" | custom-call | flops 1 | bytes 1 | tf_op jit(solution)/shard_map/band_sum/pallas_call | solution.py:403
  35.8 1.9 %collective-permute-done.10 = bf16[64,1024]{1,0:T(8,128)(2,1)S(1)} collective-permute-done((bf16[64,1024]{1,0:T(8,128)(2,1)S(1)}, bf16[64,1024]{1,0:T(8,128)(2,1)S(1)}, u32[]{:S(2)}, u32[]{:S(2)}) %collective-permute-start.10) | collective-permute-done | bytes 131104 | tf_op jit(solution)/shard_map/ppermute | solution.py:31
  37.7 1.9 %factor.1 = (f32[1024,256]{1,0:T(8,128)}, bf16[64,1024]{1,0:T(8,128)(2,1)S(1)}) custom-call(bf16[64,256]{1,0:T(8,128)(2,1)S(1)} %add_add_fusion.pivot_ref, bf16[64,1024]{1,0:T(8,128)(2,1)S(1)} %bitcast.9, f32[256,256]{1,0:T(8,128)S(1)} %get-tuple-element.14.inverse_ref, bf16[64,1024]{1,0:T(8,128)(2,1)S(1)} %add.45.awaited_ref.refs_2_), custom_call_target="tpu_custom_call" | custom-call | flops 50331648 | bytes 196608 | tf_op jit(solution)/shard_map/factor/pallas_call | solution.py:340
  39.7 0.1 collective-permute-start.11
  39.8 1.0 %collective-permute-start.13 = (bf16[128,1024]{1,0:T(8,128)(2,1)S(1)}, bf16[128,1024]{1,0:T(8,128)(2,1)S(1)}, u32[]{:S(2)}, u32[]{:S(2)}) collective-permute-start(bf16[128,1024]{1,0:T(8,128)(2,1)S(1)} %pad_maximum_fusion.2), channel_id=1, source_target_pairs={{28,0},{5,1},{30,2},{7,3},{0,4},{9,5},{2,6},{11,7},{4,8},{13,9},{6... | collective-permute-start | bytes 786440 | tf_op jit(solution)/shard_map/ppermute | solution.py:55
  40.8 1.5 %collective-permute-start.12 = (bf16[64,1024]{1,0:T(8,128)(2,1)S(1)}, bf16[64,1024]{1,0:T(8,128)(2,1)S(1)}, u32[]{:S(2)}, u32[]{:S(2)}) collective-permute-start(bf16[64,1024]{1,0:T(8,128)(2,1)S(1)} %add.46.refs_4_), channel_id=1, source_target_pairs={{1,0},{0,1},{3,2},{2,3},{5,4},{4,5},{7,6},{6,7},{9,8},{8,9},{11,10... | collective-permute-start | bytes 393224 | tf_op jit(solution)/shard_map/ppermute | solution.py:31
  42.3 2.5 %band_sum.6 = (f32[1024,64]{1,0:T(8,128)S(1)}, bf16[64,1024]{1,0:T(8,128)(2,1)}) custom-call(bf16[64,1024]{1,0:T(8,128)(2,1)S(1)} %bitcast.10, bf16[128,1024]{1,0:T(8,128)(2,1)S(1)} %collective-permute-done.1.refs_1_.refs_2_, bf16[64,1024]{1,0:T(8,128)(2,1)S(1)} %add.45.awaited_ref.refs_2_, bf16[64,1024]{1,0:T(8,128)(2,1)S(1)} %collective-permute-done.refs_3_, ...), custom_call_target="tpu_custom_call" | custom-call | flops 1073741824 | bytes 1572864 | tf_op jit(solution)/shard_map/band_sum/pallas_call | solution.py:403
  44.8 5.8 %collective-permute-done.13.refs_1_ = bf16[128,1024]{1,0:T(8,128)(2,1)S(1)} collective-permute-done((bf16[128,1024]{1,0:T(8,128)(2,1)S(1)}, bf16[128,1024]{1,0:T(8,128)(2,1)S(1)}, u32[]{:S(2)}, u32[]{:S(2)}) %collective-permute-start.13) | collective-permute-done | bytes 262176 | tf_op jit(solution)/shard_map/ppermute | solution.py:55
  50.6 1.3 %band_sum.7 = (f32[1024,64]{1,0:T(8,128)S(1)}, bf16[64,1024]{1,0:T(8,128)(2,1)S(1)}) custom-call(bf16[64,1024]{1,0:T(8,128)(2,1)S(1)} %bitcast.11, bf16[128,1024]{1,0:T(8,128)(2,1)S(1)} %collective-permute-done.13.refs_1_, f32[1024,64]{1,0:T(8,128)S(1)} %get-tuple-element.18.refs_2_), custom_call_target="tpu_custom_call" | custom-call | flops 536870912 | bytes 786432 | tf_op jit(solution)/shard_map/band_sum/pallas_call | solution.py:403
  52.0 0.1 collective-permute-start.14
  52.1 2.5 %band_sum.8 = (f32[1024,64]{1,0:T(8,128)S(1)}, bf16[64,1024]{1,0:T(8,128)(2,1)}) custom-call(bf16[64,1024]{1,0:T(8,128)(2,1)S(1)} %bitcast.12, bf16[192,1024]{1,0:T(8,128)(2,1)S(1)} %collective-permute-done.11.refs_1_, bf16[128,1024]{1,0:T(8,128)(2,1)S(1)} %collective-permute-done.1.refs_1_.refs_2_, bf16[64,1024]{1,0:T(8,128)(2,1)S(1)} %add.47.refs_3_, ...), custom_call_target="tpu_custom_call" | custom-call | flops 1073741824 | bytes 1310720 | tf_op jit(solution)/shard_map/band_sum/pallas_call | solution.py:403
  54.6 2.7 %collective-permute-done.14.refs_2_ = bf16[64,1024]{1,0:T(8,128)(2,1)S(1)} collective-permute-done((bf16[64,1024]{1,0:T(8,128)(2,1)S(1)}, bf16[64,1024]{1,0:T(8,128)(2,1)S(1)}, u32[]{:S(2)}, u32[]{:S(2)}) %collective-permute-start.14) | collective-permute-done | bytes 131104 | tf_op jit(solution)/shard_map/ppermute | solution.py:55
  57.4 2.1 %band_sum.9 = f32[64,1024]{1,0:T(8,128)} custom-call(bf16[64,1024]{1,0:T(8,128)(2,1)S(1)} %bitcast.13, bf16[192,1024]{1,0:T(8,128)(2,1)S(1)} %collective-permute-done.11.refs_1_, bf16[64,1024]{1,0:T(8,128)(2,1)S(1)} %collective-permute-done.14.refs_2_, f32[1024,64]{1,0:T(8,128)S(1)} %get-tuple-element.21.refs_3_, f32[64,1024]{1,0:T(8,128)S(1)} %get-tuple-element.22.refs_4_), custom_call_target="tpu_custom_call" | custom-call | flops 536870912 | bytes 1310720 | tf_op jit(solution)/shard_map/band_sum/pallas_call | solution.py:403
  (22 shorter events, 0.3 us)
Async XLA Ops:
  0.6 14.5 %collective-permute-start = (bf16[64,1024]{1,0:T(8,128)(2,1)}, bf16[64,1024]{1,0:T(8,128)(2,1)S(1)}, u32[]{:S(2)}, u32[]{:S(2)}) collective-permute-start(bf16[64,1024]{1,0:T(8,128)(2,1)} %bitcast.4), channel_id=1, source_target_pairs={{2,0},{3,1},{0,2},{1,3},{6,4},{7,5},{4,6},{5,7},{10,8},{11,9},{8,1... | collective-permute-start | bytes 393224 | tf_op jit(solution)/shard_map/ppermute | solution.py:31
  5.9 13.7 %copy-start = (bf16[1024,64]{0,1:T(8,128)(2,1)S(1)}, bf16[1024,64]{0,1:T(8,128)(2,1)}, u32[]{:S(2)}) copy-start(bf16[1024,64]{0,1:T(8,128)(2,1)} %param.5) | copy-start | bytes 393220
  5.9 1.3 %collective-permute-start.2 = (bf16[64,256]{1,0:T(8,128)(2,1)S(1)}, bf16[64,256]{1,0:T(8,128)(2,1)S(1)}, u32[]{:S(2)}, u32[]{:S(2)}) collective-permute-start(bf16[64,256]{1,0:T(8,128)(2,1)S(1)} %pick.1), channel_id=1, source_target_pairs={{4,0},{0,4},{12,8},{8,12},{20,16},{16,20},{28,24},{24,28},{5,1},{1... | collective-permute-start | bytes 98312 | tf_op jit(solution)/shard_map/ppermute | solution.py:31
  7.2 4.0 %collective-permute-start.3 = (bf16[64,256]{1,0:T(8,128)(2,1)S(1)}, bf16[64,256]{1,0:T(8,128)(2,1)S(1)}, u32[]{:S(2)}, u32[]{:S(2)}) collective-permute-start(bf16[64,256]{1,0:T(8,128)(2,1)S(1)} %add.36), channel_id=1, source_target_pairs={{8,0},{12,4},{0,8},{4,12},{24,16},{28,20},{16,24},{20,28},{9,1},{1... | collective-permute-start | bytes 98312 | tf_op jit(solution)/shard_map/ppermute | solution.py:31
  8.8 3.9 %collective-permute-start.4 = (bf16[64,256]{1,0:T(8,128)(2,1)S(1)}, bf16[64,256]{1,0:T(8,128)(2,1)S(1)}, u32[]{:S(2)}, u32[]{:S(2)}) collective-permute-start(bf16[64,256]{1,0:T(8,128)(2,1)S(1)} %add.36), channel_id=1, source_target_pairs={{16,0},{20,4},{24,8},{28,12},{0,16},{4,20},{8,24},{12,28},{17,1},{... | collective-permute-start | bytes 98312 | tf_op jit(solution)/shard_map/ppermute | solution.py:31
  10.3 4.8 %collective-permute-start.5 = (bf16[64,256]{1,0:T(8,128)(2,1)S(1)}, bf16[64,256]{1,0:T(8,128)(2,1)S(1)}, u32[]{:S(2)}, u32[]{:S(2)}) collective-permute-start(bf16[64,256]{1,0:T(8,128)(2,1)S(1)} %add.36), channel_id=1, source_target_pairs={{24,0},{28,4},{16,8},{20,12},{8,16},{12,20},{0,24},{4,28},{25,1},{... | collective-permute-start | bytes 98312 | tf_op jit(solution)/shard_map/ppermute | solution.py:31
  15.1 8.1 %copy-start.1 = (f32[1024,64]{0,1:T(8,128)S(1)}, f32[1024,64]{0,1:T(8,128)}, u32[]{:S(2)}) copy-start(f32[1024,64]{0,1:T(8,128)} %param.9) | copy-start | bytes 786436
  15.1 5.2 %collective-permute-start.6 = (bf16[64,256]{1,0:T(8,128)(2,1)S(1)}, bf16[64,256]{1,0:T(8,128)(2,1)S(1)}, u32[]{:S(2)}, u32[]{:S(2)}) collective-permute-start(bf16[64,256]{1,0:T(8,128)(2,1)S(1)} %fusion.1), channel_id=1, source_target_pairs={{1,0},{0,1},{3,2},{2,3},{5,4},{4,5},{7,6},{6,7},{9,8},{8,9},{11,10... | collective-permute-start | bytes 98312 | tf_op jit(solution)/shard_map/ppermute | solution.py:31
  16.8 5.2 %collective-permute-start.7 = (bf16[64,256]{1,0:T(8,128)(2,1)S(1)}, bf16[64,256]{1,0:T(8,128)(2,1)S(1)}, u32[]{:S(2)}, u32[]{:S(2)}) collective-permute-start(bf16[64,256]{1,0:T(8,128)(2,1)S(1)} %fusion.1), channel_id=1, source_target_pairs={{2,0},{3,1},{0,2},{1,3},{6,4},{7,5},{4,6},{5,7},{10,8},{11,9},{8,1... | collective-permute-start | bytes 98312 | tf_op jit(solution)/shard_map/ppermute | solution.py:31
  17.1 6.1 %collective-permute-start.8 = (bf16[64,256]{1,0:T(8,128)(2,1)S(1)}, bf16[64,256]{1,0:T(8,128)(2,1)S(1)}, u32[]{:S(2)}, u32[]{:S(2)}) collective-permute-start(bf16[64,256]{1,0:T(8,128)(2,1)S(1)} %fusion.1), channel_id=1, source_target_pairs={{3,0},{2,1},{1,2},{0,3},{7,4},{6,5},{5,6},{4,7},{11,8},{10,9},{9,1... | collective-permute-start | bytes 98312 | tf_op jit(solution)/shard_map/ppermute | solution.py:31
  19.6 3.7 %copy-start.2 = (f32[256,64]{0,1:T(8,128)S(1)}, f32[256,64]{0,1:T(8,128)}, u32[]{:S(2)}) copy-start(f32[256,64]{0,1:T(8,128)} %param.8) | copy-start | bytes 196612
  19.6 11.6 %collective-permute-start.1 = (bf16[128,1024]{1,0:T(8,128)(2,1)S(1)}, bf16[128,1024]{1,0:T(8,128)(2,1)S(1)}, u32[]{:S(2)}, u32[]{:S(2)}) collective-permute-start(bf16[128,1024]{1,0:T(8,128)(2,1)S(1)} %pad_maximum_fusion.1), channel_id=1, source_target_pairs={{1,0},{0,1},{3,2},{2,3},{5,4},{4,5},{7,6},{6,7},{9,8},{8,9},{11,10... | collective-permute-start | bytes 786440 | tf_op jit(solution)/shard_map/ppermute | solution.py:31
  31.2 6.4 %collective-permute-start.10 = (bf16[64,1024]{1,0:T(8,128)(2,1)S(1)}, bf16[64,1024]{1,0:T(8,128)(2,1)S(1)}, u32[]{:S(2)}, u32[]{:S(2)}) collective-permute-start(bf16[64,1024]{1,0:T(8,128)(2,1)S(1)} %get-tuple-element.25), channel_id=1, source_target_pairs={{1,0},{0,1},{3,2},{2,3},{5,4},{4,5},{7,6},{6,7},{9,8},{8,9},{11,10... | collective-permute-start | bytes 393224 | tf_op jit(solution)/shard_map/ppermute | solution.py:31
  31.3 8.3 %collective-permute-start.9 = (bf16[64,1024]{1,0:T(8,128)(2,1)S(1)}, bf16[64,1024]{1,0:T(8,128)(2,1)S(1)}, u32[]{:S(2)}, u32[]{:S(2)}) collective-permute-start(bf16[64,1024]{1,0:T(8,128)(2,1)S(1)} %get-tuple-element.25), channel_id=1, source_target_pairs={{2,0},{3,1},{0,2},{1,3},{6,4},{7,5},{4,6},{5,7},{10,8},{11,9},{8,1... | collective-permute-start | bytes 393224 | tf_op jit(solution)/shard_map/ppermute | solution.py:31
  39.7 12.4 %collective-permute-start.11 = (bf16[192,1024]{1,0:T(8,128)(2,1)S(1)}, bf16[192,1024]{1,0:T(8,128)(2,1)S(1)}, u32[]{:S(2)}, u32[]{:S(2)}) collective-permute-start(bf16[192,1024]{1,0:T(8,128)(2,1)S(1)} %pad_maximum_fusion), channel_id=1, source_target_pairs={{28,0},{29,1},{6,2},{7,3},{0,4},{1,5},{10,6},{11,7},{4,8},{5,9},{1... | collective-permute-start | bytes 1179656 | tf_op jit(solution)/shard_map/ppermute | solution.py:55
  39.8 10.9 %collective-permute-start.13 = (bf16[128,1024]{1,0:T(8,128)(2,1)S(1)}, bf16[128,1024]{1,0:T(8,128)(2,1)S(1)}, u32[]{:S(2)}, u32[]{:S(2)}) collective-permute-start(bf16[128,1024]{1,0:T(8,128)(2,1)S(1)} %pad_maximum_fusion.2), channel_id=1, source_target_pairs={{28,0},{5,1},{30,2},{7,3},{0,4},{9,5},{2,6},{11,7},{4,8},{13,9},{6... | collective-permute-start | bytes 786440 | tf_op jit(solution)/shard_map/ppermute | solution.py:55
  40.8 11.2 %collective-permute-start.12 = (bf16[64,1024]{1,0:T(8,128)(2,1)S(1)}, bf16[64,1024]{1,0:T(8,128)(2,1)S(1)}, u32[]{:S(2)}, u32[]{:S(2)}) collective-permute-start(bf16[64,1024]{1,0:T(8,128)(2,1)S(1)} %add.46.refs_4_), channel_id=1, source_target_pairs={{1,0},{0,1},{3,2},{2,3},{5,4},{4,5},{7,6},{6,7},{9,8},{8,9},{11,10... | collective-permute-start | bytes 393224 | tf_op jit(solution)/shard_map/ppermute | solution.py:31
  52.0 5.3 %collective-permute-start.14 = (bf16[64,1024]{1,0:T(8,128)(2,1)S(1)}, bf16[64,1024]{1,0:T(8,128)(2,1)S(1)}, u32[]{:S(2)}, u32[]{:S(2)}) collective-permute-start(bf16[64,1024]{1,0:T(8,128)(2,1)S(1)} %add.47.refs_3_), channel_id=1, source_target_pairs={{28,0},{29,1},{6,2},{7,3},{0,4},{1,5},{10,6},{11,7},{4,8},{5,9},{1... | collective-permute-start | bytes 393224 | tf_op jit(solution)/shard_map/ppermute | solution.py:55

commit v19 on v17

--- a/solution.py
+++ b/solution.py
@@ -317,7 +317,7 @@
 
 
 def tile_terms(own, other, probes):
-    return product(kernel_of(product(own, other, ((1,), (0,)))).astype(jnp.bfloat16), probes, ((1,), (1,)))
+    return product(probes, kernel_of(product(own, other, ((1,), (0,)))).astype(jnp.bfloat16), ((1,), (1,)))
 
 
 def factor_kernel(pivot_ref, point_ref, inverse_ref, awaited_ref, factor_ref, zero_ref):
@@ -366,16 +366,16 @@
         points = refs[point_at][point_row:point_row + depth, :]
         blocks.append((padded(extended(points, False)).astype(jnp.bfloat16), refs[probe_at], probe_row))
     for s in range(0, count, CHUNK):
-        total = None if first else before_ref[s:s + CHUNK, :]
+        total = None if first else before_ref[:, s:s + CHUNK]
         for other, probe_ref, probe_row in blocks:
             term = tile_terms(own[s:s + CHUNK, :], other, probe_ref[probe_row:, :])
             total = term if total is None else total + term
         if last:
             probe_ref, out_ref = rest
             scale = 1.0 / (count ** 0.5)
-            out_ref[:, s:s + CHUNK] = jnp.transpose(total) * scale + noise_weight * probe_ref[:, s:s + CHUNK]
+            out_ref[:, s:s + CHUNK] = total * scale + noise_weight * probe_ref[:, s:s + CHUNK]
         else:
-            rest[0][s:s + CHUNK, :] = total
+            rest[0][:, s:s + CHUNK] = total
     if not last:
         rest[1][...] = jnp.zeros_like(rest[1])
 
@@ -399,7 +399,7 @@
     if last:
         out_shape = jax.ShapeDtypeStruct((width, count), jnp.float32)
     else:
-        out_shape = (pltpu.VMEM((count, width), jnp.float32), pltpu.VMEM((width, count), jnp.bfloat16))
+        out_shape = (pltpu.VMEM((width, count), jnp.float32), pltpu.VMEM((width, count), jnp.bfloat16))
     return pl.pallas_call(
         functools.partial(band_kernel, tuple(places), first, last),
         out_shape=out_shape,

time: 52.4 us -> 52.5 us (level)
  Pallas kernels: 20.8 us -> 21.4 us
    pallas_call x5, Pallas kernels: 9.85 us -> 10.4 us  [band_sum(): pl.pallas_call(functools.partial(band_kernel, tuple(places), first, last)...]
  transfers between devices with their start and end apart: 15 -> 15, of which waited for: 11 -> 11; matrix products, arithmetic and copies ran while one was open for 0% -> 0% of each run, Pallas kernels for 36% -> 37%
where the time goes in v19:
time: 52.5 us; the launch traced here: 52.4 us
  Pallas kernels  21.4 us (41%)
  starting transfers between devices  15.4 us (29%)
  waiting for transfers between devices  14.4 us (27%)
  between operations  0.85 us (2%)
    ppermute x12, starting transfers between devices, swapped(): lax.ppermute(value, axis, [(i ^ bit, i) for i in range(lax.axis_size(axis...  15.1 us
    ppermute x12, waiting for transfers between devices, swapped(): lax.ppermute(value, axis, [(i ^ bit, i) for i in range(lax.axis_size(axis...  11.9 us
    pallas_call x5, Pallas kernels, band_sum(): pl.pallas_call(functools.partial(band_kernel, tuple(places), first, last)...  10.4 us
    pallas_call x1, Pallas kernels, probes_of(): pl.pallas_call(probe_kernel, out_shape=(pltpu.VMEM((size, size), jnp.floa...  7.89 us
    ppermute x3, waiting for transfers between devices, cross(): return lax.ppermute(piece, ('gx', 'gy'), pairs)  2.53 us
    pallas_call x1, Pallas kernels, factor_of(): pl.pallas_call(factor_kernel, out_shape=(jax.ShapeDtypeStruct((count, siz...  1.92 us
    pallas_call x1, Pallas kernels, pick(): pl.pallas_call(pick_kernel, out_shape=pltpu.VMEM((points_t.shape[0], 2 *...  1.17 us
  transfers between devices with their start and end apart: 15, of which 11 were waited for; matrix products, arithmetic and copies ran while one was open for 0% of the time, Pallas kernels for 37%

profile of v19, /device:TPU:0, one launch (start us, length us, event | category | flops | bytes accessed | tf_op | source)
XLA Modules:
  0.0 52.4 jit_solution(10980453427054455393)
XLA Ops:
  0.6 4.1 %collective-permute-start = (bf16[64,1024]{1,0:T(8,128)(2,1)}, bf16[64,1024]{1,0:T(8,128)(2,1)S(1)}, u32[]{:S(2)}, u32[]{:S(2)}) collective-permute-start(bf16[64,1024]{1,0:T(8,128)(2,1)} %bitcast.4), channel_id=1, source_target_pairs={{2,0},{3,1},{0,2},{1,3},{6,4},{7,5},{4,6},{5,7},{10,8},{11,9},{8,1... | collective-permute-start | bytes 393224 | tf_op jit(solution)/shard_map/ppermute | solution.py:31
  4.7 1.2 %pick.1 = bf16[64,256]{1,0:T(8,128)(2,1)S(1)} custom-call(s32[2]{0:T(128)} %owner_ref.1, s32[2,128]{1,0:T(2,128)} %pivot_ref.1, bf16[64,1024]{1,0:T(8,128)(2,1)} %bitcast.5), custom_call_target="tpu_custom_call" | custom-call | tf_op jit(solution)/shard_map/pick/pallas_call | solution.py:107
  5.9 0.1 collective-permute-start.2
  6.0 1.2 %collective-permute-done.2 = bf16[64,256]{1,0:T(8,128)(2,1)S(1)} collective-permute-done((bf16[64,256]{1,0:T(8,128)(2,1)S(1)}, bf16[64,256]{1,0:T(8,128)(2,1)S(1)}, u32[]{:S(2)}, u32[]{:S(2)}) %collective-permute-start.2) | collective-permute-done | bytes 32800 | tf_op jit(solution)/shard_map/ppermute | solution.py:31
  7.2 2.5 %collective-permute-start.5 = (bf16[64,256]{1,0:T(8,128)(2,1)S(1)}, bf16[64,256]{1,0:T(8,128)(2,1)S(1)}, u32[]{:S(2)}, u32[]{:S(2)}) collective-permute-start(bf16[64,256]{1,0:T(8,128)(2,1)S(1)} %add.36), channel_id=1, source_target_pairs={{24,0},{28,4},{16,8},{20,12},{8,16},{12,20},{0,24},{4,28},{25,1},{... | collective-permute-start | bytes 98312 | tf_op jit(solution)/shard_map/ppermute | solution.py:31
  9.7 0.5 collective-permute-start.4
  10.2 0.5 %collective-permute-start.3 = (bf16[64,256]{1,0:T(8,128)(2,1)S(1)}, bf16[64,256]{1,0:T(8,128)(2,1)S(1)}, u32[]{:S(2)}, u32[]{:S(2)}) collective-permute-start(bf16[64,256]{1,0:T(8,128)(2,1)S(1)} %add.36), channel_id=1, source_target_pairs={{8,0},{12,4},{0,8},{4,12},{24,16},{28,20},{16,24},{20,28},{9,1},{1... | collective-permute-start | bytes 98312 | tf_op jit(solution)/shard_map/ppermute | solution.py:31
  10.8 1.3 %collective-permute-done.5 = bf16[64,256]{1,0:T(8,128)(2,1)S(1)} collective-permute-done((bf16[64,256]{1,0:T(8,128)(2,1)S(1)}, bf16[64,256]{1,0:T(8,128)(2,1)S(1)}, u32[]{:S(2)}, u32[]{:S(2)}) %collective-permute-start.5) | collective-permute-done | bytes 32800 | tf_op jit(solution)/shard_map/ppermute | solution.py:31
  12.1 1.5 %collective-permute-done.4 = bf16[64,256]{1,0:T(8,128)(2,1)S(1)} collective-permute-done((bf16[64,256]{1,0:T(8,128)(2,1)S(1)}, bf16[64,256]{1,0:T(8,128)(2,1)S(1)}, u32[]{:S(2)}, u32[]{:S(2)}) %collective-permute-start.4) | collective-permute-done | bytes 32800 | tf_op jit(solution)/shard_map/ppermute | solution.py:31
  13.6 0.5 collective-permute-done.3
  14.2 1.4 %collective-permute-start.8 = (bf16[64,256]{1,0:T(8,128)(2,1)S(1)}, bf16[64,256]{1,0:T(8,128)(2,1)S(1)}, u32[]{:S(2)}, u32[]{:S(2)}) collective-permute-start(bf16[64,256]{1,0:T(8,128)(2,1)S(1)} %fusion.1), channel_id=1, source_target_pairs={{3,0},{2,1},{1,2},{0,3},{7,4},{6,5},{5,6},{4,7},{11,8},{10,9},{9,1... | collective-permute-start | bytes 98312 | tf_op jit(solution)/shard_map/ppermute | solution.py:31
  15.6 1.7 %collective-permute-start.7 = (bf16[64,256]{1,0:T(8,128)(2,1)S(1)}, bf16[64,256]{1,0:T(8,128)(2,1)S(1)}, u32[]{:S(2)}, u32[]{:S(2)}) collective-permute-start(bf16[64,256]{1,0:T(8,128)(2,1)S(1)} %fusion.1), channel_id=1, source_target_pairs={{2,0},{3,1},{0,2},{1,3},{6,4},{7,5},{4,6},{5,7},{10,8},{11,9},{8,1... | collective-permute-start | bytes 98312 | tf_op jit(solution)/shard_map/ppermute | solution.py:31
  17.3 1.3 %collective-permute-start.6 = (bf16[64,256]{1,0:T(8,128)(2,1)S(1)}, bf16[64,256]{1,0:T(8,128)(2,1)S(1)}, u32[]{:S(2)}, u32[]{:S(2)}) collective-permute-start(bf16[64,256]{1,0:T(8,128)(2,1)S(1)} %fusion.1), channel_id=1, source_target_pairs={{1,0},{0,1},{3,2},{2,3},{5,4},{4,5},{7,6},{6,7},{9,8},{8,9},{11,10... | collective-permute-start | bytes 98312 | tf_op jit(solution)/shard_map/ppermute | solution.py:31
  18.7 0.7 %collective-permute-start.1 = (bf16[128,1024]{1,0:T(8,128)(2,1)S(1)}, bf16[128,1024]{1,0:T(8,128)(2,1)S(1)}, u32[]{:S(2)}, u32[]{:S(2)}) collective-permute-start(bf16[128,1024]{1,0:T(8,128)(2,1)S(1)} %pad_maximum_fusion), channel_id=1, source_target_pairs={{1,0},{0,1},{3,2},{2,3},{5,4},{4,5},{7,6},{6,7},{9,8},{8,9},{11,10... | collective-permute-start | bytes 786440 | tf_op jit(solution)/shard_map/ppermute | solution.py:31
  19.4 1.0 %collective-permute-done.8 = bf16[64,256]{1,0:T(8,128)(2,1)S(1)} collective-permute-done((bf16[64,256]{1,0:T(8,128)(2,1)S(1)}, bf16[64,256]{1,0:T(8,128)(2,1)S(1)}, u32[]{:S(2)}, u32[]{:S(2)}) %collective-permute-start.8) | collective-permute-done | bytes 32800 | tf_op jit(solution)/shard_map/ppermute | solution.py:31
  20.4 0.3 collective-permute-done.7
  20.8 0.9 %collective-permute-done.6 = bf16[64,256]{1,0:T(8,128)(2,1)S(1)} collective-permute-done((bf16[64,256]{1,0:T(8,128)(2,1)S(1)}, bf16[64,256]{1,0:T(8,128)(2,1)S(1)}, u32[]{:S(2)}, u32[]{:S(2)}) %collective-permute-start.6) | collective-permute-done | bytes 32800 | tf_op jit(solution)/shard_map/ppermute | solution.py:31
  21.6 7.9 %probes.1 = (f32[256,256]{1,0:T(8,128)S(1)}, f32[64,1024]{1,0:T(8,128)S(1)}, bf16[64,1024]{1,0:T(8,128)(2,1)S(1)}) custom-call(bf16[64,256]{1,0:T(8,128)(2,1)S(1)} %add_add_fusion.pivot_ref, bf16[64,1024]{1,0:T(8,128)(2,1)S(1)} %bitcast.7, f32[64,256]{1,0:T(8,128)S(1)} %bitcast.15, f32[64,1024]{1,0:T(8,128)S(1)} %bitcast.14), custom_call_target="tpu_custom_call" | custom-call | flops 17179869184 | bytes 1 | tf_op jit(solution)/shard_map/probes/pallas_call | solution.py:299
  29.6 1.4 %collective-permute-start.10 = (bf16[64,1024]{1,0:T(8,128)(2,1)S(1)}, bf16[64,1024]{1,0:T(8,128)(2,1)S(1)}, u32[]{:S(2)}, u32[]{:S(2)}) collective-permute-start(bf16[64,1024]{1,0:T(8,128)(2,1)S(1)} %get-tuple-element.25), channel_id=1, source_target_pairs={{1,0},{0,1},{3,2},{2,3},{5,4},{4,5},{7,6},{6,7},{9,8},{8,9},{11,10... | collective-permute-start | bytes 393224 | tf_op jit(solution)/shard_map/ppermute | solution.py:31
  31.0 0.7 %collective-permute-start.9 = (bf16[64,1024]{1,0:T(8,128)(2,1)S(1)}, bf16[64,1024]{1,0:T(8,128)(2,1)S(1)}, u32[]{:S(2)}, u32[]{:S(2)}) collective-permute-start(bf16[64,1024]{1,0:T(8,128)(2,1)S(1)} %get-tuple-element.25), channel_id=1, source_target_pairs={{2,0},{3,1},{0,2},{1,3},{6,4},{7,5},{4,6},{5,7},{10,8},{11,9},{8,1... | collective-permute-start | bytes 393224 | tf_op jit(solution)/shard_map/ppermute | solution.py:31
  31.7 1.5 %band_sum.5 = (f32[64,1024]{1,0:T(8,128)S(1)}, bf16[64,1024]{1,0:T(8,128)(2,1)S(1)}) custom-call(bf16[64,1024]{1,0:T(8,128)(2,1)S(1)} %bitcast.8, bf16[64,1024]{1,0:T(8,128)(2,1)S(1)} %get-tuple-element.13.refs_1_), custom_call_target="tpu_custom_call" | custom-call | flops 1 | bytes 1 | tf_op jit(solution)/shard_map/band_sum/pallas_call | solution.py:403
  33.2 2.2 %collective-permute-done.10 = bf16[64,1024]{1,0:T(8,128)(2,1)S(1)} collective-permute-done((bf16[64,1024]{1,0:T(8,128)(2,1)S(1)}, bf16[64,1024]{1,0:T(8,128)(2,1)S(1)}, u32[]{:S(2)}, u32[]{:S(2)}) %collective-permute-start.10) | collective-permute-done | bytes 131104 | tf_op jit(solution)/shard_map/ppermute | solution.py:31
  35.5 1.9 %factor.1 = (f32[1024,256]{1,0:T(8,128)}, bf16[64,1024]{1,0:T(8,128)(2,1)S(1)}) custom-call(bf16[64,256]{1,0:T(8,128)(2,1)S(1)} %add_add_fusion.pivot_ref, bf16[64,1024]{1,0:T(8,128)(2,1)S(1)} %bitcast.9, f32[256,256]{1,0:T(8,128)S(1)} %get-tuple-element.14.inverse_ref, bf16[64,1024]{1,0:T(8,128)(2,1)S(1)} %add.45.awaited_ref.refs_2_), custom_call_target="tpu_custom_call" | custom-call | flops 50331648 | bytes 196608 | tf_op jit(solution)/shard_map/factor/pallas_call | solution.py:340
  37.4 0.9 %collective-permute-done.9 = bf16[64,1024]{1,0:T(8,128)(2,1)S(1)} collective-permute-done((bf16[64,1024]{1,0:T(8,128)(2,1)S(1)}, bf16[64,1024]{1,0:T(8,128)(2,1)S(1)}, u32[]{:S(2)}, u32[]{:S(2)}) %collective-permute-start.9) | collective-permute-done | bytes 131104 | tf_op jit(solution)/shard_map/ppermute | solution.py:31
  38.3 0.1 collective-permute-start.11
  38.4 0.2 collective-permute-start.13
  38.7 2.6 %band_sum.6 = (f32[64,1024]{1,0:T(8,128)S(1)}, bf16[64,1024]{1,0:T(8,128)(2,1)S(1)}) custom-call(bf16[64,1024]{1,0:T(8,128)(2,1)S(1)} %bitcast.10, bf16[128,1024]{1,0:T(8,128)(2,1)S(1)} %collective-permute-done.1.refs_1_, bf16[64,1024]{1,0:T(8,128)(2,1)S(1)} %add.45.awaited_ref.refs_2_, bf16[64,1024]{1,0:T(8,128)(2,1)S(1)} %collective-permute-done.refs_3_, ...), custom_call_target="tpu_custom_call" | custom-call | flops 1073741824 | bytes 1572864 | tf_op jit(solution)/shard_map/band_sum/pallas_call | solution.py:403
  41.3 2.0 %collective-permute-done.11.refs_2_ = bf16[64,1024]{1,0:T(8,128)(2,1)S(1)} collective-permute-done((bf16[64,1024]{1,0:T(8,128)(2,1)S(1)}, bf16[64,1024]{1,0:T(8,128)(2,1)S(1)}, u32[]{:S(2)}, u32[]{:S(2)}) %collective-permute-start.11) | collective-permute-done | bytes 131104 | tf_op jit(solution)/shard_map/ppermute | solution.py:31
  43.5 2.6 %band_sum.7 = (f32[64,1024]{1,0:T(8,128)S(1)}, bf16[64,1024]{1,0:T(8,128)(2,1)}) custom-call(bf16[64,1024]{1,0:T(8,128)(2,1)S(1)} %bitcast.11, bf16[128,1024]{1,0:T(8,128)(2,1)S(1)} %collective-permute-done.1.refs_1_, bf16[64,1024]{1,0:T(8,128)(2,1)S(1)} %collective-permute-done.11.refs_2_, bf16[128,1024]{1,0:T(8,128)(2,1)S(1)} %collective-permute-done.14.refs_3_, ...), custom_call_target="tpu_custom_call" | custom-call | flops 1073741824 | bytes 1310720 | tf_op jit(solution)/shard_map/band_sum/pallas_call | solution.py:403
  46.1 1.5 %band_sum.8 = (f32[64,1024]{1,0:T(8,128)S(1)}, bf16[64,1024]{1,0:T(8,128)(2,1)}) custom-call(bf16[64,1024]{1,0:T(8,128)(2,1)S(1)} %bitcast.12, bf16[128,1024]{1,0:T(8,128)(2,1)S(1)} %collective-permute-done.13.refs_1_, f32[64,1024]{1,0:T(8,128)S(1)} %get-tuple-element.20.refs_2_), custom_call_target="tpu_custom_call" | custom-call | flops 536870912 | bytes 786432 | tf_op jit(solution)/shard_map/band_sum/pallas_call | solution.py:403
  47.6 2.5 %collective-permute-done.12.refs_1_ = bf16[128,1024]{1,0:T(8,128)(2,1)S(1)} collective-permute-done((bf16[128,1024]{1,0:T(8,128)(2,1)S(1)}, bf16[128,1024]{1,0:T(8,128)(2,1)S(1)}, u32[]{:S(2)}, u32[]{:S(2)}) %collective-permute-start.12) | collective-permute-done | bytes 262176 | tf_op jit(solution)/shard_map/ppermute | solution.py:55
  50.2 2.2 %band_sum.9 = f32[64,1024]{1,0:T(8,128)} custom-call(bf16[64,1024]{1,0:T(8,128)(2,1)S(1)} %bitcast.13, bf16[128,1024]{1,0:T(8,128)(2,1)S(1)} %collective-permute-done.12.refs_1_, f32[64,1024]{1,0:T(8,128)S(1)} %get-tuple-element.21.refs_2_, f32[64,1024]{1,0:T(8,128)S(1)} %get-tuple-element.22.refs_3_), custom_call_target="tpu_custom_call" | custom-call | flops 536870912 | bytes 1048576 | tf_op jit(solution)/shard_map/band_sum/pallas_call | solution.py:403
  (23 shorter events, 0.4 us)
Async XLA Ops:
  0.6 13.5 %collective-permute-start = (bf16[64,1024]{1,0:T(8,128)(2,1)}, bf16[64,1024]{1,0:T(8,128)(2,1)S(1)}, u32[]{:S(2)}, u32[]{:S(2)}) collective-permute-start(bf16[64,1024]{1,0:T(8,128)(2,1)} %bitcast.4), channel_id=1, source_target_pairs={{2,0},{3,1},{0,2},{1,3},{6,4},{7,5},{4,6},{5,7},{10,8},{11,9},{8,1... | collective-permute-start | bytes 393224 | tf_op jit(solution)/shard_map/ppermute | solution.py:31
  5.9 12.7 %copy-start = (bf16[1024,64]{0,1:T(8,128)(2,1)S(1)}, bf16[1024,64]{0,1:T(8,128)(2,1)}, u32[]{:S(2)}) copy-start(bf16[1024,64]{0,1:T(8,128)(2,1)} %param.5) | copy-start | bytes 393220
  5.9 1.3 %collective-permute-start.2 = (bf16[64,256]{1,0:T(8,128)(2,1)S(1)}, bf16[64,256]{1,0:T(8,128)(2,1)S(1)}, u32[]{:S(2)}, u32[]{:S(2)}) collective-permute-start(bf16[64,256]{1,0:T(8,128)(2,1)S(1)} %pick.1), channel_id=1, source_target_pairs={{4,0},{0,4},{12,8},{8,12},{20,16},{16,20},{28,24},{24,28},{5,1},{1... | collective-permute-start | bytes 98312 | tf_op jit(solution)/shard_map/ppermute | solution.py:31
  7.2 4.9 %collective-permute-start.5 = (bf16[64,256]{1,0:T(8,128)(2,1)S(1)}, bf16[64,256]{1,0:T(8,128)(2,1)S(1)}, u32[]{:S(2)}, u32[]{:S(2)}) collective-permute-start(bf16[64,256]{1,0:T(8,128)(2,1)S(1)} %add.36), channel_id=1, source_target_pairs={{24,0},{28,4},{16,8},{20,12},{8,16},{12,20},{0,24},{4,28},{25,1},{... | collective-permute-start | bytes 98312 | tf_op jit(solution)/shard_map/ppermute | solution.py:31
  9.7 3.9 %collective-permute-start.4 = (bf16[64,256]{1,0:T(8,128)(2,1)S(1)}, bf16[64,256]{1,0:T(8,128)(2,1)S(1)}, u32[]{:S(2)}, u32[]{:S(2)}) collective-permute-start(bf16[64,256]{1,0:T(8,128)(2,1)S(1)} %add.36), channel_id=1, source_target_pairs={{16,0},{20,4},{24,8},{28,12},{0,16},{4,20},{8,24},{12,28},{17,1},{... | collective-permute-start | bytes 98312 | tf_op jit(solution)/shard_map/ppermute | solution.py:31
  10.2 3.9 %collective-permute-start.3 = (bf16[64,256]{1,0:T(8,128)(2,1)S(1)}, bf16[64,256]{1,0:T(8,128)(2,1)S(1)}, u32[]{:S(2)}, u32[]{:S(2)}) collective-permute-start(bf16[64,256]{1,0:T(8,128)(2,1)S(1)} %add.36), channel_id=1, source_target_pairs={{8,0},{12,4},{0,8},{4,12},{24,16},{28,20},{16,24},{20,28},{9,1},{1... | collective-permute-start | bytes 98312 | tf_op jit(solution)/shard_map/ppermute | solution.py:31
  14.2 7.5 %copy-start.1 = (f32[1024,64]{0,1:T(8,128)S(1)}, f32[1024,64]{0,1:T(8,128)}, u32[]{:S(2)}) copy-start(f32[1024,64]{0,1:T(8,128)} %param.9) | copy-start | bytes 786436
  14.2 6.2 %collective-permute-start.8 = (bf16[64,256]{1,0:T(8,128)(2,1)S(1)}, bf16[64,256]{1,0:T(8,128)(2,1)S(1)}, u32[]{:S(2)}, u32[]{:S(2)}) collective-permute-start(bf16[64,256]{1,0:T(8,128)(2,1)S(1)} %fusion.1), channel_id=1, source_target_pairs={{3,0},{2,1},{1,2},{0,3},{7,4},{6,5},{5,6},{4,7},{11,8},{10,9},{9,1... | collective-permute-start | bytes 98312 | tf_op jit(solution)/shard_map/ppermute | solution.py:31
  15.6 5.2 %collective-permute-start.7 = (bf16[64,256]{1,0:T(8,128)(2,1)S(1)}, bf16[64,256]{1,0:T(8,128)(2,1)S(1)}, u32[]{:S(2)}, u32[]{:S(2)}) collective-permute-start(bf16[64,256]{1,0:T(8,128)(2,1)S(1)} %fusion.1), channel_id=1, source_target_pairs={{2,0},{3,1},{0,2},{1,3},{6,4},{7,5},{4,6},{5,7},{10,8},{11,9},{8,1... | collective-permute-start | bytes 98312 | tf_op jit(solution)/shard_map/ppermute | solution.py:31
  17.3 4.3 %collective-permute-start.6 = (bf16[64,256]{1,0:T(8,128)(2,1)S(1)}, bf16[64,256]{1,0:T(8,128)(2,1)S(1)}, u32[]{:S(2)}, u32[]{:S(2)}) collective-permute-start(bf16[64,256]{1,0:T(8,128)(2,1)S(1)} %fusion.1), channel_id=1, source_target_pairs={{1,0},{0,1},{3,2},{2,3},{5,4},{4,5},{7,6},{6,7},{9,8},{8,9},{11,10... | collective-permute-start | bytes 98312 | tf_op jit(solution)/shard_map/ppermute | solution.py:31
  18.7 3.0 %copy-start.2 = (f32[256,64]{0,1:T(8,128)S(1)}, f32[256,64]{0,1:T(8,128)}, u32[]{:S(2)}) copy-start(f32[256,64]{0,1:T(8,128)} %param.8) | copy-start | bytes 196612
  18.7 10.9 %collective-permute-start.1 = (bf16[128,1024]{1,0:T(8,128)(2,1)S(1)}, bf16[128,1024]{1,0:T(8,128)(2,1)S(1)}, u32[]{:S(2)}, u32[]{:S(2)}) collective-permute-start(bf16[128,1024]{1,0:T(8,128)(2,1)S(1)} %pad_maximum_fusion), channel_id=1, source_target_pairs={{1,0},{0,1},{3,2},{2,3},{5,4},{4,5},{7,6},{6,7},{9,8},{8,9},{11,10... | collective-permute-start | bytes 786440 | tf_op jit(solution)/shard_map/ppermute | solution.py:31
  29.6 5.7 %collective-permute-start.10 = (bf16[64,1024]{1,0:T(8,128)(2,1)S(1)}, bf16[64,1024]{1,0:T(8,128)(2,1)S(1)}, u32[]{:S(2)}, u32[]{:S(2)}) collective-permute-start(bf16[64,1024]{1,0:T(8,128)(2,1)S(1)} %get-tuple-element.25), channel_id=1, source_target_pairs={{1,0},{0,1},{3,2},{2,3},{5,4},{4,5},{7,6},{6,7},{9,8},{8,9},{11,10... | collective-permute-start | bytes 393224 | tf_op jit(solution)/shard_map/ppermute | solution.py:31
  31.0 7.3 %collective-permute-start.9 = (bf16[64,1024]{1,0:T(8,128)(2,1)S(1)}, bf16[64,1024]{1,0:T(8,128)(2,1)S(1)}, u32[]{:S(2)}, u32[]{:S(2)}) collective-permute-start(bf16[64,1024]{1,0:T(8,128)(2,1)S(1)} %get-tuple-element.25), channel_id=1, source_target_pairs={{2,0},{3,1},{0,2},{1,3},{6,4},{7,5},{4,6},{5,7},{10,8},{11,9},{8,1... | collective-permute-start | bytes 393224 | tf_op jit(solution)/shard_map/ppermute | solution.py:31
  35.4 8.1 %collective-permute-start.14 = (bf16[128,1024]{1,0:T(8,128)(2,1)S(1)}, bf16[128,1024]{1,0:T(8,128)(2,1)S(1)}, u32[]{:S(2)}, u32[]{:S(2)}) collective-permute-start(bf16[128,1024]{1,0:T(8,128)(2,1)S(1)} %pad_maximum_fusion.3), channel_id=1, source_target_pairs={{28,0},{5,1},{30,2},{7,3},{0,4},{9,5},{2,6},{11,7},{4,8},{13,9},{6... | collective-permute-start | bytes 786440 | tf_op jit(solution)/shard_map/ppermute | solution.py:55
  38.3 5.0 %collective-permute-start.11 = (bf16[64,1024]{1,0:T(8,128)(2,1)S(1)}, bf16[64,1024]{1,0:T(8,128)(2,1)S(1)}, u32[]{:S(2)}, u32[]{:S(2)}) collective-permute-start(bf16[64,1024]{1,0:T(8,128)(2,1)S(1)} %add.46.refs_4_), channel_id=1, source_target_pairs={{1,0},{0,1},{3,2},{2,3},{5,4},{4,5},{7,6},{6,7},{9,8},{8,9},{11,10... | collective-permute-start | bytes 393224 | tf_op jit(solution)/shard_map/ppermute | solution.py:31
  38.4 7.7 %collective-permute-start.13 = (bf16[128,1024]{1,0:T(8,128)(2,1)S(1)}, bf16[128,1024]{1,0:T(8,128)(2,1)S(1)}, u32[]{:S(2)}, u32[]{:S(2)}) collective-permute-start(bf16[128,1024]{1,0:T(8,128)(2,1)S(1)} %pad_maximum_fusion.2), channel_id=1, source_target_pairs={{28,0},{29,1},{6,2},{7,3},{0,4},{1,5},{10,6},{11,7},{4,8},{5,9},{1... | collective-permute-start | bytes 786440 | tf_op jit(solution)/shard_map/ppermute | solution.py:55
  43.4 6.7 %collective-permute-start.12 = (bf16[128,1024]{1,0:T(8,128)(2,1)S(1)}, bf16[128,1024]{1,0:T(8,128)(2,1)S(1)}, u32[]{:S(2)}, u32[]{:S(2)}) collective-permute-start(bf16[128,1024]{1,0:T(8,128)(2,1)S(1)} %pad_maximum_fusion.1), channel_id=1, source_target_pairs={{28,0},{29,1},{6,2},{7,3},{0,4},{1,5},{10,6},{11,7},{4,8},{5,9},{1... | collective-permute-start | bytes 786440 | tf_op jit(solution)/shard_map/ppermute | solution.py:55

commit v20 on v18

--- a/solution.py
+++ b/solution.py
@@ -289,7 +289,7 @@
 
     inverse_ref[:half, :half] = one
     inverse_ref[:half, half:] = jnp.zeros((half, half), jnp.float32)
-    inverse_ref[half:, :half] = -product(two, back, ((1,), (0,)), hp)
+    inverse_ref[half:, :half] = back
     inverse_ref[half:, half:] = two
 
 
@@ -324,7 +324,11 @@
     count = point_ref.shape[1]
     own = jnp.transpose(padded(extended(point_ref[...], True))).astype(jnp.bfloat16)
     pivots = padded(extended(pivot_ref[...], False)).astype(jnp.bfloat16)
-    high, middle, _ = thirds(inverse_ref[...])
+    half = inverse_ref.shape[0] // 2
+    later = inverse_ref[half:, half:]
+    corner = -product(later, inverse_ref[half:, :half], ((1,), (0,)), lax.Precision.HIGHEST)
+    inverse = jnp.concatenate([inverse_ref[:half, :], jnp.concatenate([corner, later], axis=1)], axis=0)
+    high, middle, _ = thirds(inverse)
     for s in range(0, count, CHUNK):
         rows = own[s:s + CHUNK, :]
         cols_high, cols_middle, _ = thirds(kernel_of(product(rows, pivots, ((1,), (0,)))))
@@ -439,11 +443,11 @@
         cross_one = cross(jnp.concatenate([pair[:depth], one], axis=0), 1)
         three = swapped(two, "gy", 1)
         cross_two = cross(jnp.concatenate([far, pair[depth:], two], axis=0), 2)
-        total, _ = band_sum(points, [((pair, 0), (one, 0)), ((far, 0), (two, 0))], total)
-        total, zeros = band_sum(points, [((cross_one, 0), (cross_one, depth))], total)
+        pieces = [((pair, 0), (one, 0)), ((far, 0), (two, 0)), ((cross_one, 0), (cross_one, depth))]
+        total, zeros = band_sum(points, pieces, total)
         three = three + zeros
         cross_three = cross(three, 3)
-        total, _ = band_sum(points, [((cross_two, 0), (cross_two, 2 * depth)), ((pair, depth), (three, 0))], total)
+        total, _ = band_sum(points, [((pair, depth), (three, 0)), ((cross_two, 0), (cross_two, 2 * depth))], total)
         kernel_probes = band_sum(points, [((cross_two, depth), (cross_three, 0))], total, probes)
     else:
         factor, _ = factor_of(pivot_points, points, inverse, zeros)

time: 59.6 us -> 53.4 us (0.90)
  starting transfers between devices: 18.7 us -> 15.6 us
  waiting for transfers between devices: 18.8 us -> 15.9 us
    ppermute x3, waiting for transfers between devices: 8.53 us -> 5.99 us  [cross(): return lax.ppermute(piece, ('gx', 'gy'), pairs)]
    ppermute x12, starting transfers between devices: 17.5 us -> 15.3 us  [swapped(): lax.ppermute(value, axis, [(i ^ bit, i) for i in range(lax.axis_size(axis...]
    ppermute x3, starting transfers between devices: 1.14 us -> 0.35 us  [cross(): return lax.ppermute(piece, ('gx', 'gy'), pairs)]
    pallas_call x5 -> x4, Pallas kernels: 9.85 us -> 9.64 us  [band_sum(): pl.pallas_call(functools.partial(band_kernel, tuple(places), first, last)...]
  transfers between devices with their start and end apart: 15 -> 15, of which waited for: 9 -> 12; matrix products, arithmetic and copies ran while one was open for 0% -> 0% of each run, Pallas kernels for 32% -> 35%
where the time goes in v20:
time: 53.4 us; the launch traced here: 53.2 us
  Pallas kernels  20.7 us (39%)
  waiting for transfers between devices  15.9 us (30%)
  starting transfers between devices  15.6 us (29%)
  between operations  0.82 us (2%)
    ppermute x12, starting transfers between devices, swapped(): lax.ppermute(value, axis, [(i ^ bit, i) for i in range(lax.axis_size(axis...  15.3 us
    ppermute x12, waiting for transfers between devices, swapped(): lax.ppermute(value, axis, [(i ^ bit, i) for i in range(lax.axis_size(axis...  9.88 us
    pallas_call x4, Pallas kernels, band_sum(): pl.pallas_call(functools.partial(band_kernel, tuple(places), first, last)...  9.64 us
    pallas_call x1, Pallas kernels, probes_of(): pl.pallas_call(probe_kernel, out_shape=(pltpu.VMEM((size, size), jnp.floa...  7.89 us
    ppermute x3, waiting for transfers between devices, cross(): return lax.ppermute(piece, ('gx', 'gy'), pairs)  5.99 us
    pallas_call x1, Pallas kernels, factor_of(): pl.pallas_call(factor_kernel, out_shape=(jax.ShapeDtypeStruct((count, siz...  1.97 us
    pallas_call x1, Pallas kernels, pick(): pl.pallas_call(pick_kernel, out_shape=pltpu.VMEM((points_t.shape[0], 2 *...  1.17 us
  transfers between devices with their start and end apart: 15, of which 12 were waited for; matrix products, arithmetic and copies ran while one was open for 0% of the time, Pallas kernels for 35%

profile of v20, /device:TPU:0, one launch (start us, length us, event | category | flops | bytes accessed | tf_op | source)
XLA Modules:
  0.0 53.2 jit_solution(51872518826971938)
XLA Ops:
  0.6 4.1 %collective-permute-start = (bf16[64,1024]{1,0:T(8,128)(2,1)}, bf16[64,1024]{1,0:T(8,128)(2,1)S(1)}, u32[]{:S(2)}, u32[]{:S(2)}) collective-permute-start(bf16[64,1024]{1,0:T(8,128)(2,1)} %bitcast.4), channel_id=1, source_target_pairs={{2,0},{3,1},{0,2},{1,3},{6,4},{7,5},{4,6},{5,7},{10,8},{11,9},{8,1... | collective-permute-start | bytes 393224 | tf_op jit(solution)/shard_map/ppermute | solution.py:31
  4.7 1.2 %pick.1 = bf16[64,256]{1,0:T(8,128)(2,1)S(1)} custom-call(s32[2]{0:T(128)} %owner_ref.1, s32[2,128]{1,0:T(2,128)} %pivot_ref.1, bf16[64,1024]{1,0:T(8,128)(2,1)} %bitcast.5), custom_call_target="tpu_custom_call" | custom-call | tf_op jit(solution)/shard_map/pick/pallas_call | solution.py:107
  5.9 0.1 collective-permute-start.2
  6.0 1.2 %collective-permute-done.2 = bf16[64,256]{1,0:T(8,128)(2,1)S(1)} collective-permute-done((bf16[64,256]{1,0:T(8,128)(2,1)S(1)}, bf16[64,256]{1,0:T(8,128)(2,1)S(1)}, u32[]{:S(2)}, u32[]{:S(2)}) %collective-permute-start.2) | collective-permute-done | bytes 32800 | tf_op jit(solution)/shard_map/ppermute | solution.py:31
  7.2 2.5 %collective-permute-start.5 = (bf16[64,256]{1,0:T(8,128)(2,1)S(1)}, bf16[64,256]{1,0:T(8,128)(2,1)S(1)}, u32[]{:S(2)}, u32[]{:S(2)}) collective-permute-start(bf16[64,256]{1,0:T(8,128)(2,1)S(1)} %add.36), channel_id=1, source_target_pairs={{24,0},{28,4},{16,8},{20,12},{8,16},{12,20},{0,24},{4,28},{25,1},{... | collective-permute-start | bytes 98312 | tf_op jit(solution)/shard_map/ppermute | solution.py:31
  9.7 0.5 collective-permute-start.4
  10.2 0.5 %collective-permute-start.3 = (bf16[64,256]{1,0:T(8,128)(2,1)S(1)}, bf16[64,256]{1,0:T(8,128)(2,1)S(1)}, u32[]{:S(2)}, u32[]{:S(2)}) collective-permute-start(bf16[64,256]{1,0:T(8,128)(2,1)S(1)} %add.36), channel_id=1, source_target_pairs={{8,0},{12,4},{0,8},{4,12},{24,16},{28,20},{16,24},{20,28},{9,1},{1... | collective-permute-start | bytes 98312 | tf_op jit(solution)/shard_map/ppermute | solution.py:31
  10.8 1.3 %collective-permute-done.5 = bf16[64,256]{1,0:T(8,128)(2,1)S(1)} collective-permute-done((bf16[64,256]{1,0:T(8,128)(2,1)S(1)}, bf16[64,256]{1,0:T(8,128)(2,1)S(1)}, u32[]{:S(2)}, u32[]{:S(2)}) %collective-permute-start.5) | collective-permute-done | bytes 32800 | tf_op jit(solution)/shard_map/ppermute | solution.py:31
  12.1 1.5 %collective-permute-done.4 = bf16[64,256]{1,0:T(8,128)(2,1)S(1)} collective-permute-done((bf16[64,256]{1,0:T(8,128)(2,1)S(1)}, bf16[64,256]{1,0:T(8,128)(2,1)S(1)}, u32[]{:S(2)}, u32[]{:S(2)}) %collective-permute-start.4) | collective-permute-done | bytes 32800 | tf_op jit(solution)/shard_map/ppermute | solution.py:31
  13.6 0.5 collective-permute-done.3
  14.2 1.4 %collective-permute-start.8 = (bf16[64,256]{1,0:T(8,128)(2,1)S(1)}, bf16[64,256]{1,0:T(8,128)(2,1)S(1)}, u32[]{:S(2)}, u32[]{:S(2)}) collective-permute-start(bf16[64,256]{1,0:T(8,128)(2,1)S(1)} %fusion.1), channel_id=1, source_target_pairs={{3,0},{2,1},{1,2},{0,3},{7,4},{6,5},{5,6},{4,7},{11,8},{10,9},{9,1... | collective-permute-start | bytes 98312 | tf_op jit(solution)/shard_map/ppermute | solution.py:31
  15.6 1.7 %collective-permute-start.7 = (bf16[64,256]{1,0:T(8,128)(2,1)S(1)}, bf16[64,256]{1,0:T(8,128)(2,1)S(1)}, u32[]{:S(2)}, u32[]{:S(2)}) collective-permute-start(bf16[64,256]{1,0:T(8,128)(2,1)S(1)} %fusion.1), channel_id=1, source_target_pairs={{2,0},{3,1},{0,2},{1,3},{6,4},{7,5},{4,6},{5,7},{10,8},{11,9},{8,1... | collective-permute-start | bytes 98312 | tf_op jit(solution)/shard_map/ppermute | solution.py:31
  17.3 1.3 %collective-permute-start.6 = (bf16[64,256]{1,0:T(8,128)(2,1)S(1)}, bf16[64,256]{1,0:T(8,128)(2,1)S(1)}, u32[]{:S(2)}, u32[]{:S(2)}) collective-permute-start(bf16[64,256]{1,0:T(8,128)(2,1)S(1)} %fusion.1), channel_id=1, source_target_pairs={{1,0},{0,1},{3,2},{2,3},{5,4},{4,5},{7,6},{6,7},{9,8},{8,9},{11,10... | collective-permute-start | bytes 98312 | tf_op jit(solution)/shard_map/ppermute | solution.py:31
  18.7 0.7 %collective-permute-start.1 = (bf16[128,1024]{1,0:T(8,128)(2,1)S(1)}, bf16[128,1024]{1,0:T(8,128)(2,1)S(1)}, u32[]{:S(2)}, u32[]{:S(2)}) collective-permute-start(bf16[128,1024]{1,0:T(8,128)(2,1)S(1)} %pad_maximum_fusion.1), channel_id=1, source_target_pairs={{1,0},{0,1},{3,2},{2,3},{5,4},{4,5},{7,6},{6,7},{9,8},{8,9},{11,10... | collective-permute-start | bytes 786440 | tf_op jit(solution)/shard_map/ppermute | solution.py:31
  19.4 1.0 %collective-permute-done.8 = bf16[64,256]{1,0:T(8,128)(2,1)S(1)} collective-permute-done((bf16[64,256]{1,0:T(8,128)(2,1)S(1)}, bf16[64,256]{1,0:T(8,128)(2,1)S(1)}, u32[]{:S(2)}, u32[]{:S(2)}) %collective-permute-start.8) | collective-permute-done | bytes 32800 | tf_op jit(solution)/shard_map/ppermute | solution.py:31
  20.4 0.3 collective-permute-done.7
  20.8 0.9 %collective-permute-done.6 = bf16[64,256]{1,0:T(8,128)(2,1)S(1)} collective-permute-done((bf16[64,256]{1,0:T(8,128)(2,1)S(1)}, bf16[64,256]{1,0:T(8,128)(2,1)S(1)}, u32[]{:S(2)}, u32[]{:S(2)}) %collective-permute-start.6) | collective-permute-done | bytes 32800 | tf_op jit(solution)/shard_map/ppermute | solution.py:31
  21.6 7.9 %probes.1 = (f32[256,256]{1,0:T(8,128)S(1)}, f32[64,1024]{1,0:T(8,128)S(1)}, bf16[64,1024]{1,0:T(8,128)(2,1)S(1)}) custom-call(bf16[64,256]{1,0:T(8,128)(2,1)S(1)} %add_add_fusion.pivot_ref, bf16[64,1024]{1,0:T(8,128)(2,1)S(1)} %bitcast.7, f32[64,256]{1,0:T(8,128)S(1)} %bitcast.14, f32[64,1024]{1,0:T(8,128)S(1)} %bitcast.13), custom_call_target="tpu_custom_call" | custom-call | flops 17179869184 | bytes 1 | tf_op jit(solution)/shard_map/probes/pallas_call | solution.py:299
  29.6 1.4 %collective-permute-start.10 = (bf16[64,1024]{1,0:T(8,128)(2,1)S(1)}, bf16[64,1024]{1,0:T(8,128)(2,1)S(1)}, u32[]{:S(2)}, u32[]{:S(2)}) collective-permute-start(bf16[64,1024]{1,0:T(8,128)(2,1)S(1)} %get-tuple-element.23), channel_id=1, source_target_pairs={{1,0},{0,1},{3,2},{2,3},{5,4},{4,5},{7,6},{6,7},{9,8},{8,9},{11,10... | collective-permute-start | bytes 393224 | tf_op jit(solution)/shard_map/ppermute | solution.py:31
  31.0 0.6 %collective-permute-start.9 = (bf16[64,1024]{1,0:T(8,128)(2,1)S(1)}, bf16[64,1024]{1,0:T(8,128)(2,1)S(1)}, u32[]{:S(2)}, u32[]{:S(2)}) collective-permute-start(bf16[64,1024]{1,0:T(8,128)(2,1)S(1)} %get-tuple-element.23), channel_id=1, source_target_pairs={{2,0},{3,1},{0,2},{1,3},{6,4},{7,5},{4,6},{5,7},{10,8},{11,9},{8,1... | collective-permute-start | bytes 393224 | tf_op jit(solution)/shard_map/ppermute | solution.py:31
  31.7 1.4 %band_sum.4 = (f32[1024,64]{1,0:T(8,128)S(1)}, bf16[64,1024]{1,0:T(8,128)(2,1)S(1)}) custom-call(bf16[64,1024]{1,0:T(8,128)(2,1)S(1)} %bitcast.8, bf16[64,1024]{1,0:T(8,128)(2,1)S(1)} %get-tuple-element.12.refs_1_), custom_call_target="tpu_custom_call" | custom-call | flops 1 | bytes 1 | tf_op jit(solution)/shard_map/band_sum/pallas_call | solution.py:407
  33.1 2.2 %collective-permute-done.10 = bf16[64,1024]{1,0:T(8,128)(2,1)S(1)} collective-permute-done((bf16[64,1024]{1,0:T(8,128)(2,1)S(1)}, bf16[64,1024]{1,0:T(8,128)(2,1)S(1)}, u32[]{:S(2)}, u32[]{:S(2)}) %collective-permute-start.10) | collective-permute-done | bytes 131104 | tf_op jit(solution)/shard_map/ppermute | solution.py:31
  35.5 2.0 %factor.1 = (f32[1024,256]{1,0:T(8,128)}, bf16[64,1024]{1,0:T(8,128)(2,1)S(1)}) custom-call(bf16[64,256]{1,0:T(8,128)(2,1)S(1)} %add_add_fusion.pivot_ref, bf16[64,1024]{1,0:T(8,128)(2,1)S(1)} %bitcast.9, f32[256,256]{1,0:T(8,128)S(1)} %get-tuple-element.13.inverse_ref, bf16[64,1024]{1,0:T(8,128)(2,1)S(1)} %add.45.awaited_ref.refs_2_), custom_call_target="tpu_custom_call" | custom-call | flops 50331648 | bytes 196608 | tf_op jit(solution)/shard_map/factor/pallas_call | solution.py:344
  37.4 0.9 %collective-permute-done.9 = bf16[64,1024]{1,0:T(8,128)(2,1)S(1)} collective-permute-done((bf16[64,1024]{1,0:T(8,128)(2,1)S(1)}, bf16[64,1024]{1,0:T(8,128)(2,1)S(1)}, u32[]{:S(2)}, u32[]{:S(2)}) %collective-permute-start.9) | collective-permute-done | bytes 131104 | tf_op jit(solution)/shard_map/ppermute | solution.py:31
  38.4 0.2 collective-permute-start.11
  38.6 0.3 collective-permute-start.12
  38.9 3.2 %collective-permute-done.13.refs_5_ = bf16[128,1024]{1,0:T(8,128)(2,1)S(1)} collective-permute-done((bf16[128,1024]{1,0:T(8,128)(2,1)S(1)}, bf16[128,1024]{1,0:T(8,128)(2,1)S(1)}, u32[]{:S(2)}, u32[]{:S(2)}) %collective-permute-start.13) | collective-permute-done | bytes 262176 | tf_op jit(solution)/shard_map/ppermute | solution.py:55
  42.1 3.6 %band_sum.5 = (f32[1024,64]{1,0:T(8,128)S(1)}, bf16[64,1024]{1,0:T(8,128)(2,1)S(1)}) custom-call(bf16[64,1024]{1,0:T(8,128)(2,1)S(1)} %bitcast.10, bf16[128,1024]{1,0:T(8,128)(2,1)S(1)} %collective-permute-done.1.refs_1_, bf16[64,1024]{1,0:T(8,128)(2,1)S(1)} %add.45.awaited_ref.refs_2_, bf16[64,1024]{1,0:T(8,128)(2,1)S(1)} %collective-permute-done.refs_3_, ...), custom_call_target="tpu_custom_call" | custom-call | flops 1610612736 | bytes 1835008 | tf_op jit(solution)/shard_map/band_sum/pallas_call | solution.py:407
  45.9 0.8 %collective-permute-done.11.refs_3_.refs_1_ = bf16[192,1024]{1,0:T(8,128)(2,1)S(1)} collective-permute-done((bf16[192,1024]{1,0:T(8,128)(2,1)S(1)}, bf16[192,1024]{1,0:T(8,128)(2,1)S(1)}, u32[]{:S(2)}, u32[]{:S(2)}) %collective-permute-start.11) | collective-permute-done | bytes 393248 | tf_op jit(solution)/shard_map/ppermute | solution.py:55
  46.7 2.5 %band_sum.6 = (f32[1024,64]{1,0:T(8,128)S(1)}, bf16[64,1024]{1,0:T(8,128)(2,1)}) custom-call(bf16[64,1024]{1,0:T(8,128)(2,1)S(1)} %bitcast.11, bf16[128,1024]{1,0:T(8,128)(2,1)S(1)} %collective-permute-done.1.refs_1_, bf16[64,1024]{1,0:T(8,128)(2,1)S(1)} %add.47.refs_2_, bf16[192,1024]{1,0:T(8,128)(2,1)S(1)} %collective-permute-done.11.refs_3_.refs_1_, ...), custom_call_target="tpu_custom_call" | custom-call | flops 1073741824 | bytes 1310720 | tf_op jit(solution)/shard_map/band_sum/pallas_call | solution.py:407
  49.2 1.9 %collective-permute-done.14.refs_2_ = bf16[64,1024]{1,0:T(8,128)(2,1)S(1)} collective-permute-done((bf16[64,1024]{1,0:T(8,128)(2,1)S(1)}, bf16[64,1024]{1,0:T(8,128)(2,1)S(1)}, u32[]{:S(2)}, u32[]{:S(2)}) %collective-permute-start.14) | collective-permute-done | bytes 131104 | tf_op jit(solution)/shard_map/ppermute | solution.py:55
  51.2 2.1 %band_sum.7 = f32[64,1024]{1,0:T(8,128)} custom-call(bf16[64,1024]{1,0:T(8,128)(2,1)S(1)} %bitcast.12, bf16[192,1024]{1,0:T(8,128)(2,1)S(1)} %collective-permute-done.11.refs_3_.refs_1_, bf16[64,1024]{1,0:T(8,128)(2,1)S(1)} %collective-permute-done.14.refs_2_, f32[1024,64]{1,0:T(8,128)S(1)} %get-tuple-element.19.refs_3_, ...), custom_call_target="tpu_custom_call" | custom-call | flops 536870912 | bytes 1310720 | tf_op jit(solution)/shard_map/band_sum/pallas_call | solution.py:407
  (21 shorter events, 0.4 us)
Async XLA Ops:
  0.6 13.5 %collective-permute-start = (bf16[64,1024]{1,0:T(8,128)(2,1)}, bf16[64,1024]{1,0:T(8,128)(2,1)S(1)}, u32[]{:S(2)}, u32[]{:S(2)}) collective-permute-start(bf16[64,1024]{1,0:T(8,128)(2,1)} %bitcast.4), channel_id=1, source_target_pairs={{2,0},{3,1},{0,2},{1,3},{6,4},{7,5},{4,6},{5,7},{10,8},{11,9},{8,1... | collective-permute-start | bytes 393224 | tf_op jit(solution)/shard_map/ppermute | solution.py:31
  5.9 12.7 %copy-start = (bf16[1024,64]{0,1:T(8,128)(2,1)S(1)}, bf16[1024,64]{0,1:T(8,128)(2,1)}, u32[]{:S(2)}) copy-start(bf16[1024,64]{0,1:T(8,128)(2,1)} %param.5) | copy-start | bytes 393220
  5.9 1.3 %collective-permute-start.2 = (bf16[64,256]{1,0:T(8,128)(2,1)S(1)}, bf16[64,256]{1,0:T(8,128)(2,1)S(1)}, u32[]{:S(2)}, u32[]{:S(2)}) collective-permute-start(bf16[64,256]{1,0:T(8,128)(2,1)S(1)} %pick.1), channel_id=1, source_target_pairs={{4,0},{0,4},{12,8},{8,12},{20,16},{16,20},{28,24},{24,28},{5,1},{1... | collective-permute-start | bytes 98312 | tf_op jit(solution)/shard_map/ppermute | solution.py:31
  7.2 4.9 %collective-permute-start.5 = (bf16[64,256]{1,0:T(8,128)(2,1)S(1)}, bf16[64,256]{1,0:T(8,128)(2,1)S(1)}, u32[]{:S(2)}, u32[]{:S(2)}) collective-permute-start(bf16[64,256]{1,0:T(8,128)(2,1)S(1)} %add.36), channel_id=1, source_target_pairs={{24,0},{28,4},{16,8},{20,12},{8,16},{12,20},{0,24},{4,28},{25,1},{... | collective-permute-start | bytes 98312 | tf_op jit(solution)/shard_map/ppermute | solution.py:31
  9.7 3.9 %collective-permute-start.4 = (bf16[64,256]{1,0:T(8,128)(2,1)S(1)}, bf16[64,256]{1,0:T(8,128)(2,1)S(1)}, u32[]{:S(2)}, u32[]{:S(2)}) collective-permute-start(bf16[64,256]{1,0:T(8,128)(2,1)S(1)} %add.36), channel_id=1, source_target_pairs={{16,0},{20,4},{24,8},{28,12},{0,16},{4,20},{8,24},{12,28},{17,1},{... | collective-permute-start | bytes 98312 | tf_op jit(solution)/shard_map/ppermute | solution.py:31
  10.2 3.9 %collective-permute-start.3 = (bf16[64,256]{1,0:T(8,128)(2,1)S(1)}, bf16[64,256]{1,0:T(8,128)(2,1)S(1)}, u32[]{:S(2)}, u32[]{:S(2)}) collective-permute-start(bf16[64,256]{1,0:T(8,128)(2,1)S(1)} %add.36), channel_id=1, source_target_pairs={{8,0},{12,4},{0,8},{4,12},{24,16},{28,20},{16,24},{20,28},{9,1},{1... | collective-permute-start | bytes 98312 | tf_op jit(solution)/shard_map/ppermute | solution.py:31
  14.2 7.5 %copy-start.1 = (f32[1024,64]{0,1:T(8,128)S(1)}, f32[1024,64]{0,1:T(8,128)}, u32[]{:S(2)}) copy-start(f32[1024,64]{0,1:T(8,128)} %param.9) | copy-start | bytes 786436
  14.2 6.2 %collective-permute-start.8 = (bf16[64,256]{1,0:T(8,128)(2,1)S(1)}, bf16[64,256]{1,0:T(8,128)(2,1)S(1)}, u32[]{:S(2)}, u32[]{:S(2)}) collective-permute-start(bf16[64,256]{1,0:T(8,128)(2,1)S(1)} %fusion.1), channel_id=1, source_target_pairs={{3,0},{2,1},{1,2},{0,3},{7,4},{6,5},{5,6},{4,7},{11,8},{10,9},{9,1... | collective-permute-start | bytes 98312 | tf_op jit(solution)/shard_map/ppermute | solution.py:31
  15.6 5.2 %collective-permute-start.7 = (bf16[64,256]{1,0:T(8,128)(2,1)S(1)}, bf16[64,256]{1,0:T(8,128)(2,1)S(1)}, u32[]{:S(2)}, u32[]{:S(2)}) collective-permute-start(bf16[64,256]{1,0:T(8,128)(2,1)S(1)} %fusion.1), channel_id=1, source_target_pairs={{2,0},{3,1},{0,2},{1,3},{6,4},{7,5},{4,6},{5,7},{10,8},{11,9},{8,1... | collective-permute-start | bytes 98312 | tf_op jit(solution)/shard_map/ppermute | solution.py:31
  17.3 4.3 %collective-permute-start.6 = (bf16[64,256]{1,0:T(8,128)(2,1)S(1)}, bf16[64,256]{1,0:T(8,128)(2,1)S(1)}, u32[]{:S(2)}, u32[]{:S(2)}) collective-permute-start(bf16[64,256]{1,0:T(8,128)(2,1)S(1)} %fusion.1), channel_id=1, source_target_pairs={{1,0},{0,1},{3,2},{2,3},{5,4},{4,5},{7,6},{6,7},{9,8},{8,9},{11,10... | collective-permute-start | bytes 98312 | tf_op jit(solution)/shard_map/ppermute | solution.py:31
  18.7 3.0 %copy-start.2 = (f32[256,64]{0,1:T(8,128)S(1)}, f32[256,64]{0,1:T(8,128)}, u32[]{:S(2)}) copy-start(f32[256,64]{0,1:T(8,128)} %param.8) | copy-start | bytes 196612
  18.7 10.9 %collective-permute-start.1 = (bf16[128,1024]{1,0:T(8,128)(2,1)S(1)}, bf16[128,1024]{1,0:T(8,128)(2,1)S(1)}, u32[]{:S(2)}, u32[]{:S(2)}) collective-permute-start(bf16[128,1024]{1,0:T(8,128)(2,1)S(1)} %pad_maximum_fusion.1), channel_id=1, source_target_pairs={{1,0},{0,1},{3,2},{2,3},{5,4},{4,5},{7,6},{6,7},{9,8},{8,9},{11,10... | collective-permute-start | bytes 786440 | tf_op jit(solution)/shard_map/ppermute | solution.py:31
  29.6 5.7 %collective-permute-start.10 = (bf16[64,1024]{1,0:T(8,128)(2,1)S(1)}, bf16[64,1024]{1,0:T(8,128)(2,1)S(1)}, u32[]{:S(2)}, u32[]{:S(2)}) collective-permute-start(bf16[64,1024]{1,0:T(8,128)(2,1)S(1)} %get-tuple-element.23), channel_id=1, source_target_pairs={{1,0},{0,1},{3,2},{2,3},{5,4},{4,5},{7,6},{6,7},{9,8},{8,9},{11,10... | collective-permute-start | bytes 393224 | tf_op jit(solution)/shard_map/ppermute | solution.py:31
  31.0 7.3 %collective-permute-start.9 = (bf16[64,1024]{1,0:T(8,128)(2,1)S(1)}, bf16[64,1024]{1,0:T(8,128)(2,1)S(1)}, u32[]{:S(2)}, u32[]{:S(2)}) collective-permute-start(bf16[64,1024]{1,0:T(8,128)(2,1)S(1)} %get-tuple-element.23), channel_id=1, source_target_pairs={{2,0},{3,1},{0,2},{1,3},{6,4},{7,5},{4,6},{5,7},{10,8},{11,9},{8,1... | collective-permute-start | bytes 393224 | tf_op jit(solution)/shard_map/ppermute | solution.py:31
  35.4 6.7 %collective-permute-start.13 = (bf16[128,1024]{1,0:T(8,128)(2,1)S(1)}, bf16[128,1024]{1,0:T(8,128)(2,1)S(1)}, u32[]{:S(2)}, u32[]{:S(2)}) collective-permute-start(bf16[128,1024]{1,0:T(8,128)(2,1)S(1)} %pad_maximum_fusion.2), channel_id=1, source_target_pairs={{28,0},{5,1},{30,2},{7,3},{0,4},{9,5},{2,6},{11,7},{4,8},{13,9},{6... | collective-permute-start | bytes 786440 | tf_op jit(solution)/shard_map/ppermute | solution.py:55
  38.4 8.3 %collective-permute-start.11 = (bf16[192,1024]{1,0:T(8,128)(2,1)S(1)}, bf16[192,1024]{1,0:T(8,128)(2,1)S(1)}, u32[]{:S(2)}, u32[]{:S(2)}) collective-permute-start(bf16[192,1024]{1,0:T(8,128)(2,1)S(1)} %pad_maximum_fusion), channel_id=1, source_target_pairs={{28,0},{29,1},{6,2},{7,3},{0,4},{1,5},{10,6},{11,7},{4,8},{5,9},{1... | collective-permute-start | bytes 1179656 | tf_op jit(solution)/shard_map/ppermute | solution.py:55
  38.6 7.2 %collective-permute-start.12 = (bf16[64,1024]{1,0:T(8,128)(2,1)S(1)}, bf16[64,1024]{1,0:T(8,128)(2,1)S(1)}, u32[]{:S(2)}, u32[]{:S(2)}) collective-permute-start(bf16[64,1024]{1,0:T(8,128)(2,1)S(1)} %add.46.refs_4_), channel_id=1, source_target_pairs={{1,0},{0,1},{3,2},{2,3},{5,4},{4,5},{7,6},{6,7},{9,8},{8,9},{11,10... | collective-permute-start | bytes 393224 | tf_op jit(solution)/shard_map/ppermute | solution.py:31
  45.8 5.3 %collective-permute-start.14 = (bf16[64,1024]{1,0:T(8,128)(2,1)S(1)}, bf16[64,1024]{1,0:T(8,128)(2,1)S(1)}, u32[]{:S(2)}, u32[]{:S(2)}) collective-permute-start(bf16[64,1024]{1,0:T(8,128)(2,1)S(1)} %add.47.refs_2_), channel_id=1, source_target_pairs={{28,0},{29,1},{6,2},{7,3},{0,4},{1,5},{10,6},{11,7},{4,8},{5,9},{1... | collective-permute-start | bytes 393224 | tf_op jit(solution)/shard_map/ppermute | solution.py:55

commit v21 on v17

--- a/solution.py
+++ b/solution.py
@@ -189,7 +189,12 @@
         front, values = halfway(values)
         return front + rear(values)
 
-    return solve, upper + rear(lower), coming
+    def solve_back(values):
+        last = [total_of([two[k][m] * values[4 + k] for k in range(m, 4)]) for m in range(4)]
+        rest = [values[j] - total_of([below[m][j] * last[m] for m in range(4)]) for j in range(4)]
+        return [total_of([one[k][j] * rest[k] for k in range(j, 4)]) for j in range(4)] + last
+
+    return solve, solve_back, upper + rear(lower), coming
 
 
 def inverse_factor(strips, beside):
@@ -199,13 +204,30 @@
     result = []
     waiting = []
 
-    def finish(p, own, solve, rows):
-        def update(r):
-            factors = solve([column(strips[r], p * STRIP + j) for j in range(STRIP)])
+    def finish(p, own, solve, solve_back, rows):
+        spanned = []
+
+        def subtract(r, factors, rows):
             terms = [factors[k] * rows[k] for k in range(STRIP)]
             strips[r] = jnp.where(own, 0.0, strips[r]) - total_of(terms)
 
-        return [functools.partial(update, r) for r in range(p + 2, len(strips))]
+        def columns_of(r):
+            return [column(strips[r], p * STRIP + j) for j in range(STRIP)]
+
+        def second(r):
+            subtract(r, solve(columns_of(r)), rows)
+
+        def span():
+            spanned.extend(solve_back(rows))
+
+        def later(r):
+            subtract(r, columns_of(r), spanned)
+
+        count = len(strips)
+        steps = [functools.partial(second, p + 2)] if p + 2 < count else []
+        if p + 3 < count:
+            steps += [span] + [functools.partial(later, r) for r in range(p + 3, count)]
+        return steps
 
     columns = [column(strips[0], k) for k in range(STRIP)]
     for p in range(len(strips)):
@@ -225,7 +247,7 @@
             try:
                 next(steps)
             except StopIteration as ended:
-                solve, rows, coming = ended.value
+                solve, solve_back, rows, coming = ended.value
                 break
             for _ in range(2):
                 if waiting:
@@ -240,7 +262,7 @@
             found, columns = coming
             update = total_of([found[k] * rows[k] for k in range(STRIP)])
             strips[p + 1] = jnp.where(own, 0.0, strips[p + 1]) - update
-            waiting = finish(p, own, solve, rows)
+            waiting = finish(p, own, solve, solve_back, rows)
     return [jnp.where(lane < (p + 1) * STRIP, done, 0.0) for p, done in enumerate(result)]
 
 

time: 52.4 us -> 51.7 us (0.987)
  Pallas kernels: 20.8 us -> 20.2 us
    pallas_call x1, Pallas kernels: 7.89 us -> 7.22 us  [probes_of(): pl.pallas_call(probe_kernel, out_shape=(pltpu.VMEM((size, size), jnp.floa...]
  transfers between devices with their start and end apart: 15 -> 15, of which waited for: 11 -> 11; matrix products, arithmetic and copies ran while one was open for 0% -> 0% of each run, Pallas kernels for 36% -> 35%
where the time goes in v21:
time: 51.7 us; the launch traced here: 51.6 us
  Pallas kernels  20.2 us (39%)
  starting transfers between devices  15.4 us (30%)
  waiting for transfers between devices  14.9 us (29%)
  between operations  0.84 us (2%)
    ppermute x12, starting transfers between devices, swapped(): lax.ppermute(value, axis, [(i ^ bit, i) for i in range(lax.axis_size(axis...  15.1 us
    ppermute x12, waiting for transfers between devices, swapped(): lax.ppermute(value, axis, [(i ^ bit, i) for i in range(lax.axis_size(axis...  12.1 us
    pallas_call x5, Pallas kernels, band_sum(): pl.pallas_call(functools.partial(band_kernel, tuple(places), first, last)...  9.85 us
    pallas_call x1, Pallas kernels, probes_of(): pl.pallas_call(probe_kernel, out_shape=(pltpu.VMEM((size, size), jnp.floa...  7.22 us
    ppermute x3, waiting for transfers between devices, cross(): return lax.ppermute(piece, ('gx', 'gy'), pairs)  2.82 us
    pallas_call x1, Pallas kernels, factor_of(): pl.pallas_call(factor_kernel, out_shape=(jax.ShapeDtypeStruct((count, siz...  1.91 us
    pallas_call x1, Pallas kernels, pick(): pl.pallas_call(pick_kernel, out_shape=pltpu.VMEM((points_t.shape[0], 2 *...  1.17 us
  transfers between devices with their start and end apart: 15, of which 11 were waited for; matrix products, arithmetic and copies ran while one was open for 0% of the time, Pallas kernels for 35%

profile of v21, /device:TPU:0, one launch (start us, length us, event | category | flops | bytes accessed | tf_op | source)
XLA Modules:
  0.0 51.6 jit_solution(11891883541035951077)
XLA Ops:
  0.6 4.1 %collective-permute-start = (bf16[64,1024]{1,0:T(8,128)(2,1)}, bf16[64,1024]{1,0:T(8,128)(2,1)S(1)}, u32[]{:S(2)}, u32[]{:S(2)}) collective-permute-start(bf16[64,1024]{1,0:T(8,128)(2,1)} %bitcast.4), channel_id=1, source_target_pairs={{2,0},{3,1},{0,2},{1,3},{6,4},{7,5},{4,6},{5,7},{10,8},{11,9},{8,1... | collective-permute-start | bytes 393224 | tf_op jit(solution)/shard_map/ppermute | solution.py:31
  4.7 1.2 %pick.1 = bf16[64,256]{1,0:T(8,128)(2,1)S(1)} custom-call(s32[2]{0:T(128)} %owner_ref.1, s32[2,128]{1,0:T(2,128)} %pivot_ref.1, bf16[64,1024]{1,0:T(8,128)(2,1)} %bitcast.5), custom_call_target="tpu_custom_call" | custom-call | tf_op jit(solution)/shard_map/pick/pallas_call | solution.py:107
  5.9 0.1 collective-permute-start.2
  6.0 1.2 %collective-permute-done.2 = bf16[64,256]{1,0:T(8,128)(2,1)S(1)} collective-permute-done((bf16[64,256]{1,0:T(8,128)(2,1)S(1)}, bf16[64,256]{1,0:T(8,128)(2,1)S(1)}, u32[]{:S(2)}, u32[]{:S(2)}) %collective-permute-start.2) | collective-permute-done | bytes 32800 | tf_op jit(solution)/shard_map/ppermute | solution.py:31
  7.2 2.5 %collective-permute-start.5 = (bf16[64,256]{1,0:T(8,128)(2,1)S(1)}, bf16[64,256]{1,0:T(8,128)(2,1)S(1)}, u32[]{:S(2)}, u32[]{:S(2)}) collective-permute-start(bf16[64,256]{1,0:T(8,128)(2,1)S(1)} %add.36), channel_id=1, source_target_pairs={{24,0},{28,4},{16,8},{20,12},{8,16},{12,20},{0,24},{4,28},{25,1},{... | collective-permute-start | bytes 98312 | tf_op jit(solution)/shard_map/ppermute | solution.py:31
  9.7 0.5 collective-permute-start.4
  10.2 0.5 %collective-permute-start.3 = (bf16[64,256]{1,0:T(8,128)(2,1)S(1)}, bf16[64,256]{1,0:T(8,128)(2,1)S(1)}, u32[]{:S(2)}, u32[]{:S(2)}) collective-permute-start(bf16[64,256]{1,0:T(8,128)(2,1)S(1)} %add.36), channel_id=1, source_target_pairs={{8,0},{12,4},{0,8},{4,12},{24,16},{28,20},{16,24},{20,28},{9,1},{1... | collective-permute-start | bytes 98312 | tf_op jit(solution)/shard_map/ppermute | solution.py:31
  10.8 1.3 %collective-permute-done.5 = bf16[64,256]{1,0:T(8,128)(2,1)S(1)} collective-permute-done((bf16[64,256]{1,0:T(8,128)(2,1)S(1)}, bf16[64,256]{1,0:T(8,128)(2,1)S(1)}, u32[]{:S(2)}, u32[]{:S(2)}) %collective-permute-start.5) | collective-permute-done | bytes 32800 | tf_op jit(solution)/shard_map/ppermute | solution.py:31
  12.1 1.5 %collective-permute-done.4 = bf16[64,256]{1,0:T(8,128)(2,1)S(1)} collective-permute-done((bf16[64,256]{1,0:T(8,128)(2,1)S(1)}, bf16[64,256]{1,0:T(8,128)(2,1)S(1)}, u32[]{:S(2)}, u32[]{:S(2)}) %collective-permute-start.4) | collective-permute-done | bytes 32800 | tf_op jit(solution)/shard_map/ppermute | solution.py:31
  13.6 0.5 collective-permute-done.3
  14.2 1.4 %collective-permute-start.8 = (bf16[64,256]{1,0:T(8,128)(2,1)S(1)}, bf16[64,256]{1,0:T(8,128)(2,1)S(1)}, u32[]{:S(2)}, u32[]{:S(2)}) collective-permute-start(bf16[64,256]{1,0:T(8,128)(2,1)S(1)} %fusion.1), channel_id=1, source_target_pairs={{3,0},{2,1},{1,2},{0,3},{7,4},{6,5},{5,6},{4,7},{11,8},{10,9},{9,1... | collective-permute-start | bytes 98312 | tf_op jit(solution)/shard_map/ppermute | solution.py:31
  15.6 1.7 %collective-permute-start.7 = (bf16[64,256]{1,0:T(8,128)(2,1)S(1)}, bf16[64,256]{1,0:T(8,128)(2,1)S(1)}, u32[]{:S(2)}, u32[]{:S(2)}) collective-permute-start(bf16[64,256]{1,0:T(8,128)(2,1)S(1)} %fusion.1), channel_id=1, source_target_pairs={{2,0},{3,1},{0,2},{1,3},{6,4},{7,5},{4,6},{5,7},{10,8},{11,9},{8,1... | collective-permute-start | bytes 98312 | tf_op jit(solution)/shard_map/ppermute | solution.py:31
  17.3 1.3 %collective-permute-start.6 = (bf16[64,256]{1,0:T(8,128)(2,1)S(1)}, bf16[64,256]{1,0:T(8,128)(2,1)S(1)}, u32[]{:S(2)}, u32[]{:S(2)}) collective-permute-start(bf16[64,256]{1,0:T(8,128)(2,1)S(1)} %fusion.1), channel_id=1, source_target_pairs={{1,0},{0,1},{3,2},{2,3},{5,4},{4,5},{7,6},{6,7},{9,8},{8,9},{11,10... | collective-permute-start | bytes 98312 | tf_op jit(solution)/shard_map/ppermute | solution.py:31
  18.7 0.7 %collective-permute-start.1 = (bf16[128,1024]{1,0:T(8,128)(2,1)S(1)}, bf16[128,1024]{1,0:T(8,128)(2,1)S(1)}, u32[]{:S(2)}, u32[]{:S(2)}) collective-permute-start(bf16[128,1024]{1,0:T(8,128)(2,1)S(1)} %pad_maximum_fusion), channel_id=1, source_target_pairs={{1,0},{0,1},{3,2},{2,3},{5,4},{4,5},{7,6},{6,7},{9,8},{8,9},{11,10... | collective-permute-start | bytes 786440 | tf_op jit(solution)/shard_map/ppermute | solution.py:31
  19.4 1.0 %collective-permute-done.8 = bf16[64,256]{1,0:T(8,128)(2,1)S(1)} collective-permute-done((bf16[64,256]{1,0:T(8,128)(2,1)S(1)}, bf16[64,256]{1,0:T(8,128)(2,1)S(1)}, u32[]{:S(2)}, u32[]{:S(2)}) %collective-permute-start.8) | collective-permute-done | bytes 32800 | tf_op jit(solution)/shard_map/ppermute | solution.py:31
  20.4 0.3 collective-permute-done.7
  20.8 0.9 %collective-permute-done.6 = bf16[64,256]{1,0:T(8,128)(2,1)S(1)} collective-permute-done((bf16[64,256]{1,0:T(8,128)(2,1)S(1)}, bf16[64,256]{1,0:T(8,128)(2,1)S(1)}, u32[]{:S(2)}, u32[]{:S(2)}) %collective-permute-start.6) | collective-permute-done | bytes 32800 | tf_op jit(solution)/shard_map/ppermute | solution.py:31
  21.6 7.2 %probes.1 = (f32[256,256]{1,0:T(8,128)S(1)}, f32[64,1024]{1,0:T(8,128)S(1)}, bf16[64,1024]{1,0:T(8,128)(2,1)S(1)}) custom-call(bf16[64,256]{1,0:T(8,128)(2,1)S(1)} %add_add_fusion.pivot_ref, bf16[64,1024]{1,0:T(8,128)(2,1)S(1)} %bitcast.7, f32[64,256]{1,0:T(8,128)S(1)} %bitcast.15, f32[64,1024]{1,0:T(8,128)S(1)} %bitcast.14), custom_call_target="tpu_custom_call" | custom-call | flops 17179869184 | bytes 1 | tf_op jit(solution)/shard_map/probes/pallas_call | solution.py:321
  28.9 1.4 %collective-permute-start.10 = (bf16[64,1024]{1,0:T(8,128)(2,1)S(1)}, bf16[64,1024]{1,0:T(8,128)(2,1)S(1)}, u32[]{:S(2)}, u32[]{:S(2)}) collective-permute-start(bf16[64,1024]{1,0:T(8,128)(2,1)S(1)} %get-tuple-element.25), channel_id=1, source_target_pairs={{1,0},{0,1},{3,2},{2,3},{5,4},{4,5},{7,6},{6,7},{9,8},{8,9},{11,10... | collective-permute-start | bytes 393224 | tf_op jit(solution)/shard_map/ppermute | solution.py:31
  30.3 0.7 %collective-permute-start.9 = (bf16[64,1024]{1,0:T(8,128)(2,1)S(1)}, bf16[64,1024]{1,0:T(8,128)(2,1)S(1)}, u32[]{:S(2)}, u32[]{:S(2)}) collective-permute-start(bf16[64,1024]{1,0:T(8,128)(2,1)S(1)} %get-tuple-element.25), channel_id=1, source_target_pairs={{2,0},{3,1},{0,2},{1,3},{6,4},{7,5},{4,6},{5,7},{10,8},{11,9},{8,1... | collective-permute-start | bytes 393224 | tf_op jit(solution)/shard_map/ppermute | solution.py:31
  31.0 1.4 %band_sum.5 = (f32[1024,64]{1,0:T(8,128)S(1)}, bf16[64,1024]{1,0:T(8,128)(2,1)S(1)}) custom-call(bf16[64,1024]{1,0:T(8,128)(2,1)S(1)} %bitcast.8, bf16[64,1024]{1,0:T(8,128)(2,1)S(1)} %get-tuple-element.13.refs_1_), custom_call_target="tpu_custom_call" | custom-call | flops 1 | bytes 1 | tf_op jit(solution)/shard_map/band_sum/pallas_call | solution.py:425
  32.4 2.2 %collective-permute-done.10 = bf16[64,1024]{1,0:T(8,128)(2,1)S(1)} collective-permute-done((bf16[64,1024]{1,0:T(8,128)(2,1)S(1)}, bf16[64,1024]{1,0:T(8,128)(2,1)S(1)}, u32[]{:S(2)}, u32[]{:S(2)}) %collective-permute-start.10) | collective-permute-done | bytes 131104 | tf_op jit(solution)/shard_map/ppermute | solution.py:31
  34.8 1.9 %factor.1 = (f32[1024,256]{1,0:T(8,128)}, bf16[64,1024]{1,0:T(8,128)(2,1)S(1)}) custom-call(bf16[64,256]{1,0:T(8,128)(2,1)S(1)} %add_add_fusion.pivot_ref, bf16[64,1024]{1,0:T(8,128)(2,1)S(1)} %bitcast.9, f32[256,256]{1,0:T(8,128)S(1)} %get-tuple-element.14.inverse_ref, bf16[64,1024]{1,0:T(8,128)(2,1)S(1)} %add.45.awaited_ref.refs_2_), custom_call_target="tpu_custom_call" | custom-call | flops 50331648 | bytes 196608 | tf_op jit(solution)/shard_map/factor/pallas_call | solution.py:362
  36.7 0.9 %collective-permute-done.9 = bf16[64,1024]{1,0:T(8,128)(2,1)S(1)} collective-permute-done((bf16[64,1024]{1,0:T(8,128)(2,1)S(1)}, bf16[64,1024]{1,0:T(8,128)(2,1)S(1)}, u32[]{:S(2)}, u32[]{:S(2)}) %collective-permute-start.9) | collective-permute-done | bytes 131104 | tf_op jit(solution)/shard_map/ppermute | solution.py:31
  37.6 0.1 collective-permute-start.11
  37.7 0.2 collective-permute-start.13
  38.0 2.5 %band_sum.6 = (f32[1024,64]{1,0:T(8,128)S(1)}, bf16[64,1024]{1,0:T(8,128)(2,1)S(1)}) custom-call(bf16[64,1024]{1,0:T(8,128)(2,1)S(1)} %bitcast.10, bf16[128,1024]{1,0:T(8,128)(2,1)S(1)} %collective-permute-done.1.refs_1_, bf16[64,1024]{1,0:T(8,128)(2,1)S(1)} %add.45.awaited_ref.refs_2_, bf16[64,1024]{1,0:T(8,128)(2,1)S(1)} %collective-permute-done.refs_3_, ...), custom_call_target="tpu_custom_call" | custom-call | flops 1073741824 | bytes 1572864 | tf_op jit(solution)/shard_map/band_sum/pallas_call | solution.py:425
  40.5 2.1 %collective-permute-done.11.refs_2_ = bf16[64,1024]{1,0:T(8,128)(2,1)S(1)} collective-permute-done((bf16[64,1024]{1,0:T(8,128)(2,1)S(1)}, bf16[64,1024]{1,0:T(8,128)(2,1)S(1)}, u32[]{:S(2)}, u32[]{:S(2)}) %collective-permute-start.11) | collective-permute-done | bytes 131104 | tf_op jit(solution)/shard_map/ppermute | solution.py:31
  42.8 2.5 %band_sum.7 = (f32[1024,64]{1,0:T(8,128)S(1)}, bf16[64,1024]{1,0:T(8,128)(2,1)}) custom-call(bf16[64,1024]{1,0:T(8,128)(2,1)S(1)} %bitcast.11, bf16[128,1024]{1,0:T(8,128)(2,1)S(1)} %collective-permute-done.1.refs_1_, bf16[64,1024]{1,0:T(8,128)(2,1)S(1)} %collective-permute-done.11.refs_2_, bf16[128,1024]{1,0:T(8,128)(2,1)S(1)} %collective-permute-done.14.refs_3_, ...), custom_call_target="tpu_custom_call" | custom-call | flops 1073741824 | bytes 1310720 | tf_op jit(solution)/shard_map/band_sum/pallas_call | solution.py:425
  45.4 1.3 %band_sum.8 = (f32[1024,64]{1,0:T(8,128)S(1)}, bf16[64,1024]{1,0:T(8,128)(2,1)}) custom-call(bf16[64,1024]{1,0:T(8,128)(2,1)S(1)} %bitcast.12, bf16[128,1024]{1,0:T(8,128)(2,1)S(1)} %collective-permute-done.13.refs_1_, f32[1024,64]{1,0:T(8,128)S(1)} %get-tuple-element.20.refs_2_), custom_call_target="tpu_custom_call" | custom-call | flops 536870912 | bytes 786432 | tf_op jit(solution)/shard_map/band_sum/pallas_call | solution.py:425
  46.7 2.8 %collective-permute-done.12.refs_1_ = bf16[128,1024]{1,0:T(8,128)(2,1)S(1)} collective-permute-done((bf16[128,1024]{1,0:T(8,128)(2,1)S(1)}, bf16[128,1024]{1,0:T(8,128)(2,1)S(1)}, u32[]{:S(2)}, u32[]{:S(2)}) %collective-permute-start.12) | collective-permute-done | bytes 262176 | tf_op jit(solution)/shard_map/ppermute | solution.py:55
  49.5 2.1 %band_sum.9 = f32[64,1024]{1,0:T(8,128)} custom-call(bf16[64,1024]{1,0:T(8,128)(2,1)S(1)} %bitcast.13, bf16[128,1024]{1,0:T(8,128)(2,1)S(1)} %collective-permute-done.12.refs_1_, f32[1024,64]{1,0:T(8,128)S(1)} %get-tuple-element.21.refs_2_, f32[64,1024]{1,0:T(8,128)S(1)} %get-tuple-element.22.refs_3_), custom_call_target="tpu_custom_call" | custom-call | flops 536870912 | bytes 1048576 | tf_op jit(solution)/shard_map/band_sum/pallas_call | solution.py:425
  (23 shorter events, 0.4 us)
Async XLA Ops:
  0.6 13.5 %collective-permute-start = (bf16[64,1024]{1,0:T(8,128)(2,1)}, bf16[64,1024]{1,0:T(8,128)(2,1)S(1)}, u32[]{:S(2)}, u32[]{:S(2)}) collective-permute-start(bf16[64,1024]{1,0:T(8,128)(2,1)} %bitcast.4), channel_id=1, source_target_pairs={{2,0},{3,1},{0,2},{1,3},{6,4},{7,5},{4,6},{5,7},{10,8},{11,9},{8,1... | collective-permute-start | bytes 393224 | tf_op jit(solution)/shard_map/ppermute | solution.py:31
  5.9 12.7 %copy-start = (bf16[1024,64]{0,1:T(8,128)(2,1)S(1)}, bf16[1024,64]{0,1:T(8,128)(2,1)}, u32[]{:S(2)}) copy-start(bf16[1024,64]{0,1:T(8,128)(2,1)} %param.5) | copy-start | bytes 393220
  5.9 1.3 %collective-permute-start.2 = (bf16[64,256]{1,0:T(8,128)(2,1)S(1)}, bf16[64,256]{1,0:T(8,128)(2,1)S(1)}, u32[]{:S(2)}, u32[]{:S(2)}) collective-permute-start(bf16[64,256]{1,0:T(8,128)(2,1)S(1)} %pick.1), channel_id=1, source_target_pairs={{4,0},{0,4},{12,8},{8,12},{20,16},{16,20},{28,24},{24,28},{5,1},{1... | collective-permute-start | bytes 98312 | tf_op jit(solution)/shard_map/ppermute | solution.py:31
  7.2 4.9 %collective-permute-start.5 = (bf16[64,256]{1,0:T(8,128)(2,1)S(1)}, bf16[64,256]{1,0:T(8,128)(2,1)S(1)}, u32[]{:S(2)}, u32[]{:S(2)}) collective-permute-start(bf16[64,256]{1,0:T(8,128)(2,1)S(1)} %add.36), channel_id=1, source_target_pairs={{24,0},{28,4},{16,8},{20,12},{8,16},{12,20},{0,24},{4,28},{25,1},{... | collective-permute-start | bytes 98312 | tf_op jit(solution)/shard_map/ppermute | solution.py:31
  9.7 3.9 %collective-permute-start.4 = (bf16[64,256]{1,0:T(8,128)(2,1)S(1)}, bf16[64,256]{1,0:T(8,128)(2,1)S(1)}, u32[]{:S(2)}, u32[]{:S(2)}) collective-permute-start(bf16[64,256]{1,0:T(8,128)(2,1)S(1)} %add.36), channel_id=1, source_target_pairs={{16,0},{20,4},{24,8},{28,12},{0,16},{4,20},{8,24},{12,28},{17,1},{... | collective-permute-start | bytes 98312 | tf_op jit(solution)/shard_map/ppermute | solution.py:31
  10.2 3.9 %collective-permute-start.3 = (bf16[64,256]{1,0:T(8,128)(2,1)S(1)}, bf16[64,256]{1,0:T(8,128)(2,1)S(1)}, u32[]{:S(2)}, u32[]{:S(2)}) collective-permute-start(bf16[64,256]{1,0:T(8,128)(2,1)S(1)} %add.36), channel_id=1, source_target_pairs={{8,0},{12,4},{0,8},{4,12},{24,16},{28,20},{16,24},{20,28},{9,1},{1... | collective-permute-start | bytes 98312 | tf_op jit(solution)/shard_map/ppermute | solution.py:31
  14.2 7.5 %copy-start.1 = (f32[1024,64]{0,1:T(8,128)S(1)}, f32[1024,64]{0,1:T(8,128)}, u32[]{:S(2)}) copy-start(f32[1024,64]{0,1:T(8,128)} %param.9) | copy-start | bytes 786436
  14.2 6.2 %collective-permute-start.8 = (bf16[64,256]{1,0:T(8,128)(2,1)S(1)}, bf16[64,256]{1,0:T(8,128)(2,1)S(1)}, u32[]{:S(2)}, u32[]{:S(2)}) collective-permute-start(bf16[64,256]{1,0:T(8,128)(2,1)S(1)} %fusion.1), channel_id=1, source_target_pairs={{3,0},{2,1},{1,2},{0,3},{7,4},{6,5},{5,6},{4,7},{11,8},{10,9},{9,1... | collective-permute-start | bytes 98312 | tf_op jit(solution)/shard_map/ppermute | solution.py:31
  15.6 5.2 %collective-permute-start.7 = (bf16[64,256]{1,0:T(8,128)(2,1)S(1)}, bf16[64,256]{1,0:T(8,128)(2,1)S(1)}, u32[]{:S(2)}, u32[]{:S(2)}) collective-permute-start(bf16[64,256]{1,0:T(8,128)(2,1)S(1)} %fusion.1), channel_id=1, source_target_pairs={{2,0},{3,1},{0,2},{1,3},{6,4},{7,5},{4,6},{5,7},{10,8},{11,9},{8,1... | collective-permute-start | bytes 98312 | tf_op jit(solution)/shard_map/ppermute | solution.py:31
  17.3 4.3 %collective-permute-start.6 = (bf16[64,256]{1,0:T(8,128)(2,1)S(1)}, bf16[64,256]{1,0:T(8,128)(2,1)S(1)}, u32[]{:S(2)}, u32[]{:S(2)}) collective-permute-start(bf16[64,256]{1,0:T(8,128)(2,1)S(1)} %fusion.1), channel_id=1, source_target_pairs={{1,0},{0,1},{3,2},{2,3},{5,4},{4,5},{7,6},{6,7},{9,8},{8,9},{11,10... | collective-permute-start | bytes 98312 | tf_op jit(solution)/shard_map/ppermute | solution.py:31
  18.7 3.0 %copy-start.2 = (f32[256,64]{0,1:T(8,128)S(1)}, f32[256,64]{0,1:T(8,128)}, u32[]{:S(2)}) copy-start(f32[256,64]{0,1:T(8,128)} %param.8) | copy-start | bytes 196612
  18.7 10.2 %collective-permute-start.1 = (bf16[128,1024]{1,0:T(8,128)(2,1)S(1)}, bf16[128,1024]{1,0:T(8,128)(2,1)S(1)}, u32[]{:S(2)}, u32[]{:S(2)}) collective-permute-start(bf16[128,1024]{1,0:T(8,128)(2,1)S(1)} %pad_maximum_fusion), channel_id=1, source_target_pairs={{1,0},{0,1},{3,2},{2,3},{5,4},{4,5},{7,6},{6,7},{9,8},{8,9},{11,10... | collective-permute-start | bytes 786440 | tf_op jit(solution)/shard_map/ppermute | solution.py:31
  28.9 5.7 %collective-permute-start.10 = (bf16[64,1024]{1,0:T(8,128)(2,1)S(1)}, bf16[64,1024]{1,0:T(8,128)(2,1)S(1)}, u32[]{:S(2)}, u32[]{:S(2)}) collective-permute-start(bf16[64,1024]{1,0:T(8,128)(2,1)S(1)} %get-tuple-element.25), channel_id=1, source_target_pairs={{1,0},{0,1},{3,2},{2,3},{5,4},{4,5},{7,6},{6,7},{9,8},{8,9},{11,10... | collective-permute-start | bytes 393224 | tf_op jit(solution)/shard_map/ppermute | solution.py:31
  30.3 7.3 %collective-permute-start.9 = (bf16[64,1024]{1,0:T(8,128)(2,1)S(1)}, bf16[64,1024]{1,0:T(8,128)(2,1)S(1)}, u32[]{:S(2)}, u32[]{:S(2)}) collective-permute-start(bf16[64,1024]{1,0:T(8,128)(2,1)S(1)} %get-tuple-element.25), channel_id=1, source_target_pairs={{2,0},{3,1},{0,2},{1,3},{6,4},{7,5},{4,6},{5,7},{10,8},{11,9},{8,1... | collective-permute-start | bytes 393224 | tf_op jit(solution)/shard_map/ppermute | solution.py:31
  34.7 8.1 %collective-permute-start.14 = (bf16[128,1024]{1,0:T(8,128)(2,1)S(1)}, bf16[128,1024]{1,0:T(8,128)(2,1)S(1)}, u32[]{:S(2)}, u32[]{:S(2)}) collective-permute-start(bf16[128,1024]{1,0:T(8,128)(2,1)S(1)} %pad_maximum_fusion.3), channel_id=1, source_target_pairs={{28,0},{5,1},{30,2},{7,3},{0,4},{9,5},{2,6},{11,7},{4,8},{13,9},{6... | collective-permute-start | bytes 786440 | tf_op jit(solution)/shard_map/ppermute | solution.py:55
  37.6 5.0 %collective-permute-start.11 = (bf16[64,1024]{1,0:T(8,128)(2,1)S(1)}, bf16[64,1024]{1,0:T(8,128)(2,1)S(1)}, u32[]{:S(2)}, u32[]{:S(2)}) collective-permute-start(bf16[64,1024]{1,0:T(8,128)(2,1)S(1)} %add.46.refs_4_), channel_id=1, source_target_pairs={{1,0},{0,1},{3,2},{2,3},{5,4},{4,5},{7,6},{6,7},{9,8},{8,9},{11,10... | collective-permute-start | bytes 393224 | tf_op jit(solution)/shard_map/ppermute | solution.py:31
  37.7 7.6 %collective-permute-start.13 = (bf16[128,1024]{1,0:T(8,128)(2,1)S(1)}, bf16[128,1024]{1,0:T(8,128)(2,1)S(1)}, u32[]{:S(2)}, u32[]{:S(2)}) collective-permute-start(bf16[128,1024]{1,0:T(8,128)(2,1)S(1)} %pad_maximum_fusion.2), channel_id=1, source_target_pairs={{28,0},{29,1},{6,2},{7,3},{0,4},{1,5},{10,6},{11,7},{4,8},{5,9},{1... | collective-permute-start | bytes 786440 | tf_op jit(solution)/shard_map/ppermute | solution.py:55
  42.7 6.7 %collective-permute-start.12 = (bf16[128,1024]{1,0:T(8,128)(2,1)S(1)}, bf16[128,1024]{1,0:T(8,128)(2,1)S(1)}, u32[]{:S(2)}, u32[]{:S(2)}) collective-permute-start(bf16[128,1024]{1,0:T(8,128)(2,1)S(1)} %pad_maximum_fusion.1), channel_id=1, source_target_pairs={{28,0},{29,1},{6,2},{7,3},{0,4},{1,5},{10,6},{11,7},{4,8},{5,9},{1... | collective-permute-start | bytes 786440 | tf_op jit(solution)/shard_map/ppermute | solution.py:55
